TPU v7x, 32 devices: a whole 2x2x4 slice. The times are simulated.
32 devices in a mesh: section: 4 (over z), dp: 8 (over y, x, core).
Axes of the slice: x: 2, y: 2, z: 4, core: 2. Of those that a mesh axis runs over, the one named last changes fastest.
Arguments:
- x0: bfloat16 [4, 256, 5120], P(None, 'dp'), may hold values from -6 to 6
- w_key: bfloat16 [4, 5120, 512], P('section'), may hold values from -0.078125 to 0.078125
- w_value: bfloat16 [4, 5120, 512], P('section'), may hold values from -0.078125 to 0.078125
- w_score: float32 [5120], replicated, may hold values from -0.078125 to 0.078125
- segments: int32 [4, 256], P(None, 'dp'), may hold values from 0 to 31, as said below
- lengths: int32 [4, 8], P(None, 'dp'), may hold values from 1 to 32, as said below
- grades: int32 [4, 256], P(None, 'dp'), may hold values from 0 to 3
Outputs:
- grad_key: float32 [4, 5120, 512], P('section', 'dp')
- grad_value: float32 [4, 5120, 512], P('section', 'dp')
Inputs may be any that keep to these rules, and one draw needn't show every extreme that they name: `segments`: within each packed row of 32 slots the ids start at 0 and never fall; in every draw some packed row has a new id at every slot. `lengths`: every packed row has its live tokens at the front; in every draw some packed row is full.
All inputs are finite; a program needn't handle non-finite values.
Results may differ from a plain program's by a relative error of at most 0.035.
Values may be sent and summed in bfloat16 or wider, within the bound.
No kernel may reach another device: no remote copies, remote signals or barrier semaphores. Data moves between devices by JAX's collectives and lax.ppermute only.
A program may use at most 128 MiB of HBM per device.

v0:
```python
import jax
import jax.numpy as jnp
from jax import lax
from jax.sharding import PartitionSpec as P

HD = 128
KV_HEADS = 4


EPS = 1e-06
THETA = 1000000.0


def shifted(value, axis, steps):
    count = lax.axis_size(axis)
    first, last = (max(0, -steps), min(count, count - steps))
    return lax.ppermute(value, axis, [(source, source + steps) for source in range(first, last)])


def rope_tables(segments):
    width = segments.shape[-1]
    index = jnp.arange(width, dtype=jnp.int32)
    section_begin_offsets = jnp.concatenate(
        [jnp.ones(segments.shape[:-1] + (1,), bool), segments[..., 1:] != segments[..., :-1]],
        axis=-1,
    )
    leading_half = lax.cummax(
        jnp.where(section_begin_offsets, index, jnp.int32(0)), axis=segments.ndim - 1
    )
    offset = (index - leading_half).astype(jnp.float32)
    freqs = THETA ** (-(jnp.arange(HD // 2, dtype=jnp.float32) * 2.0) / HD)
    angles = offset[..., None] * freqs
    return (jnp.cos(angles), jnp.sin(angles))


def allowed_mask(segments, lengths):
    width = segments.shape[-1]
    index = jnp.arange(width, dtype=jnp.int32)
    same = segments[..., :, None] == segments[..., None, :]
    causal = index[None, :] <= index[:, None]
    live = index < lengths
    allowed = same & causal & live[..., :, None] & live[..., None, :]
    return allowed | jnp.eye(width, dtype=bool)


def rotate(vectors, cosine, sine_table):
    half = HD // 2
    cosine_value = cosine[..., :, None, :]
    sine_value = sine_table[..., :, None, :]
    leading_half, trailing_half = (vectors[..., :half], vectors[..., half:])
    return jnp.concatenate(
        [
            leading_half * cosine_value - trailing_half * sine_value,
            trailing_half * cosine_value + leading_half * sine_value,
        ],
        axis=-1,
    )


def rotate_back(grads, cosine, sine_table):
    half = HD // 2
    cosine_value = cosine[..., :, None, :]
    sine_value = sine_table[..., :, None, :]
    leading_half, trailing_half = (grads[..., :half], grads[..., half:])
    return jnp.concatenate(
        [
            leading_half * cosine_value + trailing_half * sine_value,
            trailing_half * cosine_value - leading_half * sine_value,
        ],
        axis=-1,
    )


def normalize(hidden):
    hfull = hidden.astype(jnp.float32)
    scale = lax.rsqrt(jnp.mean(hfull * hfull, axis=-1, keepdims=True) + EPS)
    return (hfull, scale)


def heads(array):
    return array.reshape(array.shape[:-1] + (KV_HEADS, HD))


def times_transposed(left, right):
    return lax.dot_general(
        left, right, (((1,), (1,)), ((), ())), preferred_element_type=jnp.float32
    )


def over_tokens(left, right):
    return lax.dot_general(
        left, right, (((0,), (0,)), ((), ())), preferred_element_type=jnp.float32
    )


def attend(keys_b, values_b, allowed):
    scores = jnp.einsum("ihd,jhd->hij", keys_b, keys_b, preferred_element_type=jnp.float32) / HD
    scores = jnp.where(allowed[None, :, :], scores, -1e30)
    probs = jax.nn.softmax(scores, axis=-1)
    probs_b = probs.astype(jnp.bfloat16)
    mixed = jnp.einsum("hij,jhd->ihd", probs_b, values_b, preferred_element_type=jnp.float32)
    return (probs, probs_b, mixed)


def layer_forward(hidden, w_key, w_value, cosine, sine_table, allowed):
    hfull, scale = normalize(hidden)
    normed = (hfull * scale).astype(jnp.bfloat16)
    keys = jnp.dot(normed, w_key, preferred_element_type=jnp.float32)
    keys_b = rotate(heads(keys), cosine, sine_table).astype(jnp.bfloat16)
    values_b = heads(
        jnp.dot(normed, w_value, preferred_element_type=jnp.float32).astype(jnp.bfloat16)
    )
    probs, probs_b, mixed = attend(keys_b, values_b, allowed)
    mixed_b = mixed.astype(jnp.bfloat16).reshape(hidden.shape[0], KV_HEADS * HD)
    output = hfull + times_transposed(mixed_b, w_value)
    return (output.astype(jnp.bfloat16), keys_b, values_b)


def layer_backward(hidden, keys_b, values_b, grad_out, w_key, w_value, cosine, sine_table, allowed):
    width = hidden.shape[0]
    hfull, scale = normalize(hidden)
    probs, probs_b, mixed = attend(keys_b, values_b, allowed)
    mixed_b = mixed.astype(jnp.bfloat16).reshape(width, KV_HEADS * HD)
    grad_mixed = heads(
        jnp.dot(grad_out, w_value, preferred_element_type=jnp.float32).astype(jnp.bfloat16)
    )
    grad_probs = jnp.einsum(
        "ihd,jhd->hij", grad_mixed, values_b, preferred_element_type=jnp.float32
    )
    grad_values = jnp.einsum(
        "hij,ihd->jhd", probs_b, grad_mixed, preferred_element_type=jnp.float32
    )
    grad_values = grad_values.astype(jnp.bfloat16).reshape(width, KV_HEADS * HD)
    grad_scores = (
        probs * (grad_probs - jnp.sum(probs * grad_probs, axis=-1, keepdims=True))
    ).astype(jnp.bfloat16)
    grad_keys = jnp.einsum("hij,jhd->ihd", grad_scores, keys_b, preferred_element_type=jnp.float32)
    grad_keys = (
        grad_keys
        + jnp.einsum("hij,ihd->jhd", grad_scores, keys_b, preferred_element_type=jnp.float32)
    ) / HD
    grad_keys = (
        rotate_back(grad_keys, cosine, sine_table)
        .astype(jnp.bfloat16)
        .reshape(width, KV_HEADS * HD)
    )
    grad_normed = times_transposed(grad_keys, w_key) + times_transposed(grad_values, w_value)
    incoming_gradient = (
        grad_out.astype(jnp.float32)
        + scale * grad_normed
        - hfull * scale**3 * jnp.mean(grad_normed * hfull, axis=-1, keepdims=True)
    )
    return (incoming_gradient.astype(jnp.bfloat16), grad_keys, grad_values, mixed_b)


def loss_gradient(hidden, segments, length, grades, w_score):
    hfull, scale = normalize(hidden)
    xfull = hfull * scale
    score = jnp.dot(xfull, w_score, precision=lax.Precision.HIGHEST)
    width = segments.shape[-1]
    index = jnp.arange(width, dtype=jnp.int32)
    following = jnp.concatenate([segments[1:] != segments[:-1], jnp.ones((1,), bool)], axis=-1)
    ends = (index < length) & (following | (index == length - 1))
    target = jax.nn.softmax(jnp.where(ends, grades.astype(jnp.float32), -1e30), axis=-1)
    model = jax.nn.softmax(jnp.where(ends, score, -1e30), axis=-1)
    weight = jnp.where(ends, model - target, 0.0)
    grad_x = weight[:, None] * w_score
    grad_h = scale * grad_x - hfull * scale**3 * jnp.mean(grad_x * hfull, axis=-1, keepdims=True)
    return grad_h.astype(jnp.bfloat16)


def pick(array, slot):
    return lax.dynamic_index_in_dim(array, slot, 0, keepdims=False)


def place(array, slot, value, valid):
    kept = jnp.where(valid, value, pick(array, slot))
    return lax.dynamic_update_index_in_dim(array, kept, slot, 0)


def shards(x0, w_key, w_value, w_score, segments, lengths, grades):
    sections = lax.axis_size("section")
    section = lax.axis_index("section")
    micro, width, model_width = x0.shape
    key_proj = w_key[0]
    value_proj = w_value[0]
    features = key_proj.shape[1]
    cosine, sine_table = rope_tables(segments)
    allowed = allowed_mask(segments, lengths)
    ticks = micro + sections - 1
    row_zeros = jnp.zeros((width, model_width), jnp.bfloat16)

    def forward_tick(carry, tick):
        incoming, saved_in, saved_keys, saved_values, finals = carry
        offset = tick - section
        valid = (offset >= 0) & (offset < micro)
        slot = jnp.clip(offset, 0, micro - 1)
        current = jnp.where(section == 0, pick(x0, slot), incoming)
        produced, keys_b, values_b = layer_forward(
            current,
            key_proj,
            value_proj,
            pick(cosine, slot),
            pick(sine_table, slot),
            pick(allowed, slot),
        )
        saved_in = place(saved_in, slot, current, valid)
        saved_keys = place(saved_keys, slot, keys_b, valid)
        saved_values = place(saved_values, slot, values_b, valid)
        finals = place(finals, slot, produced, valid & (section == sections - 1))
        outgoing = shifted(produced, "section", 1)
        return ((outgoing, saved_in, saved_keys, saved_values, finals), None)

    act_store = jnp.zeros((micro, width, model_width), jnp.bfloat16)
    head_store = jnp.zeros((micro, width, KV_HEADS, HD), jnp.bfloat16)
    start = (row_zeros, act_store, head_store, head_store, act_store)
    carry, unused = lax.scan(forward_tick, start, jnp.arange(ticks, dtype=jnp.int32))
    saved_in, saved_keys, saved_values, finals = (carry[1], carry[2], carry[3], carry[4])

    def backward_tick(carry, tick):
        incoming, store_keys, store_values, store_out, store_mixed = carry
        offset = tick - (sections - 1 - section)
        valid = (offset >= 0) & (offset < micro)
        slot = jnp.clip(offset, 0, micro - 1)
        first_grad = loss_gradient(
            pick(finals, slot),
            pick(segments, slot),
            pick(lengths, slot),
            pick(grades, slot),
            w_score,
        )
        grad_out = jnp.where(section == sections - 1, first_grad, incoming)
        incoming_gradient, grad_keys, grad_values, mixed_b = layer_backward(
            pick(saved_in, slot),
            pick(saved_keys, slot),
            pick(saved_values, slot),
            grad_out,
            key_proj,
            value_proj,
            pick(cosine, slot),
            pick(sine_table, slot),
            pick(allowed, slot),
        )
        store_keys = place(store_keys, slot, grad_keys, valid)
        store_values = place(store_values, slot, grad_values, valid)
        store_out = place(store_out, slot, grad_out, valid)
        store_mixed = place(store_mixed, slot, mixed_b, valid)
        outgoing = shifted(incoming_gradient, "section", -1)
        return ((outgoing, store_keys, store_values, store_out, store_mixed), None)

    flat_store = jnp.zeros((micro, width, features), jnp.bfloat16)
    start = (row_zeros, flat_store, flat_store, act_store, flat_store)
    carry, unused = lax.scan(backward_tick, start, jnp.arange(ticks, dtype=jnp.int32))
    tokens = micro * width
    key_grads = carry[1].reshape(tokens, features)
    value_grads = carry[2].reshape(tokens, features)
    out_grads = carry[3].reshape(tokens, model_width)
    mixed_all = carry[4].reshape(tokens, features)
    hfull, scale = normalize(saved_in)
    normalized_everything = (hfull * scale).astype(jnp.bfloat16).reshape(tokens, model_width)
    part_key = over_tokens(normalized_everything, key_grads)
    part_value = over_tokens(normalized_everything, value_grads) + over_tokens(out_grads, mixed_all)
    summed = lax.psum_scatter(
        jnp.concatenate([part_key, part_value], axis=1).astype(jnp.bfloat16),
        "dp",
        scatter_dimension=0,
        tiled=True,
    ).astype(jnp.float32)
    grad_key = summed[:, :features]
    grad_value = summed[:, features:]
    return (grad_key[None], grad_value[None])


def solution(mesh):
    placed = (
        P(None, "dp", None),
        P("section", None, None),
        P("section", None, None),
        P(),
        P(None, "dp"),
        P(None, "dp"),
        P(None, "dp"),
    )
    return jax.shard_map(
        shards,
        mesh=mesh,
        in_specs=placed,
        out_specs=(P("section", "dp", None), P("section", "dp", None)),
        check_vma=False,
    )
```

profile of v0, /device:TPU:0, one launch (start us, length us, event | category | flops | bytes accessed | tf_op | source)
XLA Modules:
  0.0 626.6 jit_solution(14873631917409074080)
XLA Ops:
  13.1 222.8 %while.39 = (s32[]{:T(128)}, bf16[32,5120]{1,0:T(8,128)(2,1)}, bf16[4,32,5120]{2,1,0:T(8,128)(2,1)S(1)}, bf16[4,32,4,128]{3,1,2,0:T(8,128)(2,1)S(1)}, bf16[4,32,...) while((s32[]{:T(128)}, bf16[32,5120]{1,0:T(8,128)(2,1)}, ...), condition=%wide.region_5.6_spmd, body=%wide.region_1.5_spmd.sunk | while | flops 508158016 | bytes 24565244 | solution.py:217
  21.9 3.5 convolution_convert_fusion.7
  29.4 4.8 bitcast_dynamic-update-slice_fusion.7
  34.2 5.0 collective-permute-start
  40.8 5.7 collective-permute-done
  51.7 3.5 fusion.203
  56.0 3.5 convolution_convert_fusion.7
  63.5 4.8 bitcast_dynamic-update-slice_fusion.7
  68.3 4.4 collective-permute-start
  74.2 4.9 collective-permute-done
  84.3 3.5 fusion.203
  88.6 3.5 convolution_convert_fusion.7
  96.1 4.8 bitcast_dynamic-update-slice_fusion.7
  100.9 4.4 collective-permute-start
  106.8 3.9 collective-permute-done
  116.0 3.5 fusion.203
  120.3 3.5 convolution_convert_fusion.7
  127.8 4.8 bitcast_dynamic-update-slice_fusion.7
  132.6 4.4 collective-permute-start
  151.4 3.5 convolution_convert_fusion.7
  158.9 4.8 bitcast_dynamic-update-slice_fusion.7
  163.7 4.4 collective-permute-start
  178.2 3.5 fusion.203
  182.5 3.5 convolution_convert_fusion.7
  190.0 4.8 bitcast_dynamic-update-slice_fusion.7
  194.8 4.4 collective-permute-start
  209.3 3.5 fusion.203
  213.5 3.5 convolution_convert_fusion.7
  221.0 4.8 bitcast_dynamic-update-slice_fusion.7
  225.9 4.4 collective-permute-start
  240.5 259.2 %while.40 = (s32[]{:T(128)}, bf16[32,5120]{1,0:T(8,128)(2,1)S(1)}, bf16[4,32,512]{2,1,0:T(8,128)(2,1)}, bf16[4,32,512]{2,1,0:T(8,128)(2,1)}, bf16[4,32,5120]{2,1...) while((s32[]{:T(128)}, bf16[32,5120]{1,0:T(8,128)(2,1)S(1)}, ...), condition=%wide.region_19.20_spmd, body=%wide.region_7.19_spmd.sunk | while | flops 521950272 | bytes 48383308 | solution.py:253
  254.1 3.5 fusion.237
  260.1 4.3 fusion.240
  291.5 3.5 fusion.237
  297.4 4.3 fusion.240
  328.4 3.5 fusion.237
  334.4 4.3 fusion.240
  365.4 3.5 fusion.237
  371.4 4.3 fusion.240
  402.4 3.5 fusion.237
  408.3 4.3 fusion.240
  439.4 3.5 fusion.237
  445.3 4.3 fusion.240
  476.3 3.5 fusion.237
  482.3 4.3 fusion.240
  506.6 4.8 pad_maximum_fusion
  511.3 14.4 %copy.57 = bf16[5120,1024]{1,0:T(8,128)(2,1)} copy(bf16[5120,1024]{0,1:T(8,128)(2,1)} %pad_maximum_fusion) | data formatting | bytes 20971520
  525.8 84.0 %reduce-scatter.4.cloned.1.call-done = bf16[640,1024]{1,0:T(8,128)(2,1)} async-done(((bf16[5120,1024]{1,0:T(8,128)(2,1)}), bf16[640,1024]{1,0:T(8,128)(2,1)}) %reduce-scatter.4.cloned.1.call-update) | async-done | bytes 1310736
  (525 shorter events, 321.4 us)
Async XLA Ops:
  7.2 602.6 %reduce-scatter.4.cloned.1.call-start = ((), (), s32[]{:S(2)}) async-start(), calls=%async_computation.1 | async-start | bytes 11796480
  34.2 12.3 %collective-permute-start = (bf16[32,5120]{1,0:T(8,128)(2,1)}, bf16[32,5120]{1,0:T(8,128)(2,1)S(1)}, u32[]{:S(2)}, u32[]{:S(2)}) collective-permute-start(bf16[32,5120]{1,0:T(8,128)(2,1)} %get-tuple-element.796), channel_id=1, source_target_pairs={{0,8},{8,16},{16,24},{1,9},{9,17},{17,25},{2,10},{10,18},{18,26},{... | collective-permute-start | bytes 983048 | tf_op jit(solution)/shard_map/while/body/eval_jaxpr/ppermute | solution.py:17
  68.3 10.8 %collective-permute-start = (bf16[32,5120]{1,0:T(8,128)(2,1)}, bf16[32,5120]{1,0:T(8,128)(2,1)S(1)}, u32[]{:S(2)}, u32[]{:S(2)}) collective-permute-start(bf16[32,5120]{1,0:T(8,128)(2,1)} %get-tuple-element.796), channel_id=1, source_target_pairs={{0,8},{8,16},{16,24},{1,9},{9,17},{17,25},{2,10},{10,18},{18,26},{... | collective-permute-start | bytes 983048 | tf_op jit(solution)/shard_map/while/body/eval_jaxpr/ppermute | solution.py:17
  100.9 9.8 %collective-permute-start = (bf16[32,5120]{1,0:T(8,128)(2,1)}, bf16[32,5120]{1,0:T(8,128)(2,1)S(1)}, u32[]{:S(2)}, u32[]{:S(2)}) collective-permute-start(bf16[32,5120]{1,0:T(8,128)(2,1)} %get-tuple-element.796), channel_id=1, source_target_pairs={{0,8},{8,16},{16,24},{1,9},{9,17},{17,25},{2,10},{10,18},{18,26},{... | collective-permute-start | bytes 983048 | tf_op jit(solution)/shard_map/while/body/eval_jaxpr/ppermute | solution.py:17
  132.6 9.3 %collective-permute-start = (bf16[32,5120]{1,0:T(8,128)(2,1)}, bf16[32,5120]{1,0:T(8,128)(2,1)S(1)}, u32[]{:S(2)}, u32[]{:S(2)}) collective-permute-start(bf16[32,5120]{1,0:T(8,128)(2,1)} %get-tuple-element.796), channel_id=1, source_target_pairs={{0,8},{8,16},{16,24},{1,9},{9,17},{17,25},{2,10},{10,18},{18,26},{... | collective-permute-start | bytes 983048 | tf_op jit(solution)/shard_map/while/body/eval_jaxpr/ppermute | solution.py:17
  163.7 9.3 %collective-permute-start = (bf16[32,5120]{1,0:T(8,128)(2,1)}, bf16[32,5120]{1,0:T(8,128)(2,1)S(1)}, u32[]{:S(2)}, u32[]{:S(2)}) collective-permute-start(bf16[32,5120]{1,0:T(8,128)(2,1)} %get-tuple-element.796), channel_id=1, source_target_pairs={{0,8},{8,16},{16,24},{1,9},{9,17},{17,25},{2,10},{10,18},{18,26},{... | collective-permute-start | bytes 983048 | tf_op jit(solution)/shard_map/while/body/eval_jaxpr/ppermute | solution.py:17
  194.8 9.3 %collective-permute-start = (bf16[32,5120]{1,0:T(8,128)(2,1)}, bf16[32,5120]{1,0:T(8,128)(2,1)S(1)}, u32[]{:S(2)}, u32[]{:S(2)}) collective-permute-start(bf16[32,5120]{1,0:T(8,128)(2,1)} %get-tuple-element.796), channel_id=1, source_target_pairs={{0,8},{8,16},{16,24},{1,9},{9,17},{17,25},{2,10},{10,18},{18,26},{... | collective-permute-start | bytes 983048 | tf_op jit(solution)/shard_map/while/body/eval_jaxpr/ppermute | solution.py:17
  225.9 9.3 %collective-permute-start = (bf16[32,5120]{1,0:T(8,128)(2,1)}, bf16[32,5120]{1,0:T(8,128)(2,1)S(1)}, u32[]{:S(2)}, u32[]{:S(2)}) collective-permute-start(bf16[32,5120]{1,0:T(8,128)(2,1)} %get-tuple-element.796), channel_id=1, source_target_pairs={{0,8},{8,16},{16,24},{1,9},{9,17},{17,25},{2,10},{10,18},{18,26},{... | collective-permute-start | bytes 983048 | tf_op jit(solution)/shard_map/while/body/eval_jaxpr/ppermute | solution.py:17
  236.2 4.3 copy-start.3
  253.9 12.2 %copy-start.6 = (f32[32]{0:T(128)}, f32[32]{0:T(128)S(1)}, u32[]{:S(2)}) copy-start(f32[32]{0:T(128)S(1)} %broadcast_multiply_fusion.4) | copy-start | bytes 388 | tf_op jit(solution)/shard_map/while
  253.9 3.7 copy-start.7
  254.1 4.8 copy-start.9
  260.1 4.3 copy-start
  267.3 9.6 %collective-permute-start.1 = (bf16[32,5120]{1,0:T(8,128)(2,1)}, bf16[32,5120]{1,0:T(8,128)(2,1)}, u32[]{:S(2)}, u32[]{:S(2)}) collective-permute-start(bf16[32,5120]{1,0:T(8,128)(2,1)} %fusion.242), channel_id=1, source_target_pairs={{8,0},{16,8},{24,16},{9,1},{17,9},{25,17},{10,2},{18,10},{26,18},{... | collective-permute-start | bytes 983048 | tf_op jit(solution)/shard_map/while/body/eval_jaxpr/ppermute | solution.py:17
  291.2 12.2 %copy-start.6 = (f32[32]{0:T(128)}, f32[32]{0:T(128)S(1)}, u32[]{:S(2)}) copy-start(f32[32]{0:T(128)S(1)} %broadcast_multiply_fusion.4) | copy-start | bytes 388 | tf_op jit(solution)/shard_map/while
  291.3 3.7 copy-start.7
  291.5 4.8 copy-start.9
  297.4 4.3 copy-start
  304.6 9.3 %collective-permute-start.1 = (bf16[32,5120]{1,0:T(8,128)(2,1)}, bf16[32,5120]{1,0:T(8,128)(2,1)}, u32[]{:S(2)}, u32[]{:S(2)}) collective-permute-start(bf16[32,5120]{1,0:T(8,128)(2,1)} %fusion.242), channel_id=1, source_target_pairs={{8,0},{16,8},{24,16},{9,1},{17,9},{25,17},{10,2},{18,10},{26,18},{... | collective-permute-start | bytes 983048 | tf_op jit(solution)/shard_map/while/body/eval_jaxpr/ppermute | solution.py:17
  328.2 12.2 %copy-start.6 = (f32[32]{0:T(128)}, f32[32]{0:T(128)S(1)}, u32[]{:S(2)}) copy-start(f32[32]{0:T(128)S(1)} %broadcast_multiply_fusion.4) | copy-start | bytes 388 | tf_op jit(solution)/shard_map/while
  328.2 3.7 copy-start.7
  328.4 4.8 copy-start.9
  334.4 4.3 copy-start
  341.6 9.3 %collective-permute-start.1 = (bf16[32,5120]{1,0:T(8,128)(2,1)}, bf16[32,5120]{1,0:T(8,128)(2,1)}, u32[]{:S(2)}, u32[]{:S(2)}) collective-permute-start(bf16[32,5120]{1,0:T(8,128)(2,1)} %fusion.242), channel_id=1, source_target_pairs={{8,0},{16,8},{24,16},{9,1},{17,9},{25,17},{10,2},{18,10},{26,18},{... | collective-permute-start | bytes 983048 | tf_op jit(solution)/shard_map/while/body/eval_jaxpr/ppermute | solution.py:17
  365.2 12.2 %copy-start.6 = (f32[32]{0:T(128)}, f32[32]{0:T(128)S(1)}, u32[]{:S(2)}) copy-start(f32[32]{0:T(128)S(1)} %broadcast_multiply_fusion.4) | copy-start | bytes 388 | tf_op jit(solution)/shard_map/while
  365.2 3.7 copy-start.7
  365.4 4.8 copy-start.9
  371.4 4.3 copy-start
  378.5 9.3 %collective-permute-start.1 = (bf16[32,5120]{1,0:T(8,128)(2,1)}, bf16[32,5120]{1,0:T(8,128)(2,1)}, u32[]{:S(2)}, u32[]{:S(2)}) collective-permute-start(bf16[32,5120]{1,0:T(8,128)(2,1)} %fusion.242), channel_id=1, source_target_pairs={{8,0},{16,8},{24,16},{9,1},{17,9},{25,17},{10,2},{18,10},{26,18},{... | collective-permute-start | bytes 983048 | tf_op jit(solution)/shard_map/while/body/eval_jaxpr/ppermute | solution.py:17
  402.2 12.2 %copy-start.6 = (f32[32]{0:T(128)}, f32[32]{0:T(128)S(1)}, u32[]{:S(2)}) copy-start(f32[32]{0:T(128)S(1)} %broadcast_multiply_fusion.4) | copy-start | bytes 388 | tf_op jit(solution)/shard_map/while
  402.2 3.7 copy-start.7
  402.4 4.8 copy-start.9
  408.3 4.3 copy-start
  415.5 9.3 %collective-permute-start.1 = (bf16[32,5120]{1,0:T(8,128)(2,1)}, bf16[32,5120]{1,0:T(8,128)(2,1)}, u32[]{:S(2)}, u32[]{:S(2)}) collective-permute-start(bf16[32,5120]{1,0:T(8,128)(2,1)} %fusion.242), channel_id=1, source_target_pairs={{8,0},{16,8},{24,16},{9,1},{17,9},{25,17},{10,2},{18,10},{26,18},{... | collective-permute-start | bytes 983048 | tf_op jit(solution)/shard_map/while/body/eval_jaxpr/ppermute | solution.py:17
  439.1 12.2 %copy-start.6 = (f32[32]{0:T(128)}, f32[32]{0:T(128)S(1)}, u32[]{:S(2)}) copy-start(f32[32]{0:T(128)S(1)} %broadcast_multiply_fusion.4) | copy-start | bytes 388 | tf_op jit(solution)/shard_map/while
  439.2 3.7 copy-start.7
  439.4 4.8 copy-start.9
  445.3 4.3 copy-start
  452.5 9.3 %collective-permute-start.1 = (bf16[32,5120]{1,0:T(8,128)(2,1)}, bf16[32,5120]{1,0:T(8,128)(2,1)}, u32[]{:S(2)}, u32[]{:S(2)}) collective-permute-start(bf16[32,5120]{1,0:T(8,128)(2,1)} %fusion.242), channel_id=1, source_target_pairs={{8,0},{16,8},{24,16},{9,1},{17,9},{25,17},{10,2},{18,10},{26,18},{... | collective-permute-start | bytes 983048 | tf_op jit(solution)/shard_map/while/body/eval_jaxpr/ppermute | solution.py:17
  476.1 12.2 %copy-start.6 = (f32[32]{0:T(128)}, f32[32]{0:T(128)S(1)}, u32[]{:S(2)}) copy-start(f32[32]{0:T(128)S(1)} %broadcast_multiply_fusion.4) | copy-start | bytes 388 | tf_op jit(solution)/shard_map/while
  476.1 3.7 copy-start.7
  476.3 4.8 copy-start.9
  482.3 4.3 copy-start
  489.5 9.3 %collective-permute-start.1 = (bf16[32,5120]{1,0:T(8,128)(2,1)}, bf16[32,5120]{1,0:T(8,128)(2,1)}, u32[]{:S(2)}, u32[]{:S(2)}) collective-permute-start(bf16[32,5120]{1,0:T(8,128)(2,1)} %fusion.242), channel_id=1, source_target_pairs={{8,0},{16,8},{24,16},{9,1},{17,9},{25,17},{10,2},{18,10},{26,18},{... | collective-permute-start | bytes 983048 | tf_op jit(solution)/shard_map/while/body/eval_jaxpr/ppermute | solution.py:17
  499.7 2.5 copy-start.8
  502.3 2.6 copy-start.1
  502.3 2.6 copy-start.5
  615.4 2.9 copy-start.4
  (14 other events, 8.7 us)
Sparse Core Ops, SparseCore 0:
  525.9 83.8 reduce-scatter.3
where the time goes:
time: 634 us; the launch traced here: 627 us
  matrix products  208 us (33%)
  other arithmetic  138 us (22%)
  waiting for transfers between devices  120 us (19%)
  local copies, waits for them, and re-layouts  94.3 us (15%)
  starting transfers between devices  40.4 us (6%)
  between operations  14.1 us (2%)
  loops' own time  10.9 us (2%)
    unnamed x2, waiting for transfers between devices  84 us
    dot_general x21, matrix products, times_transposed(): lax.dot_general(left, right, (((1,), (1,)), ((), ())), preferred_element_...  76 us
    dynamic_update_slice x42, other arithmetic, place(): return lax.dynamic_update_index_in_dim(array, kept, slot, 0)  50.1 us
    ppermute x14, starting transfers between devices, shifted(): lax.ppermute(value, axis, [(source, source + steps) for source in range(f...  40.3 us
    ppermute x14, waiting for transfers between devices, shifted(): lax.ppermute(value, axis, [(source, source + steps) for source in range(f...  36.4 us
    dot_general x7, matrix products, layer_forward(): jnp.dot(normed, w_value, preferred_element_type=jnp.float32)  24.8 us
    dot_general x7, matrix products, layer_backward(): jnp.dot(grad_out, w_value, preferred_element_type=jnp.float32)  24.8 us
    dot_general x7, matrix products, layer_forward(): keys = jnp.dot(normed, w_key, preferred_element_type=jnp.float32)  24.7 us
  transfers between devices with their start and end apart: 15, of which 15 were waited for; matrix products, arithmetic and copies ran while one was open for 9% of the time, Pallas kernels for 0%

commit v1 on v0

v1 whole, which is shorter than its diff:
```python
import functools

import jax
import jax.numpy as jnp
from jax import lax
from jax.experimental import pallas as pl
from jax.experimental.pallas import tpu as pltpu
from jax.sharding import PartitionSpec as P

HD = 128
KV_HEADS = 4
EPS = 1e-06
THETA = 1000000.0
NEG = -1e30
CHUNK = 1280
BF16 = jnp.bfloat16
F32 = jnp.float32

VMEM = pl.BlockSpec(memory_space=pltpu.VMEM)
HBM = pl.BlockSpec(memory_space=pl.ANY)


def params():
    return pltpu.CompilerParams(vmem_limit_bytes=12 * 1024 * 1024)


def shifted(value, axis, steps):
    count = lax.axis_size(axis)
    first, last = (max(0, -steps), min(count, count - steps))
    return lax.ppermute(value, axis, [(source, source + steps) for source in range(first, last)])


def dot(left, right):
    return jnp.dot(left, right, preferred_element_type=F32)


def dot_tb(left, right):
    return lax.dot_general(left, right, (((1,), (1,)), ((), ())), preferred_element_type=F32)


def dot_ta(left, right):
    return lax.dot_general(left, right, (((0,), (0,)), ((), ())), preferred_element_type=F32)


def to_column(row, eye):
    return jnp.sum(jnp.where(eye, jnp.broadcast_to(row, eye.shape), 0.0), axis=1, keepdims=True)


def make_tables(
    micro, segments_ref, lengths_ref, grades_ref,
    cos_ref, sin_ref, mask_ref, ends_ref, target_ref,
):
    width = segments_ref.shape[1]
    square = (width, width)
    at_row = lax.broadcasted_iota(jnp.int32, square, 0)
    at_col = lax.broadcasted_iota(jnp.int32, square, 1)
    eye = at_row == at_col
    lane = lax.broadcasted_iota(jnp.int32, (width, HD), 1)
    half_lane = jnp.where(lane < HD // 2, lane, lane - HD // 2).astype(F32)
    freqs = jnp.exp(half_lane * F32(-2.0 / HD) * jnp.log(F32(THETA)))
    sign = jnp.where(lane < HD // 2, -1.0, 1.0)
    index = lax.broadcasted_iota(jnp.int32, (width, 1), 0)
    for slot in range(micro):
        seg_row = segments_ref[slot : slot + 1, :].astype(F32)
        seg_col = to_column(seg_row, eye)
        grade_col = to_column(grades_ref[slot : slot + 1, :].astype(F32), eye)
        length = lengths_ref[0, slot]
        same = seg_col == seg_row
        offset = jnp.sum(jnp.where(same & (at_col < at_row), 1.0, 0.0), axis=1, keepdims=True)
        angles = offset * freqs
        cos_ref[slot] = jnp.cos(angles)
        sin_ref[slot] = jnp.sin(angles) * sign
        allowed = same & (at_col <= at_row) & (at_row < length) & (at_col < length)
        mask = jnp.where(allowed | eye, 1.0, 0.0)
        for head in range(KV_HEADS):
            mask_ref[slot, head * width : (head + 1) * width, :] = mask
        changes = jnp.sum(
            jnp.where((at_col == at_row + 1) & jnp.logical_not(same), 1.0, 0.0),
            axis=1, keepdims=True,
        )
        following = (changes > 0.0) | (index == width - 1)
        ends = (index < length) & (following | (index == length - 1))
        logits = jnp.where(ends, grade_col, NEG)
        weight = jnp.exp(logits - jnp.max(logits, axis=0, keepdims=True))
        target = weight / jnp.sum(weight, axis=0, keepdims=True)
        ends_ref[slot] = jnp.broadcast_to(jnp.where(ends, 1.0, 0.0), (width, HD))
        target_ref[slot] = jnp.broadcast_to(target, (width, HD))


def first_kernel(
    sections, micro, peers,
    wk_hbm, wv_hbm, x0_hbm, score_hbm, segments_hbm, lengths_hbm, grades_hbm,
    w_score, wk, wv, cosine, sine, mask, ends, target,
    saved, keys, values, probs, scales, grads, sent, *rest,
):
    outgoing = rest[-13]
    segments_ref, lengths_ref, grades_ref, small, key_sems, value_sems = rest[-12:-6]
    scratch = rest[-6:]
    model = wk.shape[0]
    copies = [
        pltpu.make_async_copy(segments_hbm, segments_ref, small.at[0]),
        pltpu.make_async_copy(lengths_hbm, lengths_ref, small.at[1]),
        pltpu.make_async_copy(grades_hbm, grades_ref, small.at[2]),
        pltpu.make_async_copy(x0_hbm, saved, small.at[3]),
        pltpu.make_async_copy(score_hbm, w_score, small.at[4]),
    ]
    for copy in copies:
        copy.start()

    def chunk_copies(c):
        cols = pl.ds(c * CHUNK, CHUNK)
        return (
            pltpu.make_async_copy(wk_hbm.at[cols], wk.at[cols], key_sems.at[c]),
            pltpu.make_async_copy(wv_hbm.at[cols], wv.at[cols], value_sems.at[c]),
        )

    for c in range(model // CHUNK):
        for copy in chunk_copies(c):
            copy.start()
    for copy in copies[:3]:
        copy.wait()
    make_tables(
        micro, segments_ref, lengths_ref, grades_ref, cosine, sine, mask, ends, target
    )
    for copy in copies[3:]:
        copy.wait()
    section = lax.axis_index("section")

    @pl.when(section == 0)
    def _():
        def wait_chunk(c):
            for copy in chunk_copies(c):
                copy.wait()

        forward_body(
            0, section, sections, peers, wait_chunk,
            w_score, wk, wv, cosine, sine, mask, ends, target,
            saved, keys, values, probs, scales, grads, sent, outgoing, *scratch,
        )

    @pl.when(section != 0)
    def _():
        for c in range(model // CHUNK):
            for copy in chunk_copies(c):
                copy.wait()


def row_scale(ref_value_chunks, model):
    total = None
    for chunk in ref_value_chunks:
        part = chunk * chunk
        total = part if total is None else total + part
    return lax.rsqrt(jnp.sum(total, axis=1, keepdims=True) / model + EPS)


def head_cols(head):
    return slice(head * HD, (head + 1) * HD)


def forward_kernel(
    tick, sections, micro, peers,
    incoming, w_score, wk, wv, cosine, sine, mask, ends, target,
    *rest,
):
    section = lax.axis_index("section")
    offset = tick - 2 * section
    slot = jnp.clip(offset, 0, micro - 1)
    saved = rest[7]

    @pl.when((offset >= 0) & (offset < micro))
    def _():
        @pl.when(section != 0)
        def _():
            saved[slot] = incoming[...]

        forward_body(
            slot, section, sections, peers, None,
            w_score, wk, wv, cosine, sine, mask, ends, target, *rest[7:],
        )


def forward_body(
    slot, section, sections, peers, wait_chunk,
    w_score, wk, wv, cosine, sine, mask, ends, target,
    saved, keys, values, probs, scales, grads, sent, outgoing,
    acc_k, acc_v, normed, mixed, block, sem,
):
    width, model = outgoing.shape
    features = KV_HEADS * HD
    step = CHUNK // 2
    share = model // peers
    wide = block.shape[2] - features

    def chunk_of(ref, start):
        return ref[slot, :, start : start + step].astype(F32)

    scale = row_scale([chunk_of(saved, c) for c in range(0, model, step)], model)
    scales[slot] = jnp.broadcast_to(scale, (width, HD))
    for c in range(0, model, step):
        normed[:, c : c + step] = (chunk_of(saved, c) * scale).astype(BF16)
    acc_k[...] = jnp.zeros_like(acc_k)
    acc_v[...] = jnp.zeros_like(acc_v)

    @pl.loop(0, model // CHUNK)
    def _(c):
        if wait_chunk is not None:
            wait_chunk(c)
        cols = pl.ds(pl.multiple_of(c * CHUNK, CHUNK), CHUNK)
        piece = normed[:, cols]
        acc_k[...] += dot(piece, wk[cols, :])
        acc_v[...] += dot(piece, wv[cols, :])

    cos_value = cosine[slot]
    sin_value = sine[slot]
    scores = []
    for head in range(KV_HEADS):
        vec = acc_k[:, head_cols(head)]
        turned = vec * cos_value + pltpu.roll(vec, HD // 2, 1) * sin_value
        key = turned.astype(BF16)
        keys[slot, :, head_cols(head)] = key
        scores.append(dot_tb(key, key))
    values[slot] = acc_v[...].astype(BF16)
    score = jnp.concatenate(scores, axis=0) / HD
    score = jnp.where(mask[slot] > 0.0, score, NEG)
    weight = jnp.exp(score - jnp.max(score, axis=1, keepdims=True))
    prob = weight / jnp.sum(weight, axis=1, keepdims=True)
    probs[slot] = prob
    prob_b = prob.astype(BF16)
    for head in range(KV_HEADS):
        out = dot(prob_b[head * width : (head + 1) * width, :], values[slot, :, head_cols(head)])
        mixed[:, head_cols(head)] = out.astype(BF16)

    for peer in range(peers):
        block[peer, :, :share] = normed[:, peer * share : (peer + 1) * share]
        block[peer, :, wide:] = mixed[...]
    copy = pltpu.make_async_copy(block, sent.at[:, slot], sem)
    copy.start()

    @pl.loop(0, model // CHUNK)
    def _(c):
        cols = pl.ds(pl.multiple_of(c * CHUNK, CHUNK), CHUNK)
        out = saved[slot, :, cols].astype(F32) + dot_tb(mixed[...], wv[cols, :])
        outgoing[:, cols] = out.astype(BF16)

    @pl.when(section == sections - 1)
    def _():
        def last_of(start):
            return outgoing[:, start : start + step].astype(F32)

        last_scale = row_scale([last_of(c) for c in range(0, model, step)], model)
        along = None
        for c in range(0, model, step):
            part = last_of(c) * w_score[:, c : c + step]
            along = part if along is None else along + part
        along = jnp.sum(along, axis=1, keepdims=True)
        is_end = ends[slot][:, :1] > 0.0
        logits = jnp.where(is_end, last_scale * along, NEG)
        part = jnp.exp(logits - jnp.max(logits, axis=0, keepdims=True))
        chosen = part / jnp.sum(part, axis=0, keepdims=True)
        g = jnp.where(is_end, chosen - target[slot][:, :1], 0.0)
        first = last_scale * g
        second = last_scale * last_scale * last_scale * (g * along / model)
        for c in range(0, model, step):
            value = first * w_score[:, c : c + step] - last_of(c) * second
            grads[slot, :, c : c + step] = value.astype(BF16)

    copy.wait()


def backward_kernel(
    tick, sections, micro, peers, slots,
    incoming, wk, wv, cosine, sine, saved, keys, values, probs, scales, grads,
    *rest,
):
    sent = rest[len(slots) + 2 : 2 * len(slots) + 2]
    outgoing = rest[2 * len(slots) + 2]
    acc, full, current, flat, block, sem = rest[2 * len(slots) + 3 :]
    section = lax.axis_index("section")
    offset = tick - 2 * (sections - 1 - section)
    slot = jnp.clip(offset, 0, micro - 1)
    width, model = incoming.shape
    features = KV_HEADS * HD
    step = CHUNK // 2
    share = model // peers
    wide = block.shape[2] - 2 * features

    @pl.when((offset >= 0) & (offset < micro))
    def _():
        @pl.when(section == sections - 1)
        def _():
            current[...] = grads[slot]

        @pl.when(section != sections - 1)
        def _():
            current[...] = incoming[...]

        acc[...] = jnp.zeros_like(acc)

        @pl.loop(0, model // CHUNK)
        def _(c):
            cols = pl.ds(pl.multiple_of(c * CHUNK, CHUNK), CHUNK)
            acc[...] += dot(current[:, cols], wv[cols, :])

        cos_value = cosine[slot]
        sin_value = sine[slot]
        prob = probs[slot]
        prob_b = prob.astype(BF16)
        grad_probs = []
        for head in range(KV_HEADS):
            rows = slice(head * width, (head + 1) * width)
            mixed_grad = acc[:, head_cols(head)].astype(BF16)
            grad_probs.append(dot_tb(mixed_grad, values[slot, :, head_cols(head)]))
            flat[:, features + head * HD : features + (head + 1) * HD] = dot_ta(
                prob_b[rows, :], mixed_grad
            ).astype(BF16)
        grad_prob = jnp.concatenate(grad_probs, axis=0)
        grad_score = prob * (grad_prob - jnp.sum(prob * grad_prob, axis=1, keepdims=True))
        grad_score = grad_score.astype(BF16)
        for head in range(KV_HEADS):
            piece = grad_score[head * width : (head + 1) * width, :]
            key = keys[slot, :, head_cols(head)]
            vec = (dot(piece, key) + dot_ta(piece, key)) / HD
            turned = vec * cos_value - pltpu.roll(vec, HD // 2, 1) * sin_value
            flat[:, head_cols(head)] = turned.astype(BF16)

        for peer in range(peers):
            block[peer, :, :share] = current[:, peer * share : (peer + 1) * share]
            block[peer, :, wide:] = flat[...]
        for which, out in zip(slots, sent):
            @pl.when(slot == which)
            def _():
                pltpu.make_async_copy(block, out, sem).start()

        @pl.when(section != 0)
        def _():
            acc[...] = jnp.zeros_like(acc)

            @pl.loop(0, model // CHUNK)
            def _(c):
                cols = pl.ds(pl.multiple_of(c * CHUNK, CHUNK), CHUNK)
                out = dot_tb(flat[:, :features], wk[cols, :])
                out = out + dot_tb(flat[:, features:], wv[cols, :])
                full[:, cols] = out
                along = out * saved[slot, :, cols].astype(F32)
                total = along[:, :HD]
                for start in range(HD, CHUNK, HD):
                    total = total + along[:, start : start + HD]
                acc[:, :HD] += total

            scale = scales[slot][:, :1]
            mean = jnp.sum(acc[:, :HD], axis=1, keepdims=True) / model
            second = scale * scale * scale * mean
            for c in range(0, model, step):
                cols = slice(c, c + step)
                value = (
                    current[:, cols].astype(F32)
                    + scale * full[:, cols]
                    - saved[slot, :, cols].astype(F32) * second
                )
                outgoing[:, cols] = value.astype(BF16)

        for which, out in zip(slots, sent):
            @pl.when(slot == which)
            def _():
                pltpu.make_async_copy(block, out, sem).wait()


def gather_kernel(slots, share, wide, features, forward, *rest):
    backward, before, (key_out, value_out) = rest[: len(slots)], rest[len(slots) : -2], rest[-2:]
    tokens = forward.shape[0] * forward.shape[2]
    key_parts = [before[0][...]] if before else []
    value_parts = [before[1][...]] if before else []
    for slot, block in zip(slots, backward):
        def rows(ref, start, size):
            return ref[:, :, start : start + size].reshape(tokens, size)

        def forward_rows(start, size):
            return forward[:, slot, :, start : start + size].reshape(tokens, size)

        normed = forward_rows(0, share)
        key_parts.append(dot_ta(normed, rows(block, wide, features)))
        value_parts.append(dot_ta(normed, rows(block, wide + features, features)))
        value_parts.append(dot_ta(rows(block, 0, share), forward_rows(wide, features)))
    key_out[...] = sum(key_parts[1:], key_parts[0])
    value_out[...] = sum(value_parts[1:], value_parts[0])


def in_vmem(shape, dtype):
    return pltpu.VMEM(shape, dtype)


def shards(x0, w_key, w_value, w_score, segments, lengths, grades):
    sections = lax.axis_size("section")
    peers = lax.axis_size("dp")
    micro, width, model = x0.shape
    wk, wv = w_key[0], w_value[0]
    features = wk.shape[1]
    share = model // peers
    wide = -(-share // HD) * HD
    last = 2 * (sections - 1)
    ticks = micro + last
    rows = KV_HEADS * width

    tables = [
        in_vmem((1, model), F32),
        in_vmem(wk.shape, BF16),
        in_vmem(wv.shape, BF16),
        in_vmem((micro, width, HD), F32),
        in_vmem((micro, width, HD), F32),
        in_vmem((micro, rows, width), F32),
        in_vmem((micro, width, HD), F32),
        in_vmem((micro, width, HD), F32),
    ]
    state = [
        in_vmem((micro, width, model), BF16),
        in_vmem((micro, width, features), BF16),
        in_vmem((micro, width, features), BF16),
        in_vmem((micro, rows, width), F32),
        in_vmem((micro, width, HD), F32),
        in_vmem((micro, width, model), BF16),
    ]
    token = in_vmem((8, HD), F32)
    send_forward = jax.ShapeDtypeStruct((peers, micro, width, wide + features), BF16)
    send_backward = jax.ShapeDtypeStruct((peers, width, wide + 2 * features), BF16)
    row = jax.ShapeDtypeStruct((width, model), BF16)
    forward_scratch = [
        pltpu.VMEM((width, features), F32),
        pltpu.VMEM((width, features), F32),
        pltpu.VMEM((width, model), BF16),
        pltpu.VMEM((width, features), BF16),
        pltpu.VMEM((peers, width, wide + features), BF16),
        pltpu.SemaphoreType.DMA,
    ]
    inputs = [wk, wv, x0, w_score.reshape(1, model), segments, lengths.reshape(1, micro), grades]
    chunks = model // CHUNK
    made = pl.pallas_call(
        functools.partial(first_kernel, sections, micro, peers),
        out_shape=tables + state + [send_forward] + [send_backward] * micro + [token, row],
        in_specs=[HBM] * len(inputs),
        out_specs=[VMEM] * (len(tables) + len(state)) + [HBM] * (1 + micro) + [VMEM, VMEM],
        scratch_shapes=[
            pltpu.VMEM(segments.shape, jnp.int32),
            pltpu.SMEM((1, micro), jnp.int32),
            pltpu.VMEM(grades.shape, jnp.int32),
            pltpu.SemaphoreType.DMA((5,)),
            pltpu.SemaphoreType.DMA((chunks,)),
            pltpu.SemaphoreType.DMA((chunks,)),
        ]
        + forward_scratch,
        compiler_params=params(),
        name="first",
    )(*[pltpu.with_memory_space_constraint(value, pltpu.HBM) for value in inputs])
    w_score, wk, wv, cosine, sine, mask, ends, target = made[: len(tables)]
    held = list(made[len(tables) : len(tables) + len(state) + 1])
    blocks = list(made[len(tables) + len(state) + 1 : -2])
    token_value, produced = made[-2:]

    cost = pl.CostEstimate(flops=1000000, bytes_accessed=1000000, transcendentals=0)
    empty = jnp.zeros((width, model), BF16)
    incoming = [empty, empty, shifted(produced, "section", 1)]
    for tick in range(1, ticks):
        args = (incoming[tick], w_score, wk, wv, cosine, sine, mask, ends, target)
        count = len(held)
        *held, produced = pl.pallas_call(
            functools.partial(forward_kernel, tick, sections, micro, peers),
            out_shape=state + [send_forward, row],
            in_specs=[VMEM] * (len(args) + len(state)) + [HBM],
            out_specs=[VMEM] * len(state) + [HBM, VMEM],
            input_output_aliases={len(args) + n: n for n in range(count)},
            scratch_shapes=forward_scratch,
            compiler_params=params(),
            cost_estimate=cost,
            name="forward",
        )(*args, *held)
        if tick < ticks - 2:
            incoming.append(shifted(produced, "section", 1))

    saved, keys, values, probs, scales, grads, sent = held
    incoming = [empty] * 2
    received = []
    for tick in range(ticks):
        slots = [tick - 2 * hop for hop in range(sections)]
        slots = tuple(slot for slot in slots if 0 <= slot < micro)
        arrived = incoming[tick]
        if tick == 2:
            sent, token_value = lax.optimization_barrier((sent, token_value))
            got_forward = lax.all_to_all(sent, "dp", split_axis=0, concat_axis=0, tiled=True)
        if tick == last + 1:
            arrived, got_forward = lax.optimization_barrier((arrived, got_forward))
        if tick > last + 1:
            arrived, received[-2] = lax.optimization_barrier((arrived, received[-2]))
        args = (arrived, wk, wv, cosine, sine, saved, keys, values, probs, scales, grads)
        token_value, *outs = pl.pallas_call(
            functools.partial(backward_kernel, tick, sections, micro, peers, slots),
            out_shape=[token] + [send_backward] * len(slots) + [row],
            in_specs=[VMEM] * (len(args) + 1) + [HBM] * len(slots),
            out_specs=[VMEM] + [HBM] * len(slots) + [VMEM],
            input_output_aliases={len(args) + n: n for n in range(1 + len(slots))},
            scratch_shapes=[
                pltpu.VMEM((width, features), F32),
                pltpu.VMEM((width, model), F32),
                pltpu.VMEM((width, model), BF16),
                pltpu.VMEM((width, 2 * features), BF16),
                pltpu.VMEM((peers, width, wide + 2 * features), BF16),
                pltpu.SemaphoreType.DMA,
            ],
            compiler_params=params(),
            cost_estimate=cost,
            name="backward",
        )(*args, token_value, *[blocks[slot] for slot in slots])
        for slot, block in zip(slots, outs):
            blocks[slot] = block
        if tick < ticks - 2:
            incoming.append(shifted(outs[-1], "section", -1))
        if tick >= last:
            block = blocks[tick - last]
            received.append(
                lax.all_to_all(block, "dp", split_axis=0, concat_axis=0, tiled=True)
            )

    whole = jax.ShapeDtypeStruct((share, features), F32)
    total = ()
    for slots in (tuple(range(micro - 1)), (micro - 1,)):
        args = [got_forward, *[received[slot] for slot in slots], *total]
        total = pl.pallas_call(
            functools.partial(gather_kernel, slots, share, wide, features),
            out_shape=[whole, whole],
            in_specs=[VMEM] * len(args),
            out_specs=[VMEM] * 2,
            compiler_params=params(),
            cost_estimate=cost,
            name="gathered",
        )(*args)
    return (total[0][None], total[1][None])


def solution(mesh):
    placed = (
        P(None, "dp", None),
        P("section", None, None),
        P("section", None, None),
        P(),
        P(None, "dp"),
        P(None, "dp"),
        P(None, "dp"),
    )
    return jax.shard_map(
        shards,
        mesh=mesh,
        in_specs=placed,
        out_specs=(P("section", "dp", None), P("section", "dp", None)),
        check_vma=False,
    )
```

time: 634 us -> 262 us (0.41)
  matrix products: 208 us -> 0 us
  other arithmetic: 138 us -> 0 us
  local copies, waits for them, and re-layouts: 94.3 us -> 39.8 us
  Pallas kernels: 0 us -> 42.2 us
  starting transfers between devices: 40.4 us -> 64 us
  between operations: 14.1 us -> 1.15 us
  loops' own time: 10.9 us -> 0 us
    dot_general x94 -> x0, matrix products: 192 us -> none  [the longest x21 76 us: times_transposed(): lax.dot_general(left, right, (((1,), (1,)), ((), ())), preferred_element_...]
    unnamed x2 -> x0, waiting for transfers between devices: 84 us -> none
    ppermute x14 -> x16, waiting for transfers between devices: 36.4 us -> 104 us  [shifted(): lax.ppermute(value, axis, [(source, source + steps) for source in range(f...]
    dynamic_update_slice x42 -> x0, other arithmetic: 50.1 us -> none  [place(): return lax.dynamic_update_index_in_dim(array, kept, slot, 0)]
    pallas_call x0 -> x22, Pallas kernels: none -> 42.2 us  [the longest x9 16.2 us: shards(): pl.pallas_call(functools.partial(forward_kernel, tick, sections, micro, p...]
    dynamic_slice x35 -> x0, local copies, waits for them, and re-layouts: 33.5 us -> none  [the longest x21 17.1 us: pick(): return lax.dynamic_index_in_dim(array, slot, 0, keepdims=False)]
    reduce_sum x36 -> x0, other arithmetic: 22.5 us -> none  [the longest x7 8.94 us: loss_gradient(): jax.nn.softmax(jnp.where(ends, grades.astype(jnp.float32), -1e+30), axis=-1)]
    all_to_all x0 -> x5, starting transfers between devices: none -> 20.9 us  [the longest x4 16.5 us: shards(): lax.all_to_all(block, 'dp', split_axis=0, concat_axis=0, tiled=True)]
  transfers between devices with their start and end apart: 15 -> 21, of which waited for: 15 -> 12; matrix products, arithmetic and copies ran while one was open for 9% -> 0% of each run, Pallas kernels for 0% -> 11%
where the time goes in v1:
time: 262 us; the launch traced here: 261 us
  waiting for transfers between devices  114 us (44%)
  starting transfers between devices  64 us (24%)
  Pallas kernels  42.2 us (16%)
  local copies, waits for them, and re-layouts  39.8 us (15%)
    ppermute x16, waiting for transfers between devices, shifted(): lax.ppermute(value, axis, [(source, source + steps) for source in range(f...  104 us
    ppermute x16, starting transfers between devices, shifted(): lax.ppermute(value, axis, [(source, source + steps) for source in range(f...  43.1 us
    unnamed x72, local copies, waits for them, and re-layouts  39.8 us
    all_to_all x4, starting transfers between devices, shards(): lax.all_to_all(block, 'dp', split_axis=0, concat_axis=0, tiled=True)  16.5 us
    pallas_call x9, Pallas kernels, shards(): pl.pallas_call(functools.partial(forward_kernel, tick, sections, micro, p...  16.2 us
    pallas_call x10, Pallas kernels, shards(): pl.pallas_call(functools.partial(backward_kernel, tick, sections, micro,...  9.95 us
    all_to_all x4, waiting for transfers between devices, shards(): lax.all_to_all(block, 'dp', split_axis=0, concat_axis=0, tiled=True)  9.2 us
    pallas_call x1, Pallas kernels, shards(): pl.pallas_call(functools.partial(first_kernel, sections, micro, peers), o...  8.45 us
  transfers between devices with their start and end apart: 21, of which 12 were waited for; matrix products, arithmetic and copies ran while one was open for 0% of the time, Pallas kernels for 11%

profile of v1, /device:TPU:0, one launch (start us, length us, event | category | flops | bytes accessed | tf_op | source)
XLA Modules:
  0.0 260.8 jit_solution(10434440520496010880)
XLA Ops:
  0.6 8.4 %first.1 = (f32[1,5120]{1,0:T(1,128)S(1)}, bf16[5120,512]{1,0:T(8,128)(2,1)S(1)}, bf16[5120,512]{1,0:T(8,128)(2,1)S(1)}, f32[4,32,128]{2,1,0:T(8,128)S(1)}, f32[...) custom-call(bf16[5120,512]{1,0:T(8,128)(2,1)} %bitcast.6, ...), custom_call_target="tpu_custom_call" | custom-call | tf_op jit(solution)/shard_map/first/pallas_call | solution.py:436
  9.1 1.3 collective-permute-start.1
  10.5 4.9 %forward.9 = (bf16[4,32,5120]{2,1,0:T(8,128)(2,1)S(1)}, bf16[4,32,512]{2,1,0:T(8,128)(2,1)S(1)}, bf16[4,32,512]{2,1,0:T(8,128)(2,1)S(1)}, f32[4,128,32]{2,1,0:T(...) custom-call(bf16[32,5120]{1,0:T(8,128)(2,1)S(1)} %broadcast_in_dim.9, ...), custom_call_target="tpu_custom_call", output_to_operand_aliasing={{0}: (9, {}), {1}: (10, {}), {2}: (11, {}), {3}: (12, {}), ... | custom-call | flops 1000000 | bytes 1000000 | tf_op jit(solution)/shard_map/forward/pallas_call | solution.py:464
  15.4 1.3 collective-permute-start
  16.7 1.8 collective-permute-done.1.incoming
  18.5 4.9 %forward.10 = (bf16[4,32,5120]{2,1,0:T(8,128)(2,1)S(1)}, bf16[4,32,512]{2,1,0:T(8,128)(2,1)S(1)}, bf16[4,32,512]{2,1,0:T(8,128)(2,1)S(1)}, f32[4,128,32]{2,1,0:T...) custom-call(bf16[32,5120]{1,0:T(8,128)(2,1)S(1)} %collective-permute, ...), custom_call_target="tpu_custom_call", output_to_operand_aliasing={{0}: (9, {}), {1}: (10, {}), {2}: (11, {}), {3}: (12, {}), ... | custom-call | flops 1000000 | bytes 1000000 | tf_op jit(solution)/shard_map/forward/pallas_call | solution.py:464
  23.4 4.4 %collective-permute-start.3 = (bf16[32,5120]{1,0:T(8,128)(2,1)S(1)}, bf16[32,5120]{1,0:T(8,128)(2,1)S(1)}, u32[]{:S(2)}, u32[]{:S(2)}) collective-permute-start(bf16[32,5120]{1,0:T(8,128)(2,1)S(1)} %get-tuple-element.170), channel_id=1, source_target_pairs={{0,8},{8,16},{16,24},{1,9},{9,17},{17,25},{2,10},{10,18},{18,26},{... | collective-permute-start | bytes 983048 | tf_op jit(solution)/shard_map/ppermute | solution.py:30
  27.8 4.9 %forward.11 = (bf16[4,32,5120]{2,1,0:T(8,128)(2,1)S(1)}, bf16[4,32,512]{2,1,0:T(8,128)(2,1)S(1)}, bf16[4,32,512]{2,1,0:T(8,128)(2,1)S(1)}, f32[4,128,32]{2,1,0:T...) custom-call(bf16[32,5120]{1,0:T(8,128)(2,1)S(1)} %collective-permute, ...), custom_call_target="tpu_custom_call", output_to_operand_aliasing={{0}: (9, {}), {1}: (10, {}), {2}: (11, {}), {3}: (12, {}), ... | custom-call | flops 1000000 | bytes 1000000 | tf_op jit(solution)/shard_map/forward/pallas_call | solution.py:464
  32.7 1.9 collective-permute-start.2
  34.7 9.1 %collective-permute-start.5 = (bf16[32,5120]{1,0:T(8,128)(2,1)S(1)}, bf16[32,5120]{1,0:T(8,128)(2,1)S(1)}, u32[]{:S(2)}, u32[]{:S(2)}) collective-permute-start(bf16[32,5120]{1,0:T(8,128)(2,1)S(1)} %get-tuple-element.186), channel_id=1, source_target_pairs={{0,8},{8,16},{16,24},{1,9},{9,17},{17,25},{2,10},{10,18},{18,26},{... | collective-permute-start | bytes 983048 | tf_op jit(solution)/shard_map/ppermute | solution.py:30
  43.9 7.1 %collective-permute-start.4 = (bf16[32,5120]{1,0:T(8,128)(2,1)S(1)}, bf16[32,5120]{1,0:T(8,128)(2,1)S(1)}, u32[]{:S(2)}, u32[]{:S(2)}) collective-permute-start(bf16[32,5120]{1,0:T(8,128)(2,1)S(1)} %get-tuple-element.185), channel_id=1, source_target_pairs={{0,8},{8,16},{16,24},{1,9},{9,17},{17,25},{2,10},{10,18},{18,26},{... | collective-permute-start | bytes 983048 | tf_op jit(solution)/shard_map/ppermute | solution.py:30
  51.0 3.1 %collective-permute-start.7 = (bf16[32,5120]{1,0:T(8,128)(2,1)S(1)}, bf16[32,5120]{1,0:T(8,128)(2,1)S(1)}, u32[]{:S(2)}, u32[]{:S(2)}) collective-permute-start(bf16[32,5120]{1,0:T(8,128)(2,1)S(1)} %get-tuple-element.202), channel_id=1, source_target_pairs={{0,8},{8,16},{16,24},{1,9},{9,17},{17,25},{2,10},{10,18},{18,26},{... | collective-permute-start | bytes 983048 | tf_op jit(solution)/shard_map/ppermute | solution.py:30
  54.1 5.0 %collective-permute-done.4.incoming = bf16[32,5120]{1,0:T(8,128)(2,1)S(1)} collective-permute-done((bf16[32,5120]{1,0:T(8,128)(2,1)S(1)}, bf16[32,5120]{1,0:T(8,128)(2,1)S(1)}, u32[]{:S(2)}, u32[]{:S(2)}) %collective-permute-start.4) | collective-permute-done | bytes 327712 | tf_op jit(solution)/shard_map/ppermute | solution.py:30
  59.1 4.4 %collective-permute-start.6 = (bf16[32,5120]{1,0:T(8,128)(2,1)S(1)}, bf16[32,5120]{1,0:T(8,128)(2,1)S(1)}, u32[]{:S(2)}, u32[]{:S(2)}) collective-permute-start(bf16[32,5120]{1,0:T(8,128)(2,1)S(1)} %get-tuple-element.201), channel_id=1, source_target_pairs={{0,8},{8,16},{16,24},{1,9},{9,17},{17,25},{2,10},{10,18},{18,26},{... | collective-permute-start | bytes 983048 | tf_op jit(solution)/shard_map/ppermute | solution.py:30
  63.5 2.6 collective-permute-done.7.incoming
  66.9 4.1 %collective-permute-done.6.incoming = bf16[32,5120]{1,0:T(8,128)(2,1)S(1)} collective-permute-done((bf16[32,5120]{1,0:T(8,128)(2,1)S(1)}, bf16[32,5120]{1,0:T(8,128)(2,1)S(1)}, u32[]{:S(2)}, u32[]{:S(2)}) %collective-permute-start.6) | collective-permute-done | bytes 327712 | tf_op jit(solution)/shard_map/ppermute | solution.py:30
  76.4 4.4 %all-to-all-start = ((bf16[8,4,32,1152]{3,2,1,0:T(8,128)(2,1)}), bf16[8,4,32,1152]{3,2,1,0:T(8,128)(2,1)}, u32[]{:S(2)}, u32[]{:S(2)}) async-start(bf16[8,4,32,1152]{3,2,1,0:T(8,128)(2,1)} %copy-done.10), calls=%async_computation | async-start | bytes 4718592 | tf_op jit(solution)/shard_map/all_to_all | solution.py:487
  80.7 1.3 collective-permute-start.9
  82.0 1.3 collective-permute-start.8
  83.3 10.6 %collective-permute-done.9.incoming = bf16[32,5120]{1,0:T(8,128)(2,1)S(1)} collective-permute-done((bf16[32,5120]{1,0:T(8,128)(2,1)}, bf16[32,5120]{1,0:T(8,128)(2,1)S(1)}, u32[]{:S(2)}, u32[]{:S(2)}) %collective-permute-start.9) | collective-permute-done | bytes 327712 | tf_op jit(solution)/shard_map/ppermute | solution.py:30
  93.9 2.5 copy-done.1
  96.4 2.5 copy-done.6
  101.2 1.4 collective-permute-start.11
  102.7 1.3 collective-permute-start.10
  104.0 9.9 %collective-permute-done.11.incoming = bf16[32,5120]{1,0:T(8,128)(2,1)S(1)} collective-permute-done((bf16[32,5120]{1,0:T(8,128)(2,1)S(1)}, bf16[32,5120]{1,0:T(8,128)(2,1)S(1)}, u32[]{:S(2)}, u32[]{:S(2)}) %collective-permute-start.11) | collective-permute-done | bytes 327712 | tf_op jit(solution)/shard_map/ppermute | solution.py:30
  115.2 4.3 %collective-permute-done.10.incoming = bf16[32,5120]{1,0:T(8,128)(2,1)S(1)} collective-permute-done((bf16[32,5120]{1,0:T(8,128)(2,1)S(1)}, bf16[32,5120]{1,0:T(8,128)(2,1)S(1)}, u32[]{:S(2)}, u32[]{:S(2)}) %collective-permute-start.10) | collective-permute-done | bytes 327712 | tf_op jit(solution)/shard_map/ppermute | solution.py:30
  121.1 26.4 %collective-permute-done.13.incoming = bf16[32,5120]{1,0:T(8,128)(2,1)S(1)} collective-permute-done((bf16[32,5120]{1,0:T(8,128)(2,1)S(1)}, bf16[32,5120]{1,0:T(8,128)(2,1)S(1)}, u32[]{:S(2)}, u32[]{:S(2)}) %collective-permute-start.13) | collective-permute-done | bytes 327712 | tf_op jit(solution)/shard_map/ppermute | solution.py:30
  147.5 2.1 backward.16
  152.1 4.2 %all-to-all-start.2 = ((bf16[8,32,1664]{2,1,0:T(8,128)(2,1)}), bf16[8,32,1664]{2,1,0:T(8,128)(2,1)}, u32[]{:S(2)}, u32[]{:S(2)}) async-start(bf16[8,32,1664]{2,1,0:T(8,128)(2,1)} %copy-done.30), calls=%async_computation.2 | async-start | bytes 1703936 | tf_op jit(solution)/shard_map/all_to_all | solution.py:518
  156.3 1.3 collective-permute-start.12
  157.6 14.6 %collective-permute-done.12.incoming = bf16[32,5120]{1,0:T(8,128)(2,1)S(1)} collective-permute-done((bf16[32,5120]{1,0:T(8,128)(2,1)}, bf16[32,5120]{1,0:T(8,128)(2,1)S(1)}, u32[]{:S(2)}, u32[]{:S(2)}) %collective-permute-start.12) | collective-permute-done | bytes 327712 | tf_op jit(solution)/shard_map/ppermute | solution.py:30
  172.2 2.5 copy-done.2
  174.7 2.5 copy-done.7
  179.5 2.1 backward.17
  184.1 4.2 %all-to-all-start.1 = ((bf16[8,32,1664]{2,1,0:T(8,128)(2,1)}), bf16[8,32,1664]{2,1,0:T(8,128)(2,1)}, u32[]{:S(2)}, u32[]{:S(2)}) async-start(bf16[8,32,1664]{2,1,0:T(8,128)(2,1)} %copy-done.27), calls=%async_computation.1 | async-start | bytes 1703936 | tf_op jit(solution)/shard_map/all_to_all | solution.py:518
  189.6 14.6 %collective-permute-done.15.incoming = bf16[32,5120]{1,0:T(8,128)(2,1)S(1)} collective-permute-done((bf16[32,5120]{1,0:T(8,128)(2,1)}, bf16[32,5120]{1,0:T(8,128)(2,1)S(1)}, u32[]{:S(2)}, u32[]{:S(2)}) %collective-permute-start.15) | collective-permute-done | bytes 327712 | tf_op jit(solution)/shard_map/ppermute | solution.py:30
  204.2 2.5 copy-done.3
  206.6 2.5 copy-done.8
  210.3 2.8 %backward.18 = (f32[8,128]{1,0:T(8,128)S(1)}, bf16[8,32,1664]{2,1,0:T(8,128)(2,1)S(1)}, bf16[32,5120]{1,0:T(8,128)(2,1)}) custom-call(bf16[32,5120]{1,0:T(8,128)(2,1)S(1)} %collective-permute-done.15.incoming, bf16[5120,512]{1,0:T(8,128)(2,1)S(1)} %copy-done.3, bf16[5120,512]{1,0:T(8,128)(2,1)S(1)} %copy-done.8, ...), custom_call_target="tpu_custom_call", output_to_operand_aliasing={{0}: (11, {}), {1}: (12, {})} | custom-call | flops 1000000 | bytes 1000000 | tf_op jit(solution)/shard_map/backward/pallas_call | solution.py:493
  214.0 4.2 %all-to-all-start.4 = ((bf16[8,32,1664]{2,1,0:T(8,128)(2,1)}), bf16[8,32,1664]{2,1,0:T(8,128)(2,1)}, u32[]{:S(2)}, u32[]{:S(2)}) async-start(bf16[8,32,1664]{2,1,0:T(8,128)(2,1)} %copy-done.22), calls=%async_computation.4 | async-start | bytes 1703936 | tf_op jit(solution)/shard_map/all_to_all | solution.py:518
  219.5 10.8 %collective-permute-done.14.incoming = bf16[32,5120]{1,0:T(8,128)(2,1)S(1)} collective-permute-done((bf16[32,5120]{1,0:T(8,128)(2,1)}, bf16[32,5120]{1,0:T(8,128)(2,1)S(1)}, u32[]{:S(2)}, u32[]{:S(2)}) %collective-permute-start.14) | collective-permute-done | bytes 327712 | tf_op jit(solution)/shard_map/ppermute | solution.py:30
  230.3 2.5 copy-done.4
  232.8 2.5 copy-done.9
  236.4 2.8 %backward.19 = (f32[8,128]{1,0:T(8,128)S(1)}, bf16[8,32,1664]{2,1,0:T(8,128)(2,1)S(1)}, bf16[32,5120]{1,0:T(8,128)(2,1)}) custom-call(bf16[32,5120]{1,0:T(8,128)(2,1)S(1)} %collective-permute-done.14.incoming, bf16[5120,512]{1,0:T(8,128)(2,1)S(1)} %copy-done.4, bf16[5120,512]{1,0:T(8,128)(2,1)S(1)} %copy-done.9, ...), custom_call_target="tpu_custom_call", output_to_operand_aliasing={{0}: (11, {}), {1}: (12, {})} | custom-call | flops 1000000 | bytes 1000000 | tf_op jit(solution)/shard_map/backward/pallas_call | solution.py:493
  240.1 3.9 %all-to-all-start.3 = ((bf16[8,32,1664]{2,1,0:T(8,128)(2,1)}), bf16[8,32,1664]{2,1,0:T(8,128)(2,1)S(1)}, u32[]{:S(2)}, u32[]{:S(2)}) async-start(bf16[8,32,1664]{2,1,0:T(8,128)(2,1)} %copy-done.17), calls=%async_computation.3 | async-start | bytes 1703936 | tf_op jit(solution)/shard_map/all_to_all | solution.py:518
  244.0 4.1 %gathered.2 = (f32[640,512]{1,0:T(8,128)S(1)}, f32[640,512]{1,0:T(8,128)S(1)}) custom-call(bf16[8,4,32,1152]{3,2,1,0:T(8,128)(2,1)} %all-to-all-done.forward, bf16[8,32,1664]{2,1,0:T(8,128)(2,1)} %all-to-all-done.2.rest_0_, bf16[8,32,1664]{2,1,0:T(8,128)(2,1)} %all-to-all-done.1.rest_1_, bf16[8,32,1664]{2,1,0:T(8,128)(2,1)} %all-to-all-done.4.rest_2_), custom_call_target="tpu_custom_call" | custom-call | flops 1000000 | bytes 1000000 | tf_op jit(solution)/shard_map/gathered/pallas_call | solution.py:525
  248.1 9.2 %all-to-all-done.3.rest_0_ = bf16[8,32,1664]{2,1,0:T(8,128)(2,1)S(1)} async-done(((bf16[8,32,1664]{2,1,0:T(8,128)(2,1)}), bf16[8,32,1664]{2,1,0:T(8,128)(2,1)S(1)}, u32[]{:S(2)}, u32[]{:S(2)}) %all-to-all-start.3) | async-done | bytes 852000 | tf_op jit(solution)/shard_map/all_to_all | solution.py:518
  257.3 3.5 %gathered.3 = (f32[640,512]{1,0:T(8,128)}, f32[640,512]{1,0:T(8,128)}) custom-call(bf16[8,4,32,1152]{3,2,1,0:T(8,128)(2,1)} %all-to-all-done.forward, bf16[8,32,1664]{2,1,0:T(8,128)(2,1)S(1)} %all-to-all-done.3.rest_0_, f32[640,512]{1,0:T(8,128)S(1)} %get-tuple-element.270.rest_1_, f32[640,512]{1,0:T(8,128)S(1)} %get-tuple-element.271.rest_2_), custom_call_target="tpu_custom_call" | custom-call | flops 1000000 | bytes 1000000 | tf_op jit(solution)/shard_map/gathered/pallas_call | solution.py:525
  (89 shorter events, 25.7 us)
Async XLA Ops:
  9.1 6.3 %copy-start.11 = (bf16[8,32,1664]{2,1,0:T(8,128)(2,1)}, bf16[8,32,1664]{2,1,0:T(8,128)(2,1)S(1)}, u32[]{:S(2)}) copy-start(bf16[8,32,1664]{2,1,0:T(8,128)(2,1)S(1)} %get-tuple-element.235.rest_1_) | copy-start | bytes 2555908
  9.1 6.3 %copy-start.18 = (bf16[8,32,1664]{2,1,0:T(8,128)(2,1)}, bf16[8,32,1664]{2,1,0:T(8,128)(2,1)S(1)}, u32[]{:S(2)}) copy-start(bf16[8,32,1664]{2,1,0:T(8,128)(2,1)S(1)} %get-tuple-element.232.rest_1_) | copy-start | bytes 2555908
  9.1 64.7 %copy-start = (bf16[5120,512]{1,0:T(8,128)(2,1)}, bf16[5120,512]{1,0:T(8,128)(2,1)S(1)}, u32[]{:S(2)}) copy-start(bf16[5120,512]{1,0:T(8,128)(2,1)S(1)} %get-tuple-element.138.wk) | copy-start | bytes 15728644
  9.1 64.7 %copy-start.5 = (bf16[5120,512]{1,0:T(8,128)(2,1)}, bf16[5120,512]{1,0:T(8,128)(2,1)S(1)}, u32[]{:S(2)}) copy-start(bf16[5120,512]{1,0:T(8,128)(2,1)S(1)} %get-tuple-element.139.wv) | copy-start | bytes 15728644
  9.1 9.4 %collective-permute-start.1 = (bf16[32,5120]{1,0:T(8,128)(2,1)S(1)}, bf16[32,5120]{1,0:T(8,128)(2,1)S(1)}, u32[]{:S(2)}, u32[]{:S(2)}) collective-permute-start(bf16[32,5120]{1,0:T(8,128)(2,1)S(1)} %get-tuple-element.154), channel_id=1, source_target_pairs={{0,8},{8,16},{16,24},{1,9},{9,17},{17,25},{2,10},{10,18},{18,26},{... | collective-permute-start | bytes 983048 | tf_op jit(solution)/shard_map/ppermute | solution.py:30
  15.4 12.4 %collective-permute-start = (bf16[32,5120]{1,0:T(8,128)(2,1)S(1)}, bf16[32,5120]{1,0:T(8,128)(2,1)S(1)}, u32[]{:S(2)}, u32[]{:S(2)}) collective-permute-start(bf16[32,5120]{1,0:T(8,128)(2,1)S(1)} %get-tuple-element.153), channel_id=1, source_target_pairs={{0,8},{8,16},{16,24},{1,9},{9,17},{17,25},{2,10},{10,18},{18,26},{... | collective-permute-start | bytes 983048 | tf_op jit(solution)/shard_map/ppermute | solution.py:30
  23.4 11.3 %collective-permute-start.3 = (bf16[32,5120]{1,0:T(8,128)(2,1)S(1)}, bf16[32,5120]{1,0:T(8,128)(2,1)S(1)}, u32[]{:S(2)}, u32[]{:S(2)}) collective-permute-start(bf16[32,5120]{1,0:T(8,128)(2,1)S(1)} %get-tuple-element.170), channel_id=1, source_target_pairs={{0,8},{8,16},{16,24},{1,9},{9,17},{17,25},{2,10},{10,18},{18,26},{... | collective-permute-start | bytes 983048 | tf_op jit(solution)/shard_map/ppermute | solution.py:30
  32.7 11.1 %collective-permute-start.2 = (bf16[32,5120]{1,0:T(8,128)(2,1)S(1)}, bf16[32,5120]{1,0:T(8,128)(2,1)S(1)}, u32[]{:S(2)}, u32[]{:S(2)}) collective-permute-start(bf16[32,5120]{1,0:T(8,128)(2,1)S(1)} %get-tuple-element.169), channel_id=1, source_target_pairs={{0,8},{8,16},{16,24},{1,9},{9,17},{17,25},{2,10},{10,18},{18,26},{... | collective-permute-start | bytes 983048 | tf_op jit(solution)/shard_map/ppermute | solution.py:30
  34.7 16.3 %collective-permute-start.5 = (bf16[32,5120]{1,0:T(8,128)(2,1)S(1)}, bf16[32,5120]{1,0:T(8,128)(2,1)S(1)}, u32[]{:S(2)}, u32[]{:S(2)}) collective-permute-start(bf16[32,5120]{1,0:T(8,128)(2,1)S(1)} %get-tuple-element.186), channel_id=1, source_target_pairs={{0,8},{8,16},{16,24},{1,9},{9,17},{17,25},{2,10},{10,18},{18,26},{... | collective-permute-start | bytes 983048 | tf_op jit(solution)/shard_map/ppermute | solution.py:30
  43.9 15.2 %collective-permute-start.4 = (bf16[32,5120]{1,0:T(8,128)(2,1)S(1)}, bf16[32,5120]{1,0:T(8,128)(2,1)S(1)}, u32[]{:S(2)}, u32[]{:S(2)}) collective-permute-start(bf16[32,5120]{1,0:T(8,128)(2,1)S(1)} %get-tuple-element.185), channel_id=1, source_target_pairs={{0,8},{8,16},{16,24},{1,9},{9,17},{17,25},{2,10},{10,18},{18,26},{... | collective-permute-start | bytes 983048 | tf_op jit(solution)/shard_map/ppermute | solution.py:30
  51.0 15.1 %collective-permute-start.7 = (bf16[32,5120]{1,0:T(8,128)(2,1)S(1)}, bf16[32,5120]{1,0:T(8,128)(2,1)S(1)}, u32[]{:S(2)}, u32[]{:S(2)}) collective-permute-start(bf16[32,5120]{1,0:T(8,128)(2,1)S(1)} %get-tuple-element.202), channel_id=1, source_target_pairs={{0,8},{8,16},{16,24},{1,9},{9,17},{17,25},{2,10},{10,18},{18,26},{... | collective-permute-start | bytes 983048 | tf_op jit(solution)/shard_map/ppermute | solution.py:30
  59.1 11.8 %collective-permute-start.6 = (bf16[32,5120]{1,0:T(8,128)(2,1)S(1)}, bf16[32,5120]{1,0:T(8,128)(2,1)S(1)}, u32[]{:S(2)}, u32[]{:S(2)}) collective-permute-start(bf16[32,5120]{1,0:T(8,128)(2,1)S(1)} %get-tuple-element.201), channel_id=1, source_target_pairs={{0,8},{8,16},{16,24},{1,9},{9,17},{17,25},{2,10},{10,18},{18,26},{... | collective-permute-start | bytes 983048 | tf_op jit(solution)/shard_map/ppermute | solution.py:30
  71.7 1.4 copy-start.10
  74.7 0.9 copy-start.23
  76.4 75.7 %all-to-all-start = ((bf16[8,4,32,1152]{3,2,1,0:T(8,128)(2,1)}), bf16[8,4,32,1152]{3,2,1,0:T(8,128)(2,1)}, u32[]{:S(2)}, u32[]{:S(2)}) async-start(bf16[8,4,32,1152]{3,2,1,0:T(8,128)(2,1)} %copy-done.10), calls=%async_computation | async-start | bytes 4718592 | tf_op jit(solution)/shard_map/all_to_all | solution.py:487
  80.7 13.2 %collective-permute-start.9 = (bf16[32,5120]{1,0:T(8,128)(2,1)}, bf16[32,5120]{1,0:T(8,128)(2,1)S(1)}, u32[]{:S(2)}, u32[]{:S(2)}) collective-permute-start(bf16[32,5120]{1,0:T(8,128)(2,1)} %copy-done.35), channel_id=1, source_target_pairs={{8,0},{16,8},{24,16},{9,1},{17,9},{25,17},{10,2},{18,10},{26,18},{... | collective-permute-start | bytes 983048 | tf_op jit(solution)/shard_map/ppermute | solution.py:30
  82.0 20.6 %collective-permute-start.8 = (bf16[32,5120]{1,0:T(8,128)(2,1)}, bf16[32,5120]{1,0:T(8,128)(2,1)S(1)}, u32[]{:S(2)}, u32[]{:S(2)}) collective-permute-start(bf16[32,5120]{1,0:T(8,128)(2,1)} %copy-done.33), channel_id=1, source_target_pairs={{8,0},{16,8},{24,16},{9,1},{17,9},{25,17},{10,2},{18,10},{26,18},{... | collective-permute-start | bytes 983048 | tf_op jit(solution)/shard_map/ppermute | solution.py:30
  93.9 2.5 copy-start.1
  96.4 2.5 copy-start.6
  98.9 1.2 copy-start.19
  100.0 1.2 copy-start.29
  101.2 1.5 copy-start.12
  101.2 1.5 copy-start.24
  101.2 12.7 %collective-permute-start.11 = (bf16[32,5120]{1,0:T(8,128)(2,1)S(1)}, bf16[32,5120]{1,0:T(8,128)(2,1)S(1)}, u32[]{:S(2)}, u32[]{:S(2)}) collective-permute-start(bf16[32,5120]{1,0:T(8,128)(2,1)S(1)} %get-tuple-element.238), channel_id=1, source_target_pairs={{8,0},{16,8},{24,16},{9,1},{17,9},{25,17},{10,2},{18,10},{26,18},{... | collective-permute-start | bytes 983048 | tf_op jit(solution)/shard_map/ppermute | solution.py:30
  102.7 16.7 %collective-permute-start.10 = (bf16[32,5120]{1,0:T(8,128)(2,1)S(1)}, bf16[32,5120]{1,0:T(8,128)(2,1)S(1)}, u32[]{:S(2)}, u32[]{:S(2)}) collective-permute-start(bf16[32,5120]{1,0:T(8,128)(2,1)S(1)} %get-tuple-element.237), channel_id=1, source_target_pairs={{8,0},{16,8},{24,16},{9,1},{17,9},{25,17},{10,2},{18,10},{26,18},{... | collective-permute-start | bytes 983048 | tf_op jit(solution)/shard_map/ppermute | solution.py:30
  113.9 33.6 %collective-permute-start.13 = (bf16[32,5120]{1,0:T(8,128)(2,1)S(1)}, bf16[32,5120]{1,0:T(8,128)(2,1)S(1)}, u32[]{:S(2)}, u32[]{:S(2)}) collective-permute-start(bf16[32,5120]{1,0:T(8,128)(2,1)S(1)} %get-tuple-element.249), channel_id=1, source_target_pairs={{8,0},{16,8},{24,16},{9,1},{17,9},{25,17},{10,2},{18,10},{26,18},{... | collective-permute-start | bytes 983048 | tf_op jit(solution)/shard_map/ppermute | solution.py:30
  121.1 26.4 %copy-start.25 = (bf16[8,32,1664]{2,1,0:T(8,128)(2,1)}, bf16[8,32,1664]{2,1,0:T(8,128)(2,1)S(1)}, u32[]{:S(2)}) copy-start(bf16[8,32,1664]{2,1,0:T(8,128)(2,1)S(1)} %get-tuple-element.255.rest_2_) | copy-start | bytes 2555908
  149.5 0.9 copy-start.20
  150.4 0.9 copy-start.30
  152.1 32.0 %all-to-all-start.2 = ((bf16[8,32,1664]{2,1,0:T(8,128)(2,1)}), bf16[8,32,1664]{2,1,0:T(8,128)(2,1)}, u32[]{:S(2)}, u32[]{:S(2)}) async-start(bf16[8,32,1664]{2,1,0:T(8,128)(2,1)} %copy-done.30), calls=%async_computation.2 | async-start | bytes 1703936 | tf_op jit(solution)/shard_map/all_to_all | solution.py:518
  156.3 15.9 %collective-permute-start.12 = (bf16[32,5120]{1,0:T(8,128)(2,1)}, bf16[32,5120]{1,0:T(8,128)(2,1)S(1)}, u32[]{:S(2)}, u32[]{:S(2)}) collective-permute-start(bf16[32,5120]{1,0:T(8,128)(2,1)} %copy-done.34), channel_id=1, source_target_pairs={{8,0},{16,8},{24,16},{9,1},{17,9},{25,17},{10,2},{18,10},{26,18},{... | collective-permute-start | bytes 983048 | tf_op jit(solution)/shard_map/ppermute | solution.py:30
  172.2 2.5 copy-start.2
  174.7 2.5 copy-start.7
  177.1 1.2 copy-start.14
  178.3 1.2 copy-start.26
  181.5 0.9 copy-start.15
  184.1 29.9 %all-to-all-start.1 = ((bf16[8,32,1664]{2,1,0:T(8,128)(2,1)}), bf16[8,32,1664]{2,1,0:T(8,128)(2,1)}, u32[]{:S(2)}, u32[]{:S(2)}) async-start(bf16[8,32,1664]{2,1,0:T(8,128)(2,1)} %copy-done.27), calls=%async_computation.1 | async-start | bytes 1703936 | tf_op jit(solution)/shard_map/all_to_all | solution.py:518
  188.3 15.9 %collective-permute-start.15 = (bf16[32,5120]{1,0:T(8,128)(2,1)}, bf16[32,5120]{1,0:T(8,128)(2,1)S(1)}, u32[]{:S(2)}, u32[]{:S(2)}) collective-permute-start(bf16[32,5120]{1,0:T(8,128)(2,1)} %copy-done.31), channel_id=1, source_target_pairs={{8,0},{16,8},{24,16},{9,1},{17,9},{25,17},{10,2},{18,10},{26,18},{... | collective-permute-start | bytes 983048 | tf_op jit(solution)/shard_map/ppermute | solution.py:30
  204.2 2.5 copy-start.3
  206.6 2.5 copy-start.8
  209.1 1.2 copy-start.21
  213.1 0.9 copy-start.22
  214.0 26.1 %all-to-all-start.4 = ((bf16[8,32,1664]{2,1,0:T(8,128)(2,1)}), bf16[8,32,1664]{2,1,0:T(8,128)(2,1)}, u32[]{:S(2)}, u32[]{:S(2)}) async-start(bf16[8,32,1664]{2,1,0:T(8,128)(2,1)} %copy-done.22), calls=%async_computation.4 | async-start | bytes 1703936 | tf_op jit(solution)/shard_map/all_to_all | solution.py:518
  218.2 12.1 %collective-permute-start.14 = (bf16[32,5120]{1,0:T(8,128)(2,1)}, bf16[32,5120]{1,0:T(8,128)(2,1)S(1)}, u32[]{:S(2)}, u32[]{:S(2)}) collective-permute-start(bf16[32,5120]{1,0:T(8,128)(2,1)} %copy-done.32), channel_id=1, source_target_pairs={{8,0},{16,8},{24,16},{9,1},{17,9},{25,17},{10,2},{18,10},{26,18},{... | collective-permute-start | bytes 983048 | tf_op jit(solution)/shard_map/ppermute | solution.py:30
  230.3 2.5 copy-start.4
  232.8 2.5 copy-start.9
  235.3 1.2 copy-start.16
  240.1 17.2 %all-to-all-start.3 = ((bf16[8,32,1664]{2,1,0:T(8,128)(2,1)}), bf16[8,32,1664]{2,1,0:T(8,128)(2,1)S(1)}, u32[]{:S(2)}, u32[]{:S(2)}) async-start(bf16[8,32,1664]{2,1,0:T(8,128)(2,1)} %copy-done.17), calls=%async_computation.3 | async-start | bytes 1703936 | tf_op jit(solution)/shard_map/all_to_all | solution.py:518
  (9 other events, 7.3 us)

commit v2 on v1

--- a/solution.py
+++ b/solution.py
@@ -20,14 +20,25 @@
 HBM = pl.BlockSpec(memory_space=pl.ANY)
 
 
-def params():
-    return pltpu.CompilerParams(vmem_limit_bytes=12 * 1024 * 1024)
-
-
-def shifted(value, axis, steps):
-    count = lax.axis_size(axis)
-    first, last = (max(0, -steps), min(count, count - steps))
-    return lax.ppermute(value, axis, [(source, source + steps) for source in range(first, last)])
+def params(mib=12):
+    return pltpu.CompilerParams(vmem_limit_bytes=mib * 1024 * 1024)
+
+
+def shifted(value, steps, senders):
+    return lax.ppermute(value, "section", [(source, source + steps) for source in senders])
+
+
+def between_chips(value, mask, chips):
+    pairs = [(2 * c + k, 2 * partner(c, mask, chips) + k) for c in range(chips) for k in range(2)]
+    return lax.ppermute(value, "dp", pairs)
+
+
+def between_cores(value, chips):
+    return lax.ppermute(value, "dp", [(d, d ^ 1) for d in range(2 * chips)])
+
+
+def partner(chip, mask, chips):
+    return chip ^ mask if chips & (chips - 1) == 0 else (mask - chip) % chips
 
 
 def dot(left, right):
@@ -88,11 +99,12 @@
 
 
 def first_kernel(
-    sections, micro, peers,
+    sections, micro, chips,
     wk_hbm, wv_hbm, x0_hbm, score_hbm, segments_hbm, lengths_hbm, grades_hbm,
     w_score, wk, wv, cosine, sine, mask, ends, target,
-    saved, keys, values, probs, scales, grads, sent, *rest,
+    saved, keys, values, probs, scales, grads, *rest,
 ):
+    sent = rest[:chips]
     outgoing = rest[-13]
     segments_ref, lengths_ref, grades_ref, small, key_sems, value_sems = rest[-12:-6]
     scratch = rest[-6:]
@@ -133,9 +145,9 @@
                 copy.wait()
 
         forward_body(
-            0, section, sections, peers, wait_chunk,
+            0, section, sections, chips, wait_chunk,
             w_score, wk, wv, cosine, sine, mask, ends, target,
-            saved, keys, values, probs, scales, grads, sent, outgoing, *scratch,
+            saved, keys, values, probs, scales, grads, *sent, outgoing, *scratch,
         )
 
     @pl.when(section != 0)
@@ -158,14 +170,15 @@
 
 
 def forward_kernel(
-    tick, sections, micro, peers,
+    tick, sections, micro, chips,
     incoming, w_score, wk, wv, cosine, sine, mask, ends, target,
     *rest,
 ):
     section = lax.axis_index("section")
     offset = tick - 2 * section
     slot = jnp.clip(offset, 0, micro - 1)
-    saved = rest[7]
+    rest = rest[6 + chips :]
+    saved = rest[0]
 
     @pl.when((offset >= 0) & (offset < micro))
     def _():
@@ -174,22 +187,41 @@
             saved[slot] = incoming[...]
 
         forward_body(
-            slot, section, sections, peers, None,
-            w_score, wk, wv, cosine, sine, mask, ends, target, *rest[7:],
+            slot, section, sections, chips, None,
+            w_score, wk, wv, cosine, sine, mask, ends, target, *rest,
         )
 
 
+def fill_block(block, columns, factors):
+    chips = block.shape[0]
+    share = columns.shape[1] // (2 * chips)
+    wide = (block.shape[2] - factors.shape[1]) // 2
+    for device in range(2 * chips):
+        start = (device % 2) * wide
+        block[device // 2, :, start : start + share] = columns[:, device * share : (device + 1) * share]
+    for chip in range(chips):
+        block[chip, :, 2 * wide :] = factors[...]
+
+
+def block_copies(block, targets, sems):
+    chips = len(targets)
+    chip = lax.axis_index("dp") // 2
+    return [
+        pltpu.make_async_copy(block.at[partner(chip, mask, chips)], target, sems.at[mask])
+        for mask, target in enumerate(targets)
+    ]
+
+
 def forward_body(
-    slot, section, sections, peers, wait_chunk,
+    slot, section, sections, chips, wait_chunk,
     w_score, wk, wv, cosine, sine, mask, ends, target,
-    saved, keys, values, probs, scales, grads, sent, outgoing,
-    acc_k, acc_v, normed, mixed, block, sem,
+    saved, keys, values, probs, scales, grads, *rest,
 ):
+    sent, outgoing = rest[:chips], rest[chips]
+    acc_k, acc_v, normed, mixed, block, sems = rest[chips + 1 :]
     width, model = outgoing.shape
     features = KV_HEADS * HD
     step = CHUNK // 2
-    share = model // peers
-    wide = block.shape[2] - features
 
     def chunk_of(ref, start):
         return ref[slot, :, start : start + step].astype(F32)
@@ -230,11 +262,10 @@
         out = dot(prob_b[head * width : (head + 1) * width, :], values[slot, :, head_cols(head)])
         mixed[:, head_cols(head)] = out.astype(BF16)
 
-    for peer in range(peers):
-        block[peer, :, :share] = normed[:, peer * share : (peer + 1) * share]
-        block[peer, :, wide:] = mixed[...]
-    copy = pltpu.make_async_copy(block, sent.at[:, slot], sem)
-    copy.start()
+    fill_block(block, normed, mixed)
+    copies = block_copies(block, [ref.at[slot] for ref in sent], sems)
+    for copy in copies:
+        copy.start()
 
     @pl.loop(0, model // CHUNK)
     def _(c):
@@ -264,25 +295,34 @@
             value = first * w_score[:, c : c + step] - last_of(c) * second
             grads[slot, :, c : c + step] = value.astype(BF16)
 
-    copy.wait()
+    for copy in copies:
+        copy.wait()
 
 
 def backward_kernel(
-    tick, sections, micro, peers, slots,
+    tick, sections, micro, chips, groups,
     incoming, wk, wv, cosine, sine, saved, keys, values, probs, scales, grads,
     *rest,
 ):
-    sent = rest[len(slots) + 2 : 2 * len(slots) + 2]
-    outgoing = rest[2 * len(slots) + 2]
-    acc, full, current, flat, block, sem = rest[2 * len(slots) + 3 :]
+    count = len(groups) * chips
+    sent = rest[count + 2 : 2 * count + 2]
+    outgoing = rest[2 * count + 2]
+    acc, full, current, flat, block, sems = rest[2 * count + 3 :]
     section = lax.axis_index("section")
     offset = tick - 2 * (sections - 1 - section)
     slot = jnp.clip(offset, 0, micro - 1)
     width, model = incoming.shape
     features = KV_HEADS * HD
     step = CHUNK // 2
-    share = model // peers
-    wide = block.shape[2] - 2 * features
+
+    def for_group(act):
+        for n, group in enumerate(groups):
+            @pl.when((slot >= group[0]) & (slot <= group[-1]))
+            def _():
+                index = jnp.clip(slot - group[0], 0, len(group) - 1)
+                targets = [ref.at[index] for ref in sent[n * chips : (n + 1) * chips]]
+                for copy in block_copies(block, targets, sems):
+                    act(copy)
 
     @pl.when((offset >= 0) & (offset < micro))
     def _():
@@ -323,13 +363,8 @@
             turned = vec * cos_value - pltpu.roll(vec, HD // 2, 1) * sin_value
             flat[:, head_cols(head)] = turned.astype(BF16)
 
-        for peer in range(peers):
-            block[peer, :, :share] = current[:, peer * share : (peer + 1) * share]
-            block[peer, :, wide:] = flat[...]
-        for which, out in zip(slots, sent):
-            @pl.when(slot == which)
-            def _():
-                pltpu.make_async_copy(block, out, sem).start()
+        fill_block(block, current, flat)
+        for_group(lambda copy: copy.start())
 
         @pl.when(section != 0)
         def _():
@@ -359,30 +394,61 @@
                 )
                 outgoing[:, cols] = value.astype(BF16)
 
-        for which, out in zip(slots, sent):
-            @pl.when(slot == which)
-            def _():
-                pltpu.make_async_copy(block, out, sem).wait()
-
-
-def gather_kernel(slots, share, wide, features, forward, *rest):
-    backward, before, (key_out, value_out) = rest[: len(slots)], rest[len(slots) : -2], rest[-2:]
-    tokens = forward.shape[0] * forward.shape[2]
-    key_parts = [before[0][...]] if before else []
-    value_parts = [before[1][...]] if before else []
-    for slot, block in zip(slots, backward):
-        def rows(ref, start, size):
-            return ref[:, :, start : start + size].reshape(tokens, size)
-
-        def forward_rows(start, size):
-            return forward[:, slot, :, start : start + size].reshape(tokens, size)
-
-        normed = forward_rows(0, share)
-        key_parts.append(dot_ta(normed, rows(block, wide, features)))
-        value_parts.append(dot_ta(normed, rows(block, wide + features, features)))
-        value_parts.append(dot_ta(rows(block, 0, share), forward_rows(wide, features)))
-    key_out[...] = sum(key_parts[1:], key_parts[0])
-    value_out[...] = sum(value_parts[1:], value_parts[0])
+        for_group(lambda copy: copy.wait())
+
+
+def gather_kernel(groups, share, wide, features, final, *rest):
+    count = 2 + 2 * len(groups)
+    forward, backward = rest[:2], rest[2:count]
+    before = rest[count : count + 2] if final else ()
+    key_out, value_out = rest[count + len(before) : count + len(before) + 2]
+    normed, mixed, grads, flat, totals, sems, out_sems = rest[count + len(before) + 2 :]
+    mine = pl.multiple_of(lax.axis_index("dp") % 2 * wide, HD)
+    first = groups[0][0]
+    slots = normed.shape[2]
+    pairs = []
+    for half, ref in enumerate(forward):
+        at = ref.at[:, pl.ds(first, slots)]
+        pairs.append((at.at[:, :, :, pl.ds(mine, wide)], normed.at[half]))
+        pairs.append((at.at[:, :, :, pl.ds(2 * wide, features)], mixed.at[half]))
+    for n, ref in enumerate(backward):
+        group = groups[n // 2]
+        inside = pl.ds(group[0] - first, len(group))
+        pairs.append((ref.at[:, :, :, pl.ds(mine, wide)], grads.at[n % 2, :, inside]))
+        pairs.append((ref.at[:, :, :, pl.ds(2 * wide, 2 * features)], flat.at[n % 2, :, inside]))
+    copies = [pltpu.make_async_copy(*pair, sems.at[n]) for n, pair in enumerate(pairs)]
+    for copy in copies:
+        copy.start()
+    for copy in copies:
+        copy.wait()
+    tokens = normed.shape[0] * normed.shape[1] * normed.shape[3]
+
+    def rows(ref, slot, start, size):
+        return ref[:, :, slot, :, start : start + size].reshape(tokens, size)
+
+    size = HD if share % HD == 0 else share
+    outs = []
+    for start in range(0, share, size):
+        at = pl.ds(start, size)
+        key_part, value_part = [ref[at, :] for ref in before] if final else (0.0, 0.0)
+        for slot in range(slots):
+            left = rows(normed, slot, start, size)
+            key_part += dot_ta(left, rows(flat, slot, 0, features))
+            value_part += dot_ta(left, rows(flat, slot, features, features))
+            value_part += dot_ta(rows(grads, slot, start, size), rows(mixed, slot, 0, features))
+        if final:
+            totals[0, at, :] = key_part
+            totals[1, at, :] = value_part
+            for n, out in enumerate((key_out, value_out)):
+                outs.append(
+                    pltpu.make_async_copy(totals.at[n, at], out.at[at], out_sems.at[len(outs)])
+                )
+                outs[-1].start()
+        else:
+            key_out[at, :] = key_part
+            value_out[at, :] = value_part
+    for copy in outs:
+        copy.wait()
 
 
 def in_vmem(shape, dtype):
@@ -392,6 +458,7 @@
 def shards(x0, w_key, w_value, w_score, segments, lengths, grades):
     sections = lax.axis_size("section")
     peers = lax.axis_size("dp")
+    chips = peers // 2
     micro, width, model = x0.shape
     wk, wv = w_key[0], w_value[0]
     features = wk.shape[1]
@@ -420,24 +487,28 @@
         in_vmem((micro, width, model), BF16),
     ]
     token = in_vmem((8, HD), F32)
-    send_forward = jax.ShapeDtypeStruct((peers, micro, width, wide + features), BF16)
-    send_backward = jax.ShapeDtypeStruct((peers, width, wide + 2 * features), BF16)
+    send_forward = pltpu.HBM((micro, width, 2 * wide + features), BF16)
+    groups = [tuple(range(micro - 2)), (micro - 2,), (micro - 1,)]
+    send_backward = [
+        pltpu.HBM((len(group), width, 2 * wide + 2 * features), BF16) for group in groups
+    ]
     row = jax.ShapeDtypeStruct((width, model), BF16)
     forward_scratch = [
         pltpu.VMEM((width, features), F32),
         pltpu.VMEM((width, features), F32),
         pltpu.VMEM((width, model), BF16),
         pltpu.VMEM((width, features), BF16),
-        pltpu.VMEM((peers, width, wide + features), BF16),
-        pltpu.SemaphoreType.DMA,
+        pltpu.VMEM((chips, width, 2 * wide + features), BF16),
+        pltpu.SemaphoreType.DMA((chips,)),
     ]
     inputs = [wk, wv, x0, w_score.reshape(1, model), segments, lengths.reshape(1, micro), grades]
     chunks = model // CHUNK
+    sends = [send_forward] * chips + [shape for shape in send_backward for _ in range(chips)]
     made = pl.pallas_call(
-        functools.partial(first_kernel, sections, micro, peers),
-        out_shape=tables + state + [send_forward] + [send_backward] * micro + [token, row],
+        functools.partial(first_kernel, sections, micro, chips),
+        out_shape=tables + state + sends + [token, row],
         in_specs=[HBM] * len(inputs),
-        out_specs=[VMEM] * (len(tables) + len(state)) + [HBM] * (1 + micro) + [VMEM, VMEM],
+        out_specs=[VMEM] * (len(tables) + len(state)) + [HBM] * len(sends) + [VMEM, VMEM],
         scratch_shapes=[
             pltpu.VMEM(segments.shape, jnp.int32),
             pltpu.SMEM((1, micro), jnp.int32),
@@ -451,21 +522,31 @@
         name="first",
     )(*[pltpu.with_memory_space_constraint(value, pltpu.HBM) for value in inputs])
     w_score, wk, wv, cosine, sine, mask, ends, target = made[: len(tables)]
-    held = list(made[len(tables) : len(tables) + len(state) + 1])
-    blocks = list(made[len(tables) + len(state) + 1 : -2])
+    held = list(made[len(tables) : len(tables) + len(state) + chips])
+    blocks = list(made[len(tables) + len(state) + chips : -2])
+    blocks = [blocks[n : n + chips] for n in range(0, len(blocks), chips)]
     token_value, produced = made[-2:]
+
+    def senders(tick, rank):
+        return [s for s in range(sections) if rank(s) < sections - 1 and 0 <= tick - 2 * rank(s) < micro]
+
+    def up(section):
+        return section
+
+    def down(section):
+        return sections - 1 - section
 
     cost = pl.CostEstimate(flops=1000000, bytes_accessed=1000000, transcendentals=0)
     empty = jnp.zeros((width, model), BF16)
-    incoming = [empty, empty, shifted(produced, "section", 1)]
+    incoming = [empty, empty, shifted(produced, 1, senders(0, up))]
     for tick in range(1, ticks):
         args = (incoming[tick], w_score, wk, wv, cosine, sine, mask, ends, target)
         count = len(held)
         *held, produced = pl.pallas_call(
-            functools.partial(forward_kernel, tick, sections, micro, peers),
-            out_shape=state + [send_forward, row],
-            in_specs=[VMEM] * (len(args) + len(state)) + [HBM],
-            out_specs=[VMEM] * len(state) + [HBM, VMEM],
+            functools.partial(forward_kernel, tick, sections, micro, chips),
+            out_shape=state + [send_forward] * chips + [row],
+            in_specs=[VMEM] * (len(args) + len(state)) + [HBM] * chips,
+            out_specs=[VMEM] * len(state) + [HBM] * chips + [VMEM],
             input_output_aliases={len(args) + n: n for n in range(count)},
             scratch_shapes=forward_scratch,
             compiler_params=params(),
@@ -473,64 +554,91 @@
             name="forward",
         )(*args, *held)
         if tick < ticks - 2:
-            incoming.append(shifted(produced, "section", 1))
-
-    saved, keys, values, probs, scales, grads, sent = held
+            incoming.append(shifted(produced, 1, senders(tick, up)))
+
+    saved, keys, values, probs, scales, grads, *sent = held
     incoming = [empty] * 2
-    received = []
+    masks = sorted(range(1, chips), key=lambda m: (-bin(m).count("1"), m))
+    per_tick = -(-len(masks) // 3)
+    gathered = [None] * len(groups)
     for tick in range(ticks):
-        slots = [tick - 2 * hop for hop in range(sections)]
-        slots = tuple(slot for slot in slots if 0 <= slot < micro)
-        arrived = incoming[tick]
-        if tick == 2:
-            sent, token_value = lax.optimization_barrier((sent, token_value))
-            got_forward = lax.all_to_all(sent, "dp", split_axis=0, concat_axis=0, tiled=True)
-        if tick == last + 1:
-            arrived, got_forward = lax.optimization_barrier((arrived, got_forward))
-        if tick > last + 1:
-            arrived, received[-2] = lax.optimization_barrier((arrived, received[-2]))
-        args = (arrived, wk, wv, cosine, sine, saved, keys, values, probs, scales, grads)
+        for m in masks[(tick - 1) * per_tick : tick * per_tick] if tick else ():
+            sent[m], token_value = lax.optimization_barrier((sent[m], token_value))
+            sent[m] = between_chips(sent[m], m, chips)
+        possible = [tick - 2 * hop for hop in range(sections)]
+        filled = [n for n, group in enumerate(groups) if set(group) & set(possible)]
+        args = (
+            incoming[tick], wk, wv, cosine, sine, saved, keys, values, probs, scales, grads,
+            token_value,
+        )
+        targets = [block for n in filled for block in blocks[n]]
+        shapes = [send_backward[n] for n in filled for _ in range(chips)]
         token_value, *outs = pl.pallas_call(
-            functools.partial(backward_kernel, tick, sections, micro, peers, slots),
-            out_shape=[token] + [send_backward] * len(slots) + [row],
-            in_specs=[VMEM] * (len(args) + 1) + [HBM] * len(slots),
-            out_specs=[VMEM] + [HBM] * len(slots) + [VMEM],
-            input_output_aliases={len(args) + n: n for n in range(1 + len(slots))},
+            functools.partial(
+                backward_kernel, tick, sections, micro, chips, [groups[n] for n in filled]
+            ),
+            out_shape=[token] + shapes + [row],
+            in_specs=[VMEM] * len(args) + [HBM] * len(targets),
+            out_specs=[VMEM] + [HBM] * len(targets) + [VMEM],
+            input_output_aliases={len(args) - 1 + n: n for n in range(1 + len(targets))},
             scratch_shapes=[
                 pltpu.VMEM((width, features), F32),
                 pltpu.VMEM((width, model), F32),
                 pltpu.VMEM((width, model), BF16),
                 pltpu.VMEM((width, 2 * features), BF16),
-                pltpu.VMEM((peers, width, wide + 2 * features), BF16),
-                pltpu.SemaphoreType.DMA,
+                pltpu.VMEM((chips, width, 2 * wide + 2 * features), BF16),
+                pltpu.SemaphoreType.DMA((chips,)),
             ],
             compiler_params=params(),
             cost_estimate=cost,
             name="backward",
-        )(*args, token_value, *[blocks[slot] for slot in slots])
-        for slot, block in zip(slots, outs):
-            blocks[slot] = block
+        )(*args, *targets)
+        for position, n in enumerate(filled):
+            blocks[n] = outs[position * chips : (position + 1) * chips]
         if tick < ticks - 2:
-            incoming.append(shifted(outs[-1], "section", -1))
-        if tick >= last:
-            block = blocks[tick - last]
-            received.append(
-                lax.all_to_all(block, "dp", split_axis=0, concat_axis=0, tiled=True)
-            )
+            incoming.append(shifted(outs[-1], -1, senders(tick, down)))
+
+        def both_cores(parts, token_value):
+            parts, token_value = lax.optimization_barrier((parts, token_value))
+            stacked = jnp.stack(parts)
+            return [stacked, between_cores(stacked, chips)], token_value
+
+        for n, group in enumerate(groups):
+            if tick == last + group[-1]:
+                for m in masks:
+                    blocks[n][m] = between_chips(blocks[n][m], m, chips)
+        if tick == last + groups[0][-1]:
+            forward_blocks, token_value = both_cores(sent, token_value)
+        for n, group in enumerate(groups[:-1]):
+            if tick == last + group[-1] + 1:
+                gathered[n], token_value = both_cores(blocks[n], token_value)
+    gathered[-1], token_value = both_cores(blocks[-1], token_value)
 
     whole = jax.ShapeDtypeStruct((share, features), F32)
     total = ()
-    for slots in (tuple(range(micro - 1)), (micro - 1,)):
-        args = [got_forward, *[received[slot] for slot in slots], *total]
+    for final, chosen in ((False, groups[:-1]), (True, groups[-1:])):
+        args = [*forward_blocks, *[value for group in chosen for value in gathered[groups.index(group)]]]
+        slots = sum(len(group) for group in chosen)
+        at = (2, chips, slots, width)
+        rows_out = share // HD if share % HD == 0 else 1
         total = pl.pallas_call(
-            functools.partial(gather_kernel, slots, share, wide, features),
+            functools.partial(gather_kernel, chosen, share, wide, features, final),
             out_shape=[whole, whole],
-            in_specs=[VMEM] * len(args),
-            out_specs=[VMEM] * 2,
-            compiler_params=params(),
+            in_specs=[HBM] * len(args) + [VMEM] * len(total),
+            out_specs=[HBM if final else VMEM] * 2,
+            scratch_shapes=[
+                pltpu.VMEM(at + (wide,), BF16),
+                pltpu.VMEM(at + (features,), BF16),
+                pltpu.VMEM(at + (wide,), BF16),
+                pltpu.VMEM(at + (2 * features,), BF16),
+                pltpu.VMEM((2, share if final else 8, features), F32),
+                pltpu.SemaphoreType.DMA((2 * len(args),)),
+                pltpu.SemaphoreType.DMA((2 * rows_out,)),
+            ],
+            compiler_params=params(24),
             cost_estimate=cost,
             name="gathered",
-        )(*args)
+        )(*args, *total)
     return (total[0][None], total[1][None])
 
 

time: 262 us -> 173 us (0.66)
  local copies, waits for them, and re-layouts: 39.8 us -> 0.14 us
  starting transfers between devices: 64 us -> 37.1 us
  waiting for transfers between devices: 114 us -> 90.8 us
    unnamed x72 -> x20, local copies, waits for them, and re-layouts: 39.8 us -> 0.12 us
    all_to_all x5 -> x0, starting transfers between devices: 20.9 us -> none  [the longest x4 16.5 us: shards(): lax.all_to_all(block, 'dp', split_axis=0, concat_axis=0, tiled=True)]
    ppermute x16 -> x32, waiting for transfers between devices: 104 us -> 90.8 us  [the longest x16 79.4 us: shifted(): lax.ppermute(value, 'section', [(source, source + steps) for source in se...]
    all_to_all x5 -> x0, waiting for transfers between devices: 9.21 us -> none  [the longest x4 9.2 us: shards(): lax.all_to_all(block, 'dp', split_axis=0, concat_axis=0, tiled=True)]
    ppermute x16 -> x32, starting transfers between devices: 43.1 us -> 37.1 us  [the longest x16 19.7 us: shifted(): lax.ppermute(value, 'section', [(source, source + steps) for source in se...]
    pallas_call x10, Pallas kernels: 9.95 us -> 13 us  [shards(): pl.pallas_call(functools.partial(backward_kernel, tick, sections, micro,...]
    pallas_call x12, Pallas kernels: 32.3 us -> 29.4 us  [the longest x9 16.5 us: shards(): pl.pallas_call(functools.partial(forward_kernel, tick, sections, micro, c...]
  transfers between devices with their start and end apart: 21 -> 32, of which waited for: 12 -> 12; matrix products, arithmetic and copies ran while one was open for 0% -> 0% of each run, Pallas kernels for 11% -> 18%
where the time goes in v2:
time: 173 us; the launch traced here: 172 us
  waiting for transfers between devices  90.8 us (52%)
  Pallas kernels  42.4 us (25%)
  starting transfers between devices  37.1 us (21%)
    ppermute x16, waiting for transfers between devices, shifted(): lax.ppermute(value, 'section', [(source, source + steps) for source in se...  79.4 us
    ppermute x16, starting transfers between devices, shifted(): lax.ppermute(value, 'section', [(source, source + steps) for source in se...  19.7 us
    ppermute x12, starting transfers between devices, between_chips(): return lax.ppermute(value, 'dp', pairs)  16.7 us
    pallas_call x9, Pallas kernels, shards(): pl.pallas_call(functools.partial(forward_kernel, tick, sections, micro, c...  16.5 us
    pallas_call x10, Pallas kernels, shards(): pl.pallas_call(functools.partial(backward_kernel, tick, sections, micro,...  13 us
    ppermute x12, waiting for transfers between devices, between_chips(): return lax.ppermute(value, 'dp', pairs)  10 us
    pallas_call x1, Pallas kernels, shards(): pl.pallas_call(functools.partial(first_kernel, sections, micro, chips), o...  8.46 us
    pallas_call x2, Pallas kernels, shards(): pl.pallas_call(functools.partial(gather_kernel, chosen, share, wide, feat...  4.39 us
  transfers between devices with their start and end apart: 32, of which 12 were waited for; matrix products, arithmetic and copies ran while one was open for 0% of the time, Pallas kernels for 18%

profile of v2, /device:TPU:0, one launch (start us, length us, event | category | flops | bytes accessed | tf_op | source)
XLA Modules:
  0.0 172.3 jit_solution(3420835900333567798)
XLA Ops:
  0.6 8.5 %first.1 = (f32[1,5120]{1,0:T(1,128)S(1)}, bf16[5120,512]{1,0:T(8,128)(2,1)S(1)}, bf16[5120,512]{1,0:T(8,128)(2,1)S(1)}, f32[4,32,128]{2,1,0:T(8,128)S(1)}, f32[...) custom-call(bf16[5120,512]{1,0:T(8,128)(2,1)} %bitcast.24, ...), custom_call_target="tpu_custom_call" | custom-call | tf_op jit(solution)/shard_map/first/pallas_call | solution.py:507
  9.1 1.3 collective-permute-start.1
  10.4 4.9 %forward.9 = (bf16[4,32,5120]{2,1,0:T(8,128)(2,1)S(1)}, bf16[4,32,512]{2,1,0:T(8,128)(2,1)S(1)}, bf16[4,32,512]{2,1,0:T(8,128)(2,1)S(1)}, f32[4,128,32]{2,1,0:T(...) custom-call(bf16[32,5120]{1,0:T(8,128)(2,1)S(1)} %broadcast_in_dim.9, ...), custom_call_target="tpu_custom_call", output_to_operand_aliasing={{0}: (9, {}), {1}: (10, {}), {2}: (11, {}), {3}: (12, {}), ... | custom-call | flops 1000000 | bytes 1000000 | tf_op jit(solution)/shard_map/forward/pallas_call | solution.py:545
  15.3 1.3 collective-permute-start
  16.7 1.8 %collective-permute-done.1.incoming = bf16[32,5120]{1,0:T(8,128)(2,1)S(1)} collective-permute-done((bf16[32,5120]{1,0:T(8,128)(2,1)S(1)}, bf16[32,5120]{1,0:T(8,128)(2,1)S(1)}, u32[]{:S(2)}, u32[]{:S(2)}) %collective-permute-start.1) | collective-permute-done | bytes 327712 | tf_op jit(solution)/shard_map/ppermute | solution.py:28
  18.5 4.8 %forward.10 = (bf16[4,32,5120]{2,1,0:T(8,128)(2,1)S(1)}, bf16[4,32,512]{2,1,0:T(8,128)(2,1)S(1)}, bf16[4,32,512]{2,1,0:T(8,128)(2,1)S(1)}, f32[4,128,32]{2,1,0:T...) custom-call(bf16[32,5120]{1,0:T(8,128)(2,1)S(1)} %collective-permute, ...), custom_call_target="tpu_custom_call", output_to_operand_aliasing={{0}: (9, {}), {1}: (10, {}), {2}: (11, {}), {3}: (12, {}), ... | custom-call | flops 1000000 | bytes 1000000 | tf_op jit(solution)/shard_map/forward/pallas_call | solution.py:545
  23.3 4.4 %collective-permute-start.3 = (bf16[32,5120]{1,0:T(8,128)(2,1)S(1)}, bf16[32,5120]{1,0:T(8,128)(2,1)S(1)}, u32[]{:S(2)}, u32[]{:S(2)}) collective-permute-start(bf16[32,5120]{1,0:T(8,128)(2,1)S(1)} %get-tuple-element.281), channel_id=1, source_target_pairs={{0,8},{8,16},{1,9},{9,17},{2,10},{10,18},{3,11},{11,19},{4,12},{12... | collective-permute-start | bytes 983048 | tf_op jit(solution)/shard_map/ppermute | solution.py:28
  27.8 4.9 %forward.11 = (bf16[4,32,5120]{2,1,0:T(8,128)(2,1)S(1)}, bf16[4,32,512]{2,1,0:T(8,128)(2,1)S(1)}, bf16[4,32,512]{2,1,0:T(8,128)(2,1)S(1)}, f32[4,128,32]{2,1,0:T...) custom-call(bf16[32,5120]{1,0:T(8,128)(2,1)S(1)} %collective-permute, ...), custom_call_target="tpu_custom_call", output_to_operand_aliasing={{0}: (9, {}), {1}: (10, {}), {2}: (11, {}), {3}: (12, {}), ... | custom-call | flops 1000000 | bytes 1000000 | tf_op jit(solution)/shard_map/forward/pallas_call | solution.py:545
  32.7 1.9 %collective-permute-start.2 = (bf16[32,5120]{1,0:T(8,128)(2,1)S(1)}, bf16[32,5120]{1,0:T(8,128)(2,1)S(1)}, u32[]{:S(2)}, u32[]{:S(2)}) collective-permute-start(bf16[32,5120]{1,0:T(8,128)(2,1)S(1)} %get-tuple-element.280), channel_id=1, source_target_pairs={{0,8},{8,16},{1,9},{9,17},{2,10},{10,18},{3,11},{11,19},{4,12},{12... | collective-permute-start | bytes 983048 | tf_op jit(solution)/shard_map/ppermute | solution.py:28
  34.7 0.7 collective-permute-start.5
  35.4 6.1 %collective-permute-done.2.incoming = bf16[32,5120]{1,0:T(8,128)(2,1)S(1)} collective-permute-done((bf16[32,5120]{1,0:T(8,128)(2,1)S(1)}, bf16[32,5120]{1,0:T(8,128)(2,1)S(1)}, u32[]{:S(2)}, u32[]{:S(2)}) %collective-permute-start.2) | collective-permute-done | bytes 327712 | tf_op jit(solution)/shard_map/ppermute | solution.py:28
  41.6 0.7 collective-permute-start.4
  42.4 0.7 collective-permute-start.7
  43.1 0.7 collective-permute-start.6
  43.8 0.8 forward.16
  44.7 0.8 forward.17
  45.8 0.7 collective-permute-start.9
  46.5 0.7 collective-permute-start.12
  47.3 0.7 collective-permute-start.14
  48.1 0.8 collective-permute-start.13
  49.0 1.9 %collective-permute-start.8 = (bf16[4,32,1792]{2,1,0:T(8,128)(2,1)S(1)}, bf16[4,32,1792]{2,1,0:T(8,128)(2,1)S(1)}, u32[]{:S(2)}, u32[]{:S(2)}) collective-permute-start(bf16[4,32,1792]{2,1,0:T(8,128)(2,1)S(1)} %copy-done.1), channel_id=1, source_target_pairs={{0,2},{1,3},{2,0},{3,1},{4,6},{5,7},{6,4},{7,5},{8,10},{9,11},{10,... | collective-permute-start | bytes 1376264 | tf_op jit(solution)/shard_map/ppermute | solution.py:33
  50.9 1.5 collective-permute-start.11
  52.6 1.3 collective-permute-start.16
  54.0 1.3 collective-permute-start.15
  55.3 64.7 %collective-permute-done.16.incoming = bf16[32,5120]{1,0:T(8,128)(2,1)S(1)} collective-permute-done((bf16[32,5120]{1,0:T(8,128)(2,1)S(1)}, bf16[32,5120]{1,0:T(8,128)(2,1)S(1)}, u32[]{:S(2)}, u32[]{:S(2)}) %collective-permute-start.16) | collective-permute-done | bytes 327712 | tf_op jit(solution)/shard_map/ppermute | solution.py:28
  120.0 2.8 %backward.16 = (f32[8,128]{1,0:T(8,128)S(1)}, bf16[2,32,2304]{2,1,0:T(8,128)(2,1)}, bf16[2,32,2304]{2,1,0:T(8,128)(2,1)}, bf16[2,32,2304]{2,1,0:T(8,128)(2,1)}, ...) custom-call(bf16[32,5120]{1,0:T(8,128)(2,1)S(1)} %collective-permute, ...), custom_call_target="tpu_custom_call", output_to_operand_aliasing={{0}: (11, {}), {1}: (12, {}), {2}: (13, {}), {3}: (14, {}),... | custom-call | flops 1000000 | bytes 1000000 | tf_op jit(solution)/shard_map/backward/pallas_call | solution.py:576
  122.7 1.3 collective-permute-start.22
  124.0 3.5 %collective-permute-done.15.incoming = bf16[32,5120]{1,0:T(8,128)(2,1)S(1)} collective-permute-done((bf16[32,5120]{1,0:T(8,128)(2,1)S(1)}, bf16[32,5120]{1,0:T(8,128)(2,1)S(1)}, u32[]{:S(2)}, u32[]{:S(2)}) %collective-permute-start.15) | collective-permute-done | bytes 327712 | tf_op jit(solution)/shard_map/ppermute | solution.py:28
  127.5 2.7 %backward.17 = (f32[8,128]{1,0:T(8,128)S(1)}, bf16[2,32,2304]{2,1,0:T(8,128)(2,1)}, bf16[2,32,2304]{2,1,0:T(8,128)(2,1)}, bf16[2,32,2304]{2,1,0:T(8,128)(2,1)}, ...) custom-call(bf16[32,5120]{1,0:T(8,128)(2,1)S(1)} %collective-permute, ...), custom_call_target="tpu_custom_call", output_to_operand_aliasing={{0}: (11, {}), {1}: (12, {}), {2}: (13, {}), {3}: (14, {}),... | custom-call | flops 1000000 | bytes 1000000 | tf_op jit(solution)/shard_map/backward/pallas_call | solution.py:576
  130.2 1.3 collective-permute-start.18
  131.6 2.8 %collective-permute-start.19 = (bf16[2,32,2304]{2,1,0:T(8,128)(2,1)}, bf16[2,32,2304]{2,1,0:T(8,128)(2,1)S(1)}, u32[]{:S(2)}, u32[]{:S(2)}) collective-permute-start(bf16[2,32,2304]{2,1,0:T(8,128)(2,1)} %get-tuple-element.439), channel_id=1, source_target_pairs={{0,2},{1,3},{2,0},{3,1},{4,6},{5,7},{6,4},{7,5},{8,10},{9,11},{10,... | collective-permute-start | bytes 884744 | tf_op jit(solution)/shard_map/ppermute | solution.py:33
  134.3 2.6 %collective-permute-start.20 = (bf16[2,32,2304]{2,1,0:T(8,128)(2,1)}, bf16[2,32,2304]{2,1,0:T(8,128)(2,1)S(1)}, u32[]{:S(2)}, u32[]{:S(2)}) collective-permute-start(bf16[2,32,2304]{2,1,0:T(8,128)(2,1)} %get-tuple-element.440), channel_id=1, source_target_pairs={{0,4},{1,5},{2,6},{3,7},{4,0},{5,1},{6,2},{7,3},{8,12},{9,13},{10,... | collective-permute-start | bytes 884744 | tf_op jit(solution)/shard_map/ppermute | solution.py:33
  137.1 2.8 %collective-permute-done.22.incoming = bf16[32,5120]{1,0:T(8,128)(2,1)S(1)} collective-permute-done((bf16[32,5120]{1,0:T(8,128)(2,1)S(1)}, bf16[32,5120]{1,0:T(8,128)(2,1)S(1)}, u32[]{:S(2)}, u32[]{:S(2)}) %collective-permute-start.22) | collective-permute-done | bytes 327712 | tf_op jit(solution)/shard_map/ppermute | solution.py:28
  140.0 3.5 %backward.18 = (f32[8,128]{1,0:T(8,128)S(1)}, bf16[1,32,2304]{2,1,0:T(8,128)(2,1)}, bf16[1,32,2304]{2,1,0:T(8,128)(2,1)}, bf16[1,32,2304]{2,1,0:T(8,128)(2,1)}, ...) custom-call(bf16[32,5120]{1,0:T(8,128)(2,1)S(1)} %collective-permute, ...), custom_call_target="tpu_custom_call", output_to_operand_aliasing={{0}: (11, {}), {1}: (12, {}), {2}: (13, {}), {3}: (14, {}),... | custom-call | flops 1000000 | bytes 1000000 | tf_op jit(solution)/shard_map/backward/pallas_call | solution.py:576
  143.4 1.5 collective-permute-done.20
  145.4 3.5 %backward.19 = (f32[8,128]{1,0:T(8,128)S(1)}, bf16[1,32,2304]{2,1,0:T(8,128)(2,1)}, bf16[1,32,2304]{2,1,0:T(8,128)(2,1)}, bf16[1,32,2304]{2,1,0:T(8,128)(2,1)}, ...) custom-call(bf16[32,5120]{1,0:T(8,128)(2,1)S(1)} %collective-permute, ...), custom_call_target="tpu_custom_call", output_to_operand_aliasing={{0}: (11, {}), {1}: (12, {}), {2}: (13, {}), {3}: (14, {}),... | custom-call | flops 1000000 | bytes 1000000 | tf_op jit(solution)/shard_map/backward/pallas_call | solution.py:576
  148.9 1.1 collective-permute-start.23
  150.0 2.0 %collective-permute-start.24 = (bf16[1,32,2304]{2,1,0:T(8,128)(2,1)}, bf16[1,32,2304]{2,1,0:T(8,128)(2,1)S(1)}, u32[]{:S(2)}, u32[]{:S(2)}) collective-permute-start(bf16[1,32,2304]{2,1,0:T(8,128)(2,1)} %get-tuple-element.456), channel_id=1, source_target_pairs={{0,4},{1,5},{2,6},{3,7},{4,0},{5,1},{6,2},{7,3},{8,12},{9,13},{10,... | collective-permute-start | bytes 442376 | tf_op jit(solution)/shard_map/ppermute | solution.py:33
  152.5 1.0 collective-permute-start.28
  153.5 1.5 collective-permute-done.23
  155.0 1.6 collective-permute-start.29
  156.6 2.9 %collective-permute-done.24 = bf16[1,32,2304]{2,1,0:T(8,128)(2,1)S(1)} collective-permute-done((bf16[1,32,2304]{2,1,0:T(8,128)(2,1)}, bf16[1,32,2304]{2,1,0:T(8,128)(2,1)S(1)}, u32[]{:S(2)}, u32[]{:S(2)}) %collective-permute-start.24) | collective-permute-done | bytes 147488 | tf_op jit(solution)/shard_map/ppermute | solution.py:33
  159.5 1.7 collective-permute-start.30
  161.4 2.2 %collective-permute-done.29 = bf16[1,32,2304]{2,1,0:T(8,128)(2,1)S(1)} collective-permute-done((bf16[1,32,2304]{2,1,0:T(8,128)(2,1)S(1)}, bf16[1,32,2304]{2,1,0:T(8,128)(2,1)S(1)}, u32[]{:S(2)}, u32[]{:S(2)}) %collective-permute-start.29) | collective-permute-done | bytes 147488 | tf_op jit(solution)/shard_map/ppermute | solution.py:33
  163.6 1.9 %collective-permute-done.30 = bf16[1,32,2304]{2,1,0:T(8,128)(2,1)S(1)} collective-permute-done((bf16[1,32,2304]{2,1,0:T(8,128)(2,1)S(1)}, bf16[1,32,2304]{2,1,0:T(8,128)(2,1)S(1)}, u32[]{:S(2)}, u32[]{:S(2)}) %collective-permute-start.30) | collective-permute-done | bytes 147488 | tf_op jit(solution)/shard_map/ppermute | solution.py:33
  166.4 1.3 collective-permute-done.31.rest_5_
  167.7 2.3 %gathered.2 = (f32[640,512]{1,0:T(8,128)S(1)}, f32[640,512]{1,0:T(8,128)S(1)}) custom-call(bf16[4,4,32,1792]{3,2,1,0:T(8,128)(2,1)S(1)} %pad_maximum_fusion.rest_0_, bf16[4,4,32,1792]{3,2,1,0:T(8,128)(2,1)S(1)} %collective-permute-done.17.rest_1_, bf16[4,2,32,2304]{3,2,1,0:T(8,128)(2,1)S(1)} %pad_maximum_fusion.1.rest_2_, ...), custom_call_target="tpu_custom_call" | custom-call | flops 1000000 | bytes 1000000 | tf_op jit(solution)/shard_map/gathered/pallas_call | solution.py:624
  170.0 2.1 %gathered.3 = (f32[640,512]{1,0:T(8,128)}, f32[640,512]{1,0:T(8,128)}) custom-call(bf16[4,4,32,1792]{3,2,1,0:T(8,128)(2,1)S(1)} %pad_maximum_fusion.rest_0_, bf16[4,4,32,1792]{3,2,1,0:T(8,128)(2,1)S(1)} %collective-permute-done.17.rest_1_, bf16[4,1,32,2304]{3,2,1,0:T(8,128)(2,1)S(1)} %pad_maximum_fusion.2.rest_2_, ...), custom_call_target="tpu_custom_call" | custom-call | flops 1000000 | bytes 1000000 | tf_op jit(solution)/shard_map/gathered/pallas_call | solution.py:624
  (63 shorter events, 3.3 us)
Async XLA Ops:
  9.1 9.4 %collective-permute-start.1 = (bf16[32,5120]{1,0:T(8,128)(2,1)S(1)}, bf16[32,5120]{1,0:T(8,128)(2,1)S(1)}, u32[]{:S(2)}, u32[]{:S(2)}) collective-permute-start(bf16[32,5120]{1,0:T(8,128)(2,1)S(1)} %get-tuple-element.259), channel_id=1, source_target_pairs={{0,8},{1,9},{2,10},{3,11},{4,12},{5,13},{6,14},{7,15}} | collective-permute-start | bytes 983048 | tf_op jit(solution)/shard_map/ppermute | solution.py:28
  15.3 12.4 %collective-permute-start = (bf16[32,5120]{1,0:T(8,128)(2,1)S(1)}, bf16[32,5120]{1,0:T(8,128)(2,1)S(1)}, u32[]{:S(2)}, u32[]{:S(2)}) collective-permute-start(bf16[32,5120]{1,0:T(8,128)(2,1)S(1)} %get-tuple-element.258), channel_id=1, source_target_pairs={{0,8},{1,9},{2,10},{3,11},{4,12},{5,13},{6,14},{7,15}} | collective-permute-start | bytes 983048 | tf_op jit(solution)/shard_map/ppermute | solution.py:28
  23.3 11.3 %collective-permute-start.3 = (bf16[32,5120]{1,0:T(8,128)(2,1)S(1)}, bf16[32,5120]{1,0:T(8,128)(2,1)S(1)}, u32[]{:S(2)}, u32[]{:S(2)}) collective-permute-start(bf16[32,5120]{1,0:T(8,128)(2,1)S(1)} %get-tuple-element.281), channel_id=1, source_target_pairs={{0,8},{8,16},{1,9},{9,17},{2,10},{10,18},{3,11},{11,19},{4,12},{12... | collective-permute-start | bytes 983048 | tf_op jit(solution)/shard_map/ppermute | solution.py:28
  32.7 8.8 %collective-permute-start.2 = (bf16[32,5120]{1,0:T(8,128)(2,1)S(1)}, bf16[32,5120]{1,0:T(8,128)(2,1)S(1)}, u32[]{:S(2)}, u32[]{:S(2)}) collective-permute-start(bf16[32,5120]{1,0:T(8,128)(2,1)S(1)} %get-tuple-element.280), channel_id=1, source_target_pairs={{0,8},{8,16},{1,9},{9,17},{2,10},{10,18},{3,11},{11,19},{4,12},{12... | collective-permute-start | bytes 983048 | tf_op jit(solution)/shard_map/ppermute | solution.py:28
  34.7 7.5 %collective-permute-start.5 = (bf16[32,5120]{1,0:T(8,128)(2,1)S(1)}, bf16[32,5120]{1,0:T(8,128)(2,1)S(1)}, u32[]{:S(2)}, u32[]{:S(2)}) collective-permute-start(bf16[32,5120]{1,0:T(8,128)(2,1)S(1)} %get-tuple-element.303), channel_id=1, source_target_pairs={{8,16},{16,24},{9,17},{17,25},{10,18},{18,26},{11,19},{19,27},{12,... | collective-permute-start | bytes 983048 | tf_op jit(solution)/shard_map/ppermute | solution.py:28
  41.6 1.5 collective-permute-start.4
  42.4 1.5 collective-permute-start.7
  43.1 1.5 collective-permute-start.6
  45.8 1.4 collective-permute-start.9
  46.5 1.5 collective-permute-start.12
  47.3 5.2 %collective-permute-start.14 = (bf16[32,5120]{1,0:T(8,128)(2,1)S(1)}, bf16[32,5120]{1,0:T(8,128)(2,1)S(1)}, u32[]{:S(2)}, u32[]{:S(2)}) collective-permute-start(bf16[32,5120]{1,0:T(8,128)(2,1)S(1)} %get-tuple-element.393), channel_id=1, source_target_pairs={{16,8},{24,16},{17,9},{25,17},{18,10},{26,18},{19,11},{27,19},{20,... | collective-permute-start | bytes 983048 | tf_op jit(solution)/shard_map/ppermute | solution.py:28
  48.0 1.0 copy-start.1
  48.0 2.9 %copy-start.3 = (bf16[4,32,1792]{2,1,0:T(8,128)(2,1)S(1)}, bf16[4,32,1792]{2,1,0:T(8,128)(2,1)}, u32[]{:S(2)}) copy-start(bf16[4,32,1792]{2,1,0:T(8,128)(2,1)} %get-tuple-element.381) | copy-start | bytes 1376260
  48.0 4.4 %copy-start.2 = (bf16[4,32,1792]{2,1,0:T(8,128)(2,1)S(1)}, bf16[4,32,1792]{2,1,0:T(8,128)(2,1)}, u32[]{:S(2)}) copy-start(bf16[4,32,1792]{2,1,0:T(8,128)(2,1)} %get-tuple-element.380) | copy-start | bytes 1376260
  48.1 5.7 %collective-permute-start.13 = (bf16[32,5120]{1,0:T(8,128)(2,1)S(1)}, bf16[32,5120]{1,0:T(8,128)(2,1)S(1)}, u32[]{:S(2)}, u32[]{:S(2)}) collective-permute-start(bf16[32,5120]{1,0:T(8,128)(2,1)S(1)} %get-tuple-element.392), channel_id=1, source_target_pairs={{16,8},{24,16},{17,9},{25,17},{18,10},{26,18},{19,11},{27,19},{20,... | collective-permute-start | bytes 983048 | tf_op jit(solution)/shard_map/ppermute | solution.py:28
  49.0 82.5 %collective-permute-start.8 = (bf16[4,32,1792]{2,1,0:T(8,128)(2,1)S(1)}, bf16[4,32,1792]{2,1,0:T(8,128)(2,1)S(1)}, u32[]{:S(2)}, u32[]{:S(2)}) collective-permute-start(bf16[4,32,1792]{2,1,0:T(8,128)(2,1)S(1)} %copy-done.1), channel_id=1, source_target_pairs={{0,2},{1,3},{2,0},{3,1},{4,6},{5,7},{6,4},{7,5},{8,10},{9,11},{10,... | collective-permute-start | bytes 1376264 | tf_op jit(solution)/shard_map/ppermute | solution.py:33
  50.9 83.4 %collective-permute-start.11 = (bf16[4,32,1792]{2,1,0:T(8,128)(2,1)S(1)}, bf16[4,32,1792]{2,1,0:T(8,128)(2,1)S(1)}, u32[]{:S(2)}, u32[]{:S(2)}) collective-permute-start(bf16[4,32,1792]{2,1,0:T(8,128)(2,1)S(1)} %copy-done.3), channel_id=1, source_target_pairs={{0,6},{1,7},{2,4},{3,5},{4,2},{5,3},{6,0},{7,1},{8,14},{9,15},{10,... | collective-permute-start | bytes 1376264 | tf_op jit(solution)/shard_map/ppermute | solution.py:33
  52.4 84.5 %collective-permute-start.10 = (bf16[4,32,1792]{2,1,0:T(8,128)(2,1)S(1)}, bf16[4,32,1792]{2,1,0:T(8,128)(2,1)S(1)}, u32[]{:S(2)}, u32[]{:S(2)}) collective-permute-start(bf16[4,32,1792]{2,1,0:T(8,128)(2,1)S(1)} %copy-done.2), channel_id=1, source_target_pairs={{0,4},{1,5},{2,6},{3,7},{4,0},{5,1},{6,2},{7,3},{8,12},{9,13},{10,... | collective-permute-start | bytes 1376264 | tf_op jit(solution)/shard_map/ppermute | solution.py:33
  52.6 67.4 %collective-permute-start.16 = (bf16[32,5120]{1,0:T(8,128)(2,1)S(1)}, bf16[32,5120]{1,0:T(8,128)(2,1)S(1)}, u32[]{:S(2)}, u32[]{:S(2)}) collective-permute-start(bf16[32,5120]{1,0:T(8,128)(2,1)S(1)} %get-tuple-element.413), channel_id=1, source_target_pairs={{8,0},{16,8},{9,1},{17,9},{10,2},{18,10},{11,3},{19,11},{12,4},{20... | collective-permute-start | bytes 983048 | tf_op jit(solution)/shard_map/ppermute | solution.py:28
  54.0 73.5 %collective-permute-start.15 = (bf16[32,5120]{1,0:T(8,128)(2,1)S(1)}, bf16[32,5120]{1,0:T(8,128)(2,1)S(1)}, u32[]{:S(2)}, u32[]{:S(2)}) collective-permute-start(bf16[32,5120]{1,0:T(8,128)(2,1)S(1)} %get-tuple-element.412), channel_id=1, source_target_pairs={{8,0},{16,8},{9,1},{17,9},{10,2},{18,10},{11,3},{19,11},{12,4},{20... | collective-permute-start | bytes 983048 | tf_op jit(solution)/shard_map/ppermute | solution.py:28
  122.7 17.2 %collective-permute-start.22 = (bf16[32,5120]{1,0:T(8,128)(2,1)S(1)}, bf16[32,5120]{1,0:T(8,128)(2,1)S(1)}, u32[]{:S(2)}, u32[]{:S(2)}) collective-permute-start(bf16[32,5120]{1,0:T(8,128)(2,1)S(1)} %get-tuple-element.442), channel_id=1, source_target_pairs={{8,0},{9,1},{10,2},{11,3},{12,4},{13,5},{14,6},{15,7}} | collective-permute-start | bytes 983048 | tf_op jit(solution)/shard_map/ppermute | solution.py:28
  127.5 9.4 %copy-start = (bf16[4,32,1792]{2,1,0:T(8,128)(2,1)S(1)}, bf16[4,32,1792]{2,1,0:T(8,128)(2,1)}, u32[]{:S(2)}) copy-start(bf16[4,32,1792]{2,1,0:T(8,128)(2,1)} %get-tuple-element.433) | copy-start | bytes 1376260
  130.2 15.2 %collective-permute-start.18 = (bf16[32,5120]{1,0:T(8,128)(2,1)S(1)}, bf16[32,5120]{1,0:T(8,128)(2,1)S(1)}, u32[]{:S(2)}, u32[]{:S(2)}) collective-permute-start(bf16[32,5120]{1,0:T(8,128)(2,1)S(1)} %get-tuple-element.437), channel_id=1, source_target_pairs={{8,0},{9,1},{10,2},{11,3},{12,4},{13,5},{14,6},{15,7}} | collective-permute-start | bytes 983048 | tf_op jit(solution)/shard_map/ppermute | solution.py:28
  131.6 11.9 %collective-permute-start.19 = (bf16[2,32,2304]{2,1,0:T(8,128)(2,1)}, bf16[2,32,2304]{2,1,0:T(8,128)(2,1)S(1)}, u32[]{:S(2)}, u32[]{:S(2)}) collective-permute-start(bf16[2,32,2304]{2,1,0:T(8,128)(2,1)} %get-tuple-element.439), channel_id=1, source_target_pairs={{0,2},{1,3},{2,0},{3,1},{4,6},{5,7},{6,4},{7,5},{8,10},{9,11},{10,... | collective-permute-start | bytes 884744 | tf_op jit(solution)/shard_map/ppermute | solution.py:33
  134.3 10.6 %collective-permute-start.20 = (bf16[2,32,2304]{2,1,0:T(8,128)(2,1)}, bf16[2,32,2304]{2,1,0:T(8,128)(2,1)S(1)}, u32[]{:S(2)}, u32[]{:S(2)}) collective-permute-start(bf16[2,32,2304]{2,1,0:T(8,128)(2,1)} %get-tuple-element.440), channel_id=1, source_target_pairs={{0,4},{1,5},{2,6},{3,7},{4,0},{5,1},{6,2},{7,3},{8,12},{9,13},{10,... | collective-permute-start | bytes 884744 | tf_op jit(solution)/shard_map/ppermute | solution.py:33
  136.9 8.1 %collective-permute-start.21 = (bf16[2,32,2304]{2,1,0:T(8,128)(2,1)}, bf16[2,32,2304]{2,1,0:T(8,128)(2,1)S(1)}, u32[]{:S(2)}, u32[]{:S(2)}) collective-permute-start(bf16[2,32,2304]{2,1,0:T(8,128)(2,1)} %get-tuple-element.441), channel_id=1, source_target_pairs={{0,6},{1,7},{2,4},{3,5},{4,2},{5,3},{6,0},{7,1},{8,14},{9,15},{10,... | collective-permute-start | bytes 884744 | tf_op jit(solution)/shard_map/ppermute | solution.py:33
  140.0 27.8 %collective-permute-start.17 = (bf16[4,4,32,1792]{3,2,1,0:T(8,128)(2,1)S(1)}, bf16[4,4,32,1792]{3,2,1,0:T(8,128)(2,1)S(1)}, u32[]{:S(2)}, u32[]{:S(2)}) collective-permute-start(bf16[4,4,32,1792]{3,2,1,0:T(8,128)(2,1)S(1)} %pad_maximum_fusion.rest_0_), channel_id=1, source_target_pairs={{0,1},{1,0},{2,3},{3,2},{4,5},{5,4},{6,7},{7,6},{8,9},{9,8},{10,11... | collective-permute-start | bytes 5505032 | tf_op jit(solution)/shard_map/ppermute | solution.py:37
  145.4 7.1 %copy-start.7 = (bf16[1,32,2304]{2,1,0:T(8,128)(2,1)S(1)}, bf16[1,32,2304]{2,1,0:T(8,128)(2,1)}, u32[]{:S(2)}) copy-start(bf16[1,32,2304]{2,1,0:T(8,128)(2,1)} %get-tuple-element.467) | copy-start | bytes 442372
  145.4 9.6 %copy-start.8 = (bf16[1,32,2304]{2,1,0:T(8,128)(2,1)S(1)}, bf16[1,32,2304]{2,1,0:T(8,128)(2,1)}, u32[]{:S(2)}) copy-start(bf16[1,32,2304]{2,1,0:T(8,128)(2,1)} %get-tuple-element.468) | copy-start | bytes 442372
  145.4 14.1 %copy-start.9 = (bf16[1,32,2304]{2,1,0:T(8,128)(2,1)S(1)}, bf16[1,32,2304]{2,1,0:T(8,128)(2,1)}, u32[]{:S(2)}) copy-start(bf16[1,32,2304]{2,1,0:T(8,128)(2,1)} %get-tuple-element.469) | copy-start | bytes 442372
  145.4 15.7 %copy-start.4 = (bf16[2,32,2304]{2,1,0:T(8,128)(2,1)S(1)}, bf16[2,32,2304]{2,1,0:T(8,128)(2,1)}, u32[]{:S(2)}) copy-start(bf16[2,32,2304]{2,1,0:T(8,128)(2,1)} %get-tuple-element.462) | copy-start | bytes 884740
  148.9 16.6 %copy-start.6 = (bf16[1,32,2304]{2,1,0:T(8,128)(2,1)S(1)}, bf16[1,32,2304]{2,1,0:T(8,128)(2,1)}, u32[]{:S(2)}) copy-start(bf16[1,32,2304]{2,1,0:T(8,128)(2,1)} %get-tuple-element.470) | copy-start | bytes 442372
  148.9 6.0 %collective-permute-start.23 = (bf16[1,32,2304]{2,1,0:T(8,128)(2,1)}, bf16[1,32,2304]{2,1,0:T(8,128)(2,1)S(1)}, u32[]{:S(2)}, u32[]{:S(2)}) collective-permute-start(bf16[1,32,2304]{2,1,0:T(8,128)(2,1)} %get-tuple-element.455), channel_id=1, source_target_pairs={{0,2},{1,3},{2,0},{3,1},{4,6},{5,7},{6,4},{7,5},{8,10},{9,11},{10,... | collective-permute-start | bytes 442376 | tf_op jit(solution)/shard_map/ppermute | solution.py:33
  150.0 9.5 %collective-permute-start.24 = (bf16[1,32,2304]{2,1,0:T(8,128)(2,1)}, bf16[1,32,2304]{2,1,0:T(8,128)(2,1)S(1)}, u32[]{:S(2)}, u32[]{:S(2)}) collective-permute-start(bf16[1,32,2304]{2,1,0:T(8,128)(2,1)} %get-tuple-element.456), channel_id=1, source_target_pairs={{0,4},{1,5},{2,6},{3,7},{4,0},{5,1},{6,2},{7,3},{8,12},{9,13},{10,... | collective-permute-start | bytes 442376 | tf_op jit(solution)/shard_map/ppermute | solution.py:33
  152.0 9.3 %collective-permute-start.25 = (bf16[1,32,2304]{2,1,0:T(8,128)(2,1)}, bf16[1,32,2304]{2,1,0:T(8,128)(2,1)S(1)}, u32[]{:S(2)}, u32[]{:S(2)}) collective-permute-start(bf16[1,32,2304]{2,1,0:T(8,128)(2,1)} %get-tuple-element.457), channel_id=1, source_target_pairs={{0,6},{1,7},{2,4},{3,5},{4,2},{5,3},{6,0},{7,1},{8,14},{9,15},{10,... | collective-permute-start | bytes 442376 | tf_op jit(solution)/shard_map/ppermute | solution.py:33
  152.5 8.9 %collective-permute-start.28 = (bf16[1,32,2304]{2,1,0:T(8,128)(2,1)S(1)}, bf16[1,32,2304]{2,1,0:T(8,128)(2,1)S(1)}, u32[]{:S(2)}, u32[]{:S(2)}) collective-permute-start(bf16[1,32,2304]{2,1,0:T(8,128)(2,1)S(1)} %copy-done.7), channel_id=1, source_target_pairs={{0,2},{1,3},{2,0},{3,1},{4,6},{5,7},{6,4},{7,5},{8,10},{9,11},{10,... | collective-permute-start | bytes 442376 | tf_op jit(solution)/shard_map/ppermute | solution.py:33
  155.0 8.6 %collective-permute-start.29 = (bf16[1,32,2304]{2,1,0:T(8,128)(2,1)S(1)}, bf16[1,32,2304]{2,1,0:T(8,128)(2,1)S(1)}, u32[]{:S(2)}, u32[]{:S(2)}) collective-permute-start(bf16[1,32,2304]{2,1,0:T(8,128)(2,1)S(1)} %copy-done.8), channel_id=1, source_target_pairs={{0,4},{1,5},{2,6},{3,7},{4,0},{5,1},{6,2},{7,3},{8,12},{9,13},{10,... | collective-permute-start | bytes 442376 | tf_op jit(solution)/shard_map/ppermute | solution.py:33
  159.5 6.0 %collective-permute-start.30 = (bf16[1,32,2304]{2,1,0:T(8,128)(2,1)S(1)}, bf16[1,32,2304]{2,1,0:T(8,128)(2,1)S(1)}, u32[]{:S(2)}, u32[]{:S(2)}) collective-permute-start(bf16[1,32,2304]{2,1,0:T(8,128)(2,1)S(1)} %copy-done.9), channel_id=1, source_target_pairs={{0,6},{1,7},{2,4},{3,5},{4,2},{5,3},{6,0},{7,1},{8,14},{9,15},{10,... | collective-permute-start | bytes 442376 | tf_op jit(solution)/shard_map/ppermute | solution.py:33
  161.2 4.5 %copy-start.5 = (bf16[1,32,2304]{2,1,0:T(8,128)(2,1)S(1)}, bf16[1,32,2304]{2,1,0:T(8,128)(2,1)}, u32[]{:S(2)}) copy-start(bf16[1,32,2304]{2,1,0:T(8,128)(2,1)} %get-tuple-element.458) | copy-start | bytes 442372
  161.3 6.4 %collective-permute-start.27 = (bf16[4,2,32,2304]{3,2,1,0:T(8,128)(2,1)S(1)}, bf16[4,2,32,2304]{3,2,1,0:T(8,128)(2,1)S(1)}, u32[]{:S(2)}, u32[]{:S(2)}) collective-permute-start(bf16[4,2,32,2304]{3,2,1,0:T(8,128)(2,1)S(1)} %pad_maximum_fusion.1.rest_2_), channel_id=1, source_target_pairs={{0,1},{1,0},{2,3},{3,2},{4,5},{5,4},{6,7},{7,6},{8,9},{9,8},{10,11... | collective-permute-start | bytes 3538952 | tf_op jit(solution)/shard_map/ppermute | solution.py:37
  165.6 2.1 %collective-permute-start.31 = (bf16[4,1,32,2304]{3,2,1,0:T(8,128)(2,1)S(1)}, bf16[4,1,32,2304]{3,2,1,0:T(8,128)(2,1)S(1)}, u32[]{:S(2)}, u32[]{:S(2)}) collective-permute-start(bf16[4,1,32,2304]{3,2,1,0:T(8,128)(2,1)S(1)} %pad_maximum_fusion.3.rest_4_), channel_id=1, source_target_pairs={{0,1},{1,0},{2,3},{3,2},{4,5},{5,4},{6,7},{7,6},{8,9},{9,8},{10,11... | collective-permute-start | bytes 1769480 | tf_op jit(solution)/shard_map/ppermute | solution.py:37
  165.8 4.2 %collective-permute-start.26 = (bf16[4,1,32,2304]{3,2,1,0:T(8,128)(2,1)S(1)}, bf16[4,1,32,2304]{3,2,1,0:T(8,128)(2,1)S(1)}, u32[]{:S(2)}, u32[]{:S(2)}) collective-permute-start(bf16[4,1,32,2304]{3,2,1,0:T(8,128)(2,1)S(1)} %pad_maximum_fusion.2.rest_2_), channel_id=1, source_target_pairs={{0,1},{1,0},{2,3},{3,2},{4,5},{5,4},{6,7},{7,6},{8,9},{9,8},{10,11... | collective-permute-start | bytes 1769480 | tf_op jit(solution)/shard_map/ppermute | solution.py:37

commit v3 on v2

--- a/solution.py
+++ b/solution.py
@@ -71,6 +71,15 @@
     freqs = jnp.exp(half_lane * F32(-2.0 / HD) * jnp.log(F32(THETA)))
     sign = jnp.where(lane < HD // 2, -1.0, 1.0)
     index = lax.broadcasted_iota(jnp.int32, (width, 1), 0)
+    angles = lax.broadcasted_iota(jnp.int32, (width, HD), 0).astype(F32) * freqs
+    cos_table = jnp.cos(angles)
+    sin_table = jnp.sin(angles) * sign
+
+    def picked(chosen, table):
+        return jnp.dot(
+            chosen, table, precision=lax.Precision.HIGHEST, preferred_element_type=F32
+        )
+
     for slot in range(micro):
         seg_row = segments_ref[slot : slot + 1, :].astype(F32)
         seg_col = to_column(seg_row, eye)
@@ -78,9 +87,9 @@
         length = lengths_ref[0, slot]
         same = seg_col == seg_row
         offset = jnp.sum(jnp.where(same & (at_col < at_row), 1.0, 0.0), axis=1, keepdims=True)
-        angles = offset * freqs
-        cos_ref[slot] = jnp.cos(angles)
-        sin_ref[slot] = jnp.sin(angles) * sign
+        chosen = jnp.where(offset == at_col.astype(F32), 1.0, 0.0)
+        cos_ref[slot] = picked(chosen, cos_table)
+        sin_ref[slot] = picked(chosen, sin_table)
         allowed = same & (at_col <= at_row) & (at_row < length) & (at_col < length)
         mask = jnp.where(allowed | eye, 1.0, 0.0)
         for head in range(KV_HEADS):
@@ -105,9 +114,9 @@
     saved, keys, values, probs, scales, grads, *rest,
 ):
     sent = rest[:chips]
-    outgoing = rest[-13]
-    segments_ref, lengths_ref, grades_ref, small, key_sems, value_sems = rest[-12:-6]
-    scratch = rest[-6:]
+    outgoing = rest[-12]
+    segments_ref, lengths_ref, grades_ref, small, key_sems, value_sems = rest[-11:-5]
+    scratch = rest[-5:]
     model = wk.shape[0]
     copies = [
         pltpu.make_async_copy(segments_hbm, segments_ref, small.at[0]),
@@ -119,16 +128,16 @@
     for copy in copies:
         copy.start()
 
-    def chunk_copies(c):
+    def key_copy(c):
         cols = pl.ds(c * CHUNK, CHUNK)
-        return (
-            pltpu.make_async_copy(wk_hbm.at[cols], wk.at[cols], key_sems.at[c]),
-            pltpu.make_async_copy(wv_hbm.at[cols], wv.at[cols], value_sems.at[c]),
-        )
+        return pltpu.make_async_copy(wk_hbm.at[cols], wk.at[cols], key_sems.at[c])
+
+    def value_copy(c):
+        cols = pl.ds(c * CHUNK, CHUNK)
+        return pltpu.make_async_copy(wv_hbm.at[cols], wv.at[cols], value_sems.at[c])
 
     for c in range(model // CHUNK):
-        for copy in chunk_copies(c):
-            copy.start()
+        key_copy(c).start()
     for copy in copies[:3]:
         copy.wait()
     make_tables(
@@ -136,16 +145,18 @@
     )
     for copy in copies[3:]:
         copy.wait()
+    for c in range(model // CHUNK):
+        value_copy(c).start()
     section = lax.axis_index("section")
 
     @pl.when(section == 0)
     def _():
-        def wait_chunk(c):
-            for copy in chunk_copies(c):
-                copy.wait()
+        def wait_values():
+            for c in range(model // CHUNK):
+                value_copy(c).wait()
 
         forward_body(
-            0, section, sections, chips, wait_chunk,
+            0, section, sections, chips, (lambda c: key_copy(c).wait(), wait_values),
             w_score, wk, wv, cosine, sine, mask, ends, target,
             saved, keys, values, probs, scales, grads, *sent, outgoing, *scratch,
         )
@@ -153,8 +164,8 @@
     @pl.when(section != 0)
     def _():
         for c in range(model // CHUNK):
-            for copy in chunk_copies(c):
-                copy.wait()
+            key_copy(c).wait()
+            value_copy(c).wait()
 
 
 def row_scale(ref_value_chunks, model):
@@ -213,12 +224,12 @@
 
 
 def forward_body(
-    slot, section, sections, chips, wait_chunk,
+    slot, section, sections, chips, waits,
     w_score, wk, wv, cosine, sine, mask, ends, target,
     saved, keys, values, probs, scales, grads, *rest,
 ):
     sent, outgoing = rest[:chips], rest[chips]
-    acc_k, acc_v, normed, mixed, block, sems = rest[chips + 1 :]
+    acc_k, normed, mixed, block, sems = rest[chips + 1 :]
     width, model = outgoing.shape
     features = KV_HEADS * HD
     step = CHUNK // 2
@@ -231,17 +242,21 @@
     for c in range(0, model, step):
         normed[:, c : c + step] = (chunk_of(saved, c) * scale).astype(BF16)
     acc_k[...] = jnp.zeros_like(acc_k)
-    acc_v[...] = jnp.zeros_like(acc_v)
 
     @pl.loop(0, model // CHUNK)
     def _(c):
-        if wait_chunk is not None:
-            wait_chunk(c)
+        if waits is not None:
+            waits[0](c)
         cols = pl.ds(pl.multiple_of(c * CHUNK, CHUNK), CHUNK)
-        piece = normed[:, cols]
-        acc_k[...] += dot(piece, wk[cols, :])
-        acc_v[...] += dot(piece, wv[cols, :])
-
+        acc_k[...] += dot(normed[:, cols], wk[cols, :])
+
+    if waits is not None:
+        waits[1]()
+    value = None
+    for c in range(0, model, CHUNK):
+        part = dot(normed[:, c : c + CHUNK], wv[c : c + CHUNK, :])
+        value = part if value is None else value + part
+    values[slot] = value.astype(BF16)
     cos_value = cosine[slot]
     sin_value = sine[slot]
     scores = []
@@ -251,7 +266,6 @@
         key = turned.astype(BF16)
         keys[slot, :, head_cols(head)] = key
         scores.append(dot_tb(key, key))
-    values[slot] = acc_v[...].astype(BF16)
     score = jnp.concatenate(scores, axis=0) / HD
     score = jnp.where(mask[slot] > 0.0, score, NEG)
     weight = jnp.exp(score - jnp.max(score, axis=1, keepdims=True))
@@ -300,14 +314,15 @@
 
 
 def backward_kernel(
-    tick, sections, micro, chips, groups,
+    tick, sections, micro, chips, groups, through,
     incoming, wk, wv, cosine, sine, saved, keys, values, probs, scales, grads,
     *rest,
 ):
     count = len(groups) * chips
-    sent = rest[count + 2 : 2 * count + 2]
-    outgoing = rest[2 * count + 2]
-    acc, full, current, flat, block, sems = rest[2 * count + 3 :]
+    total = count + through
+    sent = rest[total + 2 : total + 2 + count]
+    outgoing = rest[2 * total + 2]
+    acc, full, current, flat, block, sems = rest[2 * total + 3 :]
     section = lax.axis_index("section")
     offset = tick - 2 * (sections - 1 - section)
     slot = jnp.clip(offset, 0, micro - 1)
@@ -341,40 +356,48 @@
             cols = pl.ds(pl.multiple_of(c * CHUNK, CHUNK), CHUNK)
             acc[...] += dot(current[:, cols], wv[cols, :])
 
-        cos_value = cosine[slot]
-        sin_value = sine[slot]
-        prob = probs[slot]
-        prob_b = prob.astype(BF16)
-        grad_probs = []
-        for head in range(KV_HEADS):
-            rows = slice(head * width, (head + 1) * width)
-            mixed_grad = acc[:, head_cols(head)].astype(BF16)
-            grad_probs.append(dot_tb(mixed_grad, values[slot, :, head_cols(head)]))
-            flat[:, features + head * HD : features + (head + 1) * HD] = dot_ta(
-                prob_b[rows, :], mixed_grad
-            ).astype(BF16)
-        grad_prob = jnp.concatenate(grad_probs, axis=0)
-        grad_score = prob * (grad_prob - jnp.sum(prob * grad_prob, axis=1, keepdims=True))
-        grad_score = grad_score.astype(BF16)
-        for head in range(KV_HEADS):
-            piece = grad_score[head * width : (head + 1) * width, :]
-            key = keys[slot, :, head_cols(head)]
-            vec = (dot(piece, key) + dot_ta(piece, key)) / HD
-            turned = vec * cos_value - pltpu.roll(vec, HD // 2, 1) * sin_value
-            flat[:, head_cols(head)] = turned.astype(BF16)
-
-        fill_block(block, current, flat)
-        for_group(lambda copy: copy.start())
+        def factors(value_pass):
+            cos_value = cosine[slot]
+            sin_value = sine[slot]
+            prob = probs[slot]
+            prob_b = prob.astype(BF16)
+            grad_probs = []
+            for head in range(KV_HEADS):
+                rows = slice(head * width, (head + 1) * width)
+                mixed_grad = acc[:, head_cols(head)].astype(BF16)
+                grad_probs.append(dot_tb(mixed_grad, values[slot, :, head_cols(head)]))
+                flat[:, features + head * HD : features + (head + 1) * HD] = dot_ta(
+                    prob_b[rows, :], mixed_grad
+                ).astype(BF16)
+            if value_pass:
+                for c in range(0, model, CHUNK):
+                    full[:, c : c + CHUNK] = dot_tb(flat[:, features:], wv[c : c + CHUNK, :])
+            grad_prob = jnp.concatenate(grad_probs, axis=0)
+            grad_score = prob * (grad_prob - jnp.sum(prob * grad_prob, axis=1, keepdims=True))
+            grad_score = grad_score.astype(BF16)
+            for head in range(KV_HEADS):
+                piece = grad_score[head * width : (head + 1) * width, :]
+                key = keys[slot, :, head_cols(head)]
+                vec = (dot(piece, key) + dot_ta(piece, key)) / HD
+                turned = vec * cos_value - pltpu.roll(vec, HD // 2, 1) * sin_value
+                flat[:, head_cols(head)] = turned.astype(BF16)
+            fill_block(block, current, flat)
+
+        @pl.when(section == 0)
+        def _():
+            factors(False)
+            for_group(lambda copy: copy.start())
 
         @pl.when(section != 0)
         def _():
+            factors(True)
+            for_group(lambda copy: copy.start())
             acc[...] = jnp.zeros_like(acc)
 
             @pl.loop(0, model // CHUNK)
             def _(c):
                 cols = pl.ds(pl.multiple_of(c * CHUNK, CHUNK), CHUNK)
-                out = dot_tb(flat[:, :features], wk[cols, :])
-                out = out + dot_tb(flat[:, features:], wv[cols, :])
+                out = full[:, cols] + dot_tb(flat[:, :features], wk[cols, :])
                 full[:, cols] = out
                 along = out * saved[slot, :, cols].astype(F32)
                 total = along[:, :HD]
@@ -397,25 +420,30 @@
         for_group(lambda copy: copy.wait())
 
 
-def gather_kernel(groups, share, wide, features, final, *rest):
-    count = 2 + 2 * len(groups)
-    forward, backward = rest[:2], rest[2:count]
+def gate_kernel(*refs):
+    del refs
+
+
+def gather_kernel(group, pieces, share, wide, features, final, *rest):
+    count = sum(pieces)
+    sources = iter(rest[:count])
     before = rest[count : count + 2] if final else ()
     key_out, value_out = rest[count + len(before) : count + len(before) + 2]
     normed, mixed, grads, flat, totals, sems, out_sems = rest[count + len(before) + 2 :]
     mine = pl.multiple_of(lax.axis_index("dp") % 2 * wide, HD)
-    first = groups[0][0]
-    slots = normed.shape[2]
+    slots = len(group)
     pairs = []
-    for half, ref in enumerate(forward):
-        at = ref.at[:, pl.ds(first, slots)]
-        pairs.append((at.at[:, :, :, pl.ds(mine, wide)], normed.at[half]))
-        pairs.append((at.at[:, :, :, pl.ds(2 * wide, features)], mixed.at[half]))
-    for n, ref in enumerate(backward):
-        group = groups[n // 2]
-        inside = pl.ds(group[0] - first, len(group))
-        pairs.append((ref.at[:, :, :, pl.ds(mine, wide)], grads.at[n % 2, :, inside]))
-        pairs.append((ref.at[:, :, :, pl.ds(2 * wide, 2 * features)], flat.at[n % 2, :, inside]))
+    for half, number in enumerate(pieces):
+        chips = 0
+        for ref in [next(sources) for _ in range(number)]:
+            inside = pl.ds(chips, ref.shape[0])
+            chips += ref.shape[0]
+            if half < 2:
+                ref, size, targets = ref.at[:, pl.ds(group[0], slots)], features, (normed, mixed)
+            else:
+                size, targets = 2 * features, (grads, flat)
+            pairs.append((ref.at[:, :, :, pl.ds(mine, wide)], targets[0].at[half % 2, inside]))
+            pairs.append((ref.at[:, :, :, pl.ds(2 * wide, size)], targets[1].at[half % 2, inside]))
     copies = [pltpu.make_async_copy(*pair, sems.at[n]) for n, pair in enumerate(pairs)]
     for copy in copies:
         copy.start()
@@ -488,13 +516,12 @@
     ]
     token = in_vmem((8, HD), F32)
     send_forward = pltpu.HBM((micro, width, 2 * wide + features), BF16)
-    groups = [tuple(range(micro - 2)), (micro - 2,), (micro - 1,)]
+    groups = [tuple(range(micro - 2)), (micro - 2, micro - 1)]
     send_backward = [
         pltpu.HBM((len(group), width, 2 * wide + 2 * features), BF16) for group in groups
     ]
     row = jax.ShapeDtypeStruct((width, model), BF16)
     forward_scratch = [
-        pltpu.VMEM((width, features), F32),
         pltpu.VMEM((width, features), F32),
         pltpu.VMEM((width, model), BF16),
         pltpu.VMEM((width, features), BF16),
@@ -536,7 +563,7 @@
     def down(section):
         return sections - 1 - section
 
-    cost = pl.CostEstimate(flops=1000000, bytes_accessed=1000000, transcendentals=0)
+    cost = pl.CostEstimate(flops=1000, bytes_accessed=1000, transcendentals=0)
     empty = jnp.zeros((width, model), BF16)
     incoming = [empty, empty, shifted(produced, 1, senders(0, up))]
     for tick in range(1, ticks):
@@ -560,10 +587,8 @@
     incoming = [empty] * 2
     masks = sorted(range(1, chips), key=lambda m: (-bin(m).count("1"), m))
     per_tick = -(-len(masks) // 3)
-    gathered = [None] * len(groups)
     for tick in range(ticks):
         for m in masks[(tick - 1) * per_tick : tick * per_tick] if tick else ():
-            sent[m], token_value = lax.optimization_barrier((sent[m], token_value))
             sent[m] = between_chips(sent[m], m, chips)
         possible = [tick - 2 * hop for hop in range(sections)]
         filled = [n for n, group in enumerate(groups) if set(group) & set(possible)]
@@ -573,9 +598,14 @@
         )
         targets = [block for n in filled for block in blocks[n]]
         shapes = [send_backward[n] for n in filled for _ in range(chips)]
+        through = tick in (last - 2, last + micro - 2)
+        if through:
+            targets += sent
+            shapes += [send_forward] * chips
         token_value, *outs = pl.pallas_call(
             functools.partial(
-                backward_kernel, tick, sections, micro, chips, [groups[n] for n in filled]
+                backward_kernel, tick, sections, micro, chips, [groups[n] for n in filled],
+                chips if through else 0,
             ),
             out_shape=[token] + shapes + [row],
             in_specs=[VMEM] * len(args) + [HBM] * len(targets),
@@ -595,34 +625,44 @@
         )(*args, *targets)
         for position, n in enumerate(filled):
             blocks[n] = outs[position * chips : (position + 1) * chips]
+        if through:
+            sent = list(outs[-1 - chips : -1])
         if tick < ticks - 2:
             incoming.append(shifted(outs[-1], -1, senders(tick, down)))
-
-        def both_cores(parts, token_value):
-            parts, token_value = lax.optimization_barrier((parts, token_value))
-            stacked = jnp.stack(parts)
-            return [stacked, between_cores(stacked, chips)], token_value
 
         for n, group in enumerate(groups):
             if tick == last + group[-1]:
                 for m in masks:
                     blocks[n][m] = between_chips(blocks[n][m], m, chips)
-        if tick == last + groups[0][-1]:
-            forward_blocks, token_value = both_cores(sent, token_value)
-        for n, group in enumerate(groups[:-1]):
-            if tick == last + group[-1] + 1:
-                gathered[n], token_value = both_cores(blocks[n], token_value)
-    gathered[-1], token_value = both_cores(blocks[-1], token_value)
+
+    stacked = jnp.stack(sent)
+    forward_blocks = [stacked], [between_cores(stacked, chips)]
+    passed = blocks[0]
+    token_value, *passed = pl.pallas_call(
+        gate_kernel,
+        out_shape=[token] + [pltpu.HBM(value.shape, value.dtype) for value in passed],
+        in_specs=[VMEM] + [HBM] * len(passed),
+        out_specs=[VMEM] + [HBM] * len(passed),
+        input_output_aliases={n: n for n in range(1 + len(passed))},
+        cost_estimate=cost,
+        name="gate",
+    )(token_value, *passed)
+
+    stacked = jnp.stack(passed)
+    gathered = [([stacked], [between_cores(stacked, chips)])]
+    ours = [value[None] for value in blocks[1]]
+    gathered.append((ours, [between_cores(value, chips) for value in ours]))
 
     whole = jax.ShapeDtypeStruct((share, features), F32)
     total = ()
-    for final, chosen in ((False, groups[:-1]), (True, groups[-1:])):
-        args = [*forward_blocks, *[value for group in chosen for value in gathered[groups.index(group)]]]
-        slots = sum(len(group) for group in chosen)
-        at = (2, chips, slots, width)
+    for final, chosen in ((False, 0), (True, 1)):
+        args = [value for half in (*forward_blocks, *gathered[chosen]) for value in half]
+        pieces = [len(half) for half in (*forward_blocks, *gathered[chosen])]
+        chosen = groups[chosen]
+        at = (2, chips, len(chosen), width)
         rows_out = share // HD if share % HD == 0 else 1
         total = pl.pallas_call(
-            functools.partial(gather_kernel, chosen, share, wide, features, final),
+            functools.partial(gather_kernel, chosen, pieces, share, wide, features, final),
             out_shape=[whole, whole],
             in_specs=[HBM] * len(args) + [VMEM] * len(total),
             out_specs=[HBM if final else VMEM] * 2,

time: 173 us -> 178 us (1.029)
  starting transfers between devices: 37.1 us -> 32.7 us
  waiting for transfers between devices: 90.8 us -> 94.3 us
  other arithmetic: 0.53 us -> 3.14 us
  Pallas kernels: 42.4 us -> 44.3 us
  local copies, waits for them, and re-layouts: 0.14 us -> 1.99 us
    ppermute x12 -> x9, waiting for transfers between devices: 10 us -> 29.4 us  [between_chips(): return lax.ppermute(value, 'dp', pairs)]
    ppermute x16, waiting for transfers between devices: 79.4 us -> 64.9 us  [shifted(): lax.ppermute(value, 'section', [(source, source + steps) for source in se...]
    ppermute x12 -> x9, starting transfers between devices: 16.7 us -> 11.3 us  [between_chips(): return lax.ppermute(value, 'dp', pairs)]
    another operation x4 -> x2, other arithmetic: 0.53 us -> 3.14 us  [the longest x1 1.67 us: shards(): stacked = jnp.stack(sent)]
    unnamed x20 -> x26, local copies, waits for them, and re-layouts: 0.12 us -> 1.97 us
    pallas_call x2 -> x3, Pallas kernels: 4.39 us -> 5.92 us  [the longest x2 5.92 us: shards(): pl.pallas_call(functools.partial(gather_kernel, chosen, pieces, share, wi...]
  transfers between devices with their start and end apart: 32 -> 31, of which waited for: 12 -> 8; matrix products, arithmetic and copies ran while one was open for 0% -> 2% of each run, Pallas kernels for 18% -> 18%
where the time goes in v3:
time: 178 us
  waiting for transfers between devices  94.3 us (53%)
  Pallas kernels  44.3 us (25%)
  starting transfers between devices  32.7 us (18%)
  other arithmetic  3.14 us (2%)
  local copies, waits for them, and re-layouts  1.99 us (1%)
    ppermute x16, waiting for transfers between devices, shifted(): lax.ppermute(value, 'section', [(source, source + steps) for source in se...  64.9 us
    ppermute x9, waiting for transfers between devices, between_chips(): return lax.ppermute(value, 'dp', pairs)  29.4 us
    ppermute x16, starting transfers between devices, shifted(): lax.ppermute(value, 'section', [(source, source + steps) for source in se...  20.2 us
    pallas_call x9, Pallas kernels, shards(): pl.pallas_call(functools.partial(forward_kernel, tick, sections, micro, c...  16.5 us
    pallas_call x10, Pallas kernels, shards(): pl.pallas_call(functools.partial(backward_kernel, tick, sections, micro,...  13.1 us
    ppermute x9, starting transfers between devices, between_chips(): return lax.ppermute(value, 'dp', pairs)  11.3 us
    pallas_call x1, Pallas kernels, shards(): pl.pallas_call(functools.partial(first_kernel, sections, micro, chips), o...  8.74 us
    pallas_call x2, Pallas kernels, shards(): pl.pallas_call(functools.partial(gather_kernel, chosen, pieces, share, wi...  5.92 us
  transfers between devices with their start and end apart: 31, of which 8 were waited for; matrix products, arithmetic and copies ran while one was open for 2% of the time, Pallas kernels for 18%

profile of v3, /device:TPU:0, one launch (start us, length us, event | category | flops | bytes accessed | tf_op | source)
XLA Modules:
  0.0 177.8 jit_solution(12173269344004217134)
XLA Ops:
  0.6 8.7 %first.1 = (f32[1,5120]{1,0:T(1,128)S(1)}, bf16[5120,512]{1,0:T(8,128)(2,1)S(1)}, bf16[5120,512]{1,0:T(8,128)(2,1)S(1)}, f32[4,32,128]{2,1,0:T(8,128)S(1)}, f32[...) custom-call(bf16[5120,512]{1,0:T(8,128)(2,1)} %bitcast.28, ...), custom_call_target="tpu_custom_call" | custom-call | tf_op jit(solution)/shard_map/first/pallas_call | solution.py:534
  9.4 1.6 collective-permute-start.1
  11.1 4.9 %forward.9 = (bf16[4,32,5120]{2,1,0:T(8,128)(2,1)S(1)}, bf16[4,32,512]{2,1,0:T(8,128)(2,1)S(1)}, bf16[4,32,512]{2,1,0:T(8,128)(2,1)S(1)}, f32[4,128,32]{2,1,0:T(...) custom-call(bf16[32,5120]{1,0:T(8,128)(2,1)S(1)} %broadcast_in_dim.2, ...), custom_call_target="tpu_custom_call", output_to_operand_aliasing={{0}: (9, {}), {1}: (10, {}), {2}: (11, {}), {3}: (12, {}), ... | custom-call | flops 1000 | bytes 1000 | tf_op jit(solution)/shard_map/forward/pallas_call | solution.py:572
  15.9 1.3 collective-permute-start
  17.2 1.8 %collective-permute-done.1.incoming = bf16[32,5120]{1,0:T(8,128)(2,1)S(1)} collective-permute-done((bf16[32,5120]{1,0:T(8,128)(2,1)S(1)}, bf16[32,5120]{1,0:T(8,128)(2,1)S(1)}, u32[]{:S(2)}, u32[]{:S(2)}) %collective-permute-start.1) | collective-permute-done | bytes 327712 | tf_op jit(solution)/shard_map/ppermute | solution.py:28
  19.0 4.8 %forward.10 = (bf16[4,32,5120]{2,1,0:T(8,128)(2,1)S(1)}, bf16[4,32,512]{2,1,0:T(8,128)(2,1)S(1)}, bf16[4,32,512]{2,1,0:T(8,128)(2,1)S(1)}, f32[4,128,32]{2,1,0:T...) custom-call(bf16[32,5120]{1,0:T(8,128)(2,1)S(1)} %collective-permute, ...), custom_call_target="tpu_custom_call", output_to_operand_aliasing={{0}: (9, {}), {1}: (10, {}), {2}: (11, {}), {3}: (12, {}), ... | custom-call | flops 1000 | bytes 1000 | tf_op jit(solution)/shard_map/forward/pallas_call | solution.py:572
  23.9 4.4 %collective-permute-start.3 = (bf16[32,5120]{1,0:T(8,128)(2,1)S(1)}, bf16[32,5120]{1,0:T(8,128)(2,1)S(1)}, u32[]{:S(2)}, u32[]{:S(2)}) collective-permute-start(bf16[32,5120]{1,0:T(8,128)(2,1)S(1)} %get-tuple-element.266), channel_id=1, source_target_pairs={{0,8},{8,16},{1,9},{9,17},{2,10},{10,18},{3,11},{11,19},{4,12},{12... | collective-permute-start | bytes 983048 | tf_op jit(solution)/shard_map/ppermute | solution.py:28
  28.3 4.9 %forward.11 = (bf16[4,32,5120]{2,1,0:T(8,128)(2,1)S(1)}, bf16[4,32,512]{2,1,0:T(8,128)(2,1)S(1)}, bf16[4,32,512]{2,1,0:T(8,128)(2,1)S(1)}, f32[4,128,32]{2,1,0:T...) custom-call(bf16[32,5120]{1,0:T(8,128)(2,1)S(1)} %collective-permute, ...), custom_call_target="tpu_custom_call", output_to_operand_aliasing={{0}: (9, {}), {1}: (10, {}), {2}: (11, {}), {3}: (12, {}), ... | custom-call | flops 1000 | bytes 1000 | tf_op jit(solution)/shard_map/forward/pallas_call | solution.py:572
  33.2 1.9 %collective-permute-start.2 = (bf16[32,5120]{1,0:T(8,128)(2,1)S(1)}, bf16[32,5120]{1,0:T(8,128)(2,1)S(1)}, u32[]{:S(2)}, u32[]{:S(2)}) collective-permute-start(bf16[32,5120]{1,0:T(8,128)(2,1)S(1)} %get-tuple-element.265), channel_id=1, source_target_pairs={{0,8},{8,16},{1,9},{9,17},{2,10},{10,18},{3,11},{11,19},{4,12},{12... | collective-permute-start | bytes 983048 | tf_op jit(solution)/shard_map/ppermute | solution.py:28
  35.2 0.7 collective-permute-start.5
  35.9 5.6 %collective-permute-done.2.incoming = bf16[32,5120]{1,0:T(8,128)(2,1)S(1)} collective-permute-done((bf16[32,5120]{1,0:T(8,128)(2,1)S(1)}, bf16[32,5120]{1,0:T(8,128)(2,1)S(1)}, u32[]{:S(2)}, u32[]{:S(2)}) %collective-permute-start.2) | collective-permute-done | bytes 327712 | tf_op jit(solution)/shard_map/ppermute | solution.py:28
  41.6 0.7 collective-permute-start.4
  42.3 0.7 collective-permute-start.7
  43.1 0.9 collective-permute-start.6
  44.0 0.8 forward.16
  44.9 0.8 forward.17
  45.8 0.8 collective-permute-start.8
  46.7 2.1 %collective-permute-start.11 = (bf16[4,32,1792]{2,1,0:T(8,128)(2,1)S(1)}, bf16[4,32,1792]{2,1,0:T(8,128)(2,1)S(1)}, u32[]{:S(2)}, u32[]{:S(2)}) collective-permute-start(bf16[4,32,1792]{2,1,0:T(8,128)(2,1)S(1)} %copy-done.1), channel_id=1, source_target_pairs={{0,2},{1,3},{2,0},{3,1},{4,6},{5,7},{6,4},{7,5},{8,10},{9,11},{10,... | collective-permute-start | bytes 1376264 | tf_op jit(solution)/shard_map/ppermute | solution.py:33
  48.8 1.5 collective-permute-start.12
  50.5 0.7 collective-permute-start.10
  51.2 0.7 collective-permute-start.9
  52.0 0.7 collective-permute-start.15
  52.7 7.5 %collective-permute-done.11.rest_10_ = bf16[4,32,1792]{2,1,0:T(8,128)(2,1)S(1)} collective-permute-done((bf16[4,32,1792]{2,1,0:T(8,128)(2,1)S(1)}, bf16[4,32,1792]{2,1,0:T(8,128)(2,1)S(1)}, u32[]{:S(2)}, u32[]{:S(2)}) %collective-permute-start.11) | collective-permute-done | bytes 458784 | tf_op jit(solution)/shard_map/ppermute | solution.py:33
  60.2 8.5 %collective-permute-done.12.rest_11_ = bf16[4,32,1792]{2,1,0:T(8,128)(2,1)S(1)} collective-permute-done((bf16[4,32,1792]{2,1,0:T(8,128)(2,1)S(1)}, bf16[4,32,1792]{2,1,0:T(8,128)(2,1)S(1)}, u32[]{:S(2)}, u32[]{:S(2)}) %collective-permute-start.12) | collective-permute-done | bytes 458784 | tf_op jit(solution)/shard_map/ppermute | solution.py:33
  68.7 0.8 copy-done.8
  69.7 1.3 collective-permute-start.14
  71.4 1.3 collective-permute-start.17
  72.7 44.7 %collective-permute-done.14.incoming = bf16[32,5120]{1,0:T(8,128)(2,1)S(1)} collective-permute-done((bf16[32,5120]{1,0:T(8,128)(2,1)S(1)}, bf16[32,5120]{1,0:T(8,128)(2,1)S(1)}, u32[]{:S(2)}, u32[]{:S(2)}) %collective-permute-start.14) | collective-permute-done | bytes 327712 | tf_op jit(solution)/shard_map/ppermute | solution.py:28
  117.4 2.8 %backward.16 = (f32[8,128]{1,0:T(8,128)S(1)}, bf16[2,32,2304]{2,1,0:T(8,128)(2,1)}, bf16[2,32,2304]{2,1,0:T(8,128)(2,1)}, bf16[2,32,2304]{2,1,0:T(8,128)(2,1)}, ...) custom-call(bf16[32,5120]{1,0:T(8,128)(2,1)S(1)} %collective-permute, ...), custom_call_target="tpu_custom_call", output_to_operand_aliasing={{0}: (11, {}), {1}: (12, {}), {2}: (13, {}), {3}: (14, {}),... | custom-call | flops 1000 | bytes 1000 | tf_op jit(solution)/shard_map/backward/pallas_call | solution.py:605
  120.1 1.3 collective-permute-start.16
  121.4 12.8 %collective-permute-done.17.incoming = bf16[32,5120]{1,0:T(8,128)(2,1)S(1)} collective-permute-done((bf16[32,5120]{1,0:T(8,128)(2,1)S(1)}, bf16[32,5120]{1,0:T(8,128)(2,1)S(1)}, u32[]{:S(2)}, u32[]{:S(2)}) %collective-permute-start.17) | collective-permute-done | bytes 327712 | tf_op jit(solution)/shard_map/ppermute | solution.py:28
  134.2 2.8 %backward.17 = (f32[8,128]{1,0:T(8,128)S(1)}, bf16[2,32,2304]{2,1,0:T(8,128)(2,1)}, bf16[2,32,2304]{2,1,0:T(8,128)(2,1)}, bf16[2,32,2304]{2,1,0:T(8,128)(2,1)}, ...) custom-call(bf16[32,5120]{1,0:T(8,128)(2,1)S(1)} %collective-permute, ...), custom_call_target="tpu_custom_call", output_to_operand_aliasing={{0}: (11, {}), {1}: (12, {}), {2}: (13, {}), {3}: (14, {}),... | custom-call | flops 1000 | bytes 1000 | tf_op jit(solution)/shard_map/backward/pallas_call | solution.py:605
  137.0 1.3 collective-permute-start.19
  138.3 2.5 %collective-permute-start.27 = (bf16[2,32,2304]{2,1,0:T(8,128)(2,1)}, bf16[2,32,2304]{2,1,0:T(8,128)(2,1)S(1)}, u32[]{:S(2)}, u32[]{:S(2)}) collective-permute-start(bf16[2,32,2304]{2,1,0:T(8,128)(2,1)} %get-tuple-element.437), channel_id=1, source_target_pairs={{0,2},{1,3},{2,0},{3,1},{4,6},{5,7},{6,4},{7,5},{8,10},{9,11},{10,... | collective-permute-start | bytes 884744 | tf_op jit(solution)/shard_map/ppermute | solution.py:33
  140.8 1.5 collective-permute-start.28
  142.3 3.5 %backward.18 = (f32[8,128]{1,0:T(8,128)S(1)}, bf16[2,32,2304]{2,1,0:T(8,128)(2,1)}, bf16[2,32,2304]{2,1,0:T(8,128)(2,1)}, bf16[2,32,2304]{2,1,0:T(8,128)(2,1)}, ...) custom-call(bf16[32,5120]{1,0:T(8,128)(2,1)S(1)} %collective-permute, ...), custom_call_target="tpu_custom_call", output_to_operand_aliasing={{0}: (11, {}), {1}: (12, {}), {2}: (13, {}), {3}: (14, {}),... | custom-call | flops 1000 | bytes 1000 | tf_op jit(solution)/shard_map/backward/pallas_call | solution.py:605
  145.8 1.7 pad_maximum_fusion.rest_0_
  147.6 3.5 %backward.19 = (f32[8,128]{1,0:T(8,128)S(1)}, bf16[2,32,2304]{2,1,0:T(8,128)(2,1)}, bf16[2,32,2304]{2,1,0:T(8,128)(2,1)}, bf16[2,32,2304]{2,1,0:T(8,128)(2,1)}, ...) custom-call(bf16[32,5120]{1,0:T(8,128)(2,1)S(1)} %collective-permute, ...), custom_call_target="tpu_custom_call", output_to_operand_aliasing={{0}: (11, {}), {1}: (12, {}), {2}: (13, {}), {3}: (14, {}),... | custom-call | flops 1000 | bytes 1000 | tf_op jit(solution)/shard_map/backward/pallas_call | solution.py:605
  151.2 0.7 copy-done.10
  152.1 1.5 pad_maximum_fusion.1.rest_2_
  153.5 0.5 collective-permute-start.30
  154.1 1.9 %collective-permute-start.20 = (bf16[2,32,2304]{2,1,0:T(8,128)(2,1)S(1)}, bf16[2,32,2304]{2,1,0:T(8,128)(2,1)S(1)}, u32[]{:S(2)}, u32[]{:S(2)}) collective-permute-start(bf16[2,32,2304]{2,1,0:T(8,128)(2,1)S(1)} %copy-done.4), channel_id=1, source_target_pairs={{0,2},{1,3},{2,0},{3,1},{4,6},{5,7},{6,4},{7,5},{8,10},{9,11},{10,... | collective-permute-start | bytes 884744 | tf_op jit(solution)/shard_map/ppermute | solution.py:33
  156.0 1.5 collective-permute-start.21
  157.6 6.3 %collective-permute-done.20 = bf16[2,32,2304]{2,1,0:T(8,128)(2,1)S(1)} collective-permute-done((bf16[2,32,2304]{2,1,0:T(8,128)(2,1)S(1)}, bf16[2,32,2304]{2,1,0:T(8,128)(2,1)S(1)}, u32[]{:S(2)}, u32[]{:S(2)}) %collective-permute-start.20) | collective-permute-done | bytes 294944 | tf_op jit(solution)/shard_map/ppermute | solution.py:33
  163.9 7.2 %collective-permute-done.21 = bf16[2,32,2304]{2,1,0:T(8,128)(2,1)S(1)} collective-permute-done((bf16[2,32,2304]{2,1,0:T(8,128)(2,1)S(1)}, bf16[2,32,2304]{2,1,0:T(8,128)(2,1)S(1)}, u32[]{:S(2)}, u32[]{:S(2)}) %collective-permute-start.21) | collective-permute-done | bytes 294944 | tf_op jit(solution)/shard_map/ppermute | solution.py:33
  171.1 0.5 collective-permute-start.25
  171.6 2.5 %gathered.2 = (f32[640,512]{1,0:T(8,128)S(1)}, f32[640,512]{1,0:T(8,128)S(1)}) custom-call(bf16[4,4,32,1792]{3,2,1,0:T(8,128)(2,1)S(1)} %pad_maximum_fusion.rest_0_, bf16[4,4,32,1792]{3,2,1,0:T(8,128)(2,1)} %collective-permute-done.18.rest_1_, bf16[4,2,32,2304]{3,2,1,0:T(8,128)(2,1)S(1)} %pad_maximum_fusion.1.rest_2_, ...), custom_call_target="tpu_custom_call" | custom-call | flops 1000 | bytes 1000 | tf_op jit(solution)/shard_map/gathered/pallas_call | solution.py:664
  174.2 3.4 %gathered.3 = (f32[640,512]{1,0:T(8,128)}, f32[640,512]{1,0:T(8,128)}) custom-call(bf16[4,4,32,1792]{3,2,1,0:T(8,128)(2,1)S(1)} %pad_maximum_fusion.rest_0_, bf16[4,4,32,1792]{3,2,1,0:T(8,128)(2,1)} %collective-permute-done.18.rest_1_, bf16[1,2,32,2304]{3,2,1,0:T(8,128)(2,1)S(1)} %bitcast.19, bf16[1,2,32,2304]{3,2,1,0:T(8,128)(2,1)S(1)} %bitcast.21, ...), custom_call_target="tpu_custom_call" | custom-call | flops 1000 | bytes 1000 | tf_op jit(solution)/shard_map/gathered/pallas_call | solution.py:664
  (66 shorter events, 1.9 us)
Async XLA Ops:
  9.4 9.7 %collective-permute-start.1 = (bf16[32,5120]{1,0:T(8,128)(2,1)S(1)}, bf16[32,5120]{1,0:T(8,128)(2,1)S(1)}, u32[]{:S(2)}, u32[]{:S(2)}) collective-permute-start(bf16[32,5120]{1,0:T(8,128)(2,1)S(1)} %get-tuple-element.244), channel_id=1, source_target_pairs={{0,8},{1,9},{2,10},{3,11},{4,12},{5,13},{6,14},{7,15}} | collective-permute-start | bytes 983048 | tf_op jit(solution)/shard_map/ppermute | solution.py:28
  15.9 12.4 %collective-permute-start = (bf16[32,5120]{1,0:T(8,128)(2,1)S(1)}, bf16[32,5120]{1,0:T(8,128)(2,1)S(1)}, u32[]{:S(2)}, u32[]{:S(2)}) collective-permute-start(bf16[32,5120]{1,0:T(8,128)(2,1)S(1)} %get-tuple-element.243), channel_id=1, source_target_pairs={{0,8},{1,9},{2,10},{3,11},{4,12},{5,13},{6,14},{7,15}} | collective-permute-start | bytes 983048 | tf_op jit(solution)/shard_map/ppermute | solution.py:28
  23.9 11.3 %collective-permute-start.3 = (bf16[32,5120]{1,0:T(8,128)(2,1)S(1)}, bf16[32,5120]{1,0:T(8,128)(2,1)S(1)}, u32[]{:S(2)}, u32[]{:S(2)}) collective-permute-start(bf16[32,5120]{1,0:T(8,128)(2,1)S(1)} %get-tuple-element.266), channel_id=1, source_target_pairs={{0,8},{8,16},{1,9},{9,17},{2,10},{10,18},{3,11},{11,19},{4,12},{12... | collective-permute-start | bytes 983048 | tf_op jit(solution)/shard_map/ppermute | solution.py:28
  33.2 8.3 %collective-permute-start.2 = (bf16[32,5120]{1,0:T(8,128)(2,1)S(1)}, bf16[32,5120]{1,0:T(8,128)(2,1)S(1)}, u32[]{:S(2)}, u32[]{:S(2)}) collective-permute-start(bf16[32,5120]{1,0:T(8,128)(2,1)S(1)} %get-tuple-element.265), channel_id=1, source_target_pairs={{0,8},{8,16},{1,9},{9,17},{2,10},{10,18},{3,11},{11,19},{4,12},{12... | collective-permute-start | bytes 983048 | tf_op jit(solution)/shard_map/ppermute | solution.py:28
  35.2 7.0 %collective-permute-start.5 = (bf16[32,5120]{1,0:T(8,128)(2,1)S(1)}, bf16[32,5120]{1,0:T(8,128)(2,1)S(1)}, u32[]{:S(2)}, u32[]{:S(2)}) collective-permute-start(bf16[32,5120]{1,0:T(8,128)(2,1)S(1)} %get-tuple-element.288), channel_id=1, source_target_pairs={{8,16},{16,24},{9,17},{17,25},{10,18},{18,26},{11,19},{19,27},{12,... | collective-permute-start | bytes 983048 | tf_op jit(solution)/shard_map/ppermute | solution.py:28
  41.6 1.5 collective-permute-start.4
  42.3 1.7 collective-permute-start.7
  43.1 1.7 collective-permute-start.6
  45.7 1.0 copy-start.1
  45.7 3.1 %copy-start.2 = (bf16[4,32,1792]{2,1,0:T(8,128)(2,1)S(1)}, bf16[4,32,1792]{2,1,0:T(8,128)(2,1)}, u32[]{:S(2)}) copy-start(bf16[4,32,1792]{2,1,0:T(8,128)(2,1)} %get-tuple-element.379) | copy-start | bytes 1376260
  45.7 4.6 %copy-start.3 = (bf16[4,32,1792]{2,1,0:T(8,128)(2,1)S(1)}, bf16[4,32,1792]{2,1,0:T(8,128)(2,1)}, u32[]{:S(2)}) copy-start(bf16[4,32,1792]{2,1,0:T(8,128)(2,1)} %get-tuple-element.380) | copy-start | bytes 1376260
  45.8 5.4 %collective-permute-start.8 = (bf16[32,5120]{1,0:T(8,128)(2,1)S(1)}, bf16[32,5120]{1,0:T(8,128)(2,1)S(1)}, u32[]{:S(2)}, u32[]{:S(2)}) collective-permute-start(bf16[32,5120]{1,0:T(8,128)(2,1)S(1)} %get-tuple-element.342), channel_id=1, source_target_pairs={{24,16},{25,17},{26,18},{27,19},{28,20},{29,21},{30,22},{31,23}} | collective-permute-start | bytes 983048 | tf_op jit(solution)/shard_map/ppermute | solution.py:28
  46.7 13.5 %collective-permute-start.11 = (bf16[4,32,1792]{2,1,0:T(8,128)(2,1)S(1)}, bf16[4,32,1792]{2,1,0:T(8,128)(2,1)S(1)}, u32[]{:S(2)}, u32[]{:S(2)}) collective-permute-start(bf16[4,32,1792]{2,1,0:T(8,128)(2,1)S(1)} %copy-done.1), channel_id=1, source_target_pairs={{0,2},{1,3},{2,0},{3,1},{4,6},{5,7},{6,4},{7,5},{8,10},{9,11},{10,... | collective-permute-start | bytes 1376264 | tf_op jit(solution)/shard_map/ppermute | solution.py:33
  48.8 19.9 %collective-permute-start.12 = (bf16[4,32,1792]{2,1,0:T(8,128)(2,1)S(1)}, bf16[4,32,1792]{2,1,0:T(8,128)(2,1)S(1)}, u32[]{:S(2)}, u32[]{:S(2)}) collective-permute-start(bf16[4,32,1792]{2,1,0:T(8,128)(2,1)S(1)} %copy-done.2), channel_id=1, source_target_pairs={{0,4},{1,5},{2,6},{3,7},{4,0},{5,1},{6,2},{7,3},{8,12},{9,13},{10,... | collective-permute-start | bytes 1376264 | tf_op jit(solution)/shard_map/ppermute | solution.py:33
  50.3 18.4 %collective-permute-start.13 = (bf16[4,32,1792]{2,1,0:T(8,128)(2,1)S(1)}, bf16[4,32,1792]{2,1,0:T(8,128)(2,1)S(1)}, u32[]{:S(2)}, u32[]{:S(2)}) collective-permute-start(bf16[4,32,1792]{2,1,0:T(8,128)(2,1)S(1)} %copy-done.3), channel_id=1, source_target_pairs={{0,6},{1,7},{2,4},{3,5},{4,2},{5,3},{6,0},{7,1},{8,14},{9,15},{10,... | collective-permute-start | bytes 1376264 | tf_op jit(solution)/shard_map/ppermute | solution.py:33
  50.5 1.5 collective-permute-start.10
  51.2 17.5 %collective-permute-start.9 = (bf16[32,5120]{1,0:T(8,128)(2,1)S(1)}, bf16[32,5120]{1,0:T(8,128)(2,1)S(1)}, u32[]{:S(2)}, u32[]{:S(2)}) collective-permute-start(bf16[32,5120]{1,0:T(8,128)(2,1)S(1)} %get-tuple-element.357), channel_id=1, source_target_pairs={{16,8},{24,16},{17,9},{25,17},{18,10},{26,18},{19,11},{27,19},{20,... | collective-permute-start | bytes 983048 | tf_op jit(solution)/shard_map/ppermute | solution.py:28
  52.0 19.0 %collective-permute-start.15 = (bf16[32,5120]{1,0:T(8,128)(2,1)S(1)}, bf16[32,5120]{1,0:T(8,128)(2,1)S(1)}, u32[]{:S(2)}, u32[]{:S(2)}) collective-permute-start(bf16[32,5120]{1,0:T(8,128)(2,1)S(1)} %get-tuple-element.382), channel_id=1, source_target_pairs={{16,8},{24,16},{17,9},{25,17},{18,10},{26,18},{19,11},{27,19},{20,... | collective-permute-start | bytes 983048 | tf_op jit(solution)/shard_map/ppermute | solution.py:28
  60.2 8.5 %copy-start.7 = (bf16[4,32,1792]{2,1,0:T(8,128)(2,1)}, bf16[4,32,1792]{2,1,0:T(8,128)(2,1)S(1)}, u32[]{:S(2)}) copy-start(bf16[4,32,1792]{2,1,0:T(8,128)(2,1)S(1)} %collective-permute-done.11.rest_10_) | copy-start | bytes 1376260
  68.7 0.8 copy-start.8
  68.7 1.0 copy-start.9
  69.7 47.6 %collective-permute-start.14 = (bf16[32,5120]{1,0:T(8,128)(2,1)S(1)}, bf16[32,5120]{1,0:T(8,128)(2,1)S(1)}, u32[]{:S(2)}, u32[]{:S(2)}) collective-permute-start(bf16[32,5120]{1,0:T(8,128)(2,1)S(1)} %get-tuple-element.381), channel_id=1, source_target_pairs={{8,0},{16,8},{9,1},{17,9},{10,2},{18,10},{11,3},{19,11},{12,4},{20... | collective-permute-start | bytes 983048 | tf_op jit(solution)/shard_map/ppermute | solution.py:28
  71.4 62.9 %collective-permute-start.17 = (bf16[32,5120]{1,0:T(8,128)(2,1)S(1)}, bf16[32,5120]{1,0:T(8,128)(2,1)S(1)}, u32[]{:S(2)}, u32[]{:S(2)}) collective-permute-start(bf16[32,5120]{1,0:T(8,128)(2,1)S(1)} %get-tuple-element.402), channel_id=1, source_target_pairs={{8,0},{16,8},{9,1},{17,9},{10,2},{18,10},{11,3},{19,11},{12,4},{20... | collective-permute-start | bytes 983048 | tf_op jit(solution)/shard_map/ppermute | solution.py:28
  120.1 22.2 %collective-permute-start.16 = (bf16[32,5120]{1,0:T(8,128)(2,1)S(1)}, bf16[32,5120]{1,0:T(8,128)(2,1)S(1)}, u32[]{:S(2)}, u32[]{:S(2)}) collective-permute-start(bf16[32,5120]{1,0:T(8,128)(2,1)S(1)} %get-tuple-element.401), channel_id=1, source_target_pairs={{8,0},{9,1},{10,2},{11,3},{12,4},{13,5},{14,6},{15,7}} | collective-permute-start | bytes 983048 | tf_op jit(solution)/shard_map/ppermute | solution.py:28
  137.0 10.6 %collective-permute-start.19 = (bf16[32,5120]{1,0:T(8,128)(2,1)S(1)}, bf16[32,5120]{1,0:T(8,128)(2,1)S(1)}, u32[]{:S(2)}, u32[]{:S(2)}) collective-permute-start(bf16[32,5120]{1,0:T(8,128)(2,1)S(1)} %get-tuple-element.425), channel_id=1, source_target_pairs={{8,0},{9,1},{10,2},{11,3},{12,4},{13,5},{14,6},{15,7}} | collective-permute-start | bytes 983048 | tf_op jit(solution)/shard_map/ppermute | solution.py:28
  138.3 12.8 %collective-permute-start.27 = (bf16[2,32,2304]{2,1,0:T(8,128)(2,1)}, bf16[2,32,2304]{2,1,0:T(8,128)(2,1)S(1)}, u32[]{:S(2)}, u32[]{:S(2)}) collective-permute-start(bf16[2,32,2304]{2,1,0:T(8,128)(2,1)} %get-tuple-element.437), channel_id=1, source_target_pairs={{0,2},{1,3},{2,0},{3,1},{4,6},{5,7},{6,4},{7,5},{8,10},{9,11},{10,... | collective-permute-start | bytes 884744 | tf_op jit(solution)/shard_map/ppermute | solution.py:33
  140.8 10.4 %collective-permute-start.28 = (bf16[2,32,2304]{2,1,0:T(8,128)(2,1)}, bf16[2,32,2304]{2,1,0:T(8,128)(2,1)S(1)}, u32[]{:S(2)}, u32[]{:S(2)}) collective-permute-start(bf16[2,32,2304]{2,1,0:T(8,128)(2,1)} %get-tuple-element.438), channel_id=1, source_target_pairs={{0,4},{1,5},{2,6},{3,7},{4,0},{5,1},{6,2},{7,3},{8,12},{9,13},{10,... | collective-permute-start | bytes 884744 | tf_op jit(solution)/shard_map/ppermute | solution.py:33
  142.3 8.9 %collective-permute-start.29 = (bf16[2,32,2304]{2,1,0:T(8,128)(2,1)}, bf16[2,32,2304]{2,1,0:T(8,128)(2,1)S(1)}, u32[]{:S(2)}, u32[]{:S(2)}) collective-permute-start(bf16[2,32,2304]{2,1,0:T(8,128)(2,1)} %get-tuple-element.439), channel_id=1, source_target_pairs={{0,6},{1,7},{2,4},{3,5},{4,2},{5,3},{6,0},{7,1},{8,14},{9,15},{10,... | collective-permute-start | bytes 884744 | tf_op jit(solution)/shard_map/ppermute | solution.py:33
  147.5 24.1 %collective-permute-start.18 = (bf16[4,4,32,1792]{3,2,1,0:T(8,128)(2,1)S(1)}, bf16[4,4,32,1792]{3,2,1,0:T(8,128)(2,1)}, u32[]{:S(2)}, u32[]{:S(2)}) collective-permute-start(bf16[4,4,32,1792]{3,2,1,0:T(8,128)(2,1)S(1)} %pad_maximum_fusion.rest_0_), channel_id=1, source_target_pairs={{0,1},{1,0},{2,3},{3,2},{4,5},{5,4},{6,7},{7,6},{8,9},{9,8},{10,11... | collective-permute-start | bytes 5505032 | tf_op jit(solution)/shard_map/ppermute | solution.py:37
  151.1 0.7 copy-start.10
  151.1 0.8 copy-start.11
  151.2 0.9 copy-start.12
  152.0 2.0 %copy-start.4 = (bf16[2,32,2304]{2,1,0:T(8,128)(2,1)S(1)}, bf16[2,32,2304]{2,1,0:T(8,128)(2,1)}, u32[]{:S(2)}) copy-start(bf16[2,32,2304]{2,1,0:T(8,128)(2,1)} %get-tuple-element.432) | copy-start | bytes 884740
  152.0 4.0 %copy-start.5 = (bf16[2,32,2304]{2,1,0:T(8,128)(2,1)S(1)}, bf16[2,32,2304]{2,1,0:T(8,128)(2,1)}, u32[]{:S(2)}) copy-start(bf16[2,32,2304]{2,1,0:T(8,128)(2,1)} %get-tuple-element.433) | copy-start | bytes 884740
  152.1 5.5 %copy-start.6 = (bf16[2,32,2304]{2,1,0:T(8,128)(2,1)S(1)}, bf16[2,32,2304]{2,1,0:T(8,128)(2,1)}, u32[]{:S(2)}) copy-start(bf16[2,32,2304]{2,1,0:T(8,128)(2,1)} %get-tuple-element.434) | copy-start | bytes 884740
  152.1 11.8 %copy-start = (bf16[2,32,2304]{2,1,0:T(8,128)(2,1)S(1)}, bf16[2,32,2304]{2,1,0:T(8,128)(2,1)}, u32[]{:S(2)}) copy-start(bf16[2,32,2304]{2,1,0:T(8,128)(2,1)} %get-tuple-element.431) | copy-start | bytes 884740
  153.5 18.0 %collective-permute-start.30 = (bf16[4,2,32,2304]{3,2,1,0:T(8,128)(2,1)S(1)}, bf16[4,2,32,2304]{3,2,1,0:T(8,128)(2,1)S(1)}, u32[]{:S(2)}, u32[]{:S(2)}) collective-permute-start(bf16[4,2,32,2304]{3,2,1,0:T(8,128)(2,1)S(1)} %pad_maximum_fusion.1.rest_2_), channel_id=1, source_target_pairs={{0,1},{1,0},{2,3},{3,2},{4,5},{5,4},{6,7},{7,6},{8,9},{9,8},{10,11... | collective-permute-start | bytes 3538952 | tf_op jit(solution)/shard_map/ppermute | solution.py:37
  154.1 9.8 %collective-permute-start.20 = (bf16[2,32,2304]{2,1,0:T(8,128)(2,1)S(1)}, bf16[2,32,2304]{2,1,0:T(8,128)(2,1)S(1)}, u32[]{:S(2)}, u32[]{:S(2)}) collective-permute-start(bf16[2,32,2304]{2,1,0:T(8,128)(2,1)S(1)} %copy-done.4), channel_id=1, source_target_pairs={{0,2},{1,3},{2,0},{3,1},{4,6},{5,7},{6,4},{7,5},{8,10},{9,11},{10,... | collective-permute-start | bytes 884744 | tf_op jit(solution)/shard_map/ppermute | solution.py:33
  156.0 15.0 %collective-permute-start.21 = (bf16[2,32,2304]{2,1,0:T(8,128)(2,1)S(1)}, bf16[2,32,2304]{2,1,0:T(8,128)(2,1)S(1)}, u32[]{:S(2)}, u32[]{:S(2)}) collective-permute-start(bf16[2,32,2304]{2,1,0:T(8,128)(2,1)S(1)} %copy-done.5), channel_id=1, source_target_pairs={{0,4},{1,5},{2,6},{3,7},{4,0},{5,1},{6,2},{7,3},{8,12},{9,13},{10,... | collective-permute-start | bytes 884744 | tf_op jit(solution)/shard_map/ppermute | solution.py:33
  157.5 13.5 %collective-permute-start.22 = (bf16[2,32,2304]{2,1,0:T(8,128)(2,1)S(1)}, bf16[2,32,2304]{2,1,0:T(8,128)(2,1)S(1)}, u32[]{:S(2)}, u32[]{:S(2)}) collective-permute-start(bf16[2,32,2304]{2,1,0:T(8,128)(2,1)S(1)} %copy-done.6), channel_id=1, source_target_pairs={{0,6},{1,7},{2,4},{3,5},{4,2},{5,3},{6,0},{7,1},{8,14},{9,15},{10,... | collective-permute-start | bytes 884744 | tf_op jit(solution)/shard_map/ppermute | solution.py:33
  163.9 10.2 %collective-permute-start.23 = (bf16[1,2,32,2304]{3,2,1,0:T(8,128)(2,1)S(1)}, bf16[1,2,32,2304]{3,2,1,0:T(8,128)(2,1)S(1)}, u32[]{:S(2)}, u32[]{:S(2)}) collective-permute-start(bf16[1,2,32,2304]{3,2,1,0:T(8,128)(2,1)S(1)} %bitcast.18), channel_id=1, source_target_pairs={{0,1},{1,0},{2,3},{3,2},{4,5},{5,4},{6,7},{7,6},{8,9},{9,8},{10,11... | collective-permute-start | bytes 884744 | tf_op jit(solution)/shard_map/ppermute | solution.py:37
  171.0 3.1 %collective-permute-start.24 = (bf16[1,2,32,2304]{3,2,1,0:T(8,128)(2,1)S(1)}, bf16[1,2,32,2304]{3,2,1,0:T(8,128)(2,1)S(1)}, u32[]{:S(2)}, u32[]{:S(2)}) collective-permute-start(bf16[1,2,32,2304]{3,2,1,0:T(8,128)(2,1)S(1)} %bitcast.20), channel_id=1, source_target_pairs={{0,1},{1,0},{2,3},{3,2},{4,5},{5,4},{6,7},{7,6},{8,9},{9,8},{10,11... | collective-permute-start | bytes 884744 | tf_op jit(solution)/shard_map/ppermute | solution.py:37
  171.1 3.1 %collective-permute-start.25 = (bf16[1,2,32,2304]{3,2,1,0:T(8,128)(2,1)S(1)}, bf16[1,2,32,2304]{3,2,1,0:T(8,128)(2,1)S(1)}, u32[]{:S(2)}, u32[]{:S(2)}) collective-permute-start(bf16[1,2,32,2304]{3,2,1,0:T(8,128)(2,1)S(1)} %bitcast.22), channel_id=1, source_target_pairs={{0,1},{1,0},{2,3},{3,2},{4,5},{5,4},{6,7},{7,6},{8,9},{9,8},{10,11... | collective-permute-start | bytes 884744 | tf_op jit(solution)/shard_map/ppermute | solution.py:37
  171.6 2.6 %collective-permute-start.26 = (bf16[1,2,32,2304]{3,2,1,0:T(8,128)(2,1)S(1)}, bf16[1,2,32,2304]{3,2,1,0:T(8,128)(2,1)S(1)}, u32[]{:S(2)}, u32[]{:S(2)}) collective-permute-start(bf16[1,2,32,2304]{3,2,1,0:T(8,128)(2,1)S(1)} %bitcast.24), channel_id=1, source_target_pairs={{0,1},{1,0},{2,3},{3,2},{4,5},{5,4},{6,7},{7,6},{8,9},{9,8},{10,11... | collective-permute-start | bytes 884744 | tf_op jit(solution)/shard_map/ppermute | solution.py:37

commit v4 on v2

--- a/solution.py
+++ b/solution.py
@@ -113,11 +113,13 @@
         pltpu.make_async_copy(segments_hbm, segments_ref, small.at[0]),
         pltpu.make_async_copy(lengths_hbm, lengths_ref, small.at[1]),
         pltpu.make_async_copy(grades_hbm, grades_ref, small.at[2]),
-        pltpu.make_async_copy(x0_hbm, saved, small.at[3]),
-        pltpu.make_async_copy(score_hbm, w_score, small.at[4]),
+        pltpu.make_async_copy(x0_hbm.at[0], saved.at[0], small.at[3]),
     ]
-    for copy in copies:
-        copy.start()
+    later = [
+        pltpu.make_async_copy(x0_hbm.at[pl.ds(1, micro - 1)], saved.at[pl.ds(1, micro - 1)], small.at[4]),
+        pltpu.make_async_copy(score_hbm, w_score, small.at[5]),
+    ]
+    chunks = model // CHUNK
 
     def chunk_copies(c):
         cols = pl.ds(c * CHUNK, CHUNK)
@@ -126,35 +128,60 @@
             pltpu.make_async_copy(wv_hbm.at[cols], wv.at[cols], value_sems.at[c]),
         )
 
-    for c in range(model // CHUNK):
+    def wait_chunk(c):
+        for copy in chunk_copies(c):
+            copy.wait()
+
+        @pl.when(c + 2 < chunks)
+        def _():
+            for copy in chunk_copies(jnp.minimum(c + 2, chunks - 1)):
+                copy.start()
+
+    for copy in copies:
+        copy.start()
+    for c in range(2):
         for copy in chunk_copies(c):
             copy.start()
-    for copy in copies[:3]:
+    section = lax.axis_index("section")
+    second = lax.axis_index("dp") % 2 == 1
+    ahead = (section == 0) & jnp.logical_not(second)
+    behind = (section == 0) & second
+    for copy in copies:
         copy.wait()
+
+    @pl.when(jnp.logical_not(ahead))
+    def _():
+        @pl.loop(0, chunks)
+        def _(c):
+            wait_chunk(c)
+
+        for copy in later:
+            copy.start()
+
     make_tables(
         micro, segments_ref, lengths_ref, grades_ref, cosine, sine, mask, ends, target
     )
-    for copy in copies[3:]:
-        copy.wait()
-    section = lax.axis_index("section")
 
     @pl.when(section == 0)
     def _():
-        def wait_chunk(c):
-            for copy in chunk_copies(c):
-                copy.wait()
+        def wait_ahead(c):
+            @pl.when(ahead)
+            def _():
+                wait_chunk(c)
 
         forward_body(
-            0, section, sections, chips, wait_chunk,
+            0, section, sections, chips, wait_ahead,
             w_score, wk, wv, cosine, sine, mask, ends, target,
             saved, keys, values, probs, scales, grads, *sent, outgoing, *scratch,
         )
 
-    @pl.when(section != 0)
+    @pl.when(ahead)
     def _():
-        for c in range(model // CHUNK):
-            for copy in chunk_copies(c):
-                copy.wait()
+        for copy in later:
+            copy.start()
+
+    for copy in later:
+        copy.wait()
 
 
 def row_scale(ref_value_chunks, model):
@@ -513,7 +540,7 @@
             pltpu.VMEM(segments.shape, jnp.int32),
             pltpu.SMEM((1, micro), jnp.int32),
             pltpu.VMEM(grades.shape, jnp.int32),
-            pltpu.SemaphoreType.DMA((5,)),
+            pltpu.SemaphoreType.DMA((6,)),
             pltpu.SemaphoreType.DMA((chunks,)),
             pltpu.SemaphoreType.DMA((chunks,)),
         ]

time: 173 us -> 177 us (1.023)
  waiting for transfers between devices: 90.8 us -> 97.8 us
  starting transfers between devices: 37.1 us -> 32.8 us
    ppermute x12, starting transfers between devices: 16.7 us -> 12.1 us  [between_chips(): return lax.ppermute(value, 'dp', pairs)]
    ppermute x12, waiting for transfers between devices: 10 us -> 14.2 us  [between_chips(): return lax.ppermute(value, 'dp', pairs)]
    ppermute x16, waiting for transfers between devices: 79.4 us -> 82.3 us  [shifted(): lax.ppermute(value, 'section', [(source, source + steps) for source in se...]
  transfers between devices with their start and end apart: 32 -> 32, of which waited for: 12 -> 14; matrix products, arithmetic and copies ran while one was open for 0% -> 0% of each run, Pallas kernels for 18% -> 17%
where the time goes in v4:
time: 177 us; the launch traced here: 176 us
  waiting for transfers between devices  97.8 us (55%)
  Pallas kernels  43.3 us (24%)
  starting transfers between devices  32.8 us (19%)
    ppermute x16, waiting for transfers between devices, shifted(): lax.ppermute(value, 'section', [(source, source + steps) for source in se...  82.3 us
    ppermute x16, starting transfers between devices, shifted(): lax.ppermute(value, 'section', [(source, source + steps) for source in se...  20 us
    pallas_call x9, Pallas kernels, shards(): pl.pallas_call(functools.partial(forward_kernel, tick, sections, micro, c...  16.5 us
    ppermute x12, waiting for transfers between devices, between_chips(): return lax.ppermute(value, 'dp', pairs)  14.2 us
    pallas_call x10, Pallas kernels, shards(): pl.pallas_call(functools.partial(backward_kernel, tick, sections, micro,...  13 us
    ppermute x12, starting transfers between devices, between_chips(): return lax.ppermute(value, 'dp', pairs)  12.1 us
    pallas_call x1, Pallas kernels, shards(): pl.pallas_call(functools.partial(first_kernel, sections, micro, chips), o...  9.43 us
    pallas_call x2, Pallas kernels, shards(): pl.pallas_call(functools.partial(gather_kernel, chosen, share, wide, feat...  4.38 us
  transfers between devices with their start and end apart: 32, of which 14 were waited for; matrix products, arithmetic and copies ran while one was open for 0% of the time, Pallas kernels for 17%

profile of v4, /device:TPU:0, one launch (start us, length us, event | category | flops | bytes accessed | tf_op | source)
XLA Modules:
  0.0 176.0 jit_solution(13860920827367761603)
XLA Ops:
  0.6 9.4 %first.1 = (f32[1,5120]{1,0:T(1,128)S(1)}, bf16[5120,512]{1,0:T(8,128)(2,1)S(1)}, bf16[5120,512]{1,0:T(8,128)(2,1)S(1)}, f32[4,32,128]{2,1,0:T(8,128)S(1)}, f32[...) custom-call(bf16[5120,512]{1,0:T(8,128)(2,1)} %bitcast.24, ...), custom_call_target="tpu_custom_call" | custom-call | tf_op jit(solution)/shard_map/first/pallas_call | solution.py:534
  10.1 1.4 collective-permute-start.1
  11.5 4.9 %forward.9 = (bf16[4,32,5120]{2,1,0:T(8,128)(2,1)S(1)}, bf16[4,32,512]{2,1,0:T(8,128)(2,1)S(1)}, bf16[4,32,512]{2,1,0:T(8,128)(2,1)S(1)}, f32[4,128,32]{2,1,0:T(...) custom-call(bf16[32,5120]{1,0:T(8,128)(2,1)S(1)} %broadcast_in_dim.9, ...), custom_call_target="tpu_custom_call", output_to_operand_aliasing={{0}: (9, {}), {1}: (10, {}), {2}: (11, {}), {3}: (12, {}), ... | custom-call | flops 1000000 | bytes 1000000 | tf_op jit(solution)/shard_map/forward/pallas_call | solution.py:572
  16.4 1.3 collective-permute-start
  17.7 1.6 collective-permute-done.1.incoming
  19.3 4.8 %forward.10 = (bf16[4,32,5120]{2,1,0:T(8,128)(2,1)S(1)}, bf16[4,32,512]{2,1,0:T(8,128)(2,1)S(1)}, bf16[4,32,512]{2,1,0:T(8,128)(2,1)S(1)}, f32[4,128,32]{2,1,0:T...) custom-call(bf16[32,5120]{1,0:T(8,128)(2,1)S(1)} %collective-permute, ...), custom_call_target="tpu_custom_call", output_to_operand_aliasing={{0}: (9, {}), {1}: (10, {}), {2}: (11, {}), {3}: (12, {}), ... | custom-call | flops 1000000 | bytes 1000000 | tf_op jit(solution)/shard_map/forward/pallas_call | solution.py:572
  24.2 4.4 %collective-permute-start.3 = (bf16[32,5120]{1,0:T(8,128)(2,1)S(1)}, bf16[32,5120]{1,0:T(8,128)(2,1)S(1)}, u32[]{:S(2)}, u32[]{:S(2)}) collective-permute-start(bf16[32,5120]{1,0:T(8,128)(2,1)S(1)} %get-tuple-element.281), channel_id=1, source_target_pairs={{0,8},{8,16},{1,9},{9,17},{2,10},{10,18},{3,11},{11,19},{4,12},{12... | collective-permute-start | bytes 983048 | tf_op jit(solution)/shard_map/ppermute | solution.py:28
  28.6 4.9 %forward.11 = (bf16[4,32,5120]{2,1,0:T(8,128)(2,1)S(1)}, bf16[4,32,512]{2,1,0:T(8,128)(2,1)S(1)}, bf16[4,32,512]{2,1,0:T(8,128)(2,1)S(1)}, f32[4,128,32]{2,1,0:T...) custom-call(bf16[32,5120]{1,0:T(8,128)(2,1)S(1)} %collective-permute, ...), custom_call_target="tpu_custom_call", output_to_operand_aliasing={{0}: (9, {}), {1}: (10, {}), {2}: (11, {}), {3}: (12, {}), ... | custom-call | flops 1000000 | bytes 1000000 | tf_op jit(solution)/shard_map/forward/pallas_call | solution.py:572
  33.5 2.1 %collective-permute-start.2 = (bf16[32,5120]{1,0:T(8,128)(2,1)S(1)}, bf16[32,5120]{1,0:T(8,128)(2,1)S(1)}, u32[]{:S(2)}, u32[]{:S(2)}) collective-permute-start(bf16[32,5120]{1,0:T(8,128)(2,1)S(1)} %get-tuple-element.280), channel_id=1, source_target_pairs={{0,8},{8,16},{1,9},{9,17},{2,10},{10,18},{3,11},{11,19},{4,12},{12... | collective-permute-start | bytes 983048 | tf_op jit(solution)/shard_map/ppermute | solution.py:28
  35.6 0.6 collective-permute-done.3.incoming
  36.3 0.7 collective-permute-start.5
  37.0 6.3 %collective-permute-done.2.incoming = bf16[32,5120]{1,0:T(8,128)(2,1)S(1)} collective-permute-done((bf16[32,5120]{1,0:T(8,128)(2,1)S(1)}, bf16[32,5120]{1,0:T(8,128)(2,1)S(1)}, u32[]{:S(2)}, u32[]{:S(2)}) %collective-permute-start.2) | collective-permute-done | bytes 327712 | tf_op jit(solution)/shard_map/ppermute | solution.py:28
  43.3 0.7 collective-permute-start.4
  44.1 0.7 collective-permute-start.7
  44.9 0.7 collective-permute-start.6
  45.6 0.8 forward.16
  46.5 0.8 forward.17
  47.5 0.7 collective-permute-start.9
  48.3 0.7 collective-permute-start.12
  49.1 0.7 collective-permute-start.14
  49.9 0.8 collective-permute-start.13
  50.8 2.0 %collective-permute-start.8 = (bf16[4,32,1792]{2,1,0:T(8,128)(2,1)S(1)}, bf16[4,32,1792]{2,1,0:T(8,128)(2,1)S(1)}, u32[]{:S(2)}, u32[]{:S(2)}) collective-permute-start(bf16[4,32,1792]{2,1,0:T(8,128)(2,1)S(1)} %copy-done.1), channel_id=1, source_target_pairs={{0,2},{1,3},{2,0},{3,1},{4,6},{5,7},{6,4},{7,5},{8,10},{9,11},{10,... | collective-permute-start | bytes 1376264 | tf_op jit(solution)/shard_map/ppermute | solution.py:33
  52.8 1.5 collective-permute-start.11
  54.5 1.3 collective-permute-start.16
  55.9 1.3 collective-permute-start.15
  57.2 67.5 %collective-permute-done.16.incoming = bf16[32,5120]{1,0:T(8,128)(2,1)S(1)} collective-permute-done((bf16[32,5120]{1,0:T(8,128)(2,1)S(1)}, bf16[32,5120]{1,0:T(8,128)(2,1)S(1)}, u32[]{:S(2)}, u32[]{:S(2)}) %collective-permute-start.16) | collective-permute-done | bytes 327712 | tf_op jit(solution)/shard_map/ppermute | solution.py:28
  124.7 2.7 %backward.16 = (f32[8,128]{1,0:T(8,128)S(1)}, bf16[2,32,2304]{2,1,0:T(8,128)(2,1)}, bf16[2,32,2304]{2,1,0:T(8,128)(2,1)}, bf16[2,32,2304]{2,1,0:T(8,128)(2,1)}, ...) custom-call(bf16[32,5120]{1,0:T(8,128)(2,1)S(1)} %collective-permute, ...), custom_call_target="tpu_custom_call", output_to_operand_aliasing={{0}: (11, {}), {1}: (12, {}), {2}: (13, {}), {3}: (14, {}),... | custom-call | flops 1000000 | bytes 1000000 | tf_op jit(solution)/shard_map/backward/pallas_call | solution.py:603
  127.4 1.3 collective-permute-start.22
  128.7 3.7 %collective-permute-done.15.incoming = bf16[32,5120]{1,0:T(8,128)(2,1)S(1)} collective-permute-done((bf16[32,5120]{1,0:T(8,128)(2,1)S(1)}, bf16[32,5120]{1,0:T(8,128)(2,1)S(1)}, u32[]{:S(2)}, u32[]{:S(2)}) %collective-permute-start.15) | collective-permute-done | bytes 327712 | tf_op jit(solution)/shard_map/ppermute | solution.py:28
  132.4 2.7 %backward.17 = (f32[8,128]{1,0:T(8,128)S(1)}, bf16[2,32,2304]{2,1,0:T(8,128)(2,1)}, bf16[2,32,2304]{2,1,0:T(8,128)(2,1)}, bf16[2,32,2304]{2,1,0:T(8,128)(2,1)}, ...) custom-call(bf16[32,5120]{1,0:T(8,128)(2,1)S(1)} %collective-permute, ...), custom_call_target="tpu_custom_call", output_to_operand_aliasing={{0}: (11, {}), {1}: (12, {}), {2}: (13, {}), {3}: (14, {}),... | custom-call | flops 1000000 | bytes 1000000 | tf_op jit(solution)/shard_map/backward/pallas_call | solution.py:603
  135.2 1.3 collective-permute-start.18
  136.6 3.4 %collective-permute-start.21 = (bf16[2,32,2304]{2,1,0:T(8,128)(2,1)}, bf16[2,32,2304]{2,1,0:T(8,128)(2,1)S(1)}, u32[]{:S(2)}, u32[]{:S(2)}) collective-permute-start(bf16[2,32,2304]{2,1,0:T(8,128)(2,1)} %get-tuple-element.441), channel_id=1, source_target_pairs={{0,6},{1,7},{2,4},{3,5},{4,2},{5,3},{6,0},{7,1},{8,14},{9,15},{10,... | collective-permute-start | bytes 884744 | tf_op jit(solution)/shard_map/ppermute | solution.py:33
  140.3 2.2 %collective-permute-done.22.incoming = bf16[32,5120]{1,0:T(8,128)(2,1)S(1)} collective-permute-done((bf16[32,5120]{1,0:T(8,128)(2,1)S(1)}, bf16[32,5120]{1,0:T(8,128)(2,1)S(1)}, u32[]{:S(2)}, u32[]{:S(2)}) %collective-permute-start.22) | collective-permute-done | bytes 327712 | tf_op jit(solution)/shard_map/ppermute | solution.py:28
  142.5 3.5 %backward.18 = (f32[8,128]{1,0:T(8,128)S(1)}, bf16[1,32,2304]{2,1,0:T(8,128)(2,1)}, bf16[1,32,2304]{2,1,0:T(8,128)(2,1)}, bf16[1,32,2304]{2,1,0:T(8,128)(2,1)}, ...) custom-call(bf16[32,5120]{1,0:T(8,128)(2,1)S(1)} %collective-permute, ...), custom_call_target="tpu_custom_call", output_to_operand_aliasing={{0}: (11, {}), {1}: (12, {}), {2}: (13, {}), {3}: (14, {}),... | custom-call | flops 1000000 | bytes 1000000 | tf_op jit(solution)/shard_map/backward/pallas_call | solution.py:603
  146.0 2.4 %collective-permute-done.20 = bf16[2,32,2304]{2,1,0:T(8,128)(2,1)S(1)} collective-permute-done((bf16[2,32,2304]{2,1,0:T(8,128)(2,1)}, bf16[2,32,2304]{2,1,0:T(8,128)(2,1)S(1)}, u32[]{:S(2)}, u32[]{:S(2)}) %collective-permute-start.20) | collective-permute-done | bytes 294944 | tf_op jit(solution)/shard_map/ppermute | solution.py:33
  148.8 3.5 %backward.19 = (f32[8,128]{1,0:T(8,128)S(1)}, bf16[1,32,2304]{2,1,0:T(8,128)(2,1)}, bf16[1,32,2304]{2,1,0:T(8,128)(2,1)}, bf16[1,32,2304]{2,1,0:T(8,128)(2,1)}, ...) custom-call(bf16[32,5120]{1,0:T(8,128)(2,1)S(1)} %collective-permute, ...), custom_call_target="tpu_custom_call", output_to_operand_aliasing={{0}: (11, {}), {1}: (12, {}), {2}: (13, {}), {3}: (14, {}),... | custom-call | flops 1000000 | bytes 1000000 | tf_op jit(solution)/shard_map/backward/pallas_call | solution.py:603
  152.3 1.4 collective-permute-start.23
  154.0 1.9 %collective-permute-start.25 = (bf16[1,32,2304]{2,1,0:T(8,128)(2,1)}, bf16[1,32,2304]{2,1,0:T(8,128)(2,1)S(1)}, u32[]{:S(2)}, u32[]{:S(2)}) collective-permute-start(bf16[1,32,2304]{2,1,0:T(8,128)(2,1)} %get-tuple-element.457), channel_id=1, source_target_pairs={{0,6},{1,7},{2,4},{3,5},{4,2},{5,3},{6,0},{7,1},{8,14},{9,15},{10,... | collective-permute-start | bytes 442376 | tf_op jit(solution)/shard_map/ppermute | solution.py:33
  155.9 1.3 collective-permute-start.28
  157.2 2.2 %collective-permute-done.23 = bf16[1,32,2304]{2,1,0:T(8,128)(2,1)S(1)} collective-permute-done((bf16[1,32,2304]{2,1,0:T(8,128)(2,1)}, bf16[1,32,2304]{2,1,0:T(8,128)(2,1)S(1)}, u32[]{:S(2)}, u32[]{:S(2)}) %collective-permute-start.23) | collective-permute-done | bytes 147488 | tf_op jit(solution)/shard_map/ppermute | solution.py:33
  159.5 3.8 %collective-permute-done.24 = bf16[1,32,2304]{2,1,0:T(8,128)(2,1)S(1)} collective-permute-done((bf16[1,32,2304]{2,1,0:T(8,128)(2,1)}, bf16[1,32,2304]{2,1,0:T(8,128)(2,1)S(1)}, u32[]{:S(2)}, u32[]{:S(2)}) %collective-permute-start.24) | collective-permute-done | bytes 147488 | tf_op jit(solution)/shard_map/ppermute | solution.py:33
  163.5 0.5 collective-permute-done.28
  164.0 0.8 collective-permute-done.29
  164.8 4.5 %collective-permute-done.30 = bf16[1,32,2304]{2,1,0:T(8,128)(2,1)S(1)} collective-permute-done((bf16[1,32,2304]{2,1,0:T(8,128)(2,1)S(1)}, bf16[1,32,2304]{2,1,0:T(8,128)(2,1)S(1)}, u32[]{:S(2)}, u32[]{:S(2)}) %collective-permute-start.30) | collective-permute-done | bytes 147488 | tf_op jit(solution)/shard_map/ppermute | solution.py:33
  169.5 0.5 collective-permute-start.26
  170.1 1.3 collective-permute-done.31.rest_5_
  171.4 2.3 %gathered.2 = (f32[640,512]{1,0:T(8,128)S(1)}, f32[640,512]{1,0:T(8,128)S(1)}) custom-call(bf16[4,4,32,1792]{3,2,1,0:T(8,128)(2,1)S(1)} %pad_maximum_fusion.rest_0_, bf16[4,4,32,1792]{3,2,1,0:T(8,128)(2,1)S(1)} %collective-permute-done.17.rest_1_, bf16[4,2,32,2304]{3,2,1,0:T(8,128)(2,1)S(1)} %pad_maximum_fusion.1.rest_2_, ...), custom_call_target="tpu_custom_call" | custom-call | flops 1000000 | bytes 1000000 | tf_op jit(solution)/shard_map/gathered/pallas_call | solution.py:651
  173.7 2.1 %gathered.3 = (f32[640,512]{1,0:T(8,128)}, f32[640,512]{1,0:T(8,128)}) custom-call(bf16[4,4,32,1792]{3,2,1,0:T(8,128)(2,1)S(1)} %pad_maximum_fusion.rest_0_, bf16[4,4,32,1792]{3,2,1,0:T(8,128)(2,1)S(1)} %collective-permute-done.17.rest_1_, bf16[4,1,32,2304]{3,2,1,0:T(8,128)(2,1)S(1)} %pad_maximum_fusion.2.rest_2_, ...), custom_call_target="tpu_custom_call" | custom-call | flops 1000000 | bytes 1000000 | tf_op jit(solution)/shard_map/gathered/pallas_call | solution.py:651
  (63 shorter events, 2.7 us)
Async XLA Ops:
  10.1 9.3 %collective-permute-start.1 = (bf16[32,5120]{1,0:T(8,128)(2,1)S(1)}, bf16[32,5120]{1,0:T(8,128)(2,1)S(1)}, u32[]{:S(2)}, u32[]{:S(2)}) collective-permute-start(bf16[32,5120]{1,0:T(8,128)(2,1)S(1)} %get-tuple-element.259), channel_id=1, source_target_pairs={{0,8},{1,9},{2,10},{3,11},{4,12},{5,13},{6,14},{7,15}} | collective-permute-start | bytes 983048 | tf_op jit(solution)/shard_map/ppermute | solution.py:28
  16.4 12.2 %collective-permute-start = (bf16[32,5120]{1,0:T(8,128)(2,1)S(1)}, bf16[32,5120]{1,0:T(8,128)(2,1)S(1)}, u32[]{:S(2)}, u32[]{:S(2)}) collective-permute-start(bf16[32,5120]{1,0:T(8,128)(2,1)S(1)} %get-tuple-element.258), channel_id=1, source_target_pairs={{0,8},{1,9},{2,10},{3,11},{4,12},{5,13},{6,14},{7,15}} | collective-permute-start | bytes 983048 | tf_op jit(solution)/shard_map/ppermute | solution.py:28
  24.2 12.1 %collective-permute-start.3 = (bf16[32,5120]{1,0:T(8,128)(2,1)S(1)}, bf16[32,5120]{1,0:T(8,128)(2,1)S(1)}, u32[]{:S(2)}, u32[]{:S(2)}) collective-permute-start(bf16[32,5120]{1,0:T(8,128)(2,1)S(1)} %get-tuple-element.281), channel_id=1, source_target_pairs={{0,8},{8,16},{1,9},{9,17},{2,10},{10,18},{3,11},{11,19},{4,12},{12... | collective-permute-start | bytes 983048 | tf_op jit(solution)/shard_map/ppermute | solution.py:28
  33.5 9.8 %collective-permute-start.2 = (bf16[32,5120]{1,0:T(8,128)(2,1)S(1)}, bf16[32,5120]{1,0:T(8,128)(2,1)S(1)}, u32[]{:S(2)}, u32[]{:S(2)}) collective-permute-start(bf16[32,5120]{1,0:T(8,128)(2,1)S(1)} %get-tuple-element.280), channel_id=1, source_target_pairs={{0,8},{8,16},{1,9},{9,17},{2,10},{10,18},{3,11},{11,19},{4,12},{12... | collective-permute-start | bytes 983048 | tf_op jit(solution)/shard_map/ppermute | solution.py:28
  36.3 7.7 %collective-permute-start.5 = (bf16[32,5120]{1,0:T(8,128)(2,1)S(1)}, bf16[32,5120]{1,0:T(8,128)(2,1)S(1)}, u32[]{:S(2)}, u32[]{:S(2)}) collective-permute-start(bf16[32,5120]{1,0:T(8,128)(2,1)S(1)} %get-tuple-element.303), channel_id=1, source_target_pairs={{8,16},{16,24},{9,17},{17,25},{10,18},{18,26},{11,19},{19,27},{12,... | collective-permute-start | bytes 983048 | tf_op jit(solution)/shard_map/ppermute | solution.py:28
  43.3 1.5 collective-permute-start.4
  44.1 1.5 collective-permute-start.7
  44.9 1.5 collective-permute-start.6
  47.5 1.4 collective-permute-start.9
  48.3 1.5 collective-permute-start.12
  49.1 5.3 %collective-permute-start.14 = (bf16[32,5120]{1,0:T(8,128)(2,1)S(1)}, bf16[32,5120]{1,0:T(8,128)(2,1)S(1)}, u32[]{:S(2)}, u32[]{:S(2)}) collective-permute-start(bf16[32,5120]{1,0:T(8,128)(2,1)S(1)} %get-tuple-element.393), channel_id=1, source_target_pairs={{16,8},{24,16},{17,9},{25,17},{18,10},{26,18},{19,11},{27,19},{20,... | collective-permute-start | bytes 983048 | tf_op jit(solution)/shard_map/ppermute | solution.py:28
  49.8 1.0 copy-start.1
  49.8 3.0 %copy-start.3 = (bf16[4,32,1792]{2,1,0:T(8,128)(2,1)S(1)}, bf16[4,32,1792]{2,1,0:T(8,128)(2,1)}, u32[]{:S(2)}) copy-start(bf16[4,32,1792]{2,1,0:T(8,128)(2,1)} %get-tuple-element.381) | copy-start | bytes 1376260
  49.8 4.5 %copy-start.2 = (bf16[4,32,1792]{2,1,0:T(8,128)(2,1)S(1)}, bf16[4,32,1792]{2,1,0:T(8,128)(2,1)}, u32[]{:S(2)}) copy-start(bf16[4,32,1792]{2,1,0:T(8,128)(2,1)} %get-tuple-element.380) | copy-start | bytes 1376260
  49.9 5.9 %collective-permute-start.13 = (bf16[32,5120]{1,0:T(8,128)(2,1)S(1)}, bf16[32,5120]{1,0:T(8,128)(2,1)S(1)}, u32[]{:S(2)}, u32[]{:S(2)}) collective-permute-start(bf16[32,5120]{1,0:T(8,128)(2,1)S(1)} %get-tuple-element.392), channel_id=1, source_target_pairs={{16,8},{24,16},{17,9},{25,17},{18,10},{26,18},{19,11},{27,19},{20,... | collective-permute-start | bytes 983048 | tf_op jit(solution)/shard_map/ppermute | solution.py:28
  50.8 85.7 %collective-permute-start.8 = (bf16[4,32,1792]{2,1,0:T(8,128)(2,1)S(1)}, bf16[4,32,1792]{2,1,0:T(8,128)(2,1)S(1)}, u32[]{:S(2)}, u32[]{:S(2)}) collective-permute-start(bf16[4,32,1792]{2,1,0:T(8,128)(2,1)S(1)} %copy-done.1), channel_id=1, source_target_pairs={{0,2},{1,3},{2,0},{3,1},{4,6},{5,7},{6,4},{7,5},{8,10},{9,11},{10,... | collective-permute-start | bytes 1376264 | tf_op jit(solution)/shard_map/ppermute | solution.py:33
  52.8 83.7 %collective-permute-start.11 = (bf16[4,32,1792]{2,1,0:T(8,128)(2,1)S(1)}, bf16[4,32,1792]{2,1,0:T(8,128)(2,1)S(1)}, u32[]{:S(2)}, u32[]{:S(2)}) collective-permute-start(bf16[4,32,1792]{2,1,0:T(8,128)(2,1)S(1)} %copy-done.3), channel_id=1, source_target_pairs={{0,6},{1,7},{2,4},{3,5},{4,2},{5,3},{6,0},{7,1},{8,14},{9,15},{10,... | collective-permute-start | bytes 1376264 | tf_op jit(solution)/shard_map/ppermute | solution.py:33
  54.3 82.3 %collective-permute-start.10 = (bf16[4,32,1792]{2,1,0:T(8,128)(2,1)S(1)}, bf16[4,32,1792]{2,1,0:T(8,128)(2,1)S(1)}, u32[]{:S(2)}, u32[]{:S(2)}) collective-permute-start(bf16[4,32,1792]{2,1,0:T(8,128)(2,1)S(1)} %copy-done.2), channel_id=1, source_target_pairs={{0,4},{1,5},{2,6},{3,7},{4,0},{5,1},{6,2},{7,3},{8,12},{9,13},{10,... | collective-permute-start | bytes 1376264 | tf_op jit(solution)/shard_map/ppermute | solution.py:33
  54.5 70.2 %collective-permute-start.16 = (bf16[32,5120]{1,0:T(8,128)(2,1)S(1)}, bf16[32,5120]{1,0:T(8,128)(2,1)S(1)}, u32[]{:S(2)}, u32[]{:S(2)}) collective-permute-start(bf16[32,5120]{1,0:T(8,128)(2,1)S(1)} %get-tuple-element.413), channel_id=1, source_target_pairs={{8,0},{16,8},{9,1},{17,9},{10,2},{18,10},{11,3},{19,11},{12,4},{20... | collective-permute-start | bytes 983048 | tf_op jit(solution)/shard_map/ppermute | solution.py:28
  55.9 76.5 %collective-permute-start.15 = (bf16[32,5120]{1,0:T(8,128)(2,1)S(1)}, bf16[32,5120]{1,0:T(8,128)(2,1)S(1)}, u32[]{:S(2)}, u32[]{:S(2)}) collective-permute-start(bf16[32,5120]{1,0:T(8,128)(2,1)S(1)} %get-tuple-element.412), channel_id=1, source_target_pairs={{8,0},{16,8},{9,1},{17,9},{10,2},{18,10},{11,3},{19,11},{12,4},{20... | collective-permute-start | bytes 983048 | tf_op jit(solution)/shard_map/ppermute | solution.py:28
  127.4 15.0 %collective-permute-start.22 = (bf16[32,5120]{1,0:T(8,128)(2,1)S(1)}, bf16[32,5120]{1,0:T(8,128)(2,1)S(1)}, u32[]{:S(2)}, u32[]{:S(2)}) collective-permute-start(bf16[32,5120]{1,0:T(8,128)(2,1)S(1)} %get-tuple-element.442), channel_id=1, source_target_pairs={{8,0},{9,1},{10,2},{11,3},{12,4},{13,5},{14,6},{15,7}} | collective-permute-start | bytes 983048 | tf_op jit(solution)/shard_map/ppermute | solution.py:28
  132.4 7.6 %copy-start = (bf16[4,32,1792]{2,1,0:T(8,128)(2,1)S(1)}, bf16[4,32,1792]{2,1,0:T(8,128)(2,1)}, u32[]{:S(2)}) copy-start(bf16[4,32,1792]{2,1,0:T(8,128)(2,1)} %get-tuple-element.433) | copy-start | bytes 1376260
  135.2 13.6 %collective-permute-start.18 = (bf16[32,5120]{1,0:T(8,128)(2,1)S(1)}, bf16[32,5120]{1,0:T(8,128)(2,1)S(1)}, u32[]{:S(2)}, u32[]{:S(2)}) collective-permute-start(bf16[32,5120]{1,0:T(8,128)(2,1)S(1)} %get-tuple-element.437), channel_id=1, source_target_pairs={{8,0},{9,1},{10,2},{11,3},{12,4},{13,5},{14,6},{15,7}} | collective-permute-start | bytes 983048 | tf_op jit(solution)/shard_map/ppermute | solution.py:28
  136.5 9.5 %collective-permute-start.19 = (bf16[2,32,2304]{2,1,0:T(8,128)(2,1)}, bf16[2,32,2304]{2,1,0:T(8,128)(2,1)S(1)}, u32[]{:S(2)}, u32[]{:S(2)}) collective-permute-start(bf16[2,32,2304]{2,1,0:T(8,128)(2,1)} %get-tuple-element.439), channel_id=1, source_target_pairs={{0,2},{1,3},{2,0},{3,1},{4,6},{5,7},{6,4},{7,5},{8,10},{9,11},{10,... | collective-permute-start | bytes 884744 | tf_op jit(solution)/shard_map/ppermute | solution.py:33
  136.6 11.8 %collective-permute-start.20 = (bf16[2,32,2304]{2,1,0:T(8,128)(2,1)}, bf16[2,32,2304]{2,1,0:T(8,128)(2,1)S(1)}, u32[]{:S(2)}, u32[]{:S(2)}) collective-permute-start(bf16[2,32,2304]{2,1,0:T(8,128)(2,1)} %get-tuple-element.440), channel_id=1, source_target_pairs={{0,4},{1,5},{2,6},{3,7},{4,0},{5,1},{6,2},{7,3},{8,12},{9,13},{10,... | collective-permute-start | bytes 884744 | tf_op jit(solution)/shard_map/ppermute | solution.py:33
  136.6 11.7 %collective-permute-start.21 = (bf16[2,32,2304]{2,1,0:T(8,128)(2,1)}, bf16[2,32,2304]{2,1,0:T(8,128)(2,1)S(1)}, u32[]{:S(2)}, u32[]{:S(2)}) collective-permute-start(bf16[2,32,2304]{2,1,0:T(8,128)(2,1)} %get-tuple-element.441), channel_id=1, source_target_pairs={{0,6},{1,7},{2,4},{3,5},{4,2},{5,3},{6,0},{7,1},{8,14},{9,15},{10,... | collective-permute-start | bytes 884744 | tf_op jit(solution)/shard_map/ppermute | solution.py:33
  142.5 29.0 %collective-permute-start.17 = (bf16[4,4,32,1792]{3,2,1,0:T(8,128)(2,1)S(1)}, bf16[4,4,32,1792]{3,2,1,0:T(8,128)(2,1)S(1)}, u32[]{:S(2)}, u32[]{:S(2)}) collective-permute-start(bf16[4,4,32,1792]{3,2,1,0:T(8,128)(2,1)S(1)} %pad_maximum_fusion.rest_0_), channel_id=1, source_target_pairs={{0,1},{1,0},{2,3},{3,2},{4,5},{5,4},{6,7},{7,6},{8,9},{9,8},{10,11... | collective-permute-start | bytes 5505032 | tf_op jit(solution)/shard_map/ppermute | solution.py:37
  148.8 7.1 %copy-start.7 = (bf16[1,32,2304]{2,1,0:T(8,128)(2,1)S(1)}, bf16[1,32,2304]{2,1,0:T(8,128)(2,1)}, u32[]{:S(2)}) copy-start(bf16[1,32,2304]{2,1,0:T(8,128)(2,1)} %get-tuple-element.467) | copy-start | bytes 442372
  148.8 10.6 %copy-start.8 = (bf16[1,32,2304]{2,1,0:T(8,128)(2,1)S(1)}, bf16[1,32,2304]{2,1,0:T(8,128)(2,1)}, u32[]{:S(2)}) copy-start(bf16[1,32,2304]{2,1,0:T(8,128)(2,1)} %get-tuple-element.468) | copy-start | bytes 442372
  148.8 14.5 %copy-start.9 = (bf16[1,32,2304]{2,1,0:T(8,128)(2,1)S(1)}, bf16[1,32,2304]{2,1,0:T(8,128)(2,1)}, u32[]{:S(2)}) copy-start(bf16[1,32,2304]{2,1,0:T(8,128)(2,1)} %get-tuple-element.469) | copy-start | bytes 442372
  148.8 14.5 %copy-start.4 = (bf16[2,32,2304]{2,1,0:T(8,128)(2,1)S(1)}, bf16[2,32,2304]{2,1,0:T(8,128)(2,1)}, u32[]{:S(2)}) copy-start(bf16[2,32,2304]{2,1,0:T(8,128)(2,1)} %get-tuple-element.462) | copy-start | bytes 884740
  152.3 17.0 %copy-start.6 = (bf16[1,32,2304]{2,1,0:T(8,128)(2,1)S(1)}, bf16[1,32,2304]{2,1,0:T(8,128)(2,1)}, u32[]{:S(2)}) copy-start(bf16[1,32,2304]{2,1,0:T(8,128)(2,1)} %get-tuple-element.470) | copy-start | bytes 442372
  152.3 7.1 %collective-permute-start.23 = (bf16[1,32,2304]{2,1,0:T(8,128)(2,1)}, bf16[1,32,2304]{2,1,0:T(8,128)(2,1)S(1)}, u32[]{:S(2)}, u32[]{:S(2)}) collective-permute-start(bf16[1,32,2304]{2,1,0:T(8,128)(2,1)} %get-tuple-element.455), channel_id=1, source_target_pairs={{0,2},{1,3},{2,0},{3,1},{4,6},{5,7},{6,4},{7,5},{8,10},{9,11},{10,... | collective-permute-start | bytes 442376 | tf_op jit(solution)/shard_map/ppermute | solution.py:33
  153.7 9.6 %collective-permute-start.24 = (bf16[1,32,2304]{2,1,0:T(8,128)(2,1)}, bf16[1,32,2304]{2,1,0:T(8,128)(2,1)S(1)}, u32[]{:S(2)}, u32[]{:S(2)}) collective-permute-start(bf16[1,32,2304]{2,1,0:T(8,128)(2,1)} %get-tuple-element.456), channel_id=1, source_target_pairs={{0,4},{1,5},{2,6},{3,7},{4,0},{5,1},{6,2},{7,3},{8,12},{9,13},{10,... | collective-permute-start | bytes 442376 | tf_op jit(solution)/shard_map/ppermute | solution.py:33
  154.0 9.5 %collective-permute-start.25 = (bf16[1,32,2304]{2,1,0:T(8,128)(2,1)}, bf16[1,32,2304]{2,1,0:T(8,128)(2,1)S(1)}, u32[]{:S(2)}, u32[]{:S(2)}) collective-permute-start(bf16[1,32,2304]{2,1,0:T(8,128)(2,1)} %get-tuple-element.457), channel_id=1, source_target_pairs={{0,6},{1,7},{2,4},{3,5},{4,2},{5,3},{6,0},{7,1},{8,14},{9,15},{10,... | collective-permute-start | bytes 442376 | tf_op jit(solution)/shard_map/ppermute | solution.py:33
  155.9 8.1 %collective-permute-start.28 = (bf16[1,32,2304]{2,1,0:T(8,128)(2,1)S(1)}, bf16[1,32,2304]{2,1,0:T(8,128)(2,1)S(1)}, u32[]{:S(2)}, u32[]{:S(2)}) collective-permute-start(bf16[1,32,2304]{2,1,0:T(8,128)(2,1)S(1)} %copy-done.7), channel_id=1, source_target_pairs={{0,2},{1,3},{2,0},{3,1},{4,6},{5,7},{6,4},{7,5},{8,10},{9,11},{10,... | collective-permute-start | bytes 442376 | tf_op jit(solution)/shard_map/ppermute | solution.py:33
  159.4 5.4 %collective-permute-start.29 = (bf16[1,32,2304]{2,1,0:T(8,128)(2,1)S(1)}, bf16[1,32,2304]{2,1,0:T(8,128)(2,1)S(1)}, u32[]{:S(2)}, u32[]{:S(2)}) collective-permute-start(bf16[1,32,2304]{2,1,0:T(8,128)(2,1)S(1)} %copy-done.8), channel_id=1, source_target_pairs={{0,4},{1,5},{2,6},{3,7},{4,0},{5,1},{6,2},{7,3},{8,12},{9,13},{10,... | collective-permute-start | bytes 442376 | tf_op jit(solution)/shard_map/ppermute | solution.py:33
  163.2 6.0 %collective-permute-start.30 = (bf16[1,32,2304]{2,1,0:T(8,128)(2,1)S(1)}, bf16[1,32,2304]{2,1,0:T(8,128)(2,1)S(1)}, u32[]{:S(2)}, u32[]{:S(2)}) collective-permute-start(bf16[1,32,2304]{2,1,0:T(8,128)(2,1)S(1)} %copy-done.9), channel_id=1, source_target_pairs={{0,6},{1,7},{2,4},{3,5},{4,2},{5,3},{6,0},{7,1},{8,14},{9,15},{10,... | collective-permute-start | bytes 442376 | tf_op jit(solution)/shard_map/ppermute | solution.py:33
  163.2 6.2 %copy-start.5 = (bf16[1,32,2304]{2,1,0:T(8,128)(2,1)S(1)}, bf16[1,32,2304]{2,1,0:T(8,128)(2,1)}, u32[]{:S(2)}) copy-start(bf16[1,32,2304]{2,1,0:T(8,128)(2,1)} %get-tuple-element.458) | copy-start | bytes 442372
  163.4 8.0 %collective-permute-start.27 = (bf16[4,2,32,2304]{3,2,1,0:T(8,128)(2,1)S(1)}, bf16[4,2,32,2304]{3,2,1,0:T(8,128)(2,1)S(1)}, u32[]{:S(2)}, u32[]{:S(2)}) collective-permute-start(bf16[4,2,32,2304]{3,2,1,0:T(8,128)(2,1)S(1)} %pad_maximum_fusion.1.rest_2_), channel_id=1, source_target_pairs={{0,1},{1,0},{2,3},{3,2},{4,5},{5,4},{6,7},{7,6},{8,9},{9,8},{10,11... | collective-permute-start | bytes 3538952 | tf_op jit(solution)/shard_map/ppermute | solution.py:37
  169.4 2.1 %collective-permute-start.31 = (bf16[4,1,32,2304]{3,2,1,0:T(8,128)(2,1)S(1)}, bf16[4,1,32,2304]{3,2,1,0:T(8,128)(2,1)S(1)}, u32[]{:S(2)}, u32[]{:S(2)}) collective-permute-start(bf16[4,1,32,2304]{3,2,1,0:T(8,128)(2,1)S(1)} %pad_maximum_fusion.3.rest_4_), channel_id=1, source_target_pairs={{0,1},{1,0},{2,3},{3,2},{4,5},{5,4},{6,7},{7,6},{8,9},{9,8},{10,11... | collective-permute-start | bytes 1769480 | tf_op jit(solution)/shard_map/ppermute | solution.py:37
  169.5 4.2 %collective-permute-start.26 = (bf16[4,1,32,2304]{3,2,1,0:T(8,128)(2,1)S(1)}, bf16[4,1,32,2304]{3,2,1,0:T(8,128)(2,1)S(1)}, u32[]{:S(2)}, u32[]{:S(2)}) collective-permute-start(bf16[4,1,32,2304]{3,2,1,0:T(8,128)(2,1)S(1)} %pad_maximum_fusion.2.rest_2_), channel_id=1, source_target_pairs={{0,1},{1,0},{2,3},{3,2},{4,5},{5,4},{6,7},{7,6},{8,9},{9,8},{10,11... | collective-permute-start | bytes 1769480 | tf_op jit(solution)/shard_map/ppermute | solution.py:37

commit v5 on v4

--- a/solution.py
+++ b/solution.py
@@ -13,6 +13,7 @@
 THETA = 1000000.0
 NEG = -1e30
 CHUNK = 1280
+PIECES = 4
 BF16 = jnp.bfloat16
 F32 = jnp.float32
 
@@ -121,12 +122,16 @@
     ]
     chunks = model // CHUNK
 
+    size = CHUNK // PIECES
+
     def chunk_copies(c):
-        cols = pl.ds(c * CHUNK, CHUNK)
-        return (
-            pltpu.make_async_copy(wk_hbm.at[cols], wk.at[cols], key_sems.at[c]),
-            pltpu.make_async_copy(wv_hbm.at[cols], wv.at[cols], value_sems.at[c]),
-        )
+        copies = []
+        for piece in range(PIECES):
+            rows = pl.ds(pl.multiple_of(c * CHUNK + piece * size, 64), size)
+            at = c * PIECES + piece
+            copies.append(pltpu.make_async_copy(wk_hbm.at[rows], wk.at[rows], key_sems.at[at]))
+            copies.append(pltpu.make_async_copy(wv_hbm.at[rows], wv.at[rows], value_sems.at[at]))
+        return copies
 
     def wait_chunk(c):
         for copy in chunk_copies(c):
@@ -170,7 +175,7 @@
                 wait_chunk(c)
 
         forward_body(
-            0, section, sections, chips, wait_ahead,
+            0, 0, section, sections, chips, wait_ahead,
             w_score, wk, wv, cosine, sine, mask, ends, target,
             saved, keys, values, probs, scales, grads, *sent, outgoing, *scratch,
         )
@@ -190,6 +195,10 @@
         part = chunk * chunk
         total = part if total is None else total + part
     return lax.rsqrt(jnp.sum(total, axis=1, keepdims=True) / model + EPS)
+
+
+def when(possible, condition):
+    return pl.when(condition) if possible else lambda body: None
 
 
 def head_cols(head):
@@ -214,7 +223,7 @@
             saved[slot] = incoming[...]
 
         forward_body(
-            slot, section, sections, chips, None,
+            tick, slot, section, sections, chips, None,
             w_score, wk, wv, cosine, sine, mask, ends, target, *rest,
         )
 
@@ -240,7 +249,7 @@
 
 
 def forward_body(
-    slot, section, sections, chips, wait_chunk,
+    tick, slot, section, sections, chips, wait_chunk,
     w_score, wk, wv, cosine, sine, mask, ends, target,
     saved, keys, values, probs, scales, grads, *rest,
 ):
@@ -300,7 +309,7 @@
         out = saved[slot, :, cols].astype(F32) + dot_tb(mixed[...], wv[cols, :])
         outgoing[:, cols] = out.astype(BF16)
 
-    @pl.when(section == sections - 1)
+    @when(tick >= 2 * (sections - 1), section == sections - 1)
     def _():
         def last_of(start):
             return outgoing[:, start : start + step].astype(F32)
@@ -353,11 +362,11 @@
 
     @pl.when((offset >= 0) & (offset < micro))
     def _():
-        @pl.when(section == sections - 1)
+        @when(tick < micro, section == sections - 1)
         def _():
             current[...] = grads[slot]
 
-        @pl.when(section != sections - 1)
+        @when(tick >= 2, section != sections - 1)
         def _():
             current[...] = incoming[...]
 
@@ -368,40 +377,50 @@
             cols = pl.ds(pl.multiple_of(c * CHUNK, CHUNK), CHUNK)
             acc[...] += dot(current[:, cols], wv[cols, :])
 
-        cos_value = cosine[slot]
-        sin_value = sine[slot]
-        prob = probs[slot]
-        prob_b = prob.astype(BF16)
-        grad_probs = []
-        for head in range(KV_HEADS):
-            rows = slice(head * width, (head + 1) * width)
-            mixed_grad = acc[:, head_cols(head)].astype(BF16)
-            grad_probs.append(dot_tb(mixed_grad, values[slot, :, head_cols(head)]))
-            flat[:, features + head * HD : features + (head + 1) * HD] = dot_ta(
-                prob_b[rows, :], mixed_grad
-            ).astype(BF16)
-        grad_prob = jnp.concatenate(grad_probs, axis=0)
-        grad_score = prob * (grad_prob - jnp.sum(prob * grad_prob, axis=1, keepdims=True))
-        grad_score = grad_score.astype(BF16)
-        for head in range(KV_HEADS):
-            piece = grad_score[head * width : (head + 1) * width, :]
-            key = keys[slot, :, head_cols(head)]
-            vec = (dot(piece, key) + dot_ta(piece, key)) / HD
-            turned = vec * cos_value - pltpu.roll(vec, HD // 2, 1) * sin_value
-            flat[:, head_cols(head)] = turned.astype(BF16)
-
-        fill_block(block, current, flat)
-        for_group(lambda copy: copy.start())
-
-        @pl.when(section != 0)
+        def factors(value_pass):
+            cos_value = cosine[slot]
+            sin_value = sine[slot]
+            prob = probs[slot]
+            prob_b = prob.astype(BF16)
+            grad_probs = []
+            for head in range(KV_HEADS):
+                rows = slice(head * width, (head + 1) * width)
+                mixed_grad = acc[:, head_cols(head)].astype(BF16)
+                grad_probs.append(dot_tb(mixed_grad, values[slot, :, head_cols(head)]))
+                flat[:, features + head * HD : features + (head + 1) * HD] = dot_ta(
+                    prob_b[rows, :], mixed_grad
+                ).astype(BF16)
+            if value_pass:
+                for c in range(0, model, CHUNK):
+                    full[:, c : c + CHUNK] = dot_tb(flat[:, features:], wv[c : c + CHUNK, :])
+            grad_prob = jnp.concatenate(grad_probs, axis=0)
+            grad_score = prob * (grad_prob - jnp.sum(prob * grad_prob, axis=1, keepdims=True))
+            grad_score = grad_score.astype(BF16)
+            for head in range(KV_HEADS):
+                piece = grad_score[head * width : (head + 1) * width, :]
+                key = keys[slot, :, head_cols(head)]
+                vec = (dot(piece, key) + dot_ta(piece, key)) / HD
+                turned = vec * cos_value - pltpu.roll(vec, HD // 2, 1) * sin_value
+                flat[:, head_cols(head)] = turned.astype(BF16)
+            fill_block(block, current, flat)
+
+        lowest = tick - 2 * (sections - 1)
+
+        @when(lowest >= 0, section == 0)
         def _():
+            factors(False)
+            for_group(lambda copy: copy.start())
+
+        @when(lowest + 2 < micro, section != 0)
+        def _():
+            factors(True)
+            for_group(lambda copy: copy.start())
             acc[...] = jnp.zeros_like(acc)
 
             @pl.loop(0, model // CHUNK)
             def _(c):
                 cols = pl.ds(pl.multiple_of(c * CHUNK, CHUNK), CHUNK)
-                out = dot_tb(flat[:, :features], wk[cols, :])
-                out = out + dot_tb(flat[:, features:], wv[cols, :])
+                out = full[:, cols] + dot_tb(flat[:, :features], wk[cols, :])
                 full[:, cols] = out
                 along = out * saved[slot, :, cols].astype(F32)
                 total = along[:, :HD]
@@ -541,8 +560,8 @@
             pltpu.SMEM((1, micro), jnp.int32),
             pltpu.VMEM(grades.shape, jnp.int32),
             pltpu.SemaphoreType.DMA((6,)),
-            pltpu.SemaphoreType.DMA((chunks,)),
-            pltpu.SemaphoreType.DMA((chunks,)),
+            pltpu.SemaphoreType.DMA((PIECES * chunks,)),
+            pltpu.SemaphoreType.DMA((PIECES * chunks,)),
         ]
         + forward_scratch,
         compiler_params=params(),

time: 177 us -> 177 us (level)
  transfers between devices with their start and end apart: 32 -> 32, of which waited for: 14 -> 14; matrix products, arithmetic and copies ran while one was open for 0% -> 0% of each run, Pallas kernels for 17% -> 18%
where the time goes in v5:
time: 177 us; the launch traced here: 175 us
  waiting for transfers between devices  96.4 us (54%)
  Pallas kernels  44.4 us (25%)
  starting transfers between devices  32.2 us (18%)
    ppermute x16, waiting for transfers between devices, shifted(): lax.ppermute(value, 'section', [(source, source + steps) for source in se...  81.6 us
    ppermute x16, starting transfers between devices, shifted(): lax.ppermute(value, 'section', [(source, source + steps) for source in se...  19.9 us
    pallas_call x9, Pallas kernels, shards(): pl.pallas_call(functools.partial(forward_kernel, tick, sections, micro, c...  16.5 us
    ppermute x12, waiting for transfers between devices, between_chips(): return lax.ppermute(value, 'dp', pairs)  13.5 us
    pallas_call x10, Pallas kernels, shards(): pl.pallas_call(functools.partial(backward_kernel, tick, sections, micro,...  13.1 us
    ppermute x12, starting transfers between devices, between_chips(): return lax.ppermute(value, 'dp', pairs)  11.6 us
    pallas_call x1, Pallas kernels, shards(): pl.pallas_call(functools.partial(first_kernel, sections, micro, chips), o...  10.4 us
    pallas_call x2, Pallas kernels, shards(): pl.pallas_call(functools.partial(gather_kernel, chosen, share, wide, feat...  4.38 us
  transfers between devices with their start and end apart: 32, of which 14 were waited for; matrix products, arithmetic and copies ran while one was open for 0% of the time, Pallas kernels for 18%

profile of v5, /device:TPU:0, one launch (start us, length us, event | category | flops | bytes accessed | tf_op | source)
XLA Modules:
  0.0 175.0 jit_solution(8484434908873988925)
XLA Ops:
  0.6 10.4 %first.1 = (f32[1,5120]{1,0:T(1,128)S(1)}, bf16[5120,512]{1,0:T(8,128)(2,1)S(1)}, bf16[5120,512]{1,0:T(8,128)(2,1)S(1)}, f32[4,32,128]{2,1,0:T(8,128)S(1)}, f32[...) custom-call(bf16[5120,512]{1,0:T(8,128)(2,1)} %bitcast.24, ...), custom_call_target="tpu_custom_call" | custom-call | tf_op jit(solution)/shard_map/first/pallas_call | solution.py:553
  11.0 1.3 collective-permute-start.1
  12.4 4.9 %forward.9 = (bf16[4,32,5120]{2,1,0:T(8,128)(2,1)S(1)}, bf16[4,32,512]{2,1,0:T(8,128)(2,1)S(1)}, bf16[4,32,512]{2,1,0:T(8,128)(2,1)S(1)}, f32[4,128,32]{2,1,0:T(...) custom-call(bf16[32,5120]{1,0:T(8,128)(2,1)S(1)} %broadcast_in_dim.9, ...), custom_call_target="tpu_custom_call", output_to_operand_aliasing={{0}: (9, {}), {1}: (10, {}), {2}: (11, {}), {3}: (12, {}), ... | custom-call | flops 1000000 | bytes 1000000 | tf_op jit(solution)/shard_map/forward/pallas_call | solution.py:591
  17.3 1.3 collective-permute-start
  18.6 1.7 collective-permute-done.1.incoming
  20.3 4.8 %forward.10 = (bf16[4,32,5120]{2,1,0:T(8,128)(2,1)S(1)}, bf16[4,32,512]{2,1,0:T(8,128)(2,1)S(1)}, bf16[4,32,512]{2,1,0:T(8,128)(2,1)S(1)}, f32[4,128,32]{2,1,0:T...) custom-call(bf16[32,5120]{1,0:T(8,128)(2,1)S(1)} %collective-permute, ...), custom_call_target="tpu_custom_call", output_to_operand_aliasing={{0}: (9, {}), {1}: (10, {}), {2}: (11, {}), {3}: (12, {}), ... | custom-call | flops 1000000 | bytes 1000000 | tf_op jit(solution)/shard_map/forward/pallas_call | solution.py:591
  25.1 4.4 %collective-permute-start.3 = (bf16[32,5120]{1,0:T(8,128)(2,1)S(1)}, bf16[32,5120]{1,0:T(8,128)(2,1)S(1)}, u32[]{:S(2)}, u32[]{:S(2)}) collective-permute-start(bf16[32,5120]{1,0:T(8,128)(2,1)S(1)} %get-tuple-element.281), channel_id=1, source_target_pairs={{0,8},{8,16},{1,9},{9,17},{2,10},{10,18},{3,11},{11,19},{4,12},{12... | collective-permute-start | bytes 983048 | tf_op jit(solution)/shard_map/ppermute | solution.py:29
  29.6 4.9 %forward.11 = (bf16[4,32,5120]{2,1,0:T(8,128)(2,1)S(1)}, bf16[4,32,512]{2,1,0:T(8,128)(2,1)S(1)}, bf16[4,32,512]{2,1,0:T(8,128)(2,1)S(1)}, f32[4,128,32]{2,1,0:T...) custom-call(bf16[32,5120]{1,0:T(8,128)(2,1)S(1)} %collective-permute, ...), custom_call_target="tpu_custom_call", output_to_operand_aliasing={{0}: (9, {}), {1}: (10, {}), {2}: (11, {}), {3}: (12, {}), ... | custom-call | flops 1000000 | bytes 1000000 | tf_op jit(solution)/shard_map/forward/pallas_call | solution.py:591
  34.5 2.1 %collective-permute-start.2 = (bf16[32,5120]{1,0:T(8,128)(2,1)S(1)}, bf16[32,5120]{1,0:T(8,128)(2,1)S(1)}, u32[]{:S(2)}, u32[]{:S(2)}) collective-permute-start(bf16[32,5120]{1,0:T(8,128)(2,1)S(1)} %get-tuple-element.280), channel_id=1, source_target_pairs={{0,8},{8,16},{1,9},{9,17},{2,10},{10,18},{3,11},{11,19},{4,12},{12... | collective-permute-start | bytes 983048 | tf_op jit(solution)/shard_map/ppermute | solution.py:29
  37.2 0.7 collective-permute-start.5
  37.9 6.2 %collective-permute-done.2.incoming = bf16[32,5120]{1,0:T(8,128)(2,1)S(1)} collective-permute-done((bf16[32,5120]{1,0:T(8,128)(2,1)S(1)}, bf16[32,5120]{1,0:T(8,128)(2,1)S(1)}, u32[]{:S(2)}, u32[]{:S(2)}) %collective-permute-start.2) | collective-permute-done | bytes 327712 | tf_op jit(solution)/shard_map/ppermute | solution.py:29
  44.1 0.7 collective-permute-start.4
  44.9 0.7 collective-permute-start.7
  45.7 0.7 collective-permute-start.6
  46.4 0.8 forward.16
  47.2 0.8 forward.17
  48.1 0.7 collective-permute-start.9
  49.0 0.7 collective-permute-start.12
  49.8 0.7 collective-permute-start.14
  50.7 0.8 collective-permute-start.13
  51.6 1.9 %collective-permute-start.8 = (bf16[4,32,1792]{2,1,0:T(8,128)(2,1)S(1)}, bf16[4,32,1792]{2,1,0:T(8,128)(2,1)S(1)}, u32[]{:S(2)}, u32[]{:S(2)}) collective-permute-start(bf16[4,32,1792]{2,1,0:T(8,128)(2,1)S(1)} %copy-done.1), channel_id=1, source_target_pairs={{0,2},{1,3},{2,0},{3,1},{4,6},{5,7},{6,4},{7,5},{8,10},{9,11},{10,... | collective-permute-start | bytes 1376264 | tf_op jit(solution)/shard_map/ppermute | solution.py:34
  53.5 1.5 collective-permute-start.11
  55.1 1.3 collective-permute-start.16
  56.5 1.3 collective-permute-start.15
  57.8 66.0 %collective-permute-done.16.incoming = bf16[32,5120]{1,0:T(8,128)(2,1)S(1)} collective-permute-done((bf16[32,5120]{1,0:T(8,128)(2,1)S(1)}, bf16[32,5120]{1,0:T(8,128)(2,1)S(1)}, u32[]{:S(2)}, u32[]{:S(2)}) %collective-permute-start.16) | collective-permute-done | bytes 327712 | tf_op jit(solution)/shard_map/ppermute | solution.py:29
  123.8 2.8 %backward.16 = (f32[8,128]{1,0:T(8,128)S(1)}, bf16[2,32,2304]{2,1,0:T(8,128)(2,1)}, bf16[2,32,2304]{2,1,0:T(8,128)(2,1)}, bf16[2,32,2304]{2,1,0:T(8,128)(2,1)}, ...) custom-call(bf16[32,5120]{1,0:T(8,128)(2,1)S(1)} %collective-permute, ...), custom_call_target="tpu_custom_call", output_to_operand_aliasing={{0}: (11, {}), {1}: (12, {}), {2}: (13, {}), {3}: (14, {}),... | custom-call | flops 1000000 | bytes 1000000 | tf_op jit(solution)/shard_map/backward/pallas_call | solution.py:622
  126.6 1.3 collective-permute-start.22
  127.9 3.5 %collective-permute-done.15.incoming = bf16[32,5120]{1,0:T(8,128)(2,1)S(1)} collective-permute-done((bf16[32,5120]{1,0:T(8,128)(2,1)S(1)}, bf16[32,5120]{1,0:T(8,128)(2,1)S(1)}, u32[]{:S(2)}, u32[]{:S(2)}) %collective-permute-start.15) | collective-permute-done | bytes 327712 | tf_op jit(solution)/shard_map/ppermute | solution.py:29
  131.4 2.8 %backward.17 = (f32[8,128]{1,0:T(8,128)S(1)}, bf16[2,32,2304]{2,1,0:T(8,128)(2,1)}, bf16[2,32,2304]{2,1,0:T(8,128)(2,1)}, bf16[2,32,2304]{2,1,0:T(8,128)(2,1)}, ...) custom-call(bf16[32,5120]{1,0:T(8,128)(2,1)S(1)} %collective-permute, ...), custom_call_target="tpu_custom_call", output_to_operand_aliasing={{0}: (11, {}), {1}: (12, {}), {2}: (13, {}), {3}: (14, {}),... | custom-call | flops 1000000 | bytes 1000000 | tf_op jit(solution)/shard_map/backward/pallas_call | solution.py:622
  134.1 1.3 collective-permute-start.18
  135.6 3.4 %collective-permute-start.21 = (bf16[2,32,2304]{2,1,0:T(8,128)(2,1)}, bf16[2,32,2304]{2,1,0:T(8,128)(2,1)S(1)}, u32[]{:S(2)}, u32[]{:S(2)}) collective-permute-start(bf16[2,32,2304]{2,1,0:T(8,128)(2,1)} %get-tuple-element.441), channel_id=1, source_target_pairs={{0,6},{1,7},{2,4},{3,5},{4,2},{5,3},{6,0},{7,1},{8,14},{9,15},{10,... | collective-permute-start | bytes 884744 | tf_op jit(solution)/shard_map/ppermute | solution.py:34
  139.3 2.7 %collective-permute-done.22.incoming = bf16[32,5120]{1,0:T(8,128)(2,1)S(1)} collective-permute-done((bf16[32,5120]{1,0:T(8,128)(2,1)S(1)}, bf16[32,5120]{1,0:T(8,128)(2,1)S(1)}, u32[]{:S(2)}, u32[]{:S(2)}) %collective-permute-start.22) | collective-permute-done | bytes 327712 | tf_op jit(solution)/shard_map/ppermute | solution.py:29
  142.0 3.5 %backward.18 = (f32[8,128]{1,0:T(8,128)S(1)}, bf16[1,32,2304]{2,1,0:T(8,128)(2,1)}, bf16[1,32,2304]{2,1,0:T(8,128)(2,1)}, bf16[1,32,2304]{2,1,0:T(8,128)(2,1)}, ...) custom-call(bf16[32,5120]{1,0:T(8,128)(2,1)S(1)} %collective-permute, ...), custom_call_target="tpu_custom_call", output_to_operand_aliasing={{0}: (11, {}), {1}: (12, {}), {2}: (13, {}), {3}: (14, {}),... | custom-call | flops 1000000 | bytes 1000000 | tf_op jit(solution)/shard_map/backward/pallas_call | solution.py:622
  145.5 1.7 collective-permute-done.20
  147.2 0.9 collective-permute-done.18.incoming
  148.1 3.5 %backward.19 = (f32[8,128]{1,0:T(8,128)S(1)}, bf16[1,32,2304]{2,1,0:T(8,128)(2,1)}, bf16[1,32,2304]{2,1,0:T(8,128)(2,1)}, bf16[1,32,2304]{2,1,0:T(8,128)(2,1)}, ...) custom-call(bf16[32,5120]{1,0:T(8,128)(2,1)S(1)} %collective-permute, ...), custom_call_target="tpu_custom_call", output_to_operand_aliasing={{0}: (11, {}), {1}: (12, {}), {2}: (13, {}), {3}: (14, {}),... | custom-call | flops 1000000 | bytes 1000000 | tf_op jit(solution)/shard_map/backward/pallas_call | solution.py:622
  151.7 0.8 collective-permute-start.23
  152.8 2.4 %collective-permute-start.25 = (bf16[1,32,2304]{2,1,0:T(8,128)(2,1)}, bf16[1,32,2304]{2,1,0:T(8,128)(2,1)S(1)}, u32[]{:S(2)}, u32[]{:S(2)}) collective-permute-start(bf16[1,32,2304]{2,1,0:T(8,128)(2,1)} %get-tuple-element.457), channel_id=1, source_target_pairs={{0,6},{1,7},{2,4},{3,5},{4,2},{5,3},{6,0},{7,1},{8,14},{9,15},{10,... | collective-permute-start | bytes 442376 | tf_op jit(solution)/shard_map/ppermute | solution.py:34
  155.3 0.7 collective-permute-start.28
  156.0 2.7 %collective-permute-done.23 = bf16[1,32,2304]{2,1,0:T(8,128)(2,1)S(1)} collective-permute-done((bf16[1,32,2304]{2,1,0:T(8,128)(2,1)}, bf16[1,32,2304]{2,1,0:T(8,128)(2,1)S(1)}, u32[]{:S(2)}, u32[]{:S(2)}) %collective-permute-start.23) | collective-permute-done | bytes 147488 | tf_op jit(solution)/shard_map/ppermute | solution.py:34
  159.0 3.2 %collective-permute-done.24 = bf16[1,32,2304]{2,1,0:T(8,128)(2,1)S(1)} collective-permute-done((bf16[1,32,2304]{2,1,0:T(8,128)(2,1)}, bf16[1,32,2304]{2,1,0:T(8,128)(2,1)S(1)}, u32[]{:S(2)}, u32[]{:S(2)}) %collective-permute-start.24) | collective-permute-done | bytes 147488 | tf_op jit(solution)/shard_map/ppermute | solution.py:34
  162.5 1.0 collective-permute-done.28
  163.5 0.6 collective-permute-done.29
  164.2 4.1 %collective-permute-done.30 = bf16[1,32,2304]{2,1,0:T(8,128)(2,1)S(1)} collective-permute-done((bf16[1,32,2304]{2,1,0:T(8,128)(2,1)S(1)}, bf16[1,32,2304]{2,1,0:T(8,128)(2,1)S(1)}, u32[]{:S(2)}, u32[]{:S(2)}) %collective-permute-start.30) | collective-permute-done | bytes 147488 | tf_op jit(solution)/shard_map/ppermute | solution.py:34
  168.5 0.5 collective-permute-start.26
  169.1 1.3 collective-permute-done.31.rest_5_
  170.4 2.3 %gathered.2 = (f32[640,512]{1,0:T(8,128)S(1)}, f32[640,512]{1,0:T(8,128)S(1)}) custom-call(bf16[4,4,32,1792]{3,2,1,0:T(8,128)(2,1)S(1)} %pad_maximum_fusion.rest_0_, bf16[4,4,32,1792]{3,2,1,0:T(8,128)(2,1)S(1)} %collective-permute-done.17.rest_1_, bf16[4,2,32,2304]{3,2,1,0:T(8,128)(2,1)S(1)} %pad_maximum_fusion.1.rest_2_, ...), custom_call_target="tpu_custom_call" | custom-call | flops 1000000 | bytes 1000000 | tf_op jit(solution)/shard_map/gathered/pallas_call | solution.py:670
  172.7 2.1 %gathered.3 = (f32[640,512]{1,0:T(8,128)}, f32[640,512]{1,0:T(8,128)}) custom-call(bf16[4,4,32,1792]{3,2,1,0:T(8,128)(2,1)S(1)} %pad_maximum_fusion.rest_0_, bf16[4,4,32,1792]{3,2,1,0:T(8,128)(2,1)S(1)} %collective-permute-done.17.rest_1_, bf16[4,1,32,2304]{3,2,1,0:T(8,128)(2,1)S(1)} %pad_maximum_fusion.2.rest_2_, ...), custom_call_target="tpu_custom_call" | custom-call | flops 1000000 | bytes 1000000 | tf_op jit(solution)/shard_map/gathered/pallas_call | solution.py:670
  (63 shorter events, 3.0 us)
Async XLA Ops:
  11.0 9.3 %collective-permute-start.1 = (bf16[32,5120]{1,0:T(8,128)(2,1)S(1)}, bf16[32,5120]{1,0:T(8,128)(2,1)S(1)}, u32[]{:S(2)}, u32[]{:S(2)}) collective-permute-start(bf16[32,5120]{1,0:T(8,128)(2,1)S(1)} %get-tuple-element.259), channel_id=1, source_target_pairs={{0,8},{1,9},{2,10},{3,11},{4,12},{5,13},{6,14},{7,15}} | collective-permute-start | bytes 983048 | tf_op jit(solution)/shard_map/ppermute | solution.py:29
  17.3 12.3 %collective-permute-start = (bf16[32,5120]{1,0:T(8,128)(2,1)S(1)}, bf16[32,5120]{1,0:T(8,128)(2,1)S(1)}, u32[]{:S(2)}, u32[]{:S(2)}) collective-permute-start(bf16[32,5120]{1,0:T(8,128)(2,1)S(1)} %get-tuple-element.258), channel_id=1, source_target_pairs={{0,8},{1,9},{2,10},{3,11},{4,12},{5,13},{6,14},{7,15}} | collective-permute-start | bytes 983048 | tf_op jit(solution)/shard_map/ppermute | solution.py:29
  25.1 12.0 %collective-permute-start.3 = (bf16[32,5120]{1,0:T(8,128)(2,1)S(1)}, bf16[32,5120]{1,0:T(8,128)(2,1)S(1)}, u32[]{:S(2)}, u32[]{:S(2)}) collective-permute-start(bf16[32,5120]{1,0:T(8,128)(2,1)S(1)} %get-tuple-element.281), channel_id=1, source_target_pairs={{0,8},{8,16},{1,9},{9,17},{2,10},{10,18},{3,11},{11,19},{4,12},{12... | collective-permute-start | bytes 983048 | tf_op jit(solution)/shard_map/ppermute | solution.py:29
  34.5 9.6 %collective-permute-start.2 = (bf16[32,5120]{1,0:T(8,128)(2,1)S(1)}, bf16[32,5120]{1,0:T(8,128)(2,1)S(1)}, u32[]{:S(2)}, u32[]{:S(2)}) collective-permute-start(bf16[32,5120]{1,0:T(8,128)(2,1)S(1)} %get-tuple-element.280), channel_id=1, source_target_pairs={{0,8},{8,16},{1,9},{9,17},{2,10},{10,18},{3,11},{11,19},{4,12},{12... | collective-permute-start | bytes 983048 | tf_op jit(solution)/shard_map/ppermute | solution.py:29
  37.2 7.6 %collective-permute-start.5 = (bf16[32,5120]{1,0:T(8,128)(2,1)S(1)}, bf16[32,5120]{1,0:T(8,128)(2,1)S(1)}, u32[]{:S(2)}, u32[]{:S(2)}) collective-permute-start(bf16[32,5120]{1,0:T(8,128)(2,1)S(1)} %get-tuple-element.303), channel_id=1, source_target_pairs={{8,16},{16,24},{9,17},{17,25},{10,18},{18,26},{11,19},{19,27},{12,... | collective-permute-start | bytes 983048 | tf_op jit(solution)/shard_map/ppermute | solution.py:29
  44.1 1.5 collective-permute-start.4
  44.9 1.5 collective-permute-start.7
  45.7 1.5 collective-permute-start.6
  48.1 1.6 collective-permute-start.9
  49.0 1.5 collective-permute-start.12
  49.8 5.2 %collective-permute-start.14 = (bf16[32,5120]{1,0:T(8,128)(2,1)S(1)}, bf16[32,5120]{1,0:T(8,128)(2,1)S(1)}, u32[]{:S(2)}, u32[]{:S(2)}) collective-permute-start(bf16[32,5120]{1,0:T(8,128)(2,1)S(1)} %get-tuple-element.393), channel_id=1, source_target_pairs={{16,8},{24,16},{17,9},{25,17},{18,10},{26,18},{19,11},{27,19},{20,... | collective-permute-start | bytes 983048 | tf_op jit(solution)/shard_map/ppermute | solution.py:29
  50.5 1.0 copy-start.1
  50.5 2.9 %copy-start.3 = (bf16[4,32,1792]{2,1,0:T(8,128)(2,1)S(1)}, bf16[4,32,1792]{2,1,0:T(8,128)(2,1)}, u32[]{:S(2)}) copy-start(bf16[4,32,1792]{2,1,0:T(8,128)(2,1)} %get-tuple-element.381) | copy-start | bytes 1376260
  50.6 4.4 %copy-start.2 = (bf16[4,32,1792]{2,1,0:T(8,128)(2,1)S(1)}, bf16[4,32,1792]{2,1,0:T(8,128)(2,1)}, u32[]{:S(2)}) copy-start(bf16[4,32,1792]{2,1,0:T(8,128)(2,1)} %get-tuple-element.380) | copy-start | bytes 1376260
  50.7 5.8 %collective-permute-start.13 = (bf16[32,5120]{1,0:T(8,128)(2,1)S(1)}, bf16[32,5120]{1,0:T(8,128)(2,1)S(1)}, u32[]{:S(2)}, u32[]{:S(2)}) collective-permute-start(bf16[32,5120]{1,0:T(8,128)(2,1)S(1)} %get-tuple-element.392), channel_id=1, source_target_pairs={{16,8},{24,16},{17,9},{25,17},{18,10},{26,18},{19,11},{27,19},{20,... | collective-permute-start | bytes 983048 | tf_op jit(solution)/shard_map/ppermute | solution.py:29
  51.6 83.9 %collective-permute-start.8 = (bf16[4,32,1792]{2,1,0:T(8,128)(2,1)S(1)}, bf16[4,32,1792]{2,1,0:T(8,128)(2,1)S(1)}, u32[]{:S(2)}, u32[]{:S(2)}) collective-permute-start(bf16[4,32,1792]{2,1,0:T(8,128)(2,1)S(1)} %copy-done.1), channel_id=1, source_target_pairs={{0,2},{1,3},{2,0},{3,1},{4,6},{5,7},{6,4},{7,5},{8,10},{9,11},{10,... | collective-permute-start | bytes 1376264 | tf_op jit(solution)/shard_map/ppermute | solution.py:34
  53.5 82.1 %collective-permute-start.11 = (bf16[4,32,1792]{2,1,0:T(8,128)(2,1)S(1)}, bf16[4,32,1792]{2,1,0:T(8,128)(2,1)S(1)}, u32[]{:S(2)}, u32[]{:S(2)}) collective-permute-start(bf16[4,32,1792]{2,1,0:T(8,128)(2,1)S(1)} %copy-done.3), channel_id=1, source_target_pairs={{0,6},{1,7},{2,4},{3,5},{4,2},{5,3},{6,0},{7,1},{8,14},{9,15},{10,... | collective-permute-start | bytes 1376264 | tf_op jit(solution)/shard_map/ppermute | solution.py:34
  54.9 80.7 %collective-permute-start.10 = (bf16[4,32,1792]{2,1,0:T(8,128)(2,1)S(1)}, bf16[4,32,1792]{2,1,0:T(8,128)(2,1)S(1)}, u32[]{:S(2)}, u32[]{:S(2)}) collective-permute-start(bf16[4,32,1792]{2,1,0:T(8,128)(2,1)S(1)} %copy-done.2), channel_id=1, source_target_pairs={{0,4},{1,5},{2,6},{3,7},{4,0},{5,1},{6,2},{7,3},{8,12},{9,13},{10,... | collective-permute-start | bytes 1376264 | tf_op jit(solution)/shard_map/ppermute | solution.py:34
  55.1 68.7 %collective-permute-start.16 = (bf16[32,5120]{1,0:T(8,128)(2,1)S(1)}, bf16[32,5120]{1,0:T(8,128)(2,1)S(1)}, u32[]{:S(2)}, u32[]{:S(2)}) collective-permute-start(bf16[32,5120]{1,0:T(8,128)(2,1)S(1)} %get-tuple-element.413), channel_id=1, source_target_pairs={{8,0},{16,8},{9,1},{17,9},{10,2},{18,10},{11,3},{19,11},{12,4},{20... | collective-permute-start | bytes 983048 | tf_op jit(solution)/shard_map/ppermute | solution.py:29
  56.5 74.9 %collective-permute-start.15 = (bf16[32,5120]{1,0:T(8,128)(2,1)S(1)}, bf16[32,5120]{1,0:T(8,128)(2,1)S(1)}, u32[]{:S(2)}, u32[]{:S(2)}) collective-permute-start(bf16[32,5120]{1,0:T(8,128)(2,1)S(1)} %get-tuple-element.412), channel_id=1, source_target_pairs={{8,0},{16,8},{9,1},{17,9},{10,2},{18,10},{11,3},{19,11},{12,4},{20... | collective-permute-start | bytes 983048 | tf_op jit(solution)/shard_map/ppermute | solution.py:29
  126.6 15.4 %collective-permute-start.22 = (bf16[32,5120]{1,0:T(8,128)(2,1)S(1)}, bf16[32,5120]{1,0:T(8,128)(2,1)S(1)}, u32[]{:S(2)}, u32[]{:S(2)}) collective-permute-start(bf16[32,5120]{1,0:T(8,128)(2,1)S(1)} %get-tuple-element.442), channel_id=1, source_target_pairs={{8,0},{9,1},{10,2},{11,3},{12,4},{13,5},{14,6},{15,7}} | collective-permute-start | bytes 983048 | tf_op jit(solution)/shard_map/ppermute | solution.py:29
  131.4 7.6 %copy-start = (bf16[4,32,1792]{2,1,0:T(8,128)(2,1)S(1)}, bf16[4,32,1792]{2,1,0:T(8,128)(2,1)}, u32[]{:S(2)}) copy-start(bf16[4,32,1792]{2,1,0:T(8,128)(2,1)} %get-tuple-element.433) | copy-start | bytes 1376260
  134.1 14.0 %collective-permute-start.18 = (bf16[32,5120]{1,0:T(8,128)(2,1)S(1)}, bf16[32,5120]{1,0:T(8,128)(2,1)S(1)}, u32[]{:S(2)}, u32[]{:S(2)}) collective-permute-start(bf16[32,5120]{1,0:T(8,128)(2,1)S(1)} %get-tuple-element.437), channel_id=1, source_target_pairs={{8,0},{9,1},{10,2},{11,3},{12,4},{13,5},{14,6},{15,7}} | collective-permute-start | bytes 983048 | tf_op jit(solution)/shard_map/ppermute | solution.py:29
  135.5 10.0 %collective-permute-start.19 = (bf16[2,32,2304]{2,1,0:T(8,128)(2,1)}, bf16[2,32,2304]{2,1,0:T(8,128)(2,1)S(1)}, u32[]{:S(2)}, u32[]{:S(2)}) collective-permute-start(bf16[2,32,2304]{2,1,0:T(8,128)(2,1)} %get-tuple-element.439), channel_id=1, source_target_pairs={{0,2},{1,3},{2,0},{3,1},{4,6},{5,7},{6,4},{7,5},{8,10},{9,11},{10,... | collective-permute-start | bytes 884744 | tf_op jit(solution)/shard_map/ppermute | solution.py:34
  135.5 11.7 %collective-permute-start.20 = (bf16[2,32,2304]{2,1,0:T(8,128)(2,1)}, bf16[2,32,2304]{2,1,0:T(8,128)(2,1)S(1)}, u32[]{:S(2)}, u32[]{:S(2)}) collective-permute-start(bf16[2,32,2304]{2,1,0:T(8,128)(2,1)} %get-tuple-element.440), channel_id=1, source_target_pairs={{0,4},{1,5},{2,6},{3,7},{4,0},{5,1},{6,2},{7,3},{8,12},{9,13},{10,... | collective-permute-start | bytes 884744 | tf_op jit(solution)/shard_map/ppermute | solution.py:34
  135.6 11.6 %collective-permute-start.21 = (bf16[2,32,2304]{2,1,0:T(8,128)(2,1)}, bf16[2,32,2304]{2,1,0:T(8,128)(2,1)S(1)}, u32[]{:S(2)}, u32[]{:S(2)}) collective-permute-start(bf16[2,32,2304]{2,1,0:T(8,128)(2,1)} %get-tuple-element.441), channel_id=1, source_target_pairs={{0,6},{1,7},{2,4},{3,5},{4,2},{5,3},{6,0},{7,1},{8,14},{9,15},{10,... | collective-permute-start | bytes 884744 | tf_op jit(solution)/shard_map/ppermute | solution.py:34
  142.0 28.4 %collective-permute-start.17 = (bf16[4,4,32,1792]{3,2,1,0:T(8,128)(2,1)S(1)}, bf16[4,4,32,1792]{3,2,1,0:T(8,128)(2,1)S(1)}, u32[]{:S(2)}, u32[]{:S(2)}) collective-permute-start(bf16[4,4,32,1792]{3,2,1,0:T(8,128)(2,1)S(1)} %pad_maximum_fusion.rest_0_), channel_id=1, source_target_pairs={{0,1},{1,0},{2,3},{3,2},{4,5},{5,4},{6,7},{7,6},{8,9},{9,8},{10,11... | collective-permute-start | bytes 5505032 | tf_op jit(solution)/shard_map/ppermute | solution.py:38
  148.1 7.1 %copy-start.7 = (bf16[1,32,2304]{2,1,0:T(8,128)(2,1)S(1)}, bf16[1,32,2304]{2,1,0:T(8,128)(2,1)}, u32[]{:S(2)}) copy-start(bf16[1,32,2304]{2,1,0:T(8,128)(2,1)} %get-tuple-element.467) | copy-start | bytes 442372
  148.1 10.6 %copy-start.8 = (bf16[1,32,2304]{2,1,0:T(8,128)(2,1)S(1)}, bf16[1,32,2304]{2,1,0:T(8,128)(2,1)}, u32[]{:S(2)}) copy-start(bf16[1,32,2304]{2,1,0:T(8,128)(2,1)} %get-tuple-element.468) | copy-start | bytes 442372
  148.1 14.1 %copy-start.9 = (bf16[1,32,2304]{2,1,0:T(8,128)(2,1)S(1)}, bf16[1,32,2304]{2,1,0:T(8,128)(2,1)}, u32[]{:S(2)}) copy-start(bf16[1,32,2304]{2,1,0:T(8,128)(2,1)} %get-tuple-element.469) | copy-start | bytes 442372
  148.1 14.1 %copy-start.4 = (bf16[2,32,2304]{2,1,0:T(8,128)(2,1)S(1)}, bf16[2,32,2304]{2,1,0:T(8,128)(2,1)}, u32[]{:S(2)}) copy-start(bf16[2,32,2304]{2,1,0:T(8,128)(2,1)} %get-tuple-element.462) | copy-start | bytes 884740
  151.7 16.6 %copy-start.6 = (bf16[1,32,2304]{2,1,0:T(8,128)(2,1)S(1)}, bf16[1,32,2304]{2,1,0:T(8,128)(2,1)}, u32[]{:S(2)}) copy-start(bf16[1,32,2304]{2,1,0:T(8,128)(2,1)} %get-tuple-element.470) | copy-start | bytes 442372
  151.7 7.1 %collective-permute-start.23 = (bf16[1,32,2304]{2,1,0:T(8,128)(2,1)}, bf16[1,32,2304]{2,1,0:T(8,128)(2,1)S(1)}, u32[]{:S(2)}, u32[]{:S(2)}) collective-permute-start(bf16[1,32,2304]{2,1,0:T(8,128)(2,1)} %get-tuple-element.455), channel_id=1, source_target_pairs={{0,2},{1,3},{2,0},{3,1},{4,6},{5,7},{6,4},{7,5},{8,10},{9,11},{10,... | collective-permute-start | bytes 442376 | tf_op jit(solution)/shard_map/ppermute | solution.py:34
  152.5 9.7 %collective-permute-start.24 = (bf16[1,32,2304]{2,1,0:T(8,128)(2,1)}, bf16[1,32,2304]{2,1,0:T(8,128)(2,1)S(1)}, u32[]{:S(2)}, u32[]{:S(2)}) collective-permute-start(bf16[1,32,2304]{2,1,0:T(8,128)(2,1)} %get-tuple-element.456), channel_id=1, source_target_pairs={{0,4},{1,5},{2,6},{3,7},{4,0},{5,1},{6,2},{7,3},{8,12},{9,13},{10,... | collective-permute-start | bytes 442376 | tf_op jit(solution)/shard_map/ppermute | solution.py:34
  152.8 9.6 %collective-permute-start.25 = (bf16[1,32,2304]{2,1,0:T(8,128)(2,1)}, bf16[1,32,2304]{2,1,0:T(8,128)(2,1)S(1)}, u32[]{:S(2)}, u32[]{:S(2)}) collective-permute-start(bf16[1,32,2304]{2,1,0:T(8,128)(2,1)} %get-tuple-element.457), channel_id=1, source_target_pairs={{0,6},{1,7},{2,4},{3,5},{4,2},{5,3},{6,0},{7,1},{8,14},{9,15},{10,... | collective-permute-start | bytes 442376 | tf_op jit(solution)/shard_map/ppermute | solution.py:34
  155.3 8.3 %collective-permute-start.28 = (bf16[1,32,2304]{2,1,0:T(8,128)(2,1)S(1)}, bf16[1,32,2304]{2,1,0:T(8,128)(2,1)S(1)}, u32[]{:S(2)}, u32[]{:S(2)}) collective-permute-start(bf16[1,32,2304]{2,1,0:T(8,128)(2,1)S(1)} %copy-done.7), channel_id=1, source_target_pairs={{0,2},{1,3},{2,0},{3,1},{4,6},{5,7},{6,4},{7,5},{8,10},{9,11},{10,... | collective-permute-start | bytes 442376 | tf_op jit(solution)/shard_map/ppermute | solution.py:34
  158.7 5.4 %collective-permute-start.29 = (bf16[1,32,2304]{2,1,0:T(8,128)(2,1)S(1)}, bf16[1,32,2304]{2,1,0:T(8,128)(2,1)S(1)}, u32[]{:S(2)}, u32[]{:S(2)}) collective-permute-start(bf16[1,32,2304]{2,1,0:T(8,128)(2,1)S(1)} %copy-done.8), channel_id=1, source_target_pairs={{0,4},{1,5},{2,6},{3,7},{4,0},{5,1},{6,2},{7,3},{8,12},{9,13},{10,... | collective-permute-start | bytes 442376 | tf_op jit(solution)/shard_map/ppermute | solution.py:34
  162.2 6.0 %collective-permute-start.30 = (bf16[1,32,2304]{2,1,0:T(8,128)(2,1)S(1)}, bf16[1,32,2304]{2,1,0:T(8,128)(2,1)S(1)}, u32[]{:S(2)}, u32[]{:S(2)}) collective-permute-start(bf16[1,32,2304]{2,1,0:T(8,128)(2,1)S(1)} %copy-done.9), channel_id=1, source_target_pairs={{0,6},{1,7},{2,4},{3,5},{4,2},{5,3},{6,0},{7,1},{8,14},{9,15},{10,... | collective-permute-start | bytes 442376 | tf_op jit(solution)/shard_map/ppermute | solution.py:34
  162.2 6.2 %copy-start.5 = (bf16[1,32,2304]{2,1,0:T(8,128)(2,1)S(1)}, bf16[1,32,2304]{2,1,0:T(8,128)(2,1)}, u32[]{:S(2)}) copy-start(bf16[1,32,2304]{2,1,0:T(8,128)(2,1)} %get-tuple-element.458) | copy-start | bytes 442372
  162.4 8.0 %collective-permute-start.27 = (bf16[4,2,32,2304]{3,2,1,0:T(8,128)(2,1)S(1)}, bf16[4,2,32,2304]{3,2,1,0:T(8,128)(2,1)S(1)}, u32[]{:S(2)}, u32[]{:S(2)}) collective-permute-start(bf16[4,2,32,2304]{3,2,1,0:T(8,128)(2,1)S(1)} %pad_maximum_fusion.1.rest_2_), channel_id=1, source_target_pairs={{0,1},{1,0},{2,3},{3,2},{4,5},{5,4},{6,7},{7,6},{8,9},{9,8},{10,11... | collective-permute-start | bytes 3538952 | tf_op jit(solution)/shard_map/ppermute | solution.py:38
  168.3 2.1 %collective-permute-start.31 = (bf16[4,1,32,2304]{3,2,1,0:T(8,128)(2,1)S(1)}, bf16[4,1,32,2304]{3,2,1,0:T(8,128)(2,1)S(1)}, u32[]{:S(2)}, u32[]{:S(2)}) collective-permute-start(bf16[4,1,32,2304]{3,2,1,0:T(8,128)(2,1)S(1)} %pad_maximum_fusion.3.rest_4_), channel_id=1, source_target_pairs={{0,1},{1,0},{2,3},{3,2},{4,5},{5,4},{6,7},{7,6},{8,9},{9,8},{10,11... | collective-permute-start | bytes 1769480 | tf_op jit(solution)/shard_map/ppermute | solution.py:38
  168.5 4.2 %collective-permute-start.26 = (bf16[4,1,32,2304]{3,2,1,0:T(8,128)(2,1)S(1)}, bf16[4,1,32,2304]{3,2,1,0:T(8,128)(2,1)S(1)}, u32[]{:S(2)}, u32[]{:S(2)}) collective-permute-start(bf16[4,1,32,2304]{3,2,1,0:T(8,128)(2,1)S(1)} %pad_maximum_fusion.2.rest_2_), channel_id=1, source_target_pairs={{0,1},{1,0},{2,3},{3,2},{4,5},{5,4},{6,7},{7,6},{8,9},{9,8},{10,11... | collective-permute-start | bytes 1769480 | tf_op jit(solution)/shard_map/ppermute | solution.py:38

commit v6 on v5

--- a/solution.py
+++ b/solution.py
@@ -13,7 +13,6 @@
 THETA = 1000000.0
 NEG = -1e30
 CHUNK = 1280
-PIECES = 4
 BF16 = jnp.bfloat16
 F32 = jnp.float32
 
@@ -114,79 +113,48 @@
         pltpu.make_async_copy(segments_hbm, segments_ref, small.at[0]),
         pltpu.make_async_copy(lengths_hbm, lengths_ref, small.at[1]),
         pltpu.make_async_copy(grades_hbm, grades_ref, small.at[2]),
-        pltpu.make_async_copy(x0_hbm.at[0], saved.at[0], small.at[3]),
+        pltpu.make_async_copy(x0_hbm, saved, small.at[3]),
+        pltpu.make_async_copy(score_hbm, w_score, small.at[4]),
     ]
-    later = [
-        pltpu.make_async_copy(x0_hbm.at[pl.ds(1, micro - 1)], saved.at[pl.ds(1, micro - 1)], small.at[4]),
-        pltpu.make_async_copy(score_hbm, w_score, small.at[5]),
-    ]
-    chunks = model // CHUNK
-
-    size = CHUNK // PIECES
-
-    def chunk_copies(c):
-        copies = []
-        for piece in range(PIECES):
-            rows = pl.ds(pl.multiple_of(c * CHUNK + piece * size, 64), size)
-            at = c * PIECES + piece
-            copies.append(pltpu.make_async_copy(wk_hbm.at[rows], wk.at[rows], key_sems.at[at]))
-            copies.append(pltpu.make_async_copy(wv_hbm.at[rows], wv.at[rows], value_sems.at[at]))
-        return copies
-
-    def wait_chunk(c):
-        for copy in chunk_copies(c):
-            copy.wait()
-
-        @pl.when(c + 2 < chunks)
-        def _():
-            for copy in chunk_copies(jnp.minimum(c + 2, chunks - 1)):
-                copy.start()
-
     for copy in copies:
         copy.start()
-    for c in range(2):
+
+    def chunk_copies(c):
+        cols = pl.ds(c * CHUNK, CHUNK)
+        return (
+            pltpu.make_async_copy(wk_hbm.at[cols], wk.at[cols], key_sems.at[c]),
+            pltpu.make_async_copy(wv_hbm.at[cols], wv.at[cols], value_sems.at[c]),
+        )
+
+    for c in range(model // CHUNK):
         for copy in chunk_copies(c):
             copy.start()
-    section = lax.axis_index("section")
-    second = lax.axis_index("dp") % 2 == 1
-    ahead = (section == 0) & jnp.logical_not(second)
-    behind = (section == 0) & second
-    for copy in copies:
+    for copy in copies[:3]:
         copy.wait()
-
-    @pl.when(jnp.logical_not(ahead))
-    def _():
-        @pl.loop(0, chunks)
-        def _(c):
-            wait_chunk(c)
-
-        for copy in later:
-            copy.start()
-
     make_tables(
         micro, segments_ref, lengths_ref, grades_ref, cosine, sine, mask, ends, target
     )
+    for copy in copies[3:]:
+        copy.wait()
+    section = lax.axis_index("section")
 
     @pl.when(section == 0)
     def _():
-        def wait_ahead(c):
-            @pl.when(ahead)
-            def _():
-                wait_chunk(c)
+        def wait_chunk(c):
+            for copy in chunk_copies(c):
+                copy.wait()
 
         forward_body(
-            0, 0, section, sections, chips, wait_ahead,
+            0, 0, section, sections, chips, wait_chunk,
             w_score, wk, wv, cosine, sine, mask, ends, target,
             saved, keys, values, probs, scales, grads, *sent, outgoing, *scratch,
         )
 
-    @pl.when(ahead)
+    @pl.when(section != 0)
     def _():
-        for copy in later:
-            copy.start()
-
-    for copy in later:
-        copy.wait()
+        for c in range(model // CHUNK):
+            for copy in chunk_copies(c):
+                copy.wait()
 
 
 def row_scale(ref_value_chunks, model):
@@ -559,9 +527,9 @@
             pltpu.VMEM(segments.shape, jnp.int32),
             pltpu.SMEM((1, micro), jnp.int32),
             pltpu.VMEM(grades.shape, jnp.int32),
-            pltpu.SemaphoreType.DMA((6,)),
-            pltpu.SemaphoreType.DMA((PIECES * chunks,)),
-            pltpu.SemaphoreType.DMA((PIECES * chunks,)),
+            pltpu.SemaphoreType.DMA((5,)),
+            pltpu.SemaphoreType.DMA((chunks,)),
+            pltpu.SemaphoreType.DMA((chunks,)),
         ]
         + forward_scratch,
         compiler_params=params(),
@@ -662,7 +630,7 @@
 
     whole = jax.ShapeDtypeStruct((share, features), F32)
     total = ()
-    for final, chosen in ((False, groups[:-1]), (True, groups[-1:])):
+    for final, chosen in ((False, groups[:1]), (True, groups[1:])):
         args = [*forward_blocks, *[value for group in chosen for value in gathered[groups.index(group)]]]
         slots = sum(len(group) for group in chosen)
         at = (2, chips, slots, width)

time: 177 us -> 172 us (0.972)
  waiting for transfers between devices: 96.4 us -> 88.5 us
  starting transfers between devices: 32.2 us -> 37.5 us
  Pallas kernels: 44.4 us -> 42.2 us
    ppermute x12, starting transfers between devices: 11.6 us -> 17.1 us  [between_chips(): return lax.ppermute(value, 'dp', pairs)]
    ppermute x16, waiting for transfers between devices: 81.6 us -> 77.8 us  [shifted(): lax.ppermute(value, 'section', [(source, source + steps) for source in se...]
    ppermute x12, waiting for transfers between devices: 13.5 us -> 10.2 us  [between_chips(): return lax.ppermute(value, 'dp', pairs)]
    pallas_call x1, Pallas kernels: 10.4 us -> 8.46 us  [shards(): pl.pallas_call(functools.partial(first_kernel, sections, micro, chips), o...]
  transfers between devices with their start and end apart: 32 -> 32, of which waited for: 14 -> 13; matrix products, arithmetic and copies ran while one was open for 0% -> 0% of each run, Pallas kernels for 18% -> 18%
where the time goes in v6:
time: 172 us; the launch traced here: 170 us
  waiting for transfers between devices  88.5 us (51%)
  Pallas kernels  42.2 us (25%)
  starting transfers between devices  37.5 us (22%)
    ppermute x16, waiting for transfers between devices, shifted(): lax.ppermute(value, 'section', [(source, source + steps) for source in se...  77.8 us
    ppermute x16, starting transfers between devices, shifted(): lax.ppermute(value, 'section', [(source, source + steps) for source in se...  19.7 us
    ppermute x12, starting transfers between devices, between_chips(): return lax.ppermute(value, 'dp', pairs)  17.1 us
    pallas_call x9, Pallas kernels, shards(): pl.pallas_call(functools.partial(forward_kernel, tick, sections, micro, c...  16.5 us
    pallas_call x10, Pallas kernels, shards(): pl.pallas_call(functools.partial(backward_kernel, tick, sections, micro,...  13.1 us
    ppermute x12, waiting for transfers between devices, between_chips(): return lax.ppermute(value, 'dp', pairs)  10.2 us
    pallas_call x1, Pallas kernels, shards(): pl.pallas_call(functools.partial(first_kernel, sections, micro, chips), o...  8.46 us
    pallas_call x2, Pallas kernels, shards(): pl.pallas_call(functools.partial(gather_kernel, chosen, share, wide, feat...  4.09 us
  transfers between devices with their start and end apart: 32, of which 13 were waited for; matrix products, arithmetic and copies ran while one was open for 0% of the time, Pallas kernels for 18%

profile of v6, /device:TPU:0, one launch (start us, length us, event | category | flops | bytes accessed | tf_op | source)
XLA Modules:
  0.0 170.2 jit_solution(6896532509394166196)
XLA Ops:
  0.6 8.5 %first.1 = (f32[1,5120]{1,0:T(1,128)S(1)}, bf16[5120,512]{1,0:T(8,128)(2,1)S(1)}, bf16[5120,512]{1,0:T(8,128)(2,1)S(1)}, f32[4,32,128]{2,1,0:T(8,128)S(1)}, f32[...) custom-call(bf16[5120,512]{1,0:T(8,128)(2,1)} %bitcast.24, ...), custom_call_target="tpu_custom_call" | custom-call | tf_op jit(solution)/shard_map/first/pallas_call | solution.py:521
  9.1 1.3 collective-permute-start.1
  10.4 4.9 %forward.9 = (bf16[4,32,5120]{2,1,0:T(8,128)(2,1)S(1)}, bf16[4,32,512]{2,1,0:T(8,128)(2,1)S(1)}, bf16[4,32,512]{2,1,0:T(8,128)(2,1)S(1)}, f32[4,128,32]{2,1,0:T(...) custom-call(bf16[32,5120]{1,0:T(8,128)(2,1)S(1)} %broadcast_in_dim.9, ...), custom_call_target="tpu_custom_call", output_to_operand_aliasing={{0}: (9, {}), {1}: (10, {}), {2}: (11, {}), {3}: (12, {}), ... | custom-call | flops 1000000 | bytes 1000000 | tf_op jit(solution)/shard_map/forward/pallas_call | solution.py:559
  15.3 1.3 collective-permute-start
  16.7 1.8 %collective-permute-done.1.incoming = bf16[32,5120]{1,0:T(8,128)(2,1)S(1)} collective-permute-done((bf16[32,5120]{1,0:T(8,128)(2,1)S(1)}, bf16[32,5120]{1,0:T(8,128)(2,1)S(1)}, u32[]{:S(2)}, u32[]{:S(2)}) %collective-permute-start.1) | collective-permute-done | bytes 327712 | tf_op jit(solution)/shard_map/ppermute | solution.py:28
  18.5 4.8 %forward.10 = (bf16[4,32,5120]{2,1,0:T(8,128)(2,1)S(1)}, bf16[4,32,512]{2,1,0:T(8,128)(2,1)S(1)}, bf16[4,32,512]{2,1,0:T(8,128)(2,1)S(1)}, f32[4,128,32]{2,1,0:T...) custom-call(bf16[32,5120]{1,0:T(8,128)(2,1)S(1)} %collective-permute, ...), custom_call_target="tpu_custom_call", output_to_operand_aliasing={{0}: (9, {}), {1}: (10, {}), {2}: (11, {}), {3}: (12, {}), ... | custom-call | flops 1000000 | bytes 1000000 | tf_op jit(solution)/shard_map/forward/pallas_call | solution.py:559
  23.3 4.4 %collective-permute-start.3 = (bf16[32,5120]{1,0:T(8,128)(2,1)S(1)}, bf16[32,5120]{1,0:T(8,128)(2,1)S(1)}, u32[]{:S(2)}, u32[]{:S(2)}) collective-permute-start(bf16[32,5120]{1,0:T(8,128)(2,1)S(1)} %get-tuple-element.281), channel_id=1, source_target_pairs={{0,8},{8,16},{1,9},{9,17},{2,10},{10,18},{3,11},{11,19},{4,12},{12... | collective-permute-start | bytes 983048 | tf_op jit(solution)/shard_map/ppermute | solution.py:28
  27.8 4.9 %forward.11 = (bf16[4,32,5120]{2,1,0:T(8,128)(2,1)S(1)}, bf16[4,32,512]{2,1,0:T(8,128)(2,1)S(1)}, bf16[4,32,512]{2,1,0:T(8,128)(2,1)S(1)}, f32[4,128,32]{2,1,0:T...) custom-call(bf16[32,5120]{1,0:T(8,128)(2,1)S(1)} %collective-permute, ...), custom_call_target="tpu_custom_call", output_to_operand_aliasing={{0}: (9, {}), {1}: (10, {}), {2}: (11, {}), {3}: (12, {}), ... | custom-call | flops 1000000 | bytes 1000000 | tf_op jit(solution)/shard_map/forward/pallas_call | solution.py:559
  32.7 1.9 %collective-permute-start.2 = (bf16[32,5120]{1,0:T(8,128)(2,1)S(1)}, bf16[32,5120]{1,0:T(8,128)(2,1)S(1)}, u32[]{:S(2)}, u32[]{:S(2)}) collective-permute-start(bf16[32,5120]{1,0:T(8,128)(2,1)S(1)} %get-tuple-element.280), channel_id=1, source_target_pairs={{0,8},{8,16},{1,9},{9,17},{2,10},{10,18},{3,11},{11,19},{4,12},{12... | collective-permute-start | bytes 983048 | tf_op jit(solution)/shard_map/ppermute | solution.py:28
  34.7 0.7 collective-permute-start.5
  35.4 6.1 %collective-permute-done.2.incoming = bf16[32,5120]{1,0:T(8,128)(2,1)S(1)} collective-permute-done((bf16[32,5120]{1,0:T(8,128)(2,1)S(1)}, bf16[32,5120]{1,0:T(8,128)(2,1)S(1)}, u32[]{:S(2)}, u32[]{:S(2)}) %collective-permute-start.2) | collective-permute-done | bytes 327712 | tf_op jit(solution)/shard_map/ppermute | solution.py:28
  41.6 0.7 collective-permute-start.4
  42.4 0.7 collective-permute-start.7
  43.1 0.7 collective-permute-start.6
  43.8 0.8 forward.16
  44.7 0.8 forward.17
  45.6 0.7 collective-permute-start.9
  46.5 0.7 collective-permute-start.12
  47.3 0.7 collective-permute-start.14
  48.1 0.8 collective-permute-start.13
  49.0 1.9 %collective-permute-start.8 = (bf16[4,32,1792]{2,1,0:T(8,128)(2,1)S(1)}, bf16[4,32,1792]{2,1,0:T(8,128)(2,1)S(1)}, u32[]{:S(2)}, u32[]{:S(2)}) collective-permute-start(bf16[4,32,1792]{2,1,0:T(8,128)(2,1)S(1)} %copy-done.1), channel_id=1, source_target_pairs={{0,2},{1,3},{2,0},{3,1},{4,6},{5,7},{6,4},{7,5},{8,10},{9,11},{10,... | collective-permute-start | bytes 1376264 | tf_op jit(solution)/shard_map/ppermute | solution.py:33
  50.9 1.5 collective-permute-start.11
  52.6 1.3 collective-permute-start.16
  54.0 1.3 collective-permute-start.15
  55.3 64.2 %collective-permute-done.16.incoming = bf16[32,5120]{1,0:T(8,128)(2,1)S(1)} collective-permute-done((bf16[32,5120]{1,0:T(8,128)(2,1)S(1)}, bf16[32,5120]{1,0:T(8,128)(2,1)S(1)}, u32[]{:S(2)}, u32[]{:S(2)}) %collective-permute-start.16) | collective-permute-done | bytes 327712 | tf_op jit(solution)/shard_map/ppermute | solution.py:28
  119.4 2.8 %backward.16 = (f32[8,128]{1,0:T(8,128)S(1)}, bf16[2,32,2304]{2,1,0:T(8,128)(2,1)}, bf16[2,32,2304]{2,1,0:T(8,128)(2,1)}, bf16[2,32,2304]{2,1,0:T(8,128)(2,1)}, ...) custom-call(bf16[32,5120]{1,0:T(8,128)(2,1)S(1)} %collective-permute, ...), custom_call_target="tpu_custom_call", output_to_operand_aliasing={{0}: (11, {}), {1}: (12, {}), {2}: (13, {}), {3}: (14, {}),... | custom-call | flops 1000000 | bytes 1000000 | tf_op jit(solution)/shard_map/backward/pallas_call | solution.py:590
  122.2 1.3 collective-permute-start.18
  123.5 3.1 %collective-permute-done.15.incoming = bf16[32,5120]{1,0:T(8,128)(2,1)S(1)} collective-permute-done((bf16[32,5120]{1,0:T(8,128)(2,1)S(1)}, bf16[32,5120]{1,0:T(8,128)(2,1)S(1)}, u32[]{:S(2)}, u32[]{:S(2)}) %collective-permute-start.15) | collective-permute-done | bytes 327712 | tf_op jit(solution)/shard_map/ppermute | solution.py:28
  126.6 2.8 %backward.17 = (f32[8,128]{1,0:T(8,128)S(1)}, bf16[2,32,2304]{2,1,0:T(8,128)(2,1)}, bf16[2,32,2304]{2,1,0:T(8,128)(2,1)}, bf16[2,32,2304]{2,1,0:T(8,128)(2,1)}, ...) custom-call(bf16[32,5120]{1,0:T(8,128)(2,1)S(1)} %collective-permute, ...), custom_call_target="tpu_custom_call", output_to_operand_aliasing={{0}: (11, {}), {1}: (12, {}), {2}: (13, {}), {3}: (14, {}),... | custom-call | flops 1000000 | bytes 1000000 | tf_op jit(solution)/shard_map/backward/pallas_call | solution.py:590
  129.4 1.3 collective-permute-start.23
  130.7 2.9 %collective-permute-start.24 = (bf16[2,32,2304]{2,1,0:T(8,128)(2,1)}, bf16[2,32,2304]{2,1,0:T(8,128)(2,1)S(1)}, u32[]{:S(2)}, u32[]{:S(2)}) collective-permute-start(bf16[2,32,2304]{2,1,0:T(8,128)(2,1)} %get-tuple-element.453), channel_id=1, source_target_pairs={{0,2},{1,3},{2,0},{3,1},{4,6},{5,7},{6,4},{7,5},{8,10},{9,11},{10,... | collective-permute-start | bytes 884744 | tf_op jit(solution)/shard_map/ppermute | solution.py:33
  133.6 2.6 %collective-permute-start.25 = (bf16[2,32,2304]{2,1,0:T(8,128)(2,1)}, bf16[2,32,2304]{2,1,0:T(8,128)(2,1)S(1)}, u32[]{:S(2)}, u32[]{:S(2)}) collective-permute-start(bf16[2,32,2304]{2,1,0:T(8,128)(2,1)} %get-tuple-element.454), channel_id=1, source_target_pairs={{0,4},{1,5},{2,6},{3,7},{4,0},{5,1},{6,2},{7,3},{8,12},{9,13},{10,... | collective-permute-start | bytes 884744 | tf_op jit(solution)/shard_map/ppermute | solution.py:33
  136.5 2.4 %collective-permute-done.18.incoming = bf16[32,5120]{1,0:T(8,128)(2,1)S(1)} collective-permute-done((bf16[32,5120]{1,0:T(8,128)(2,1)S(1)}, bf16[32,5120]{1,0:T(8,128)(2,1)S(1)}, u32[]{:S(2)}, u32[]{:S(2)}) %collective-permute-start.18) | collective-permute-done | bytes 327712 | tf_op jit(solution)/shard_map/ppermute | solution.py:28
  138.9 3.5 %backward.18 = (f32[8,128]{1,0:T(8,128)S(1)}, bf16[1,32,2304]{2,1,0:T(8,128)(2,1)}, bf16[1,32,2304]{2,1,0:T(8,128)(2,1)}, bf16[1,32,2304]{2,1,0:T(8,128)(2,1)}, ...) custom-call(bf16[32,5120]{1,0:T(8,128)(2,1)S(1)} %collective-permute, ...), custom_call_target="tpu_custom_call", output_to_operand_aliasing={{0}: (11, {}), {1}: (12, {}), {2}: (13, {}), {3}: (14, {}),... | custom-call | flops 1000000 | bytes 1000000 | tf_op jit(solution)/shard_map/backward/pallas_call | solution.py:590
  142.4 1.9 %collective-permute-done.25 = bf16[2,32,2304]{2,1,0:T(8,128)(2,1)S(1)} collective-permute-done((bf16[2,32,2304]{2,1,0:T(8,128)(2,1)}, bf16[2,32,2304]{2,1,0:T(8,128)(2,1)S(1)}, u32[]{:S(2)}, u32[]{:S(2)}) %collective-permute-start.25) | collective-permute-done | bytes 294944 | tf_op jit(solution)/shard_map/ppermute | solution.py:33
  144.4 3.5 %backward.19 = (f32[8,128]{1,0:T(8,128)S(1)}, bf16[1,32,2304]{2,1,0:T(8,128)(2,1)}, bf16[1,32,2304]{2,1,0:T(8,128)(2,1)}, bf16[1,32,2304]{2,1,0:T(8,128)(2,1)}, ...) custom-call(bf16[32,5120]{1,0:T(8,128)(2,1)S(1)} %collective-permute, ...), custom_call_target="tpu_custom_call", output_to_operand_aliasing={{0}: (11, {}), {1}: (12, {}), {2}: (13, {}), {3}: (14, {}),... | custom-call | flops 1000000 | bytes 1000000 | tf_op jit(solution)/shard_map/backward/pallas_call | solution.py:590
  148.0 1.4 collective-permute-start.27
  149.4 1.7 %collective-permute-start.28 = (bf16[1,32,2304]{2,1,0:T(8,128)(2,1)}, bf16[1,32,2304]{2,1,0:T(8,128)(2,1)S(1)}, u32[]{:S(2)}, u32[]{:S(2)}) collective-permute-start(bf16[1,32,2304]{2,1,0:T(8,128)(2,1)} %get-tuple-element.464), channel_id=1, source_target_pairs={{0,4},{1,5},{2,6},{3,7},{4,0},{5,1},{6,2},{7,3},{8,12},{9,13},{10,... | collective-permute-start | bytes 442376 | tf_op jit(solution)/shard_map/ppermute | solution.py:33
  151.5 1.3 collective-permute-start.19
  152.9 1.2 collective-permute-done.27
  154.1 2.1 %collective-permute-start.20 = (bf16[1,32,2304]{2,1,0:T(8,128)(2,1)S(1)}, bf16[1,32,2304]{2,1,0:T(8,128)(2,1)S(1)}, u32[]{:S(2)}, u32[]{:S(2)}) collective-permute-start(bf16[1,32,2304]{2,1,0:T(8,128)(2,1)S(1)} %copy-done.8), channel_id=1, source_target_pairs={{0,4},{1,5},{2,6},{3,7},{4,0},{5,1},{6,2},{7,3},{8,12},{9,13},{10,... | collective-permute-start | bytes 442376 | tf_op jit(solution)/shard_map/ppermute | solution.py:33
  156.2 2.3 %collective-permute-done.28 = bf16[1,32,2304]{2,1,0:T(8,128)(2,1)S(1)} collective-permute-done((bf16[1,32,2304]{2,1,0:T(8,128)(2,1)}, bf16[1,32,2304]{2,1,0:T(8,128)(2,1)S(1)}, u32[]{:S(2)}, u32[]{:S(2)}) %collective-permute-start.28) | collective-permute-done | bytes 147488 | tf_op jit(solution)/shard_map/ppermute | solution.py:33
  158.5 1.1 collective-permute-start.21
  160.0 2.1 %collective-permute-done.20 = bf16[1,32,2304]{2,1,0:T(8,128)(2,1)S(1)} collective-permute-done((bf16[1,32,2304]{2,1,0:T(8,128)(2,1)S(1)}, bf16[1,32,2304]{2,1,0:T(8,128)(2,1)S(1)}, u32[]{:S(2)}, u32[]{:S(2)}) %collective-permute-start.20) | collective-permute-done | bytes 147488 | tf_op jit(solution)/shard_map/ppermute | solution.py:33
  162.1 2.5 %collective-permute-done.21 = bf16[1,32,2304]{2,1,0:T(8,128)(2,1)S(1)} collective-permute-done((bf16[1,32,2304]{2,1,0:T(8,128)(2,1)S(1)}, bf16[1,32,2304]{2,1,0:T(8,128)(2,1)S(1)}, u32[]{:S(2)}, u32[]{:S(2)}) %collective-permute-start.21) | collective-permute-done | bytes 147488 | tf_op jit(solution)/shard_map/ppermute | solution.py:33
  164.8 0.5 collective-permute-start.30
  165.4 1.6 gathered.2
  167.6 2.5 %gathered.3 = (f32[640,512]{1,0:T(8,128)}, f32[640,512]{1,0:T(8,128)}) custom-call(bf16[4,4,32,1792]{3,2,1,0:T(8,128)(2,1)S(1)} %pad_maximum_fusion.rest_0_, bf16[4,4,32,1792]{3,2,1,0:T(8,128)(2,1)S(1)} %collective-permute-done.17.rest_1_, bf16[4,1,32,2304]{3,2,1,0:T(8,128)(2,1)S(1)} %pad_maximum_fusion.2.rest_2_, ...), custom_call_target="tpu_custom_call" | custom-call | flops 1000000 | bytes 1000000 | tf_op jit(solution)/shard_map/gathered/pallas_call | solution.py:638
  (63 shorter events, 3.1 us)
Async XLA Ops:
  9.1 9.4 %collective-permute-start.1 = (bf16[32,5120]{1,0:T(8,128)(2,1)S(1)}, bf16[32,5120]{1,0:T(8,128)(2,1)S(1)}, u32[]{:S(2)}, u32[]{:S(2)}) collective-permute-start(bf16[32,5120]{1,0:T(8,128)(2,1)S(1)} %get-tuple-element.259), channel_id=1, source_target_pairs={{0,8},{1,9},{2,10},{3,11},{4,12},{5,13},{6,14},{7,15}} | collective-permute-start | bytes 983048 | tf_op jit(solution)/shard_map/ppermute | solution.py:28
  15.3 12.4 %collective-permute-start = (bf16[32,5120]{1,0:T(8,128)(2,1)S(1)}, bf16[32,5120]{1,0:T(8,128)(2,1)S(1)}, u32[]{:S(2)}, u32[]{:S(2)}) collective-permute-start(bf16[32,5120]{1,0:T(8,128)(2,1)S(1)} %get-tuple-element.258), channel_id=1, source_target_pairs={{0,8},{1,9},{2,10},{3,11},{4,12},{5,13},{6,14},{7,15}} | collective-permute-start | bytes 983048 | tf_op jit(solution)/shard_map/ppermute | solution.py:28
  23.3 11.3 %collective-permute-start.3 = (bf16[32,5120]{1,0:T(8,128)(2,1)S(1)}, bf16[32,5120]{1,0:T(8,128)(2,1)S(1)}, u32[]{:S(2)}, u32[]{:S(2)}) collective-permute-start(bf16[32,5120]{1,0:T(8,128)(2,1)S(1)} %get-tuple-element.281), channel_id=1, source_target_pairs={{0,8},{8,16},{1,9},{9,17},{2,10},{10,18},{3,11},{11,19},{4,12},{12... | collective-permute-start | bytes 983048 | tf_op jit(solution)/shard_map/ppermute | solution.py:28
  32.7 8.9 %collective-permute-start.2 = (bf16[32,5120]{1,0:T(8,128)(2,1)S(1)}, bf16[32,5120]{1,0:T(8,128)(2,1)S(1)}, u32[]{:S(2)}, u32[]{:S(2)}) collective-permute-start(bf16[32,5120]{1,0:T(8,128)(2,1)S(1)} %get-tuple-element.280), channel_id=1, source_target_pairs={{0,8},{8,16},{1,9},{9,17},{2,10},{10,18},{3,11},{11,19},{4,12},{12... | collective-permute-start | bytes 983048 | tf_op jit(solution)/shard_map/ppermute | solution.py:28
  34.7 7.5 %collective-permute-start.5 = (bf16[32,5120]{1,0:T(8,128)(2,1)S(1)}, bf16[32,5120]{1,0:T(8,128)(2,1)S(1)}, u32[]{:S(2)}, u32[]{:S(2)}) collective-permute-start(bf16[32,5120]{1,0:T(8,128)(2,1)S(1)} %get-tuple-element.303), channel_id=1, source_target_pairs={{8,16},{16,24},{9,17},{17,25},{10,18},{18,26},{11,19},{19,27},{12,... | collective-permute-start | bytes 983048 | tf_op jit(solution)/shard_map/ppermute | solution.py:28
  41.6 1.5 collective-permute-start.4
  42.4 1.5 collective-permute-start.7
  43.1 1.5 collective-permute-start.6
  45.6 1.6 collective-permute-start.9
  46.5 1.5 collective-permute-start.12
  47.3 5.2 %collective-permute-start.14 = (bf16[32,5120]{1,0:T(8,128)(2,1)S(1)}, bf16[32,5120]{1,0:T(8,128)(2,1)S(1)}, u32[]{:S(2)}, u32[]{:S(2)}) collective-permute-start(bf16[32,5120]{1,0:T(8,128)(2,1)S(1)} %get-tuple-element.393), channel_id=1, source_target_pairs={{16,8},{24,16},{17,9},{25,17},{18,10},{26,18},{19,11},{27,19},{20,... | collective-permute-start | bytes 983048 | tf_op jit(solution)/shard_map/ppermute | solution.py:28
  48.0 1.0 copy-start.1
  48.0 2.9 %copy-start.3 = (bf16[4,32,1792]{2,1,0:T(8,128)(2,1)S(1)}, bf16[4,32,1792]{2,1,0:T(8,128)(2,1)}, u32[]{:S(2)}) copy-start(bf16[4,32,1792]{2,1,0:T(8,128)(2,1)} %get-tuple-element.381) | copy-start | bytes 1376260
  48.0 4.3 %copy-start.2 = (bf16[4,32,1792]{2,1,0:T(8,128)(2,1)S(1)}, bf16[4,32,1792]{2,1,0:T(8,128)(2,1)}, u32[]{:S(2)}) copy-start(bf16[4,32,1792]{2,1,0:T(8,128)(2,1)} %get-tuple-element.380) | copy-start | bytes 1376260
  48.1 5.7 %collective-permute-start.13 = (bf16[32,5120]{1,0:T(8,128)(2,1)S(1)}, bf16[32,5120]{1,0:T(8,128)(2,1)S(1)}, u32[]{:S(2)}, u32[]{:S(2)}) collective-permute-start(bf16[32,5120]{1,0:T(8,128)(2,1)S(1)} %get-tuple-element.392), channel_id=1, source_target_pairs={{16,8},{24,16},{17,9},{25,17},{18,10},{26,18},{19,11},{27,19},{20,... | collective-permute-start | bytes 983048 | tf_op jit(solution)/shard_map/ppermute | solution.py:28
  49.0 81.6 %collective-permute-start.8 = (bf16[4,32,1792]{2,1,0:T(8,128)(2,1)S(1)}, bf16[4,32,1792]{2,1,0:T(8,128)(2,1)S(1)}, u32[]{:S(2)}, u32[]{:S(2)}) collective-permute-start(bf16[4,32,1792]{2,1,0:T(8,128)(2,1)S(1)} %copy-done.1), channel_id=1, source_target_pairs={{0,2},{1,3},{2,0},{3,1},{4,6},{5,7},{6,4},{7,5},{8,10},{9,11},{10,... | collective-permute-start | bytes 1376264 | tf_op jit(solution)/shard_map/ppermute | solution.py:33
  50.9 82.7 %collective-permute-start.11 = (bf16[4,32,1792]{2,1,0:T(8,128)(2,1)S(1)}, bf16[4,32,1792]{2,1,0:T(8,128)(2,1)S(1)}, u32[]{:S(2)}, u32[]{:S(2)}) collective-permute-start(bf16[4,32,1792]{2,1,0:T(8,128)(2,1)S(1)} %copy-done.3), channel_id=1, source_target_pairs={{0,6},{1,7},{2,4},{3,5},{4,2},{5,3},{6,0},{7,1},{8,14},{9,15},{10,... | collective-permute-start | bytes 1376264 | tf_op jit(solution)/shard_map/ppermute | solution.py:33
  52.4 83.9 %collective-permute-start.10 = (bf16[4,32,1792]{2,1,0:T(8,128)(2,1)S(1)}, bf16[4,32,1792]{2,1,0:T(8,128)(2,1)S(1)}, u32[]{:S(2)}, u32[]{:S(2)}) collective-permute-start(bf16[4,32,1792]{2,1,0:T(8,128)(2,1)S(1)} %copy-done.2), channel_id=1, source_target_pairs={{0,4},{1,5},{2,6},{3,7},{4,0},{5,1},{6,2},{7,3},{8,12},{9,13},{10,... | collective-permute-start | bytes 1376264 | tf_op jit(solution)/shard_map/ppermute | solution.py:33
  52.6 66.9 %collective-permute-start.16 = (bf16[32,5120]{1,0:T(8,128)(2,1)S(1)}, bf16[32,5120]{1,0:T(8,128)(2,1)S(1)}, u32[]{:S(2)}, u32[]{:S(2)}) collective-permute-start(bf16[32,5120]{1,0:T(8,128)(2,1)S(1)} %get-tuple-element.413), channel_id=1, source_target_pairs={{8,0},{16,8},{9,1},{17,9},{10,2},{18,10},{11,3},{19,11},{12,4},{20... | collective-permute-start | bytes 983048 | tf_op jit(solution)/shard_map/ppermute | solution.py:28
  54.0 72.6 %collective-permute-start.15 = (bf16[32,5120]{1,0:T(8,128)(2,1)S(1)}, bf16[32,5120]{1,0:T(8,128)(2,1)S(1)}, u32[]{:S(2)}, u32[]{:S(2)}) collective-permute-start(bf16[32,5120]{1,0:T(8,128)(2,1)S(1)} %get-tuple-element.412), channel_id=1, source_target_pairs={{8,0},{16,8},{9,1},{17,9},{10,2},{18,10},{11,3},{19,11},{12,4},{20... | collective-permute-start | bytes 983048 | tf_op jit(solution)/shard_map/ppermute | solution.py:28
  122.2 16.7 %collective-permute-start.18 = (bf16[32,5120]{1,0:T(8,128)(2,1)S(1)}, bf16[32,5120]{1,0:T(8,128)(2,1)S(1)}, u32[]{:S(2)}, u32[]{:S(2)}) collective-permute-start(bf16[32,5120]{1,0:T(8,128)(2,1)S(1)} %get-tuple-element.437), channel_id=1, source_target_pairs={{8,0},{9,1},{10,2},{11,3},{12,4},{13,5},{14,6},{15,7}} | collective-permute-start | bytes 983048 | tf_op jit(solution)/shard_map/ppermute | solution.py:28
  126.6 9.6 %copy-start = (bf16[4,32,1792]{2,1,0:T(8,128)(2,1)S(1)}, bf16[4,32,1792]{2,1,0:T(8,128)(2,1)}, u32[]{:S(2)}) copy-start(bf16[4,32,1792]{2,1,0:T(8,128)(2,1)} %get-tuple-element.433) | copy-start | bytes 1376260
  129.4 15.1 %collective-permute-start.23 = (bf16[32,5120]{1,0:T(8,128)(2,1)S(1)}, bf16[32,5120]{1,0:T(8,128)(2,1)S(1)}, u32[]{:S(2)}, u32[]{:S(2)}) collective-permute-start(bf16[32,5120]{1,0:T(8,128)(2,1)S(1)} %get-tuple-element.451), channel_id=1, source_target_pairs={{8,0},{9,1},{10,2},{11,3},{12,4},{13,5},{14,6},{15,7}} | collective-permute-start | bytes 983048 | tf_op jit(solution)/shard_map/ppermute | solution.py:28
  130.7 11.7 %collective-permute-start.24 = (bf16[2,32,2304]{2,1,0:T(8,128)(2,1)}, bf16[2,32,2304]{2,1,0:T(8,128)(2,1)S(1)}, u32[]{:S(2)}, u32[]{:S(2)}) collective-permute-start(bf16[2,32,2304]{2,1,0:T(8,128)(2,1)} %get-tuple-element.453), channel_id=1, source_target_pairs={{0,2},{1,3},{2,0},{3,1},{4,6},{5,7},{6,4},{7,5},{8,10},{9,11},{10,... | collective-permute-start | bytes 884744 | tf_op jit(solution)/shard_map/ppermute | solution.py:33
  133.6 10.7 %collective-permute-start.25 = (bf16[2,32,2304]{2,1,0:T(8,128)(2,1)}, bf16[2,32,2304]{2,1,0:T(8,128)(2,1)S(1)}, u32[]{:S(2)}, u32[]{:S(2)}) collective-permute-start(bf16[2,32,2304]{2,1,0:T(8,128)(2,1)} %get-tuple-element.454), channel_id=1, source_target_pairs={{0,4},{1,5},{2,6},{3,7},{4,0},{5,1},{6,2},{7,3},{8,12},{9,13},{10,... | collective-permute-start | bytes 884744 | tf_op jit(solution)/shard_map/ppermute | solution.py:33
  136.2 8.1 %collective-permute-start.26 = (bf16[2,32,2304]{2,1,0:T(8,128)(2,1)}, bf16[2,32,2304]{2,1,0:T(8,128)(2,1)S(1)}, u32[]{:S(2)}, u32[]{:S(2)}) collective-permute-start(bf16[2,32,2304]{2,1,0:T(8,128)(2,1)} %get-tuple-element.455), channel_id=1, source_target_pairs={{0,6},{1,7},{2,4},{3,5},{4,2},{5,3},{6,0},{7,1},{8,14},{9,15},{10,... | collective-permute-start | bytes 884744 | tf_op jit(solution)/shard_map/ppermute | solution.py:33
  138.9 26.5 %collective-permute-start.17 = (bf16[4,4,32,1792]{3,2,1,0:T(8,128)(2,1)S(1)}, bf16[4,4,32,1792]{3,2,1,0:T(8,128)(2,1)S(1)}, u32[]{:S(2)}, u32[]{:S(2)}) collective-permute-start(bf16[4,4,32,1792]{3,2,1,0:T(8,128)(2,1)S(1)} %pad_maximum_fusion.rest_0_), channel_id=1, source_target_pairs={{0,1},{1,0},{2,3},{3,2},{4,5},{5,4},{6,7},{7,6},{8,9},{9,8},{10,11... | collective-permute-start | bytes 5505032 | tf_op jit(solution)/shard_map/ppermute | solution.py:37
  144.4 7.1 %copy-start.7 = (bf16[1,32,2304]{2,1,0:T(8,128)(2,1)S(1)}, bf16[1,32,2304]{2,1,0:T(8,128)(2,1)}, u32[]{:S(2)}) copy-start(bf16[1,32,2304]{2,1,0:T(8,128)(2,1)} %get-tuple-element.444) | copy-start | bytes 442372
  144.4 9.6 %copy-start.8 = (bf16[1,32,2304]{2,1,0:T(8,128)(2,1)S(1)}, bf16[1,32,2304]{2,1,0:T(8,128)(2,1)}, u32[]{:S(2)}) copy-start(bf16[1,32,2304]{2,1,0:T(8,128)(2,1)} %get-tuple-element.445) | copy-start | bytes 442372
  144.4 14.1 %copy-start.9 = (bf16[1,32,2304]{2,1,0:T(8,128)(2,1)S(1)}, bf16[1,32,2304]{2,1,0:T(8,128)(2,1)}, u32[]{:S(2)}) copy-start(bf16[1,32,2304]{2,1,0:T(8,128)(2,1)} %get-tuple-element.446) | copy-start | bytes 442372
  144.4 15.2 %copy-start.4 = (bf16[2,32,2304]{2,1,0:T(8,128)(2,1)S(1)}, bf16[2,32,2304]{2,1,0:T(8,128)(2,1)}, u32[]{:S(2)}) copy-start(bf16[2,32,2304]{2,1,0:T(8,128)(2,1)} %get-tuple-element.470) | copy-start | bytes 884740
  148.0 16.6 %copy-start.6 = (bf16[1,32,2304]{2,1,0:T(8,128)(2,1)S(1)}, bf16[1,32,2304]{2,1,0:T(8,128)(2,1)}, u32[]{:S(2)}) copy-start(bf16[1,32,2304]{2,1,0:T(8,128)(2,1)} %get-tuple-element.447) | copy-start | bytes 442372
  148.0 6.1 %collective-permute-start.27 = (bf16[1,32,2304]{2,1,0:T(8,128)(2,1)}, bf16[1,32,2304]{2,1,0:T(8,128)(2,1)S(1)}, u32[]{:S(2)}, u32[]{:S(2)}) collective-permute-start(bf16[1,32,2304]{2,1,0:T(8,128)(2,1)} %get-tuple-element.463), channel_id=1, source_target_pairs={{0,2},{1,3},{2,0},{3,1},{4,6},{5,7},{6,4},{7,5},{8,10},{9,11},{10,... | collective-permute-start | bytes 442376 | tf_op jit(solution)/shard_map/ppermute | solution.py:33
  149.4 9.2 %collective-permute-start.28 = (bf16[1,32,2304]{2,1,0:T(8,128)(2,1)}, bf16[1,32,2304]{2,1,0:T(8,128)(2,1)S(1)}, u32[]{:S(2)}, u32[]{:S(2)}) collective-permute-start(bf16[1,32,2304]{2,1,0:T(8,128)(2,1)} %get-tuple-element.464), channel_id=1, source_target_pairs={{0,4},{1,5},{2,6},{3,7},{4,0},{5,1},{6,2},{7,3},{8,12},{9,13},{10,... | collective-permute-start | bytes 442376 | tf_op jit(solution)/shard_map/ppermute | solution.py:33
  151.1 8.7 %collective-permute-start.29 = (bf16[1,32,2304]{2,1,0:T(8,128)(2,1)}, bf16[1,32,2304]{2,1,0:T(8,128)(2,1)S(1)}, u32[]{:S(2)}, u32[]{:S(2)}) collective-permute-start(bf16[1,32,2304]{2,1,0:T(8,128)(2,1)} %get-tuple-element.465), channel_id=1, source_target_pairs={{0,6},{1,7},{2,4},{3,5},{4,2},{5,3},{6,0},{7,1},{8,14},{9,15},{10,... | collective-permute-start | bytes 442376 | tf_op jit(solution)/shard_map/ppermute | solution.py:33
  151.5 8.5 %collective-permute-start.19 = (bf16[1,32,2304]{2,1,0:T(8,128)(2,1)S(1)}, bf16[1,32,2304]{2,1,0:T(8,128)(2,1)S(1)}, u32[]{:S(2)}, u32[]{:S(2)}) collective-permute-start(bf16[1,32,2304]{2,1,0:T(8,128)(2,1)S(1)} %copy-done.7), channel_id=1, source_target_pairs={{0,2},{1,3},{2,0},{3,1},{4,6},{5,7},{6,4},{7,5},{8,10},{9,11},{10,... | collective-permute-start | bytes 442376 | tf_op jit(solution)/shard_map/ppermute | solution.py:33
  154.1 8.0 %collective-permute-start.20 = (bf16[1,32,2304]{2,1,0:T(8,128)(2,1)S(1)}, bf16[1,32,2304]{2,1,0:T(8,128)(2,1)S(1)}, u32[]{:S(2)}, u32[]{:S(2)}) collective-permute-start(bf16[1,32,2304]{2,1,0:T(8,128)(2,1)S(1)} %copy-done.8), channel_id=1, source_target_pairs={{0,4},{1,5},{2,6},{3,7},{4,0},{5,1},{6,2},{7,3},{8,12},{9,13},{10,... | collective-permute-start | bytes 442376 | tf_op jit(solution)/shard_map/ppermute | solution.py:33
  158.5 6.0 %collective-permute-start.21 = (bf16[1,32,2304]{2,1,0:T(8,128)(2,1)S(1)}, bf16[1,32,2304]{2,1,0:T(8,128)(2,1)S(1)}, u32[]{:S(2)}, u32[]{:S(2)}) collective-permute-start(bf16[1,32,2304]{2,1,0:T(8,128)(2,1)S(1)} %copy-done.9), channel_id=1, source_target_pairs={{0,6},{1,7},{2,4},{3,5},{4,2},{5,3},{6,0},{7,1},{8,14},{9,15},{10,... | collective-permute-start | bytes 442376 | tf_op jit(solution)/shard_map/ppermute | solution.py:33
  159.6 5.1 %copy-start.5 = (bf16[1,32,2304]{2,1,0:T(8,128)(2,1)S(1)}, bf16[1,32,2304]{2,1,0:T(8,128)(2,1)}, u32[]{:S(2)}) copy-start(bf16[1,32,2304]{2,1,0:T(8,128)(2,1)} %get-tuple-element.466) | copy-start | bytes 442372
  159.8 5.6 %collective-permute-start.31 = (bf16[4,2,32,2304]{3,2,1,0:T(8,128)(2,1)S(1)}, bf16[4,2,32,2304]{3,2,1,0:T(8,128)(2,1)S(1)}, u32[]{:S(2)}, u32[]{:S(2)}) collective-permute-start(bf16[4,2,32,2304]{3,2,1,0:T(8,128)(2,1)S(1)} %pad_maximum_fusion.1.rest_2_), channel_id=1, source_target_pairs={{0,1},{1,0},{2,3},{3,2},{4,5},{5,4},{6,7},{7,6},{8,9},{9,8},{10,11... | collective-permute-start | bytes 3538952 | tf_op jit(solution)/shard_map/ppermute | solution.py:37
  164.6 2.4 %collective-permute-start.22 = (bf16[4,1,32,2304]{3,2,1,0:T(8,128)(2,1)S(1)}, bf16[4,1,32,2304]{3,2,1,0:T(8,128)(2,1)S(1)}, u32[]{:S(2)}, u32[]{:S(2)}) collective-permute-start(bf16[4,1,32,2304]{3,2,1,0:T(8,128)(2,1)S(1)} %pad_maximum_fusion.2.rest_2_), channel_id=1, source_target_pairs={{0,1},{1,0},{2,3},{3,2},{4,5},{5,4},{6,7},{7,6},{8,9},{9,8},{10,11... | collective-permute-start | bytes 1769480 | tf_op jit(solution)/shard_map/ppermute | solution.py:37
  164.8 2.7 %collective-permute-start.30 = (bf16[4,1,32,2304]{3,2,1,0:T(8,128)(2,1)S(1)}, bf16[4,1,32,2304]{3,2,1,0:T(8,128)(2,1)S(1)}, u32[]{:S(2)}, u32[]{:S(2)}) collective-permute-start(bf16[4,1,32,2304]{3,2,1,0:T(8,128)(2,1)S(1)} %pad_maximum_fusion.3.rest_4_), channel_id=1, source_target_pairs={{0,1},{1,0},{2,3},{3,2},{4,5},{5,4},{6,7},{7,6},{8,9},{9,8},{10,11... | collective-permute-start | bytes 1769480 | tf_op jit(solution)/shard_map/ppermute | solution.py:37

commit v7 on v6

--- a/solution.py
+++ b/solution.py
@@ -556,19 +556,21 @@
     for tick in range(1, ticks):
         args = (incoming[tick], w_score, wk, wv, cosine, sine, mask, ends, target)
         count = len(held)
-        *held, produced = pl.pallas_call(
+        sends = tick < ticks - 2
+        outs = pl.pallas_call(
             functools.partial(forward_kernel, tick, sections, micro, chips),
-            out_shape=state + [send_forward] * chips + [row],
+            out_shape=state + [send_forward] * chips + [row] * sends,
             in_specs=[VMEM] * (len(args) + len(state)) + [HBM] * chips,
-            out_specs=[VMEM] * len(state) + [HBM] * chips + [VMEM],
+            out_specs=[VMEM] * len(state) + [HBM] * chips + [VMEM] * sends,
             input_output_aliases={len(args) + n: n for n in range(count)},
-            scratch_shapes=forward_scratch,
+            scratch_shapes=[pltpu.VMEM(row.shape, row.dtype)] * (not sends) + forward_scratch,
             compiler_params=params(),
             cost_estimate=cost,
             name="forward",
         )(*args, *held)
-        if tick < ticks - 2:
-            incoming.append(shifted(produced, 1, senders(tick, up)))
+        held = list(outs[:count])
+        if sends:
+            incoming.append(shifted(outs[-1], 1, senders(tick, up)))
 
     saved, keys, values, probs, scales, grads, *sent = held
     incoming = [empty] * 2
@@ -587,15 +589,17 @@
         )
         targets = [block for n in filled for block in blocks[n]]
         shapes = [send_backward[n] for n in filled for _ in range(chips)]
+        sends = tick < ticks - 2
         token_value, *outs = pl.pallas_call(
             functools.partial(
                 backward_kernel, tick, sections, micro, chips, [groups[n] for n in filled]
             ),
-            out_shape=[token] + shapes + [row],
+            out_shape=[token] + shapes + [row] * sends,
             in_specs=[VMEM] * len(args) + [HBM] * len(targets),
-            out_specs=[VMEM] + [HBM] * len(targets) + [VMEM],
+            out_specs=[VMEM] + [HBM] * len(targets) + [VMEM] * sends,
             input_output_aliases={len(args) - 1 + n: n for n in range(1 + len(targets))},
-            scratch_shapes=[
+            scratch_shapes=[pltpu.VMEM(row.shape, row.dtype)] * (not sends)
+            + [
                 pltpu.VMEM((width, features), F32),
                 pltpu.VMEM((width, model), F32),
                 pltpu.VMEM((width, model), BF16),
@@ -609,7 +613,7 @@
         )(*args, *targets)
         for position, n in enumerate(filled):
             blocks[n] = outs[position * chips : (position + 1) * chips]
-        if tick < ticks - 2:
+        if sends:
             incoming.append(shifted(outs[-1], -1, senders(tick, down)))
 
         def both_cores(parts, token_value):

time: 172 us -> 171 us (level)
  waiting for transfers between devices: 88.5 us -> 91.7 us
  Pallas kernels: 42.2 us -> 39.2 us
    ppermute x12, waiting for transfers between devices: 10.2 us -> 12.7 us  [between_chips(): return lax.ppermute(value, 'dp', pairs)]
  transfers between devices with their start and end apart: 32 -> 32, of which waited for: 13 -> 13; matrix products, arithmetic and copies ran while one was open for 0% -> 0% of each run, Pallas kernels for 18% -> 17%
where the time goes in v7:
time: 171 us; the launch traced here: 170 us
  waiting for transfers between devices  91.7 us (54%)
  Pallas kernels  39.2 us (23%)
  starting transfers between devices  36.5 us (21%)
    ppermute x16, waiting for transfers between devices, shifted(): lax.ppermute(value, 'section', [(source, source + steps) for source in se...  78.5 us
    ppermute x16, starting transfers between devices, shifted(): lax.ppermute(value, 'section', [(source, source + steps) for source in se...  19.7 us
    ppermute x12, starting transfers between devices, between_chips(): return lax.ppermute(value, 'dp', pairs)  16.1 us
    pallas_call x9, Pallas kernels, shards(): pl.pallas_call(functools.partial(forward_kernel, tick, sections, micro, c...  15 us
    ppermute x12, waiting for transfers between devices, between_chips(): return lax.ppermute(value, 'dp', pairs)  12.7 us
    pallas_call x10, Pallas kernels, shards(): pl.pallas_call(functools.partial(backward_kernel, tick, sections, micro,...  11.7 us
    pallas_call x1, Pallas kernels, shards(): pl.pallas_call(functools.partial(first_kernel, sections, micro, chips), o...  8.46 us
    pallas_call x2, Pallas kernels, shards(): pl.pallas_call(functools.partial(gather_kernel, chosen, share, wide, feat...  4.08 us
  transfers between devices with their start and end apart: 32, of which 13 were waited for; matrix products, arithmetic and copies ran while one was open for 0% of the time, Pallas kernels for 17%

profile of v7, /device:TPU:0, one launch (start us, length us, event | category | flops | bytes accessed | tf_op | source)
XLA Modules:
  0.0 169.5 jit_solution(18357889617938746319)
XLA Ops:
  0.6 8.5 %first.1 = (f32[1,5120]{1,0:T(1,128)S(1)}, bf16[5120,512]{1,0:T(8,128)(2,1)S(1)}, bf16[5120,512]{1,0:T(8,128)(2,1)S(1)}, f32[4,32,128]{2,1,0:T(8,128)S(1)}, f32[...) custom-call(bf16[5120,512]{1,0:T(8,128)(2,1)} %bitcast.24, ...), custom_call_target="tpu_custom_call" | custom-call | tf_op jit(solution)/shard_map/first/pallas_call | solution.py:521
  9.1 1.3 collective-permute-start.1
  10.4 4.9 %forward.9 = (bf16[4,32,5120]{2,1,0:T(8,128)(2,1)S(1)}, bf16[4,32,512]{2,1,0:T(8,128)(2,1)S(1)}, bf16[4,32,512]{2,1,0:T(8,128)(2,1)S(1)}, f32[4,128,32]{2,1,0:T(...) custom-call(bf16[32,5120]{1,0:T(8,128)(2,1)S(1)} %broadcast_in_dim.9, ...), custom_call_target="tpu_custom_call", output_to_operand_aliasing={{0}: (9, {}), {1}: (10, {}), {2}: (11, {}), {3}: (12, {}), ... | custom-call | flops 1000000 | bytes 1000000 | tf_op jit(solution)/shard_map/forward/pallas_call | solution.py:560
  15.3 1.3 collective-permute-start
  16.7 1.8 %collective-permute-done.1.incoming = bf16[32,5120]{1,0:T(8,128)(2,1)S(1)} collective-permute-done((bf16[32,5120]{1,0:T(8,128)(2,1)S(1)}, bf16[32,5120]{1,0:T(8,128)(2,1)S(1)}, u32[]{:S(2)}, u32[]{:S(2)}) %collective-permute-start.1) | collective-permute-done | bytes 327712 | tf_op jit(solution)/shard_map/ppermute | solution.py:28
  18.5 4.8 %forward.10 = (bf16[4,32,5120]{2,1,0:T(8,128)(2,1)S(1)}, bf16[4,32,512]{2,1,0:T(8,128)(2,1)S(1)}, bf16[4,32,512]{2,1,0:T(8,128)(2,1)S(1)}, f32[4,128,32]{2,1,0:T...) custom-call(bf16[32,5120]{1,0:T(8,128)(2,1)S(1)} %collective-permute, ...), custom_call_target="tpu_custom_call", output_to_operand_aliasing={{0}: (9, {}), {1}: (10, {}), {2}: (11, {}), {3}: (12, {}), ... | custom-call | flops 1000000 | bytes 1000000 | tf_op jit(solution)/shard_map/forward/pallas_call | solution.py:560
  23.3 4.4 %collective-permute-start.3 = (bf16[32,5120]{1,0:T(8,128)(2,1)S(1)}, bf16[32,5120]{1,0:T(8,128)(2,1)S(1)}, u32[]{:S(2)}, u32[]{:S(2)}) collective-permute-start(bf16[32,5120]{1,0:T(8,128)(2,1)S(1)} %get-tuple-element.281), channel_id=1, source_target_pairs={{0,8},{8,16},{1,9},{9,17},{2,10},{10,18},{3,11},{11,19},{4,12},{12... | collective-permute-start | bytes 983048 | tf_op jit(solution)/shard_map/ppermute | solution.py:28
  27.8 4.9 %forward.11 = (bf16[4,32,5120]{2,1,0:T(8,128)(2,1)S(1)}, bf16[4,32,512]{2,1,0:T(8,128)(2,1)S(1)}, bf16[4,32,512]{2,1,0:T(8,128)(2,1)S(1)}, f32[4,128,32]{2,1,0:T...) custom-call(bf16[32,5120]{1,0:T(8,128)(2,1)S(1)} %collective-permute, ...), custom_call_target="tpu_custom_call", output_to_operand_aliasing={{0}: (9, {}), {1}: (10, {}), {2}: (11, {}), {3}: (12, {}), ... | custom-call | flops 1000000 | bytes 1000000 | tf_op jit(solution)/shard_map/forward/pallas_call | solution.py:560
  32.7 1.9 %collective-permute-start.2 = (bf16[32,5120]{1,0:T(8,128)(2,1)S(1)}, bf16[32,5120]{1,0:T(8,128)(2,1)S(1)}, u32[]{:S(2)}, u32[]{:S(2)}) collective-permute-start(bf16[32,5120]{1,0:T(8,128)(2,1)S(1)} %get-tuple-element.280), channel_id=1, source_target_pairs={{0,8},{8,16},{1,9},{9,17},{2,10},{10,18},{3,11},{11,19},{4,12},{12... | collective-permute-start | bytes 983048 | tf_op jit(solution)/shard_map/ppermute | solution.py:28
  34.7 0.7 collective-permute-start.5
  35.4 6.1 %collective-permute-done.2.incoming = bf16[32,5120]{1,0:T(8,128)(2,1)S(1)} collective-permute-done((bf16[32,5120]{1,0:T(8,128)(2,1)S(1)}, bf16[32,5120]{1,0:T(8,128)(2,1)S(1)}, u32[]{:S(2)}, u32[]{:S(2)}) %collective-permute-start.2) | collective-permute-done | bytes 327712 | tf_op jit(solution)/shard_map/ppermute | solution.py:28
  41.6 0.7 collective-permute-start.4
  42.4 0.7 collective-permute-start.7
  43.1 0.7 collective-permute-start.6
  44.1 0.7 collective-permute-start.9
  45.0 0.7 collective-permute-start.12
  45.8 0.7 collective-permute-start.14
  46.6 0.8 collective-permute-start.13
  47.5 1.9 %collective-permute-start.8 = (bf16[4,32,1792]{2,1,0:T(8,128)(2,1)S(1)}, bf16[4,32,1792]{2,1,0:T(8,128)(2,1)S(1)}, u32[]{:S(2)}, u32[]{:S(2)}) collective-permute-start(bf16[4,32,1792]{2,1,0:T(8,128)(2,1)S(1)} %copy-done.1), channel_id=1, source_target_pairs={{0,2},{1,3},{2,0},{3,1},{4,6},{5,7},{6,4},{7,5},{8,10},{9,11},{10,... | collective-permute-start | bytes 1376264 | tf_op jit(solution)/shard_map/ppermute | solution.py:33
  49.4 1.5 collective-permute-start.11
  51.1 1.3 collective-permute-start.16
  52.5 1.3 collective-permute-start.15
  53.8 64.9 %collective-permute-done.16.incoming = bf16[32,5120]{1,0:T(8,128)(2,1)S(1)} collective-permute-done((bf16[32,5120]{1,0:T(8,128)(2,1)S(1)}, bf16[32,5120]{1,0:T(8,128)(2,1)S(1)}, u32[]{:S(2)}, u32[]{:S(2)}) %collective-permute-start.16) | collective-permute-done | bytes 327712 | tf_op jit(solution)/shard_map/ppermute | solution.py:28
  118.7 2.8 %backward.16 = (f32[8,128]{1,0:T(8,128)S(1)}, bf16[2,32,2304]{2,1,0:T(8,128)(2,1)}, bf16[2,32,2304]{2,1,0:T(8,128)(2,1)}, bf16[2,32,2304]{2,1,0:T(8,128)(2,1)}, ...) custom-call(bf16[32,5120]{1,0:T(8,128)(2,1)S(1)} %collective-permute, ...), custom_call_target="tpu_custom_call", output_to_operand_aliasing={{0}: (11, {}), {1}: (12, {}), {2}: (13, {}), {3}: (14, {}),... | custom-call | flops 1000000 | bytes 1000000 | tf_op jit(solution)/shard_map/backward/pallas_call | solution.py:593
  121.5 1.3 collective-permute-start.18
  122.8 3.1 %collective-permute-done.15.incoming = bf16[32,5120]{1,0:T(8,128)(2,1)S(1)} collective-permute-done((bf16[32,5120]{1,0:T(8,128)(2,1)S(1)}, bf16[32,5120]{1,0:T(8,128)(2,1)S(1)}, u32[]{:S(2)}, u32[]{:S(2)}) %collective-permute-start.15) | collective-permute-done | bytes 327712 | tf_op jit(solution)/shard_map/ppermute | solution.py:28
  125.9 2.8 %backward.17 = (f32[8,128]{1,0:T(8,128)S(1)}, bf16[2,32,2304]{2,1,0:T(8,128)(2,1)}, bf16[2,32,2304]{2,1,0:T(8,128)(2,1)}, bf16[2,32,2304]{2,1,0:T(8,128)(2,1)}, ...) custom-call(bf16[32,5120]{1,0:T(8,128)(2,1)S(1)} %collective-permute, ...), custom_call_target="tpu_custom_call", output_to_operand_aliasing={{0}: (11, {}), {1}: (12, {}), {2}: (13, {}), {3}: (14, {}),... | custom-call | flops 1000000 | bytes 1000000 | tf_op jit(solution)/shard_map/backward/pallas_call | solution.py:593
  128.7 1.3 collective-permute-start.23
  130.0 2.9 %collective-permute-start.24 = (bf16[2,32,2304]{2,1,0:T(8,128)(2,1)}, bf16[2,32,2304]{2,1,0:T(8,128)(2,1)S(1)}, u32[]{:S(2)}, u32[]{:S(2)}) collective-permute-start(bf16[2,32,2304]{2,1,0:T(8,128)(2,1)} %get-tuple-element.453), channel_id=1, source_target_pairs={{0,2},{1,3},{2,0},{3,1},{4,6},{5,7},{6,4},{7,5},{8,10},{9,11},{10,... | collective-permute-start | bytes 884744 | tf_op jit(solution)/shard_map/ppermute | solution.py:33
  132.9 2.6 %collective-permute-start.25 = (bf16[2,32,2304]{2,1,0:T(8,128)(2,1)}, bf16[2,32,2304]{2,1,0:T(8,128)(2,1)S(1)}, u32[]{:S(2)}, u32[]{:S(2)}) collective-permute-start(bf16[2,32,2304]{2,1,0:T(8,128)(2,1)} %get-tuple-element.454), channel_id=1, source_target_pairs={{0,4},{1,5},{2,6},{3,7},{4,0},{5,1},{6,2},{7,3},{8,12},{9,13},{10,... | collective-permute-start | bytes 884744 | tf_op jit(solution)/shard_map/ppermute | solution.py:33
  135.8 2.4 %collective-permute-done.18.incoming = bf16[32,5120]{1,0:T(8,128)(2,1)S(1)} collective-permute-done((bf16[32,5120]{1,0:T(8,128)(2,1)S(1)}, bf16[32,5120]{1,0:T(8,128)(2,1)S(1)}, u32[]{:S(2)}, u32[]{:S(2)}) %collective-permute-start.18) | collective-permute-done | bytes 327712 | tf_op jit(solution)/shard_map/ppermute | solution.py:28
  138.2 2.8 %backward.18 = (f32[8,128]{1,0:T(8,128)S(1)}, bf16[1,32,2304]{2,1,0:T(8,128)(2,1)}, bf16[1,32,2304]{2,1,0:T(8,128)(2,1)}, bf16[1,32,2304]{2,1,0:T(8,128)(2,1)}, bf16[1,32,2304]{2,1,0:T(8,128)(2,1)}) custom-call(bf16[32,5120]{1,0:T(8,128)(2,1)S(1)} %collective-permute-done.18.incoming, ...), custom_call_target="tpu_custom_call", output_to_operand_aliasing={{0}: (11, {}), {1}: (12, {}), {2}: (13, {}), {3}: (14, {}),... | custom-call | flops 1000000 | bytes 1000000 | tf_op jit(solution)/shard_map/backward/pallas_call | solution.py:593
  140.9 2.7 %collective-permute-done.25 = bf16[2,32,2304]{2,1,0:T(8,128)(2,1)S(1)} collective-permute-done((bf16[2,32,2304]{2,1,0:T(8,128)(2,1)}, bf16[2,32,2304]{2,1,0:T(8,128)(2,1)S(1)}, u32[]{:S(2)}, u32[]{:S(2)}) %collective-permute-start.25) | collective-permute-done | bytes 294944 | tf_op jit(solution)/shard_map/ppermute | solution.py:33
  143.7 2.8 %backward.19 = (f32[8,128]{1,0:T(8,128)S(1)}, bf16[1,32,2304]{2,1,0:T(8,128)(2,1)}, bf16[1,32,2304]{2,1,0:T(8,128)(2,1)}, bf16[1,32,2304]{2,1,0:T(8,128)(2,1)}, bf16[1,32,2304]{2,1,0:T(8,128)(2,1)}) custom-call(bf16[32,5120]{1,0:T(8,128)(2,1)S(1)} %collective-permute-done.23.incoming, ...), custom_call_target="tpu_custom_call", output_to_operand_aliasing={{0}: (11, {}), {1}: (12, {}), {2}: (13, {}), {3}: (14, {}),... | custom-call | flops 1000000 | bytes 1000000 | tf_op jit(solution)/shard_map/backward/pallas_call | solution.py:593
  146.5 1.4 collective-permute-start.27
  147.9 1.7 collective-permute-start.28
  149.6 0.4 collective-permute-start.29
  150.1 1.4 collective-permute-start.19
  151.4 1.9 %collective-permute-done.27 = bf16[1,32,2304]{2,1,0:T(8,128)(2,1)S(1)} collective-permute-done((bf16[1,32,2304]{2,1,0:T(8,128)(2,1)}, bf16[1,32,2304]{2,1,0:T(8,128)(2,1)S(1)}, u32[]{:S(2)}, u32[]{:S(2)}) %collective-permute-start.27) | collective-permute-done | bytes 147488 | tf_op jit(solution)/shard_map/ppermute | solution.py:33
  153.3 2.1 %collective-permute-start.20 = (bf16[1,32,2304]{2,1,0:T(8,128)(2,1)S(1)}, bf16[1,32,2304]{2,1,0:T(8,128)(2,1)S(1)}, u32[]{:S(2)}, u32[]{:S(2)}) collective-permute-start(bf16[1,32,2304]{2,1,0:T(8,128)(2,1)S(1)} %copy-done.8), channel_id=1, source_target_pairs={{0,4},{1,5},{2,6},{3,7},{4,0},{5,1},{6,2},{7,3},{8,12},{9,13},{10,... | collective-permute-start | bytes 442376 | tf_op jit(solution)/shard_map/ppermute | solution.py:33
  155.4 2.4 %collective-permute-done.28 = bf16[1,32,2304]{2,1,0:T(8,128)(2,1)S(1)} collective-permute-done((bf16[1,32,2304]{2,1,0:T(8,128)(2,1)}, bf16[1,32,2304]{2,1,0:T(8,128)(2,1)S(1)}, u32[]{:S(2)}, u32[]{:S(2)}) %collective-permute-start.28) | collective-permute-done | bytes 147488 | tf_op jit(solution)/shard_map/ppermute | solution.py:33
  158.1 1.5 collective-permute-done.19
  159.6 1.6 collective-permute-done.20
  161.2 2.7 %collective-permute-done.21 = bf16[1,32,2304]{2,1,0:T(8,128)(2,1)S(1)} collective-permute-done((bf16[1,32,2304]{2,1,0:T(8,128)(2,1)S(1)}, bf16[1,32,2304]{2,1,0:T(8,128)(2,1)S(1)}, u32[]{:S(2)}, u32[]{:S(2)}) %collective-permute-start.21) | collective-permute-done | bytes 147488 | tf_op jit(solution)/shard_map/ppermute | solution.py:33
  164.2 0.5 collective-permute-start.30
  164.7 1.6 gathered.2
  166.4 0.5 collective-permute-done.30.rest_5_
  166.9 2.5 %gathered.3 = (f32[640,512]{1,0:T(8,128)}, f32[640,512]{1,0:T(8,128)}) custom-call(bf16[4,4,32,1792]{3,2,1,0:T(8,128)(2,1)S(1)} %pad_maximum_fusion.rest_0_, bf16[4,4,32,1792]{3,2,1,0:T(8,128)(2,1)S(1)} %collective-permute-done.17.rest_1_, bf16[4,1,32,2304]{3,2,1,0:T(8,128)(2,1)S(1)} %pad_maximum_fusion.2.rest_2_, ...), custom_call_target="tpu_custom_call" | custom-call | flops 1000000 | bytes 1000000 | tf_op jit(solution)/shard_map/gathered/pallas_call | solution.py:642
  (63 shorter events, 2.1 us)
Async XLA Ops:
  9.1 9.4 %collective-permute-start.1 = (bf16[32,5120]{1,0:T(8,128)(2,1)S(1)}, bf16[32,5120]{1,0:T(8,128)(2,1)S(1)}, u32[]{:S(2)}, u32[]{:S(2)}) collective-permute-start(bf16[32,5120]{1,0:T(8,128)(2,1)S(1)} %get-tuple-element.259), channel_id=1, source_target_pairs={{0,8},{1,9},{2,10},{3,11},{4,12},{5,13},{6,14},{7,15}} | collective-permute-start | bytes 983048 | tf_op jit(solution)/shard_map/ppermute | solution.py:28
  15.3 12.4 %collective-permute-start = (bf16[32,5120]{1,0:T(8,128)(2,1)S(1)}, bf16[32,5120]{1,0:T(8,128)(2,1)S(1)}, u32[]{:S(2)}, u32[]{:S(2)}) collective-permute-start(bf16[32,5120]{1,0:T(8,128)(2,1)S(1)} %get-tuple-element.258), channel_id=1, source_target_pairs={{0,8},{1,9},{2,10},{3,11},{4,12},{5,13},{6,14},{7,15}} | collective-permute-start | bytes 983048 | tf_op jit(solution)/shard_map/ppermute | solution.py:28
  23.3 11.3 %collective-permute-start.3 = (bf16[32,5120]{1,0:T(8,128)(2,1)S(1)}, bf16[32,5120]{1,0:T(8,128)(2,1)S(1)}, u32[]{:S(2)}, u32[]{:S(2)}) collective-permute-start(bf16[32,5120]{1,0:T(8,128)(2,1)S(1)} %get-tuple-element.281), channel_id=1, source_target_pairs={{0,8},{8,16},{1,9},{9,17},{2,10},{10,18},{3,11},{11,19},{4,12},{12... | collective-permute-start | bytes 983048 | tf_op jit(solution)/shard_map/ppermute | solution.py:28
  32.7 8.9 %collective-permute-start.2 = (bf16[32,5120]{1,0:T(8,128)(2,1)S(1)}, bf16[32,5120]{1,0:T(8,128)(2,1)S(1)}, u32[]{:S(2)}, u32[]{:S(2)}) collective-permute-start(bf16[32,5120]{1,0:T(8,128)(2,1)S(1)} %get-tuple-element.280), channel_id=1, source_target_pairs={{0,8},{8,16},{1,9},{9,17},{2,10},{10,18},{3,11},{11,19},{4,12},{12... | collective-permute-start | bytes 983048 | tf_op jit(solution)/shard_map/ppermute | solution.py:28
  34.7 7.5 %collective-permute-start.5 = (bf16[32,5120]{1,0:T(8,128)(2,1)S(1)}, bf16[32,5120]{1,0:T(8,128)(2,1)S(1)}, u32[]{:S(2)}, u32[]{:S(2)}) collective-permute-start(bf16[32,5120]{1,0:T(8,128)(2,1)S(1)} %get-tuple-element.303), channel_id=1, source_target_pairs={{8,16},{16,24},{9,17},{17,25},{10,18},{18,26},{11,19},{19,27},{12,... | collective-permute-start | bytes 983048 | tf_op jit(solution)/shard_map/ppermute | solution.py:28
  41.6 1.5 collective-permute-start.4
  42.4 1.5 collective-permute-start.7
  43.1 0.8 collective-permute-start.6
  44.1 1.6 collective-permute-start.9
  45.0 1.5 collective-permute-start.12
  45.8 5.2 %collective-permute-start.14 = (bf16[32,5120]{1,0:T(8,128)(2,1)S(1)}, bf16[32,5120]{1,0:T(8,128)(2,1)S(1)}, u32[]{:S(2)}, u32[]{:S(2)}) collective-permute-start(bf16[32,5120]{1,0:T(8,128)(2,1)S(1)} %get-tuple-element.393), channel_id=1, source_target_pairs={{16,8},{24,16},{17,9},{25,17},{18,10},{26,18},{19,11},{27,19},{20,... | collective-permute-start | bytes 983048 | tf_op jit(solution)/shard_map/ppermute | solution.py:28
  46.5 1.0 copy-start.1
  46.5 2.9 %copy-start.3 = (bf16[4,32,1792]{2,1,0:T(8,128)(2,1)S(1)}, bf16[4,32,1792]{2,1,0:T(8,128)(2,1)}, u32[]{:S(2)}) copy-start(bf16[4,32,1792]{2,1,0:T(8,128)(2,1)} %get-tuple-element.381) | copy-start | bytes 1376260
  46.5 4.3 %copy-start.2 = (bf16[4,32,1792]{2,1,0:T(8,128)(2,1)S(1)}, bf16[4,32,1792]{2,1,0:T(8,128)(2,1)}, u32[]{:S(2)}) copy-start(bf16[4,32,1792]{2,1,0:T(8,128)(2,1)} %get-tuple-element.380) | copy-start | bytes 1376260
  46.6 5.7 %collective-permute-start.13 = (bf16[32,5120]{1,0:T(8,128)(2,1)S(1)}, bf16[32,5120]{1,0:T(8,128)(2,1)S(1)}, u32[]{:S(2)}, u32[]{:S(2)}) collective-permute-start(bf16[32,5120]{1,0:T(8,128)(2,1)S(1)} %get-tuple-element.392), channel_id=1, source_target_pairs={{16,8},{24,16},{17,9},{25,17},{18,10},{26,18},{19,11},{27,19},{20,... | collective-permute-start | bytes 983048 | tf_op jit(solution)/shard_map/ppermute | solution.py:28
  47.5 82.5 %collective-permute-start.8 = (bf16[4,32,1792]{2,1,0:T(8,128)(2,1)S(1)}, bf16[4,32,1792]{2,1,0:T(8,128)(2,1)S(1)}, u32[]{:S(2)}, u32[]{:S(2)}) collective-permute-start(bf16[4,32,1792]{2,1,0:T(8,128)(2,1)S(1)} %copy-done.1), channel_id=1, source_target_pairs={{0,2},{1,3},{2,0},{3,1},{4,6},{5,7},{6,4},{7,5},{8,10},{9,11},{10,... | collective-permute-start | bytes 1376264 | tf_op jit(solution)/shard_map/ppermute | solution.py:33
  49.4 83.5 %collective-permute-start.11 = (bf16[4,32,1792]{2,1,0:T(8,128)(2,1)S(1)}, bf16[4,32,1792]{2,1,0:T(8,128)(2,1)S(1)}, u32[]{:S(2)}, u32[]{:S(2)}) collective-permute-start(bf16[4,32,1792]{2,1,0:T(8,128)(2,1)S(1)} %copy-done.3), channel_id=1, source_target_pairs={{0,6},{1,7},{2,4},{3,5},{4,2},{5,3},{6,0},{7,1},{8,14},{9,15},{10,... | collective-permute-start | bytes 1376264 | tf_op jit(solution)/shard_map/ppermute | solution.py:33
  50.9 84.7 %collective-permute-start.10 = (bf16[4,32,1792]{2,1,0:T(8,128)(2,1)S(1)}, bf16[4,32,1792]{2,1,0:T(8,128)(2,1)S(1)}, u32[]{:S(2)}, u32[]{:S(2)}) collective-permute-start(bf16[4,32,1792]{2,1,0:T(8,128)(2,1)S(1)} %copy-done.2), channel_id=1, source_target_pairs={{0,4},{1,5},{2,6},{3,7},{4,0},{5,1},{6,2},{7,3},{8,12},{9,13},{10,... | collective-permute-start | bytes 1376264 | tf_op jit(solution)/shard_map/ppermute | solution.py:33
  51.1 67.6 %collective-permute-start.16 = (bf16[32,5120]{1,0:T(8,128)(2,1)S(1)}, bf16[32,5120]{1,0:T(8,128)(2,1)S(1)}, u32[]{:S(2)}, u32[]{:S(2)}) collective-permute-start(bf16[32,5120]{1,0:T(8,128)(2,1)S(1)} %get-tuple-element.413), channel_id=1, source_target_pairs={{8,0},{16,8},{9,1},{17,9},{10,2},{18,10},{11,3},{19,11},{12,4},{20... | collective-permute-start | bytes 983048 | tf_op jit(solution)/shard_map/ppermute | solution.py:28
  52.5 73.4 %collective-permute-start.15 = (bf16[32,5120]{1,0:T(8,128)(2,1)S(1)}, bf16[32,5120]{1,0:T(8,128)(2,1)S(1)}, u32[]{:S(2)}, u32[]{:S(2)}) collective-permute-start(bf16[32,5120]{1,0:T(8,128)(2,1)S(1)} %get-tuple-element.412), channel_id=1, source_target_pairs={{8,0},{16,8},{9,1},{17,9},{10,2},{18,10},{11,3},{19,11},{12,4},{20... | collective-permute-start | bytes 983048 | tf_op jit(solution)/shard_map/ppermute | solution.py:28
  121.5 16.7 %collective-permute-start.18 = (bf16[32,5120]{1,0:T(8,128)(2,1)S(1)}, bf16[32,5120]{1,0:T(8,128)(2,1)S(1)}, u32[]{:S(2)}, u32[]{:S(2)}) collective-permute-start(bf16[32,5120]{1,0:T(8,128)(2,1)S(1)} %get-tuple-element.437), channel_id=1, source_target_pairs={{8,0},{9,1},{10,2},{11,3},{12,4},{13,5},{14,6},{15,7}} | collective-permute-start | bytes 983048 | tf_op jit(solution)/shard_map/ppermute | solution.py:28
  125.8 9.7 %copy-start = (bf16[4,32,1792]{2,1,0:T(8,128)(2,1)S(1)}, bf16[4,32,1792]{2,1,0:T(8,128)(2,1)}, u32[]{:S(2)}) copy-start(bf16[4,32,1792]{2,1,0:T(8,128)(2,1)} %get-tuple-element.433) | copy-start | bytes 1376260
  128.7 15.0 %collective-permute-start.23 = (bf16[32,5120]{1,0:T(8,128)(2,1)S(1)}, bf16[32,5120]{1,0:T(8,128)(2,1)S(1)}, u32[]{:S(2)}, u32[]{:S(2)}) collective-permute-start(bf16[32,5120]{1,0:T(8,128)(2,1)S(1)} %get-tuple-element.451), channel_id=1, source_target_pairs={{8,0},{9,1},{10,2},{11,3},{12,4},{13,5},{14,6},{15,7}} | collective-permute-start | bytes 983048 | tf_op jit(solution)/shard_map/ppermute | solution.py:28
  130.0 10.9 %collective-permute-start.24 = (bf16[2,32,2304]{2,1,0:T(8,128)(2,1)}, bf16[2,32,2304]{2,1,0:T(8,128)(2,1)S(1)}, u32[]{:S(2)}, u32[]{:S(2)}) collective-permute-start(bf16[2,32,2304]{2,1,0:T(8,128)(2,1)} %get-tuple-element.453), channel_id=1, source_target_pairs={{0,2},{1,3},{2,0},{3,1},{4,6},{5,7},{6,4},{7,5},{8,10},{9,11},{10,... | collective-permute-start | bytes 884744 | tf_op jit(solution)/shard_map/ppermute | solution.py:33
  132.9 10.7 %collective-permute-start.25 = (bf16[2,32,2304]{2,1,0:T(8,128)(2,1)}, bf16[2,32,2304]{2,1,0:T(8,128)(2,1)S(1)}, u32[]{:S(2)}, u32[]{:S(2)}) collective-permute-start(bf16[2,32,2304]{2,1,0:T(8,128)(2,1)} %get-tuple-element.454), channel_id=1, source_target_pairs={{0,4},{1,5},{2,6},{3,7},{4,0},{5,1},{6,2},{7,3},{8,12},{9,13},{10,... | collective-permute-start | bytes 884744 | tf_op jit(solution)/shard_map/ppermute | solution.py:33
  135.5 8.1 %collective-permute-start.26 = (bf16[2,32,2304]{2,1,0:T(8,128)(2,1)}, bf16[2,32,2304]{2,1,0:T(8,128)(2,1)S(1)}, u32[]{:S(2)}, u32[]{:S(2)}) collective-permute-start(bf16[2,32,2304]{2,1,0:T(8,128)(2,1)} %get-tuple-element.455), channel_id=1, source_target_pairs={{0,6},{1,7},{2,4},{3,5},{4,2},{5,3},{6,0},{7,1},{8,14},{9,15},{10,... | collective-permute-start | bytes 884744 | tf_op jit(solution)/shard_map/ppermute | solution.py:33
  138.2 26.6 %collective-permute-start.17 = (bf16[4,4,32,1792]{3,2,1,0:T(8,128)(2,1)S(1)}, bf16[4,4,32,1792]{3,2,1,0:T(8,128)(2,1)S(1)}, u32[]{:S(2)}, u32[]{:S(2)}) collective-permute-start(bf16[4,4,32,1792]{3,2,1,0:T(8,128)(2,1)S(1)} %pad_maximum_fusion.rest_0_), channel_id=1, source_target_pairs={{0,1},{1,0},{2,3},{3,2},{4,5},{5,4},{6,7},{7,6},{8,9},{9,8},{10,11... | collective-permute-start | bytes 5505032 | tf_op jit(solution)/shard_map/ppermute | solution.py:37
  143.7 6.4 %copy-start.7 = (bf16[1,32,2304]{2,1,0:T(8,128)(2,1)S(1)}, bf16[1,32,2304]{2,1,0:T(8,128)(2,1)}, u32[]{:S(2)}) copy-start(bf16[1,32,2304]{2,1,0:T(8,128)(2,1)} %get-tuple-element.444) | copy-start | bytes 442372
  143.7 9.6 %copy-start.8 = (bf16[1,32,2304]{2,1,0:T(8,128)(2,1)S(1)}, bf16[1,32,2304]{2,1,0:T(8,128)(2,1)}, u32[]{:S(2)}) copy-start(bf16[1,32,2304]{2,1,0:T(8,128)(2,1)} %get-tuple-element.445) | copy-start | bytes 442372
  143.7 14.2 %copy-start.9 = (bf16[1,32,2304]{2,1,0:T(8,128)(2,1)S(1)}, bf16[1,32,2304]{2,1,0:T(8,128)(2,1)}, u32[]{:S(2)}) copy-start(bf16[1,32,2304]{2,1,0:T(8,128)(2,1)} %get-tuple-element.446) | copy-start | bytes 442372
  143.7 14.2 %copy-start.4 = (bf16[2,32,2304]{2,1,0:T(8,128)(2,1)S(1)}, bf16[2,32,2304]{2,1,0:T(8,128)(2,1)}, u32[]{:S(2)}) copy-start(bf16[2,32,2304]{2,1,0:T(8,128)(2,1)} %get-tuple-element.470) | copy-start | bytes 884740
  146.5 17.4 %copy-start.6 = (bf16[1,32,2304]{2,1,0:T(8,128)(2,1)S(1)}, bf16[1,32,2304]{2,1,0:T(8,128)(2,1)}, u32[]{:S(2)}) copy-start(bf16[1,32,2304]{2,1,0:T(8,128)(2,1)} %get-tuple-element.447) | copy-start | bytes 442372
  146.5 6.8 %collective-permute-start.27 = (bf16[1,32,2304]{2,1,0:T(8,128)(2,1)}, bf16[1,32,2304]{2,1,0:T(8,128)(2,1)S(1)}, u32[]{:S(2)}, u32[]{:S(2)}) collective-permute-start(bf16[1,32,2304]{2,1,0:T(8,128)(2,1)} %get-tuple-element.463), channel_id=1, source_target_pairs={{0,2},{1,3},{2,0},{3,1},{4,6},{5,7},{6,4},{7,5},{8,10},{9,11},{10,... | collective-permute-start | bytes 442376 | tf_op jit(solution)/shard_map/ppermute | solution.py:33
  147.9 9.9 %collective-permute-start.28 = (bf16[1,32,2304]{2,1,0:T(8,128)(2,1)}, bf16[1,32,2304]{2,1,0:T(8,128)(2,1)S(1)}, u32[]{:S(2)}, u32[]{:S(2)}) collective-permute-start(bf16[1,32,2304]{2,1,0:T(8,128)(2,1)} %get-tuple-element.464), channel_id=1, source_target_pairs={{0,4},{1,5},{2,6},{3,7},{4,0},{5,1},{6,2},{7,3},{8,12},{9,13},{10,... | collective-permute-start | bytes 442376 | tf_op jit(solution)/shard_map/ppermute | solution.py:33
  149.6 8.4 %collective-permute-start.29 = (bf16[1,32,2304]{2,1,0:T(8,128)(2,1)}, bf16[1,32,2304]{2,1,0:T(8,128)(2,1)S(1)}, u32[]{:S(2)}, u32[]{:S(2)}) collective-permute-start(bf16[1,32,2304]{2,1,0:T(8,128)(2,1)} %get-tuple-element.465), channel_id=1, source_target_pairs={{0,6},{1,7},{2,4},{3,5},{4,2},{5,3},{6,0},{7,1},{8,14},{9,15},{10,... | collective-permute-start | bytes 442376 | tf_op jit(solution)/shard_map/ppermute | solution.py:33
  150.1 9.6 %collective-permute-start.19 = (bf16[1,32,2304]{2,1,0:T(8,128)(2,1)S(1)}, bf16[1,32,2304]{2,1,0:T(8,128)(2,1)S(1)}, u32[]{:S(2)}, u32[]{:S(2)}) collective-permute-start(bf16[1,32,2304]{2,1,0:T(8,128)(2,1)S(1)} %copy-done.7), channel_id=1, source_target_pairs={{0,2},{1,3},{2,0},{3,1},{4,6},{5,7},{6,4},{7,5},{8,10},{9,11},{10,... | collective-permute-start | bytes 442376 | tf_op jit(solution)/shard_map/ppermute | solution.py:33
  153.3 7.9 %collective-permute-start.20 = (bf16[1,32,2304]{2,1,0:T(8,128)(2,1)S(1)}, bf16[1,32,2304]{2,1,0:T(8,128)(2,1)S(1)}, u32[]{:S(2)}, u32[]{:S(2)}) collective-permute-start(bf16[1,32,2304]{2,1,0:T(8,128)(2,1)S(1)} %copy-done.8), channel_id=1, source_target_pairs={{0,4},{1,5},{2,6},{3,7},{4,0},{5,1},{6,2},{7,3},{8,12},{9,13},{10,... | collective-permute-start | bytes 442376 | tf_op jit(solution)/shard_map/ppermute | solution.py:33
  157.9 6.0 %collective-permute-start.21 = (bf16[1,32,2304]{2,1,0:T(8,128)(2,1)S(1)}, bf16[1,32,2304]{2,1,0:T(8,128)(2,1)S(1)}, u32[]{:S(2)}, u32[]{:S(2)}) collective-permute-start(bf16[1,32,2304]{2,1,0:T(8,128)(2,1)S(1)} %copy-done.9), channel_id=1, source_target_pairs={{0,6},{1,7},{2,4},{3,5},{4,2},{5,3},{6,0},{7,1},{8,14},{9,15},{10,... | collective-permute-start | bytes 442376 | tf_op jit(solution)/shard_map/ppermute | solution.py:33
  157.9 6.2 %copy-start.5 = (bf16[1,32,2304]{2,1,0:T(8,128)(2,1)S(1)}, bf16[1,32,2304]{2,1,0:T(8,128)(2,1)}, u32[]{:S(2)}) copy-start(bf16[1,32,2304]{2,1,0:T(8,128)(2,1)} %get-tuple-element.466) | copy-start | bytes 442372
  158.0 6.7 %collective-permute-start.31 = (bf16[4,2,32,2304]{3,2,1,0:T(8,128)(2,1)S(1)}, bf16[4,2,32,2304]{3,2,1,0:T(8,128)(2,1)S(1)}, u32[]{:S(2)}, u32[]{:S(2)}) collective-permute-start(bf16[4,2,32,2304]{3,2,1,0:T(8,128)(2,1)S(1)} %pad_maximum_fusion.1.rest_2_), channel_id=1, source_target_pairs={{0,1},{1,0},{2,3},{3,2},{4,5},{5,4},{6,7},{7,6},{8,9},{9,8},{10,11... | collective-permute-start | bytes 3538952 | tf_op jit(solution)/shard_map/ppermute | solution.py:37
  164.0 2.4 %collective-permute-start.22 = (bf16[4,1,32,2304]{3,2,1,0:T(8,128)(2,1)S(1)}, bf16[4,1,32,2304]{3,2,1,0:T(8,128)(2,1)S(1)}, u32[]{:S(2)}, u32[]{:S(2)}) collective-permute-start(bf16[4,1,32,2304]{3,2,1,0:T(8,128)(2,1)S(1)} %pad_maximum_fusion.2.rest_2_), channel_id=1, source_target_pairs={{0,1},{1,0},{2,3},{3,2},{4,5},{5,4},{6,7},{7,6},{8,9},{9,8},{10,11... | collective-permute-start | bytes 1769480 | tf_op jit(solution)/shard_map/ppermute | solution.py:37
  164.2 2.7 %collective-permute-start.30 = (bf16[4,1,32,2304]{3,2,1,0:T(8,128)(2,1)S(1)}, bf16[4,1,32,2304]{3,2,1,0:T(8,128)(2,1)S(1)}, u32[]{:S(2)}, u32[]{:S(2)}) collective-permute-start(bf16[4,1,32,2304]{3,2,1,0:T(8,128)(2,1)S(1)} %pad_maximum_fusion.3.rest_4_), channel_id=1, source_target_pairs={{0,1},{1,0},{2,3},{3,2},{4,5},{5,4},{6,7},{7,6},{8,9},{9,8},{10,11... | collective-permute-start | bytes 1769480 | tf_op jit(solution)/shard_map/ppermute | solution.py:37

commit v8 on v7

--- a/solution.py
+++ b/solution.py
@@ -197,14 +197,18 @@
 
 
 def fill_block(block, columns, factors):
+    fill_columns(block, columns)
+    for chip in range(block.shape[0]):
+        block[chip, :, block.shape[2] - factors.shape[1] :] = factors[...]
+
+
+def fill_columns(block, columns):
     chips = block.shape[0]
     share = columns.shape[1] // (2 * chips)
-    wide = (block.shape[2] - factors.shape[1]) // 2
+    wide = -(-share // HD) * HD
     for device in range(2 * chips):
         start = (device % 2) * wide
         block[device // 2, :, start : start + share] = columns[:, device * share : (device + 1) * share]
-    for chip in range(chips):
-        block[chip, :, 2 * wide :] = factors[...]
 
 
 def block_copies(block, targets, sems):
@@ -319,14 +323,22 @@
     features = KV_HEADS * HD
     step = CHUNK // 2
 
-    def for_group(act):
+    split = block.shape[2]
+    chip = lax.axis_index("dp") // 2
+
+    def for_group(act, columns):
         for n, group in enumerate(groups):
             @pl.when((slot >= group[0]) & (slot <= group[-1]))
             def _():
                 index = jnp.clip(slot - group[0], 0, len(group) - 1)
-                targets = [ref.at[index] for ref in sent[n * chips : (n + 1) * chips]]
-                for copy in block_copies(block, targets, sems):
-                    act(copy)
+                for mask, ref in enumerate(sent[n * chips : (n + 1) * chips]):
+                    if columns:
+                        source, part = block.at[partner(chip, mask, chips)], pl.ds(0, split)
+                    else:
+                        source, part = flat, pl.ds(split, 2 * features)
+                    target = ref.at[index, :, part]
+                    at = mask if columns else chips + mask
+                    act(pltpu.make_async_copy(source, target, sems.at[at]))
 
     @pl.when((offset >= 0) & (offset < micro))
     def _():
@@ -338,6 +350,8 @@
         def _():
             current[...] = incoming[...]
 
+        fill_columns(block, current)
+        for_group(lambda copy: copy.start(), True)
         acc[...] = jnp.zeros_like(acc)
 
         @pl.loop(0, model // CHUNK)
@@ -370,19 +384,18 @@
                 vec = (dot(piece, key) + dot_ta(piece, key)) / HD
                 turned = vec * cos_value - pltpu.roll(vec, HD // 2, 1) * sin_value
                 flat[:, head_cols(head)] = turned.astype(BF16)
-            fill_block(block, current, flat)
 
         lowest = tick - 2 * (sections - 1)
 
         @when(lowest >= 0, section == 0)
         def _():
             factors(False)
-            for_group(lambda copy: copy.start())
+            for_group(lambda copy: copy.start(), False)
 
         @when(lowest + 2 < micro, section != 0)
         def _():
             factors(True)
-            for_group(lambda copy: copy.start())
+            for_group(lambda copy: copy.start(), False)
             acc[...] = jnp.zeros_like(acc)
 
             @pl.loop(0, model // CHUNK)
@@ -408,7 +421,8 @@
                 )
                 outgoing[:, cols] = value.astype(BF16)
 
-        for_group(lambda copy: copy.wait())
+        for_group(lambda copy: copy.wait(), True)
+        for_group(lambda copy: copy.wait(), False)
 
 
 def gather_kernel(groups, share, wide, features, final, *rest):
@@ -604,8 +618,8 @@
                 pltpu.VMEM((width, model), F32),
                 pltpu.VMEM((width, model), BF16),
                 pltpu.VMEM((width, 2 * features), BF16),
-                pltpu.VMEM((chips, width, 2 * wide + 2 * features), BF16),
-                pltpu.SemaphoreType.DMA((chips,)),
+                pltpu.VMEM((chips, width, 2 * wide), BF16),
+                pltpu.SemaphoreType.DMA((2 * chips,)),
             ],
             compiler_params=params(),
             cost_estimate=cost,

time: 171 us -> 171 us (level)
  no operation moved by 1% of the time
where the time goes in v8:
time: 171 us; the launch traced here: 169 us
  waiting for transfers between devices  91.4 us (53%)
  Pallas kernels  39.3 us (23%)
  starting transfers between devices  36.3 us (21%)
    ppermute x16, waiting for transfers between devices, shifted(): lax.ppermute(value, 'section', [(source, source + steps) for source in se...  79.3 us
    ppermute x16, starting transfers between devices, shifted(): lax.ppermute(value, 'section', [(source, source + steps) for source in se...  19.7 us
    ppermute x12, starting transfers between devices, between_chips(): return lax.ppermute(value, 'dp', pairs)  15.9 us
    pallas_call x9, Pallas kernels, shards(): pl.pallas_call(functools.partial(forward_kernel, tick, sections, micro, c...  15 us
    pallas_call x10, Pallas kernels, shards(): pl.pallas_call(functools.partial(backward_kernel, tick, sections, micro,...  11.7 us
    ppermute x12, waiting for transfers between devices, between_chips(): return lax.ppermute(value, 'dp', pairs)  11.5 us
    pallas_call x1, Pallas kernels, shards(): pl.pallas_call(functools.partial(first_kernel, sections, micro, chips), o...  8.46 us
    pallas_call x2, Pallas kernels, shards(): pl.pallas_call(functools.partial(gather_kernel, chosen, share, wide, feat...  4.09 us
  transfers between devices with their start and end apart: 32, of which 13 were waited for; matrix products, arithmetic and copies ran while one was open for 0% of the time, Pallas kernels for 17%

profile of v8, /device:TPU:0, one launch (start us, length us, event | category | flops | bytes accessed | tf_op | source)
XLA Modules:
  0.0 168.9 jit_solution(4897412614965587237)
XLA Ops:
  0.6 8.5 %first.1 = (f32[1,5120]{1,0:T(1,128)S(1)}, bf16[5120,512]{1,0:T(8,128)(2,1)S(1)}, bf16[5120,512]{1,0:T(8,128)(2,1)S(1)}, f32[4,32,128]{2,1,0:T(8,128)S(1)}, f32[...) custom-call(bf16[5120,512]{1,0:T(8,128)(2,1)} %bitcast.24, ...), custom_call_target="tpu_custom_call" | custom-call | tf_op jit(solution)/shard_map/first/pallas_call | solution.py:535
  9.1 1.3 collective-permute-start.1
  10.4 4.9 %forward.9 = (bf16[4,32,5120]{2,1,0:T(8,128)(2,1)S(1)}, bf16[4,32,512]{2,1,0:T(8,128)(2,1)S(1)}, bf16[4,32,512]{2,1,0:T(8,128)(2,1)S(1)}, f32[4,128,32]{2,1,0:T(...) custom-call(bf16[32,5120]{1,0:T(8,128)(2,1)S(1)} %broadcast_in_dim.9, ...), custom_call_target="tpu_custom_call", output_to_operand_aliasing={{0}: (9, {}), {1}: (10, {}), {2}: (11, {}), {3}: (12, {}), ... | custom-call | flops 1000000 | bytes 1000000 | tf_op jit(solution)/shard_map/forward/pallas_call | solution.py:574
  15.3 1.3 collective-permute-start
  16.7 1.8 %collective-permute-done.1.incoming = bf16[32,5120]{1,0:T(8,128)(2,1)S(1)} collective-permute-done((bf16[32,5120]{1,0:T(8,128)(2,1)S(1)}, bf16[32,5120]{1,0:T(8,128)(2,1)S(1)}, u32[]{:S(2)}, u32[]{:S(2)}) %collective-permute-start.1) | collective-permute-done | bytes 327712 | tf_op jit(solution)/shard_map/ppermute | solution.py:28
  18.5 4.8 %forward.10 = (bf16[4,32,5120]{2,1,0:T(8,128)(2,1)S(1)}, bf16[4,32,512]{2,1,0:T(8,128)(2,1)S(1)}, bf16[4,32,512]{2,1,0:T(8,128)(2,1)S(1)}, f32[4,128,32]{2,1,0:T...) custom-call(bf16[32,5120]{1,0:T(8,128)(2,1)S(1)} %collective-permute, ...), custom_call_target="tpu_custom_call", output_to_operand_aliasing={{0}: (9, {}), {1}: (10, {}), {2}: (11, {}), {3}: (12, {}), ... | custom-call | flops 1000000 | bytes 1000000 | tf_op jit(solution)/shard_map/forward/pallas_call | solution.py:574
  23.3 4.4 %collective-permute-start.3 = (bf16[32,5120]{1,0:T(8,128)(2,1)S(1)}, bf16[32,5120]{1,0:T(8,128)(2,1)S(1)}, u32[]{:S(2)}, u32[]{:S(2)}) collective-permute-start(bf16[32,5120]{1,0:T(8,128)(2,1)S(1)} %get-tuple-element.281), channel_id=1, source_target_pairs={{0,8},{8,16},{1,9},{9,17},{2,10},{10,18},{3,11},{11,19},{4,12},{12... | collective-permute-start | bytes 983048 | tf_op jit(solution)/shard_map/ppermute | solution.py:28
  27.8 4.9 %forward.11 = (bf16[4,32,5120]{2,1,0:T(8,128)(2,1)S(1)}, bf16[4,32,512]{2,1,0:T(8,128)(2,1)S(1)}, bf16[4,32,512]{2,1,0:T(8,128)(2,1)S(1)}, f32[4,128,32]{2,1,0:T...) custom-call(bf16[32,5120]{1,0:T(8,128)(2,1)S(1)} %collective-permute, ...), custom_call_target="tpu_custom_call", output_to_operand_aliasing={{0}: (9, {}), {1}: (10, {}), {2}: (11, {}), {3}: (12, {}), ... | custom-call | flops 1000000 | bytes 1000000 | tf_op jit(solution)/shard_map/forward/pallas_call | solution.py:574
  32.7 1.9 %collective-permute-start.2 = (bf16[32,5120]{1,0:T(8,128)(2,1)S(1)}, bf16[32,5120]{1,0:T(8,128)(2,1)S(1)}, u32[]{:S(2)}, u32[]{:S(2)}) collective-permute-start(bf16[32,5120]{1,0:T(8,128)(2,1)S(1)} %get-tuple-element.280), channel_id=1, source_target_pairs={{0,8},{8,16},{1,9},{9,17},{2,10},{10,18},{3,11},{11,19},{4,12},{12... | collective-permute-start | bytes 983048 | tf_op jit(solution)/shard_map/ppermute | solution.py:28
  34.7 0.7 collective-permute-start.5
  35.4 6.1 %collective-permute-done.2.incoming = bf16[32,5120]{1,0:T(8,128)(2,1)S(1)} collective-permute-done((bf16[32,5120]{1,0:T(8,128)(2,1)S(1)}, bf16[32,5120]{1,0:T(8,128)(2,1)S(1)}, u32[]{:S(2)}, u32[]{:S(2)}) %collective-permute-start.2) | collective-permute-done | bytes 327712 | tf_op jit(solution)/shard_map/ppermute | solution.py:28
  41.6 0.7 collective-permute-start.4
  42.4 0.7 collective-permute-start.7
  43.1 0.7 collective-permute-start.6
  44.1 0.7 collective-permute-start.9
  45.1 0.7 collective-permute-start.12
  45.9 0.7 collective-permute-start.14
  46.8 0.8 collective-permute-start.13
  47.6 1.9 %collective-permute-start.8 = (bf16[4,32,1792]{2,1,0:T(8,128)(2,1)S(1)}, bf16[4,32,1792]{2,1,0:T(8,128)(2,1)S(1)}, u32[]{:S(2)}, u32[]{:S(2)}) collective-permute-start(bf16[4,32,1792]{2,1,0:T(8,128)(2,1)S(1)} %copy-done.1), channel_id=1, source_target_pairs={{0,2},{1,3},{2,0},{3,1},{4,6},{5,7},{6,4},{7,5},{8,10},{9,11},{10,... | collective-permute-start | bytes 1376264 | tf_op jit(solution)/shard_map/ppermute | solution.py:33
  49.5 1.5 collective-permute-start.11
  51.2 1.3 collective-permute-start.16
  52.7 1.3 collective-permute-start.15
  54.0 64.8 %collective-permute-done.16.incoming = bf16[32,5120]{1,0:T(8,128)(2,1)S(1)} collective-permute-done((bf16[32,5120]{1,0:T(8,128)(2,1)S(1)}, bf16[32,5120]{1,0:T(8,128)(2,1)S(1)}, u32[]{:S(2)}, u32[]{:S(2)}) %collective-permute-start.16) | collective-permute-done | bytes 327712 | tf_op jit(solution)/shard_map/ppermute | solution.py:28
  118.8 2.7 %backward.16 = (f32[8,128]{1,0:T(8,128)S(1)}, bf16[2,32,2304]{2,1,0:T(8,128)(2,1)}, bf16[2,32,2304]{2,1,0:T(8,128)(2,1)}, bf16[2,32,2304]{2,1,0:T(8,128)(2,1)}, ...) custom-call(bf16[32,5120]{1,0:T(8,128)(2,1)S(1)} %collective-permute, ...), custom_call_target="tpu_custom_call", output_to_operand_aliasing={{0}: (11, {}), {1}: (12, {}), {2}: (13, {}), {3}: (14, {}),... | custom-call | flops 1000000 | bytes 1000000 | tf_op jit(solution)/shard_map/backward/pallas_call | solution.py:607
  121.5 1.3 collective-permute-start.18
  122.8 3.3 %collective-permute-done.15.incoming = bf16[32,5120]{1,0:T(8,128)(2,1)S(1)} collective-permute-done((bf16[32,5120]{1,0:T(8,128)(2,1)S(1)}, bf16[32,5120]{1,0:T(8,128)(2,1)S(1)}, u32[]{:S(2)}, u32[]{:S(2)}) %collective-permute-start.15) | collective-permute-done | bytes 327712 | tf_op jit(solution)/shard_map/ppermute | solution.py:28
  126.1 2.7 %backward.17 = (f32[8,128]{1,0:T(8,128)S(1)}, bf16[2,32,2304]{2,1,0:T(8,128)(2,1)}, bf16[2,32,2304]{2,1,0:T(8,128)(2,1)}, bf16[2,32,2304]{2,1,0:T(8,128)(2,1)}, ...) custom-call(bf16[32,5120]{1,0:T(8,128)(2,1)S(1)} %collective-permute, ...), custom_call_target="tpu_custom_call", output_to_operand_aliasing={{0}: (11, {}), {1}: (12, {}), {2}: (13, {}), {3}: (14, {}),... | custom-call | flops 1000000 | bytes 1000000 | tf_op jit(solution)/shard_map/backward/pallas_call | solution.py:607
  128.8 1.3 collective-permute-start.23
  130.1 2.8 %collective-permute-start.24 = (bf16[2,32,2304]{2,1,0:T(8,128)(2,1)}, bf16[2,32,2304]{2,1,0:T(8,128)(2,1)S(1)}, u32[]{:S(2)}, u32[]{:S(2)}) collective-permute-start(bf16[2,32,2304]{2,1,0:T(8,128)(2,1)} %get-tuple-element.453), channel_id=1, source_target_pairs={{0,2},{1,3},{2,0},{3,1},{4,6},{5,7},{6,4},{7,5},{8,10},{9,11},{10,... | collective-permute-start | bytes 884744 | tf_op jit(solution)/shard_map/ppermute | solution.py:33
  132.8 2.6 %collective-permute-start.25 = (bf16[2,32,2304]{2,1,0:T(8,128)(2,1)}, bf16[2,32,2304]{2,1,0:T(8,128)(2,1)S(1)}, u32[]{:S(2)}, u32[]{:S(2)}) collective-permute-start(bf16[2,32,2304]{2,1,0:T(8,128)(2,1)} %get-tuple-element.454), channel_id=1, source_target_pairs={{0,4},{1,5},{2,6},{3,7},{4,0},{5,1},{6,2},{7,3},{8,12},{9,13},{10,... | collective-permute-start | bytes 884744 | tf_op jit(solution)/shard_map/ppermute | solution.py:33
  135.7 2.9 %collective-permute-done.18.incoming = bf16[32,5120]{1,0:T(8,128)(2,1)S(1)} collective-permute-done((bf16[32,5120]{1,0:T(8,128)(2,1)S(1)}, bf16[32,5120]{1,0:T(8,128)(2,1)S(1)}, u32[]{:S(2)}, u32[]{:S(2)}) %collective-permute-start.18) | collective-permute-done | bytes 327712 | tf_op jit(solution)/shard_map/ppermute | solution.py:28
  138.6 2.7 %backward.18 = (f32[8,128]{1,0:T(8,128)S(1)}, bf16[1,32,2304]{2,1,0:T(8,128)(2,1)}, bf16[1,32,2304]{2,1,0:T(8,128)(2,1)}, bf16[1,32,2304]{2,1,0:T(8,128)(2,1)}, bf16[1,32,2304]{2,1,0:T(8,128)(2,1)}) custom-call(bf16[32,5120]{1,0:T(8,128)(2,1)S(1)} %collective-permute-done.18.incoming, ...), custom_call_target="tpu_custom_call", output_to_operand_aliasing={{0}: (11, {}), {1}: (12, {}), {2}: (13, {}), {3}: (14, {}),... | custom-call | flops 1000000 | bytes 1000000 | tf_op jit(solution)/shard_map/backward/pallas_call | solution.py:607
  141.4 2.1 %collective-permute-done.25 = bf16[2,32,2304]{2,1,0:T(8,128)(2,1)S(1)} collective-permute-done((bf16[2,32,2304]{2,1,0:T(8,128)(2,1)}, bf16[2,32,2304]{2,1,0:T(8,128)(2,1)S(1)}, u32[]{:S(2)}, u32[]{:S(2)}) %collective-permute-start.25) | collective-permute-done | bytes 294944 | tf_op jit(solution)/shard_map/ppermute | solution.py:33
  143.9 2.8 %backward.19 = (f32[8,128]{1,0:T(8,128)S(1)}, bf16[1,32,2304]{2,1,0:T(8,128)(2,1)}, bf16[1,32,2304]{2,1,0:T(8,128)(2,1)}, bf16[1,32,2304]{2,1,0:T(8,128)(2,1)}, bf16[1,32,2304]{2,1,0:T(8,128)(2,1)}) custom-call(bf16[32,5120]{1,0:T(8,128)(2,1)S(1)} %collective-permute-done.23.incoming, ...), custom_call_target="tpu_custom_call", output_to_operand_aliasing={{0}: (11, {}), {1}: (12, {}), {2}: (13, {}), {3}: (14, {}),... | custom-call | flops 1000000 | bytes 1000000 | tf_op jit(solution)/shard_map/backward/pallas_call | solution.py:607
  146.7 1.1 collective-permute-start.27
  147.8 1.9 %collective-permute-start.28 = (bf16[1,32,2304]{2,1,0:T(8,128)(2,1)}, bf16[1,32,2304]{2,1,0:T(8,128)(2,1)S(1)}, u32[]{:S(2)}, u32[]{:S(2)}) collective-permute-start(bf16[1,32,2304]{2,1,0:T(8,128)(2,1)} %get-tuple-element.464), channel_id=1, source_target_pairs={{0,4},{1,5},{2,6},{3,7},{4,0},{5,1},{6,2},{7,3},{8,12},{9,13},{10,... | collective-permute-start | bytes 442376 | tf_op jit(solution)/shard_map/ppermute | solution.py:33
  150.2 1.1 collective-permute-start.19
  151.3 2.1 %collective-permute-done.27 = bf16[1,32,2304]{2,1,0:T(8,128)(2,1)S(1)} collective-permute-done((bf16[1,32,2304]{2,1,0:T(8,128)(2,1)}, bf16[1,32,2304]{2,1,0:T(8,128)(2,1)S(1)}, u32[]{:S(2)}, u32[]{:S(2)}) %collective-permute-start.27) | collective-permute-done | bytes 147488 | tf_op jit(solution)/shard_map/ppermute | solution.py:33
  153.4 1.6 collective-permute-start.20
  155.0 2.2 %collective-permute-done.28 = bf16[1,32,2304]{2,1,0:T(8,128)(2,1)S(1)} collective-permute-done((bf16[1,32,2304]{2,1,0:T(8,128)(2,1)}, bf16[1,32,2304]{2,1,0:T(8,128)(2,1)S(1)}, u32[]{:S(2)}, u32[]{:S(2)}) %collective-permute-start.28) | collective-permute-done | bytes 147488 | tf_op jit(solution)/shard_map/ppermute | solution.py:33
  157.2 0.8 collective-permute-start.21
  158.3 1.4 collective-permute-done.19
  159.7 1.0 collective-permute-done.20
  160.7 2.6 %collective-permute-done.21 = bf16[1,32,2304]{2,1,0:T(8,128)(2,1)S(1)} collective-permute-done((bf16[1,32,2304]{2,1,0:T(8,128)(2,1)S(1)}, bf16[1,32,2304]{2,1,0:T(8,128)(2,1)S(1)}, u32[]{:S(2)}, u32[]{:S(2)}) %collective-permute-start.21) | collective-permute-done | bytes 147488 | tf_op jit(solution)/shard_map/ppermute | solution.py:33
  163.5 0.5 collective-permute-start.30
  164.1 1.6 gathered.2
  165.7 0.5 collective-permute-done.30.rest_5_
  166.3 2.5 %gathered.3 = (f32[640,512]{1,0:T(8,128)}, f32[640,512]{1,0:T(8,128)}) custom-call(bf16[4,4,32,1792]{3,2,1,0:T(8,128)(2,1)S(1)} %pad_maximum_fusion.rest_0_, bf16[4,4,32,1792]{3,2,1,0:T(8,128)(2,1)S(1)} %collective-permute-done.17.rest_1_, bf16[4,1,32,2304]{3,2,1,0:T(8,128)(2,1)S(1)} %pad_maximum_fusion.2.rest_2_, ...), custom_call_target="tpu_custom_call" | custom-call | flops 1000000 | bytes 1000000 | tf_op jit(solution)/shard_map/gathered/pallas_call | solution.py:656
  (63 shorter events, 3.1 us)
Async XLA Ops:
  9.1 9.4 %collective-permute-start.1 = (bf16[32,5120]{1,0:T(8,128)(2,1)S(1)}, bf16[32,5120]{1,0:T(8,128)(2,1)S(1)}, u32[]{:S(2)}, u32[]{:S(2)}) collective-permute-start(bf16[32,5120]{1,0:T(8,128)(2,1)S(1)} %get-tuple-element.259), channel_id=1, source_target_pairs={{0,8},{1,9},{2,10},{3,11},{4,12},{5,13},{6,14},{7,15}} | collective-permute-start | bytes 983048 | tf_op jit(solution)/shard_map/ppermute | solution.py:28
  15.3 12.4 %collective-permute-start = (bf16[32,5120]{1,0:T(8,128)(2,1)S(1)}, bf16[32,5120]{1,0:T(8,128)(2,1)S(1)}, u32[]{:S(2)}, u32[]{:S(2)}) collective-permute-start(bf16[32,5120]{1,0:T(8,128)(2,1)S(1)} %get-tuple-element.258), channel_id=1, source_target_pairs={{0,8},{1,9},{2,10},{3,11},{4,12},{5,13},{6,14},{7,15}} | collective-permute-start | bytes 983048 | tf_op jit(solution)/shard_map/ppermute | solution.py:28
  23.3 11.3 %collective-permute-start.3 = (bf16[32,5120]{1,0:T(8,128)(2,1)S(1)}, bf16[32,5120]{1,0:T(8,128)(2,1)S(1)}, u32[]{:S(2)}, u32[]{:S(2)}) collective-permute-start(bf16[32,5120]{1,0:T(8,128)(2,1)S(1)} %get-tuple-element.281), channel_id=1, source_target_pairs={{0,8},{8,16},{1,9},{9,17},{2,10},{10,18},{3,11},{11,19},{4,12},{12... | collective-permute-start | bytes 983048 | tf_op jit(solution)/shard_map/ppermute | solution.py:28
  32.7 8.9 %collective-permute-start.2 = (bf16[32,5120]{1,0:T(8,128)(2,1)S(1)}, bf16[32,5120]{1,0:T(8,128)(2,1)S(1)}, u32[]{:S(2)}, u32[]{:S(2)}) collective-permute-start(bf16[32,5120]{1,0:T(8,128)(2,1)S(1)} %get-tuple-element.280), channel_id=1, source_target_pairs={{0,8},{8,16},{1,9},{9,17},{2,10},{10,18},{3,11},{11,19},{4,12},{12... | collective-permute-start | bytes 983048 | tf_op jit(solution)/shard_map/ppermute | solution.py:28
  34.7 7.5 %collective-permute-start.5 = (bf16[32,5120]{1,0:T(8,128)(2,1)S(1)}, bf16[32,5120]{1,0:T(8,128)(2,1)S(1)}, u32[]{:S(2)}, u32[]{:S(2)}) collective-permute-start(bf16[32,5120]{1,0:T(8,128)(2,1)S(1)} %get-tuple-element.303), channel_id=1, source_target_pairs={{8,16},{16,24},{9,17},{17,25},{10,18},{18,26},{11,19},{19,27},{12,... | collective-permute-start | bytes 983048 | tf_op jit(solution)/shard_map/ppermute | solution.py:28
  41.6 1.5 collective-permute-start.4
  42.4 1.5 collective-permute-start.7
  43.1 0.8 collective-permute-start.6
  44.1 1.7 collective-permute-start.9
  45.1 1.5 collective-permute-start.12
  45.9 5.3 %collective-permute-start.14 = (bf16[32,5120]{1,0:T(8,128)(2,1)S(1)}, bf16[32,5120]{1,0:T(8,128)(2,1)S(1)}, u32[]{:S(2)}, u32[]{:S(2)}) collective-permute-start(bf16[32,5120]{1,0:T(8,128)(2,1)S(1)} %get-tuple-element.393), channel_id=1, source_target_pairs={{16,8},{24,16},{17,9},{25,17},{18,10},{26,18},{19,11},{27,19},{20,... | collective-permute-start | bytes 983048 | tf_op jit(solution)/shard_map/ppermute | solution.py:28
  46.6 1.0 copy-start.1
  46.6 2.9 %copy-start.3 = (bf16[4,32,1792]{2,1,0:T(8,128)(2,1)S(1)}, bf16[4,32,1792]{2,1,0:T(8,128)(2,1)}, u32[]{:S(2)}) copy-start(bf16[4,32,1792]{2,1,0:T(8,128)(2,1)} %get-tuple-element.381) | copy-start | bytes 1376260
  46.6 4.4 %copy-start.2 = (bf16[4,32,1792]{2,1,0:T(8,128)(2,1)S(1)}, bf16[4,32,1792]{2,1,0:T(8,128)(2,1)}, u32[]{:S(2)}) copy-start(bf16[4,32,1792]{2,1,0:T(8,128)(2,1)} %get-tuple-element.380) | copy-start | bytes 1376260
  46.8 5.8 %collective-permute-start.13 = (bf16[32,5120]{1,0:T(8,128)(2,1)S(1)}, bf16[32,5120]{1,0:T(8,128)(2,1)S(1)}, u32[]{:S(2)}, u32[]{:S(2)}) collective-permute-start(bf16[32,5120]{1,0:T(8,128)(2,1)S(1)} %get-tuple-element.392), channel_id=1, source_target_pairs={{16,8},{24,16},{17,9},{25,17},{18,10},{26,18},{19,11},{27,19},{20,... | collective-permute-start | bytes 983048 | tf_op jit(solution)/shard_map/ppermute | solution.py:28
  47.6 82.5 %collective-permute-start.8 = (bf16[4,32,1792]{2,1,0:T(8,128)(2,1)S(1)}, bf16[4,32,1792]{2,1,0:T(8,128)(2,1)S(1)}, u32[]{:S(2)}, u32[]{:S(2)}) collective-permute-start(bf16[4,32,1792]{2,1,0:T(8,128)(2,1)S(1)} %copy-done.1), channel_id=1, source_target_pairs={{0,2},{1,3},{2,0},{3,1},{4,6},{5,7},{6,4},{7,5},{8,10},{9,11},{10,... | collective-permute-start | bytes 1376264 | tf_op jit(solution)/shard_map/ppermute | solution.py:33
  49.5 83.3 %collective-permute-start.11 = (bf16[4,32,1792]{2,1,0:T(8,128)(2,1)S(1)}, bf16[4,32,1792]{2,1,0:T(8,128)(2,1)S(1)}, u32[]{:S(2)}, u32[]{:S(2)}) collective-permute-start(bf16[4,32,1792]{2,1,0:T(8,128)(2,1)S(1)} %copy-done.3), channel_id=1, source_target_pairs={{0,6},{1,7},{2,4},{3,5},{4,2},{5,3},{6,0},{7,1},{8,14},{9,15},{10,... | collective-permute-start | bytes 1376264 | tf_op jit(solution)/shard_map/ppermute | solution.py:33
  51.0 84.4 %collective-permute-start.10 = (bf16[4,32,1792]{2,1,0:T(8,128)(2,1)S(1)}, bf16[4,32,1792]{2,1,0:T(8,128)(2,1)S(1)}, u32[]{:S(2)}, u32[]{:S(2)}) collective-permute-start(bf16[4,32,1792]{2,1,0:T(8,128)(2,1)S(1)} %copy-done.2), channel_id=1, source_target_pairs={{0,4},{1,5},{2,6},{3,7},{4,0},{5,1},{6,2},{7,3},{8,12},{9,13},{10,... | collective-permute-start | bytes 1376264 | tf_op jit(solution)/shard_map/ppermute | solution.py:33
  51.2 67.6 %collective-permute-start.16 = (bf16[32,5120]{1,0:T(8,128)(2,1)S(1)}, bf16[32,5120]{1,0:T(8,128)(2,1)S(1)}, u32[]{:S(2)}, u32[]{:S(2)}) collective-permute-start(bf16[32,5120]{1,0:T(8,128)(2,1)S(1)} %get-tuple-element.413), channel_id=1, source_target_pairs={{8,0},{16,8},{9,1},{17,9},{10,2},{18,10},{11,3},{19,11},{12,4},{20... | collective-permute-start | bytes 983048 | tf_op jit(solution)/shard_map/ppermute | solution.py:28
  52.7 73.4 %collective-permute-start.15 = (bf16[32,5120]{1,0:T(8,128)(2,1)S(1)}, bf16[32,5120]{1,0:T(8,128)(2,1)S(1)}, u32[]{:S(2)}, u32[]{:S(2)}) collective-permute-start(bf16[32,5120]{1,0:T(8,128)(2,1)S(1)} %get-tuple-element.412), channel_id=1, source_target_pairs={{8,0},{16,8},{9,1},{17,9},{10,2},{18,10},{11,3},{19,11},{12,4},{20... | collective-permute-start | bytes 983048 | tf_op jit(solution)/shard_map/ppermute | solution.py:28
  121.5 17.1 %collective-permute-start.18 = (bf16[32,5120]{1,0:T(8,128)(2,1)S(1)}, bf16[32,5120]{1,0:T(8,128)(2,1)S(1)}, u32[]{:S(2)}, u32[]{:S(2)}) collective-permute-start(bf16[32,5120]{1,0:T(8,128)(2,1)S(1)} %get-tuple-element.437), channel_id=1, source_target_pairs={{8,0},{9,1},{10,2},{11,3},{12,4},{13,5},{14,6},{15,7}} | collective-permute-start | bytes 983048 | tf_op jit(solution)/shard_map/ppermute | solution.py:28
  126.1 9.4 %copy-start = (bf16[4,32,1792]{2,1,0:T(8,128)(2,1)S(1)}, bf16[4,32,1792]{2,1,0:T(8,128)(2,1)}, u32[]{:S(2)}) copy-start(bf16[4,32,1792]{2,1,0:T(8,128)(2,1)} %get-tuple-element.433) | copy-start | bytes 1376260
  128.8 15.1 %collective-permute-start.23 = (bf16[32,5120]{1,0:T(8,128)(2,1)S(1)}, bf16[32,5120]{1,0:T(8,128)(2,1)S(1)}, u32[]{:S(2)}, u32[]{:S(2)}) collective-permute-start(bf16[32,5120]{1,0:T(8,128)(2,1)S(1)} %get-tuple-element.451), channel_id=1, source_target_pairs={{8,0},{9,1},{10,2},{11,3},{12,4},{13,5},{14,6},{15,7}} | collective-permute-start | bytes 983048 | tf_op jit(solution)/shard_map/ppermute | solution.py:28
  130.1 11.3 %collective-permute-start.24 = (bf16[2,32,2304]{2,1,0:T(8,128)(2,1)}, bf16[2,32,2304]{2,1,0:T(8,128)(2,1)S(1)}, u32[]{:S(2)}, u32[]{:S(2)}) collective-permute-start(bf16[2,32,2304]{2,1,0:T(8,128)(2,1)} %get-tuple-element.453), channel_id=1, source_target_pairs={{0,2},{1,3},{2,0},{3,1},{4,6},{5,7},{6,4},{7,5},{8,10},{9,11},{10,... | collective-permute-start | bytes 884744 | tf_op jit(solution)/shard_map/ppermute | solution.py:33
  132.8 10.7 %collective-permute-start.25 = (bf16[2,32,2304]{2,1,0:T(8,128)(2,1)}, bf16[2,32,2304]{2,1,0:T(8,128)(2,1)S(1)}, u32[]{:S(2)}, u32[]{:S(2)}) collective-permute-start(bf16[2,32,2304]{2,1,0:T(8,128)(2,1)} %get-tuple-element.454), channel_id=1, source_target_pairs={{0,4},{1,5},{2,6},{3,7},{4,0},{5,1},{6,2},{7,3},{8,12},{9,13},{10,... | collective-permute-start | bytes 884744 | tf_op jit(solution)/shard_map/ppermute | solution.py:33
  135.4 8.1 %collective-permute-start.26 = (bf16[2,32,2304]{2,1,0:T(8,128)(2,1)}, bf16[2,32,2304]{2,1,0:T(8,128)(2,1)S(1)}, u32[]{:S(2)}, u32[]{:S(2)}) collective-permute-start(bf16[2,32,2304]{2,1,0:T(8,128)(2,1)} %get-tuple-element.455), channel_id=1, source_target_pairs={{0,6},{1,7},{2,4},{3,5},{4,2},{5,3},{6,0},{7,1},{8,14},{9,15},{10,... | collective-permute-start | bytes 884744 | tf_op jit(solution)/shard_map/ppermute | solution.py:33
  138.6 25.5 %collective-permute-start.17 = (bf16[4,4,32,1792]{3,2,1,0:T(8,128)(2,1)S(1)}, bf16[4,4,32,1792]{3,2,1,0:T(8,128)(2,1)S(1)}, u32[]{:S(2)}, u32[]{:S(2)}) collective-permute-start(bf16[4,4,32,1792]{3,2,1,0:T(8,128)(2,1)S(1)} %pad_maximum_fusion.rest_0_), channel_id=1, source_target_pairs={{0,1},{1,0},{2,3},{3,2},{4,5},{5,4},{6,7},{7,6},{8,9},{9,8},{10,11... | collective-permute-start | bytes 5505032 | tf_op jit(solution)/shard_map/ppermute | solution.py:37
  143.9 6.3 %copy-start.7 = (bf16[1,32,2304]{2,1,0:T(8,128)(2,1)S(1)}, bf16[1,32,2304]{2,1,0:T(8,128)(2,1)}, u32[]{:S(2)}) copy-start(bf16[1,32,2304]{2,1,0:T(8,128)(2,1)} %get-tuple-element.444) | copy-start | bytes 442372
  143.9 9.5 %copy-start.8 = (bf16[1,32,2304]{2,1,0:T(8,128)(2,1)S(1)}, bf16[1,32,2304]{2,1,0:T(8,128)(2,1)}, u32[]{:S(2)}) copy-start(bf16[1,32,2304]{2,1,0:T(8,128)(2,1)} %get-tuple-element.445) | copy-start | bytes 442372
  143.9 13.3 %copy-start.9 = (bf16[1,32,2304]{2,1,0:T(8,128)(2,1)S(1)}, bf16[1,32,2304]{2,1,0:T(8,128)(2,1)}, u32[]{:S(2)}) copy-start(bf16[1,32,2304]{2,1,0:T(8,128)(2,1)} %get-tuple-element.446) | copy-start | bytes 442372
  143.9 14.1 %copy-start.4 = (bf16[2,32,2304]{2,1,0:T(8,128)(2,1)S(1)}, bf16[2,32,2304]{2,1,0:T(8,128)(2,1)}, u32[]{:S(2)}) copy-start(bf16[2,32,2304]{2,1,0:T(8,128)(2,1)} %get-tuple-element.470) | copy-start | bytes 884740
  146.7 16.6 %copy-start.6 = (bf16[1,32,2304]{2,1,0:T(8,128)(2,1)S(1)}, bf16[1,32,2304]{2,1,0:T(8,128)(2,1)}, u32[]{:S(2)}) copy-start(bf16[1,32,2304]{2,1,0:T(8,128)(2,1)} %get-tuple-element.447) | copy-start | bytes 442372
  146.7 6.7 %collective-permute-start.27 = (bf16[1,32,2304]{2,1,0:T(8,128)(2,1)}, bf16[1,32,2304]{2,1,0:T(8,128)(2,1)S(1)}, u32[]{:S(2)}, u32[]{:S(2)}) collective-permute-start(bf16[1,32,2304]{2,1,0:T(8,128)(2,1)} %get-tuple-element.463), channel_id=1, source_target_pairs={{0,2},{1,3},{2,0},{3,1},{4,6},{5,7},{6,4},{7,5},{8,10},{9,11},{10,... | collective-permute-start | bytes 442376 | tf_op jit(solution)/shard_map/ppermute | solution.py:33
  147.8 9.4 %collective-permute-start.28 = (bf16[1,32,2304]{2,1,0:T(8,128)(2,1)}, bf16[1,32,2304]{2,1,0:T(8,128)(2,1)S(1)}, u32[]{:S(2)}, u32[]{:S(2)}) collective-permute-start(bf16[1,32,2304]{2,1,0:T(8,128)(2,1)} %get-tuple-element.464), channel_id=1, source_target_pairs={{0,4},{1,5},{2,6},{3,7},{4,0},{5,1},{6,2},{7,3},{8,12},{9,13},{10,... | collective-permute-start | bytes 442376 | tf_op jit(solution)/shard_map/ppermute | solution.py:33
  149.7 8.5 %collective-permute-start.29 = (bf16[1,32,2304]{2,1,0:T(8,128)(2,1)}, bf16[1,32,2304]{2,1,0:T(8,128)(2,1)S(1)}, u32[]{:S(2)}, u32[]{:S(2)}) collective-permute-start(bf16[1,32,2304]{2,1,0:T(8,128)(2,1)} %get-tuple-element.465), channel_id=1, source_target_pairs={{0,6},{1,7},{2,4},{3,5},{4,2},{5,3},{6,0},{7,1},{8,14},{9,15},{10,... | collective-permute-start | bytes 442376 | tf_op jit(solution)/shard_map/ppermute | solution.py:33
  150.2 9.5 %collective-permute-start.19 = (bf16[1,32,2304]{2,1,0:T(8,128)(2,1)S(1)}, bf16[1,32,2304]{2,1,0:T(8,128)(2,1)S(1)}, u32[]{:S(2)}, u32[]{:S(2)}) collective-permute-start(bf16[1,32,2304]{2,1,0:T(8,128)(2,1)S(1)} %copy-done.7), channel_id=1, source_target_pairs={{0,2},{1,3},{2,0},{3,1},{4,6},{5,7},{6,4},{7,5},{8,10},{9,11},{10,... | collective-permute-start | bytes 442376 | tf_op jit(solution)/shard_map/ppermute | solution.py:33
  153.4 7.3 %collective-permute-start.20 = (bf16[1,32,2304]{2,1,0:T(8,128)(2,1)S(1)}, bf16[1,32,2304]{2,1,0:T(8,128)(2,1)S(1)}, u32[]{:S(2)}, u32[]{:S(2)}) collective-permute-start(bf16[1,32,2304]{2,1,0:T(8,128)(2,1)S(1)} %copy-done.8), channel_id=1, source_target_pairs={{0,4},{1,5},{2,6},{3,7},{4,0},{5,1},{6,2},{7,3},{8,12},{9,13},{10,... | collective-permute-start | bytes 442376 | tf_op jit(solution)/shard_map/ppermute | solution.py:33
  157.2 6.0 %collective-permute-start.21 = (bf16[1,32,2304]{2,1,0:T(8,128)(2,1)S(1)}, bf16[1,32,2304]{2,1,0:T(8,128)(2,1)S(1)}, u32[]{:S(2)}, u32[]{:S(2)}) collective-permute-start(bf16[1,32,2304]{2,1,0:T(8,128)(2,1)S(1)} %copy-done.9), channel_id=1, source_target_pairs={{0,6},{1,7},{2,4},{3,5},{4,2},{5,3},{6,0},{7,1},{8,14},{9,15},{10,... | collective-permute-start | bytes 442376 | tf_op jit(solution)/shard_map/ppermute | solution.py:33
  158.0 5.4 %copy-start.5 = (bf16[1,32,2304]{2,1,0:T(8,128)(2,1)S(1)}, bf16[1,32,2304]{2,1,0:T(8,128)(2,1)}, u32[]{:S(2)}) copy-start(bf16[1,32,2304]{2,1,0:T(8,128)(2,1)} %get-tuple-element.466) | copy-start | bytes 442372
  158.2 5.9 %collective-permute-start.31 = (bf16[4,2,32,2304]{3,2,1,0:T(8,128)(2,1)S(1)}, bf16[4,2,32,2304]{3,2,1,0:T(8,128)(2,1)S(1)}, u32[]{:S(2)}, u32[]{:S(2)}) collective-permute-start(bf16[4,2,32,2304]{3,2,1,0:T(8,128)(2,1)S(1)} %pad_maximum_fusion.1.rest_2_), channel_id=1, source_target_pairs={{0,1},{1,0},{2,3},{3,2},{4,5},{5,4},{6,7},{7,6},{8,9},{9,8},{10,11... | collective-permute-start | bytes 3538952 | tf_op jit(solution)/shard_map/ppermute | solution.py:37
  163.4 2.4 %collective-permute-start.22 = (bf16[4,1,32,2304]{3,2,1,0:T(8,128)(2,1)S(1)}, bf16[4,1,32,2304]{3,2,1,0:T(8,128)(2,1)S(1)}, u32[]{:S(2)}, u32[]{:S(2)}) collective-permute-start(bf16[4,1,32,2304]{3,2,1,0:T(8,128)(2,1)S(1)} %pad_maximum_fusion.2.rest_2_), channel_id=1, source_target_pairs={{0,1},{1,0},{2,3},{3,2},{4,5},{5,4},{6,7},{7,6},{8,9},{9,8},{10,11... | collective-permute-start | bytes 1769480 | tf_op jit(solution)/shard_map/ppermute | solution.py:37
  163.5 2.7 %collective-permute-start.30 = (bf16[4,1,32,2304]{3,2,1,0:T(8,128)(2,1)S(1)}, bf16[4,1,32,2304]{3,2,1,0:T(8,128)(2,1)S(1)}, u32[]{:S(2)}, u32[]{:S(2)}) collective-permute-start(bf16[4,1,32,2304]{3,2,1,0:T(8,128)(2,1)S(1)} %pad_maximum_fusion.3.rest_4_), channel_id=1, source_target_pairs={{0,1},{1,0},{2,3},{3,2},{4,5},{5,4},{6,7},{7,6},{8,9},{9,8},{10,11... | collective-permute-start | bytes 1769480 | tf_op jit(solution)/shard_map/ppermute | solution.py:37
